TPU v7x, 256 devices: a whole 4x4x8 slice. The times are simulated.
256 devices in a mesh: tm: 64 (over y_hi, x, z), slab: 4 (over y_lo, core).
Axes of the slice: x: 4, y: 4 (y_hi: 2, y_lo: 2; y = y_hi * 2 + y_lo), z: 8, core: 2. Of those that a mesh axis runs over, the one named last changes fastest.
Arguments:
- adjoint_end: float32 [64, 32, 32, 512], P('tm', 'slab'), may hold values from -6 to 6
- forcing: float32 [64, 32, 32, 512], P('tm', 'slab'), may hold values from -0.5 to 0.5
- velocity: float32 [3, 32, 32, 512], P(None, 'slab'), may hold values from -0.1 to 0.1
- uptake: float32 [32, 32, 512], P('slab'), may hold values from 0.0005 to 0.04
Outputs:
- corrected: float32 [64, 32, 32, 512], P('tm', 'slab')
- coarse_new: float32 [64, 8, 8, 128], P('tm')
All inputs are finite; a program needn't handle non-finite values.
Results may differ from a plain program's by a relative error of at most 0.00002.
Values sent between devices are 32-bit elements; how exact they have to be, the bound alone decides.
No kernel may reach another device: no remote copies, remote signals or barrier semaphores. Data moves between devices by JAX's collectives and lax.ppermute only.
A program may use at most 256 MiB of HBM per device.

v0:
```python
import jax
import jax.numpy as jnp
from jax import lax
from jax.sharding import PartitionSpec as P

STEPS = 8


diffusion_fine = 0.15
diffusion_coarse = 0.0375


def extended_2(block, sides, width):
    for axis, dim in sides:
        count = lax.axis_size(axis)
        forward = [(i, i + 1) for i in range(count - 1)]
        backward = [(target, source) for source, target in forward]
        low = lax.ppermute(
            lax.slice_in_dim(block, block.shape[dim] - width, None, axis=dim), axis, forward
        )
        high = lax.ppermute(lax.slice_in_dim(block, 0, width, axis=dim), axis, backward)
        block = jnp.concatenate([low, block, high], axis=dim)
    return block


def passed_along(block, axis, distance):
    devices = range(lax.axis_size(axis))
    route = [(i - distance, i) for i in devices if i - distance in devices]
    return lax.ppermute(block, axis, route)


def restrict(grid_field):
    shape_now = grid_field.shape
    blocked = grid_field.reshape(shape_now[0] // 4, 4, shape_now[1] // 4, 4, shape_now[2] // 4, 4)
    return jnp.mean(blocked, axis=(1, 3, 5))


def prolong(grid_field):
    return jnp.repeat(jnp.repeat(jnp.repeat(grid_field, 4, axis=0), 4, axis=1), 4, axis=2)


def fine_step(extended, velocity, uptake, source_slice):
    center = extended[1:-1]
    padded = jnp.pad(center, ((0, 0), (1, 1), (1, 1)))
    upper_z = extended[2:]
    lower_z = extended[:-2]
    upper_y = padded[:, 2:, 1:-1]
    lower_y = padded[:, :-2, 1:-1]
    upper_x = padded[:, 1:-1, 2:]
    lower_x = padded[:, 1:-1, :-2]
    spread = upper_z + lower_z + upper_y + lower_y + upper_x + lower_x - 6.0 * center
    carried = (
        velocity[0] * (upper_z - lower_z)
        + velocity[1] * (upper_y - lower_y)
        + velocity[2] * (upper_x - lower_x)
    )
    return center + diffusion_fine * spread + 0.5 * carried - uptake * center + source_slice


def coarse_half(coarse_field, coarse_velocity, coarse_uptake):
    padded = jnp.pad(coarse_field, 1)
    neighbours = (
        (padded[2:, 1:-1, 1:-1], padded[:-2, 1:-1, 1:-1]),
        (padded[1:-1, 2:, 1:-1], padded[1:-1, :-2, 1:-1]),
        (padded[1:-1, 1:-1, 2:], padded[1:-1, 1:-1, :-2]),
    )
    spread = -6.0 * coarse_field
    carried = jnp.zeros_like(coarse_field)
    for axis_no in range(3):
        upper_side, lower_side = neighbours[axis_no]
        spread = spread + upper_side + lower_side
        advect = coarse_velocity[axis_no]
        carried = (
            carried
            + jnp.maximum(advect, 0.0) * (upper_side - coarse_field)
            + jnp.minimum(advect, 0.0) * (coarse_field - lower_side)
        )
    return coarse_field + diffusion_coarse * spread + carried - 4.0 * coarse_uptake * coarse_field


def coarse_step(coarse_field, coarse_velocity, coarse_uptake):
    halfway = coarse_half(coarse_field, coarse_velocity, coarse_uptake)
    return coarse_half(halfway, coarse_velocity, coarse_uptake)


def per_device(adjoint_end, forcing, velocity, uptake):
    start_state = adjoint_end[0]
    source_slice = forcing[0]
    slab_no = lax.axis_index("slab")
    slab_depth = start_state.shape[0]
    adjoint = start_state
    for step_no in range(STEPS):
        extended = extended_2(adjoint, (("slab", 0),), 1)
        adjoint = fine_step(extended, velocity, uptake, source_slice)
    local_stack = jnp.stack(
        [
            restrict(adjoint),
            restrict(start_state),
            restrict(velocity[0]),
            restrict(velocity[1]),
            restrict(velocity[2]),
            restrict(uptake),
        ]
    )
    gathered = lax.all_gather(local_stack, "slab", axis=1, tiled=True)
    coarse_prop = gathered[0]
    coarse_end = gathered[1]
    coarse_velocity = gathered[2:5]
    coarse_uptake = gathered[5]
    stepped_end = coarse_step(coarse_end, coarse_velocity, coarse_uptake)
    jump_here = coarse_prop - stepped_end
    time_count = lax.axis_size("tm")
    time_no = lax.axis_index("tm")
    at_end = time_no == time_count - 1

    def relay_turn(turn_no, inbound):
        arrived = passed_along(
            coarse_step(inbound, coarse_velocity, coarse_uptake) + jump_here, "tm", -1
        )
        return jnp.where(at_end, inbound, arrived)

    inbound = lax.fori_loop(0, time_count - 1, relay_turn, coarse_end)
    advanced = coarse_step(inbound, coarse_velocity, coarse_uptake)
    coarse_new = advanced + jump_here
    coarse_depth = slab_depth // 4
    slab_part = lax.dynamic_slice_in_dim(
        advanced - stepped_end, slab_no * coarse_depth, coarse_depth, 0
    )
    corrected = adjoint + prolong(slab_part)
    return (corrected[None], coarse_new[None])


def solution(mesh):
    in_specs = (
        P("tm", "slab", None, None),
        P("tm", "slab", None, None),
        P(None, "slab", None, None),
        P("slab", None, None),
    )
    out_specs = (P("tm", "slab", None, None), P("tm", None, None, None))
    return jax.shard_map(
        per_device, mesh=mesh, in_specs=in_specs, out_specs=out_specs, check_vma=False
    )
```

profile of v0, /device:TPU:24, one launch (start us, length us, event | category | flops | bytes accessed | tf_op | source)
XLA Modules:
  0.0 978.8 jit_solution(2124854432151862512)
XLA Ops:
  68.9 18.6 %reshape_squeeze.12 = f32[2,4,8,4,128,4]{5,4,3,2,1,0:T(8,128)} reshape(f32[1,8,32,512]{3,2,1,0:T(8,128)S(1)} %copy-done.3) | data formatting | bytes 1048576 | tf_op jit(solution)/shard_map/reshape;squeeze | solution.py:34
  87.5 18.6 %reshape.100 = f32[2,4,8,4,128,4]{5,4,3,2,1,0:T(8,128)} reshape(f32[8,32,512]{2,1,0:T(8,128)S(1)} %copy-done.1) | data formatting | bytes 1048576 | tf_op jit(solution)/shard_map/reshape | solution.py:34
  106.1 19.5 %reshape_squeeze.15 = f32[2,4,8,4,128,4]{5,4,3,2,1,0:T(8,128)} reshape(f32[1,8,32,512]{3,2,1,0:T(8,128)} %get-tuple-element.104) | data formatting | bytes 1048576 | tf_op jit(solution)/shard_map/reshape;squeeze | solution.py:34
  125.6 18.6 %reshape_squeeze.13 = f32[2,4,8,4,128,4]{5,4,3,2,1,0:T(8,128)} reshape(f32[1,8,32,512]{3,2,1,0:T(8,128)S(1)} %copy-done.6) | data formatting | bytes 1048576 | tf_op jit(solution)/shard_map/reshape;squeeze | solution.py:34
  158.2 18.7 %reshape_squeeze.14 = f32[2,4,8,4,128,4]{5,4,3,2,1,0:T(8,128)} reshape(f32[1,8,32,512]{3,2,1,0:T(8,128)S(1)} %copy-done.5) | data formatting | bytes 1048576 | tf_op jit(solution)/shard_map/reshape;squeeze | solution.py:34
  201.1 18.6 %reshape.99 = f32[2,4,8,4,128,4]{5,4,3,2,1,0:T(8,128)} reshape(f32[8,32,512]{2,1,0:T(8,128)S(1)} %bitcast_add_fusion) | data formatting | bytes 1048576 | tf_op jit(solution)/shard_map/reshape | solution.py:34
  232.6 740.5 %while.12 = (s32[]{:T(128)}, f32[8,8,128]{2,1,0:T(8,128)S(1)}, pred[]{:T(512)}, f32[3,8,8,128]{3,2,1,0:T(8,128)S(1)}, f32[8,8,128]{2,1,0:T(8,128)S(1)}, /*index=5*/f32[8,8,128]{2,1,0:T(8,128)S(1)}, s32[]{:T(128)}) while((s32[]{:T(128)}, f32[8,8,128]{2,1,0:T(8,128)S(1)}, pred[]{:T(512)}, f32[3,8,8,128]{3,2,1,0:T(8,128)S(1)}, ...), condition=%wide.region_7.8_spmd, body=%wide.region_6.7_spmd.sunk | while | flops 606210 | bytes 655478 | solution.py:122
  232.8 10.6 %collective-permute-start = (f32[8,8,128]{2,1,0:T(8,128)S(1)}, f32[8,8,128]{2,1,0:T(8,128)S(1)}, u32[]{:S(2)}, u32[]{:S(2)}) collective-permute-start(f32[8,8,128]{2,1,0:T(8,128)S(1)} %fusion.97), channel_id=1, source_target_pairs={{4,0},{8,4},{12,8},{16,12},{20,16},{24,20},{28,24},{32,28},{36,32}... | collective-permute-start | bytes 98312 | tf_op jit(solution)/shard_map/while/body/eval_jaxpr/ppermute | solution.py:29
  245.2 9.9 %collective-permute-start = (f32[8,8,128]{2,1,0:T(8,128)S(1)}, f32[8,8,128]{2,1,0:T(8,128)S(1)}, u32[]{:S(2)}, u32[]{:S(2)}) collective-permute-start(f32[8,8,128]{2,1,0:T(8,128)S(1)} %fusion.97), channel_id=1, source_target_pairs={{4,0},{8,4},{12,8},{16,12},{20,16},{24,20},{28,24},{32,28},{36,32}... | collective-permute-start | bytes 98312 | tf_op jit(solution)/shard_map/while/body/eval_jaxpr/ppermute | solution.py:29
  257.0 9.9 %collective-permute-start = (f32[8,8,128]{2,1,0:T(8,128)S(1)}, f32[8,8,128]{2,1,0:T(8,128)S(1)}, u32[]{:S(2)}, u32[]{:S(2)}) collective-permute-start(f32[8,8,128]{2,1,0:T(8,128)S(1)} %fusion.97), channel_id=1, source_target_pairs={{4,0},{8,4},{12,8},{16,12},{20,16},{24,20},{28,24},{32,28},{36,32}... | collective-permute-start | bytes 98312 | tf_op jit(solution)/shard_map/while/body/eval_jaxpr/ppermute | solution.py:29
  268.7 9.9 %collective-permute-start = (f32[8,8,128]{2,1,0:T(8,128)S(1)}, f32[8,8,128]{2,1,0:T(8,128)S(1)}, u32[]{:S(2)}, u32[]{:S(2)}) collective-permute-start(f32[8,8,128]{2,1,0:T(8,128)S(1)} %fusion.97), channel_id=1, source_target_pairs={{4,0},{8,4},{12,8},{16,12},{20,16},{24,20},{28,24},{32,28},{36,32}... | collective-permute-start | bytes 98312 | tf_op jit(solution)/shard_map/while/body/eval_jaxpr/ppermute | solution.py:29
  280.4 9.9 %collective-permute-start = (f32[8,8,128]{2,1,0:T(8,128)S(1)}, f32[8,8,128]{2,1,0:T(8,128)S(1)}, u32[]{:S(2)}, u32[]{:S(2)}) collective-permute-start(f32[8,8,128]{2,1,0:T(8,128)S(1)} %fusion.97), channel_id=1, source_target_pairs={{4,0},{8,4},{12,8},{16,12},{20,16},{24,20},{28,24},{32,28},{36,32}... | collective-permute-start | bytes 98312 | tf_op jit(solution)/shard_map/while/body/eval_jaxpr/ppermute | solution.py:29
  292.2 9.9 %collective-permute-start = (f32[8,8,128]{2,1,0:T(8,128)S(1)}, f32[8,8,128]{2,1,0:T(8,128)S(1)}, u32[]{:S(2)}, u32[]{:S(2)}) collective-permute-start(f32[8,8,128]{2,1,0:T(8,128)S(1)} %fusion.97), channel_id=1, source_target_pairs={{4,0},{8,4},{12,8},{16,12},{20,16},{24,20},{28,24},{32,28},{36,32}... | collective-permute-start | bytes 98312 | tf_op jit(solution)/shard_map/while/body/eval_jaxpr/ppermute | solution.py:29
  303.9 9.9 %collective-permute-start = (f32[8,8,128]{2,1,0:T(8,128)S(1)}, f32[8,8,128]{2,1,0:T(8,128)S(1)}, u32[]{:S(2)}, u32[]{:S(2)}) collective-permute-start(f32[8,8,128]{2,1,0:T(8,128)S(1)} %fusion.97), channel_id=1, source_target_pairs={{4,0},{8,4},{12,8},{16,12},{20,16},{24,20},{28,24},{32,28},{36,32}... | collective-permute-start | bytes 98312 | tf_op jit(solution)/shard_map/while/body/eval_jaxpr/ppermute | solution.py:29
  315.6 9.9 %collective-permute-start = (f32[8,8,128]{2,1,0:T(8,128)S(1)}, f32[8,8,128]{2,1,0:T(8,128)S(1)}, u32[]{:S(2)}, u32[]{:S(2)}) collective-permute-start(f32[8,8,128]{2,1,0:T(8,128)S(1)} %fusion.97), channel_id=1, source_target_pairs={{4,0},{8,4},{12,8},{16,12},{20,16},{24,20},{28,24},{32,28},{36,32}... | collective-permute-start | bytes 98312 | tf_op jit(solution)/shard_map/while/body/eval_jaxpr/ppermute | solution.py:29
  327.4 9.9 %collective-permute-start = (f32[8,8,128]{2,1,0:T(8,128)S(1)}, f32[8,8,128]{2,1,0:T(8,128)S(1)}, u32[]{:S(2)}, u32[]{:S(2)}) collective-permute-start(f32[8,8,128]{2,1,0:T(8,128)S(1)} %fusion.97), channel_id=1, source_target_pairs={{4,0},{8,4},{12,8},{16,12},{20,16},{24,20},{28,24},{32,28},{36,32}... | collective-permute-start | bytes 98312 | tf_op jit(solution)/shard_map/while/body/eval_jaxpr/ppermute | solution.py:29
  339.1 9.9 %collective-permute-start = (f32[8,8,128]{2,1,0:T(8,128)S(1)}, f32[8,8,128]{2,1,0:T(8,128)S(1)}, u32[]{:S(2)}, u32[]{:S(2)}) collective-permute-start(f32[8,8,128]{2,1,0:T(8,128)S(1)} %fusion.97), channel_id=1, source_target_pairs={{4,0},{8,4},{12,8},{16,12},{20,16},{24,20},{28,24},{32,28},{36,32}... | collective-permute-start | bytes 98312 | tf_op jit(solution)/shard_map/while/body/eval_jaxpr/ppermute | solution.py:29
  350.9 9.9 %collective-permute-start = (f32[8,8,128]{2,1,0:T(8,128)S(1)}, f32[8,8,128]{2,1,0:T(8,128)S(1)}, u32[]{:S(2)}, u32[]{:S(2)}) collective-permute-start(f32[8,8,128]{2,1,0:T(8,128)S(1)} %fusion.97), channel_id=1, source_target_pairs={{4,0},{8,4},{12,8},{16,12},{20,16},{24,20},{28,24},{32,28},{36,32}... | collective-permute-start | bytes 98312 | tf_op jit(solution)/shard_map/while/body/eval_jaxpr/ppermute | solution.py:29
  362.6 9.9 %collective-permute-start = (f32[8,8,128]{2,1,0:T(8,128)S(1)}, f32[8,8,128]{2,1,0:T(8,128)S(1)}, u32[]{:S(2)}, u32[]{:S(2)}) collective-permute-start(f32[8,8,128]{2,1,0:T(8,128)S(1)} %fusion.97), channel_id=1, source_target_pairs={{4,0},{8,4},{12,8},{16,12},{20,16},{24,20},{28,24},{32,28},{36,32}... | collective-permute-start | bytes 98312 | tf_op jit(solution)/shard_map/while/body/eval_jaxpr/ppermute | solution.py:29
  456.5 10.1 %collective-permute-start = (f32[8,8,128]{2,1,0:T(8,128)S(1)}, f32[8,8,128]{2,1,0:T(8,128)S(1)}, u32[]{:S(2)}, u32[]{:S(2)}) collective-permute-start(f32[8,8,128]{2,1,0:T(8,128)S(1)} %fusion.97), channel_id=1, source_target_pairs={{4,0},{8,4},{12,8},{16,12},{20,16},{24,20},{28,24},{32,28},{36,32}... | collective-permute-start | bytes 98312 | tf_op jit(solution)/shard_map/while/body/eval_jaxpr/ppermute | solution.py:29
  668.0 9.9 %collective-permute-start = (f32[8,8,128]{2,1,0:T(8,128)S(1)}, f32[8,8,128]{2,1,0:T(8,128)S(1)}, u32[]{:S(2)}, u32[]{:S(2)}) collective-permute-start(f32[8,8,128]{2,1,0:T(8,128)S(1)} %fusion.97), channel_id=1, source_target_pairs={{4,0},{8,4},{12,8},{16,12},{20,16},{24,20},{28,24},{32,28},{36,32}... | collective-permute-start | bytes 98312 | tf_op jit(solution)/shard_map/while/body/eval_jaxpr/ppermute | solution.py:29
  785.4 10.0 %collective-permute-start = (f32[8,8,128]{2,1,0:T(8,128)S(1)}, f32[8,8,128]{2,1,0:T(8,128)S(1)}, u32[]{:S(2)}, u32[]{:S(2)}) collective-permute-start(f32[8,8,128]{2,1,0:T(8,128)S(1)} %fusion.97), channel_id=1, source_target_pairs={{4,0},{8,4},{12,8},{16,12},{20,16},{24,20},{28,24},{32,28},{36,32}... | collective-permute-start | bytes 98312 | tf_op jit(solution)/shard_map/while/body/eval_jaxpr/ppermute | solution.py:29
  808.9 9.9 %collective-permute-start = (f32[8,8,128]{2,1,0:T(8,128)S(1)}, f32[8,8,128]{2,1,0:T(8,128)S(1)}, u32[]{:S(2)}, u32[]{:S(2)}) collective-permute-start(f32[8,8,128]{2,1,0:T(8,128)S(1)} %fusion.97), channel_id=1, source_target_pairs={{4,0},{8,4},{12,8},{16,12},{20,16},{24,20},{28,24},{32,28},{36,32}... | collective-permute-start | bytes 98312 | tf_op jit(solution)/shard_map/while/body/eval_jaxpr/ppermute | solution.py:29
  891.1 10.0 %collective-permute-start = (f32[8,8,128]{2,1,0:T(8,128)S(1)}, f32[8,8,128]{2,1,0:T(8,128)S(1)}, u32[]{:S(2)}, u32[]{:S(2)}) collective-permute-start(f32[8,8,128]{2,1,0:T(8,128)S(1)} %fusion.97), channel_id=1, source_target_pairs={{4,0},{8,4},{12,8},{16,12},{20,16},{24,20},{28,24},{32,28},{36,32}... | collective-permute-start | bytes 98312 | tf_op jit(solution)/shard_map/while/body/eval_jaxpr/ppermute | solution.py:29
  (388 shorter events, 694.0 us)
Async XLA Ops:
  61.7 136.0 %collective-permute-start.16 = (f32[1,32,512]{2,1,0:T(8,128)S(1)}, f32[1,32,512]{2,1,0:T(8,128)S(1)}, u32[]{:S(2)}, u32[]{:S(2)}) collective-permute-start(f32[1,32,512]{2,1,0:T(8,128)S(1)} %get-tuple-element.107), channel_id=1, source_target_pairs={{0,1},{1,2},{2,3},{4,5},{5,6},{6,7},{8,9},{9,10},{10,11},{12,13},{... | collective-permute-start | bytes 196616 | tf_op jit(solution)/shard_map/ppermute | solution.py:18
  63.7 134.1 %collective-permute-start.15 = (f32[1,32,512]{2,1,0:T(8,128)S(1)}, f32[1,32,512]{2,1,0:T(8,128)S(1)}, u32[]{:S(2)}, u32[]{:S(2)}) collective-permute-start(f32[1,32,512]{2,1,0:T(8,128)S(1)} %get-tuple-element.108), channel_id=1, source_target_pairs={{1,0},{2,1},{3,2},{5,4},{6,5},{7,6},{9,8},{10,9},{11,10},{13,12},{... | collective-permute-start | bytes 196616 | tf_op jit(solution)/shard_map/ppermute | solution.py:21
  232.8 12.2 %collective-permute-start = (f32[8,8,128]{2,1,0:T(8,128)S(1)}, f32[8,8,128]{2,1,0:T(8,128)S(1)}, u32[]{:S(2)}, u32[]{:S(2)}) collective-permute-start(f32[8,8,128]{2,1,0:T(8,128)S(1)} %fusion.97), channel_id=1, source_target_pairs={{4,0},{8,4},{12,8},{16,12},{20,16},{24,20},{28,24},{32,28},{36,32}... | collective-permute-start | bytes 98312 | tf_op jit(solution)/shard_map/while/body/eval_jaxpr/ppermute | solution.py:29
  245.2 11.5 %collective-permute-start = (f32[8,8,128]{2,1,0:T(8,128)S(1)}, f32[8,8,128]{2,1,0:T(8,128)S(1)}, u32[]{:S(2)}, u32[]{:S(2)}) collective-permute-start(f32[8,8,128]{2,1,0:T(8,128)S(1)} %fusion.97), channel_id=1, source_target_pairs={{4,0},{8,4},{12,8},{16,12},{20,16},{24,20},{28,24},{32,28},{36,32}... | collective-permute-start | bytes 98312 | tf_op jit(solution)/shard_map/while/body/eval_jaxpr/ppermute | solution.py:29
  292.2 11.5 %collective-permute-start = (f32[8,8,128]{2,1,0:T(8,128)S(1)}, f32[8,8,128]{2,1,0:T(8,128)S(1)}, u32[]{:S(2)}, u32[]{:S(2)}) collective-permute-start(f32[8,8,128]{2,1,0:T(8,128)S(1)} %fusion.97), channel_id=1, source_target_pairs={{4,0},{8,4},{12,8},{16,12},{20,16},{24,20},{28,24},{32,28},{36,32}... | collective-permute-start | bytes 98312 | tf_op jit(solution)/shard_map/while/body/eval_jaxpr/ppermute | solution.py:29
  350.9 11.5 %collective-permute-start = (f32[8,8,128]{2,1,0:T(8,128)S(1)}, f32[8,8,128]{2,1,0:T(8,128)S(1)}, u32[]{:S(2)}, u32[]{:S(2)}) collective-permute-start(f32[8,8,128]{2,1,0:T(8,128)S(1)} %fusion.97), channel_id=1, source_target_pairs={{4,0},{8,4},{12,8},{16,12},{20,16},{24,20},{28,24},{32,28},{36,32}... | collective-permute-start | bytes 98312 | tf_op jit(solution)/shard_map/while/body/eval_jaxpr/ppermute | solution.py:29
  374.3 11.5 %collective-permute-start = (f32[8,8,128]{2,1,0:T(8,128)S(1)}, f32[8,8,128]{2,1,0:T(8,128)S(1)}, u32[]{:S(2)}, u32[]{:S(2)}) collective-permute-start(f32[8,8,128]{2,1,0:T(8,128)S(1)} %fusion.97), channel_id=1, source_target_pairs={{4,0},{8,4},{12,8},{16,12},{20,16},{24,20},{28,24},{32,28},{36,32}... | collective-permute-start | bytes 98312 | tf_op jit(solution)/shard_map/while/body/eval_jaxpr/ppermute | solution.py:29
  433.0 11.5 %collective-permute-start = (f32[8,8,128]{2,1,0:T(8,128)S(1)}, f32[8,8,128]{2,1,0:T(8,128)S(1)}, u32[]{:S(2)}, u32[]{:S(2)}) collective-permute-start(f32[8,8,128]{2,1,0:T(8,128)S(1)} %fusion.97), channel_id=1, source_target_pairs={{4,0},{8,4},{12,8},{16,12},{20,16},{24,20},{28,24},{32,28},{36,32}... | collective-permute-start | bytes 98312 | tf_op jit(solution)/shard_map/while/body/eval_jaxpr/ppermute | solution.py:29
  444.8 11.6 %collective-permute-start = (f32[8,8,128]{2,1,0:T(8,128)S(1)}, f32[8,8,128]{2,1,0:T(8,128)S(1)}, u32[]{:S(2)}, u32[]{:S(2)}) collective-permute-start(f32[8,8,128]{2,1,0:T(8,128)S(1)} %fusion.97), channel_id=1, source_target_pairs={{4,0},{8,4},{12,8},{16,12},{20,16},{24,20},{28,24},{32,28},{36,32}... | collective-permute-start | bytes 98312 | tf_op jit(solution)/shard_map/while/body/eval_jaxpr/ppermute | solution.py:29
  456.5 11.7 %collective-permute-start = (f32[8,8,128]{2,1,0:T(8,128)S(1)}, f32[8,8,128]{2,1,0:T(8,128)S(1)}, u32[]{:S(2)}, u32[]{:S(2)}) collective-permute-start(f32[8,8,128]{2,1,0:T(8,128)S(1)} %fusion.97), channel_id=1, source_target_pairs={{4,0},{8,4},{12,8},{16,12},{20,16},{24,20},{28,24},{32,28},{36,32}... | collective-permute-start | bytes 98312 | tf_op jit(solution)/shard_map/while/body/eval_jaxpr/ppermute | solution.py:29
  468.4 11.5 %collective-permute-start = (f32[8,8,128]{2,1,0:T(8,128)S(1)}, f32[8,8,128]{2,1,0:T(8,128)S(1)}, u32[]{:S(2)}, u32[]{:S(2)}) collective-permute-start(f32[8,8,128]{2,1,0:T(8,128)S(1)} %fusion.97), channel_id=1, source_target_pairs={{4,0},{8,4},{12,8},{16,12},{20,16},{24,20},{28,24},{32,28},{36,32}... | collective-permute-start | bytes 98312 | tf_op jit(solution)/shard_map/while/body/eval_jaxpr/ppermute | solution.py:29
  527.1 11.5 %collective-permute-start = (f32[8,8,128]{2,1,0:T(8,128)S(1)}, f32[8,8,128]{2,1,0:T(8,128)S(1)}, u32[]{:S(2)}, u32[]{:S(2)}) collective-permute-start(f32[8,8,128]{2,1,0:T(8,128)S(1)} %fusion.97), channel_id=1, source_target_pairs={{4,0},{8,4},{12,8},{16,12},{20,16},{24,20},{28,24},{32,28},{36,32}... | collective-permute-start | bytes 98312 | tf_op jit(solution)/shard_map/while/body/eval_jaxpr/ppermute | solution.py:29
  550.6 11.5 %collective-permute-start = (f32[8,8,128]{2,1,0:T(8,128)S(1)}, f32[8,8,128]{2,1,0:T(8,128)S(1)}, u32[]{:S(2)}, u32[]{:S(2)}) collective-permute-start(f32[8,8,128]{2,1,0:T(8,128)S(1)} %fusion.97), channel_id=1, source_target_pairs={{4,0},{8,4},{12,8},{16,12},{20,16},{24,20},{28,24},{32,28},{36,32}... | collective-permute-start | bytes 98312 | tf_op jit(solution)/shard_map/while/body/eval_jaxpr/ppermute | solution.py:29
  609.3 11.5 %collective-permute-start = (f32[8,8,128]{2,1,0:T(8,128)S(1)}, f32[8,8,128]{2,1,0:T(8,128)S(1)}, u32[]{:S(2)}, u32[]{:S(2)}) collective-permute-start(f32[8,8,128]{2,1,0:T(8,128)S(1)} %fusion.97), channel_id=1, source_target_pairs={{4,0},{8,4},{12,8},{16,12},{20,16},{24,20},{28,24},{32,28},{36,32}... | collective-permute-start | bytes 98312 | tf_op jit(solution)/shard_map/while/body/eval_jaxpr/ppermute | solution.py:29
  668.0 11.5 %collective-permute-start = (f32[8,8,128]{2,1,0:T(8,128)S(1)}, f32[8,8,128]{2,1,0:T(8,128)S(1)}, u32[]{:S(2)}, u32[]{:S(2)}) collective-permute-start(f32[8,8,128]{2,1,0:T(8,128)S(1)} %fusion.97), channel_id=1, source_target_pairs={{4,0},{8,4},{12,8},{16,12},{20,16},{24,20},{28,24},{32,28},{36,32}... | collective-permute-start | bytes 98312 | tf_op jit(solution)/shard_map/while/body/eval_jaxpr/ppermute | solution.py:29
  691.5 11.5 %collective-permute-start = (f32[8,8,128]{2,1,0:T(8,128)S(1)}, f32[8,8,128]{2,1,0:T(8,128)S(1)}, u32[]{:S(2)}, u32[]{:S(2)}) collective-permute-start(f32[8,8,128]{2,1,0:T(8,128)S(1)} %fusion.97), channel_id=1, source_target_pairs={{4,0},{8,4},{12,8},{16,12},{20,16},{24,20},{28,24},{32,28},{36,32}... | collective-permute-start | bytes 98312 | tf_op jit(solution)/shard_map/while/body/eval_jaxpr/ppermute | solution.py:29
  750.1 11.5 %collective-permute-start = (f32[8,8,128]{2,1,0:T(8,128)S(1)}, f32[8,8,128]{2,1,0:T(8,128)S(1)}, u32[]{:S(2)}, u32[]{:S(2)}) collective-permute-start(f32[8,8,128]{2,1,0:T(8,128)S(1)} %fusion.97), channel_id=1, source_target_pairs={{4,0},{8,4},{12,8},{16,12},{20,16},{24,20},{28,24},{32,28},{36,32}... | collective-permute-start | bytes 98312 | tf_op jit(solution)/shard_map/while/body/eval_jaxpr/ppermute | solution.py:29
  773.6 11.5 %collective-permute-start = (f32[8,8,128]{2,1,0:T(8,128)S(1)}, f32[8,8,128]{2,1,0:T(8,128)S(1)}, u32[]{:S(2)}, u32[]{:S(2)}) collective-permute-start(f32[8,8,128]{2,1,0:T(8,128)S(1)} %fusion.97), channel_id=1, source_target_pairs={{4,0},{8,4},{12,8},{16,12},{20,16},{24,20},{28,24},{32,28},{36,32}... | collective-permute-start | bytes 98312 | tf_op jit(solution)/shard_map/while/body/eval_jaxpr/ppermute | solution.py:29
  785.4 11.6 %collective-permute-start = (f32[8,8,128]{2,1,0:T(8,128)S(1)}, f32[8,8,128]{2,1,0:T(8,128)S(1)}, u32[]{:S(2)}, u32[]{:S(2)}) collective-permute-start(f32[8,8,128]{2,1,0:T(8,128)S(1)} %fusion.97), channel_id=1, source_target_pairs={{4,0},{8,4},{12,8},{16,12},{20,16},{24,20},{28,24},{32,28},{36,32}... | collective-permute-start | bytes 98312 | tf_op jit(solution)/shard_map/while/body/eval_jaxpr/ppermute | solution.py:29
  808.9 11.5 %collective-permute-start = (f32[8,8,128]{2,1,0:T(8,128)S(1)}, f32[8,8,128]{2,1,0:T(8,128)S(1)}, u32[]{:S(2)}, u32[]{:S(2)}) collective-permute-start(f32[8,8,128]{2,1,0:T(8,128)S(1)} %fusion.97), channel_id=1, source_target_pairs={{4,0},{8,4},{12,8},{16,12},{20,16},{24,20},{28,24},{32,28},{36,32}... | collective-permute-start | bytes 98312 | tf_op jit(solution)/shard_map/while/body/eval_jaxpr/ppermute | solution.py:29
  832.4 11.5 %collective-permute-start = (f32[8,8,128]{2,1,0:T(8,128)S(1)}, f32[8,8,128]{2,1,0:T(8,128)S(1)}, u32[]{:S(2)}, u32[]{:S(2)}) collective-permute-start(f32[8,8,128]{2,1,0:T(8,128)S(1)} %fusion.97), channel_id=1, source_target_pairs={{4,0},{8,4},{12,8},{16,12},{20,16},{24,20},{28,24},{32,28},{36,32}... | collective-permute-start | bytes 98312 | tf_op jit(solution)/shard_map/while/body/eval_jaxpr/ppermute | solution.py:29
  891.1 11.6 %collective-permute-start = (f32[8,8,128]{2,1,0:T(8,128)S(1)}, f32[8,8,128]{2,1,0:T(8,128)S(1)}, u32[]{:S(2)}, u32[]{:S(2)}) collective-permute-start(f32[8,8,128]{2,1,0:T(8,128)S(1)} %fusion.97), channel_id=1, source_target_pairs={{4,0},{8,4},{12,8},{16,12},{20,16},{24,20},{28,24},{32,28},{36,32}... | collective-permute-start | bytes 98312 | tf_op jit(solution)/shard_map/while/body/eval_jaxpr/ppermute | solution.py:29
  902.9 11.5 %collective-permute-start = (f32[8,8,128]{2,1,0:T(8,128)S(1)}, f32[8,8,128]{2,1,0:T(8,128)S(1)}, u32[]{:S(2)}, u32[]{:S(2)}) collective-permute-start(f32[8,8,128]{2,1,0:T(8,128)S(1)} %fusion.97), channel_id=1, source_target_pairs={{4,0},{8,4},{12,8},{16,12},{20,16},{24,20},{28,24},{32,28},{36,32}... | collective-permute-start | bytes 98312 | tf_op jit(solution)/shard_map/while/body/eval_jaxpr/ppermute | solution.py:29
  961.6 11.5 %collective-permute-start = (f32[8,8,128]{2,1,0:T(8,128)S(1)}, f32[8,8,128]{2,1,0:T(8,128)S(1)}, u32[]{:S(2)}, u32[]{:S(2)}) collective-permute-start(f32[8,8,128]{2,1,0:T(8,128)S(1)} %fusion.97), channel_id=1, source_target_pairs={{4,0},{8,4},{12,8},{16,12},{20,16},{24,20},{28,24},{32,28},{36,32}... | collective-permute-start | bytes 98312 | tf_op jit(solution)/shard_map/while/body/eval_jaxpr/ppermute | solution.py:29
  (62 other events, 625.3 us)
where the time goes:
time: 981 us; the launch traced here: 979 us
  starting transfers between devices  673 us (69%)
  local copies, waits for them, and re-layouts  119 us (12%)
  waiting for transfers between devices  112 us (11%)
  other arithmetic  67 us (7%)
    ppermute x63, starting transfers between devices, passed_along(): return lax.ppermute(block, axis, route)  628 us
    ppermute x63, waiting for transfers between devices, passed_along(): return lax.ppermute(block, axis, route)  99.3 us
    another operation x4, local copies, waits for them, and re-layouts, restrict(): grid_field.reshape(shape_now[0] // 4, 4, shape_now[1] // 4, 4, shape_now[...  75.4 us
    reduce_sum x6, other arithmetic, restrict(): return jnp.mean(blocked, axis=(1, 3, 5))  41.7 us
    reshape x2, local copies, waits for them, and re-layouts, restrict(): grid_field.reshape(shape_now[0] // 4, 4, shape_now[1] // 4, 4, shape_now[...  37.3 us
    ppermute x8, starting transfers between devices, extended_2(): lax.ppermute(lax.slice_in_dim(block, 0, width, axis=dim), axis, backward)  29.8 us
  transfers between devices with their start and end apart: 79, of which 70 were waited for; matrix products, arithmetic and copies ran while one was open for 13% of the time, Pallas kernels for 0%

commit v1 on v0

v1 whole, which is shorter than its diff:
```python
import functools

import jax
import jax.numpy as jnp
from jax import lax
from jax.experimental import pallas as pl
from jax.experimental.pallas import tpu as pltpu
from jax.sharding import PartitionSpec as P

STEPS = 8
WIDE = 4
AXES = ("tm", "slab")
DIFFUSION_FINE = 0.15
DIFFUSION_COARSE = 0.0375
HIGH = lax.Precision.HIGHEST
ANY = pl.BlockSpec(memory_space=pl.ANY)
SMEM = pl.BlockSpec(memory_space=pltpu.SMEM)
VMEM = pl.BlockSpec(memory_space=pltpu.VMEM)
PARAMS = pltpu.CompilerParams(vmem_limit_bytes=48 * 2**20)


def f32(*shape):
    return jax.ShapeDtypeStruct(shape, jnp.float32)


def pack_kernel(slab_ref, adj, force, vel, upt, chip_out, near_out, vel_out, sem):
    depth = adj.shape[0]
    slab = slab_ref[0]
    top = depth - WIDE
    odd = lax.rem(slab, 2)
    chip_first = (1 - odd) * top
    chip_inner = (1 - odd) * (top + 1)
    near_first = odd * top
    near_inner = odd * (top + 1)
    thin = WIDE - 1
    copies = []

    def add(src, dst):
        copies.append(pltpu.make_async_copy(src, dst, sem.at[len(copies)]))

    add(adj.at[pl.ds(chip_first, WIDE)], chip_out.at[pl.ds(0, WIDE)])
    add(force.at[pl.ds(chip_inner, thin)], chip_out.at[pl.ds(WIDE, thin)])
    add(upt.at[pl.ds(chip_inner, thin)], chip_out.at[pl.ds(WIDE + thin, thin)])
    for part in range(3):
        add(
            vel.at[part, pl.ds(chip_inner, thin)],
            chip_out.at[pl.ds(WIDE + (2 + part) * thin, thin)],
        )
    add(adj.at[pl.ds(near_first, WIDE)], near_out.at[pl.ds(0, WIDE)])
    add(force.at[pl.ds(near_inner, thin)], near_out.at[pl.ds(WIDE, thin)])
    add(upt.at[pl.ds(near_inner, thin)], near_out.at[pl.ds(WIDE + thin, thin)])
    for part in range(3):
        add(vel.at[part, pl.ds(near_inner, thin)], vel_out.at[pl.ds(part * thin, thin)])
    for copy in copies:
        copy.start()
    for copy in copies:
        copy.wait()


def pack(slab, adj, force, vel, upt):
    _, rows, cols = adj.shape
    thin = WIDE - 1
    return pl.pallas_call(
        pack_kernel,
        out_shape=(
            f32(WIDE + 5 * thin, rows, cols),
            f32(WIDE + 2 * thin, rows, cols),
            f32(3 * thin, rows, cols),
        ),
        in_specs=[SMEM, ANY, ANY, ANY, ANY],
        out_specs=(ANY, ANY, ANY),
        scratch_shapes=[pltpu.SemaphoreType.DMA((12,))],
        compiler_params=PARAMS,
        name="pack",
    )(slab, adj, force, vel, upt)


def averaging(cols, scale):
    fine = lax.broadcasted_iota(jnp.int32, (cols, cols // 4), 0)
    coarse = lax.broadcasted_iota(jnp.int32, (cols, cols // 4), 1)
    return jnp.where(lax.shift_right_logical(fine, 2) == coarse, scale, 0.0)


def row_sums(rows):
    coarse = lax.broadcasted_iota(jnp.int32, (rows // 4, rows), 0)
    fine = lax.broadcasted_iota(jnp.int32, (rows // 4, rows), 1)
    return jnp.where(lax.shift_right_logical(fine, 2) == coarse, 1.0, 0.0)


def restrict_summed(summed):
    count, rows, cols = summed.shape
    flat = summed.reshape(count * rows, cols)
    across = jnp.dot(flat, averaging(cols, 1.0 / 64.0), precision=HIGH)
    down = jnp.dot(row_sums(count * rows), across, precision=HIGH)
    return down.reshape(count, rows // 4, cols // 4)


def layer_sums(read, depth):
    parts = []
    for z in range(0, depth, 4):
        parts.append((read(z) + read(z + 1)) + (read(z + 2) + read(z + 3)))
    return parts


def restrict_kernel(adj, vel, upt, out):
    depth = adj.shape[0]
    parts = layer_sums(lambda z: adj[z], depth)
    for part in range(3):
        parts += layer_sums(lambda z: vel[part, z], depth)
    parts += layer_sums(lambda z: upt[z], depth)
    out[...] = restrict_summed(jnp.stack(parts))


def restrict_inputs(adj, vel, upt):
    depth, rows, cols = adj.shape
    return pl.pallas_call(
        restrict_kernel,
        out_shape=f32(5 * depth // 4, rows // 4, cols // 4),
        in_specs=[VMEM] * 3,
        out_specs=VMEM,
        compiler_params=PARAMS,
        name="restrict",
    )(adj, vel, upt)


def fine_kernel(last, steps, slab_ref, adj, force, vel, upt, *refs):
    depth, rows, cols = adj.shape
    tiles = cols // 128
    thin = WIDE - 1
    extended = depth + 2 * WIDE
    if last:
        chip_adj, near_adj, chip, near, near_vel, out, coarse = refs[:7]
        refs = refs[7:]
    else:
        chip, near, near_vel, out, chip_out, near_out = refs[:6]
        chip_adj, near_adj = chip.at[pl.ds(0, WIDE)], near.at[pl.ds(0, WIDE)]
        refs = refs[6:]
    state, force_x, vel_x, upt_x, sem, halo_sem = refs
    slab = slab_ref[0]
    odd = lax.rem(slab, 2) == 1
    has_near = jnp.logical_and(slab > 0, slab < 3)

    own = []

    def add(src, dst):
        own.append(pltpu.make_async_copy(src, dst, sem.at[len(own)]))

    for tile in range(tiles):
        add(
            adj.at[:, :, pl.ds(tile * 128, 128)],
            state.at[0, pl.ds(WIDE, depth), tile, pl.ds(8, rows)],
        )
    add(force, force_x.at[pl.ds(WIDE, depth)])
    add(upt, upt_x.at[pl.ds(WIDE, depth)])
    for part in range(3):
        add(vel.at[part], vel_x.at[part, pl.ds(WIDE, depth)])

    def halo(first, inner, adj_src, rest, rest_vel, at):
        made = []

        def add_halo(src, dst):
            made.append(pltpu.make_async_copy(src, dst, halo_sem.at[at + len(made)]))

        for tile in range(tiles):
            add_halo(
                adj_src.at[:, :, pl.ds(tile * 128, 128)],
                state.at[0, pl.ds(first, WIDE), tile, pl.ds(8, rows)],
            )
        add_halo(rest.at[pl.ds(WIDE, thin)], force_x.at[pl.ds(inner, thin)])
        add_halo(rest.at[pl.ds(WIDE + thin, thin)], upt_x.at[pl.ds(inner, thin)])
        for part in range(3):
            add_halo(rest_vel(part), vel_x.at[part, pl.ds(inner, thin)])
        return made

    low = (0, 1)
    high = (depth + WIDE, depth + WIDE)
    per_side = tiles + 5

    def chip_vel(part):
        return chip.at[pl.ds(WIDE + (2 + part) * thin, thin)]

    def far_vel(part):
        return near_vel.at[pl.ds(part * thin, thin)]

    chip_low = halo(*low, chip_adj, chip, chip_vel, 0)
    chip_high = halo(*high, chip_adj, chip, chip_vel, 0)
    near_low = halo(*low, near_adj, near, far_vel, per_side)
    near_high = halo(*high, near_adj, near, far_vel, per_side)

    def zero_state(which, first, count):
        state[which, pl.ds(first, count)] = jnp.zeros((count,) + state.shape[2:], jnp.float32)

    for which in range(2):
        for edge in (0, rows + 8):
            state[which, :, :, pl.ds(edge, 8)] = jnp.zeros((extended, tiles, 8, 128), jnp.float32)

    @pl.when(slab == 0)
    def _():
        zero_state(0, WIDE - 1, 1)
        zero_state(1, WIDE - 1, 1)

    @pl.when(slab == 3)
    def _():
        zero_state(0, depth + WIDE, 1)
        zero_state(1, depth + WIDE, 1)

    for copy in own:
        copy.start()

    def each(copies, act):
        for copy in copies:
            act(copy)

    for act in (lambda c: c.start(), lambda c: c.wait()):

        @pl.when(odd)
        def _():
            each(chip_low, act)

        @pl.when(jnp.logical_not(odd))
        def _():
            each(chip_high, act)

        @pl.when(jnp.logical_and(has_near, odd))
        def _():
            each(near_high, act)

        @pl.when(jnp.logical_and(has_near, jnp.logical_not(odd)))
        def _():
            each(near_low, act)

    for copy in own:
        copy.wait()

    lane = lax.broadcasted_iota(jnp.int32, (8, 128), 1)
    first_lane = lane == 0
    last_lane = lane == 127

    def layer(z, now, put):
        for block in range(rows // 8):
            y = 8 + 8 * block
            mid = [state[now, z, t, pl.ds(y, 8)] for t in range(tiles)]
            ahead = [pltpu.roll(m, 127, 1) for m in mid]
            behind = [pltpu.roll(m, 1, 1) for m in mid]
            zero = jnp.zeros((8, 128), jnp.float32)
            for t in range(tiles):
                xp = jnp.where(last_lane, ahead[t + 1] if t + 1 < tiles else zero, ahead[t])
                xm = jnp.where(first_lane, behind[t - 1] if t else zero, behind[t])
                zp = state[now, z + 1, t, pl.ds(y, 8)]
                zm = state[now, z - 1, t, pl.ds(y, 8)]
                yp = state[now, z, t, pl.ds(y + 1, 8)]
                ym = state[now, z, t, pl.ds(y - 1, 8)]
                at = (z, pl.ds(8 * block, 8), pl.ds(128 * t, 128))
                spread = ((zp + zm) + (yp + ym)) + (xp + xm)
                carried = (
                    vel_x[(0,) + at] * (zp - zm)
                    + vel_x[(1,) + at] * (yp - ym)
                    + vel_x[(2,) + at] * (xp - xm)
                )
                kept = ((1.0 - 6.0 * DIFFUSION_FINE) - upt_x[at]) * mid[t]
                put(block, t, (DIFFUSION_FINE * spread + 0.5 * carried) + (kept + force_x[at]))

    for step in range(1, steps + 1):
        now, later = (step - 1) % 2, step % 2
        begin = jnp.where(slab == 0, WIDE, step)
        end = jnp.where(slab == 3, depth + WIDE, extended - step)
        if step < steps:

            def body(z, carry):
                def put(block, t, value):
                    state[later, z, t, pl.ds(8 + 8 * block, 8)] = value

                layer(z, now, put)
                return carry

            lax.fori_loop(begin, end, body, 0)
        else:

            def body(z, carry):
                def put(block, t, value):
                    out[z, pl.ds(8 * block, 8), pl.ds(128 * t, 128)] = value

                layer(z + WIDE, now, put)
                return carry

            lax.fori_loop(0, depth, body, 0)
    if last:
        coarse[...] = restrict_summed(jnp.stack(layer_sums(lambda z: out[z], depth)))
    else:

        @pl.when(odd)
        def _():
            chip_out[...] = out[pl.ds(0, WIDE)]
            near_out[...] = out[pl.ds(depth - WIDE, WIDE)]

        @pl.when(jnp.logical_not(odd))
        def _():
            chip_out[...] = out[pl.ds(depth - WIDE, WIDE)]
            near_out[...] = out[pl.ds(0, WIDE)]


def fine(slab, adj, force, vel, upt, halos, last, steps):
    depth, rows, cols = adj.shape
    extended = depth + 2 * WIDE
    tiles = cols // 128
    if last:
        out_shape = (f32(depth, rows, cols), f32(depth // 4, rows // 4, cols // 4))
    else:
        out_shape = (f32(depth, rows, cols), f32(WIDE, rows, cols), f32(WIDE, rows, cols))
    return pl.pallas_call(
        functools.partial(fine_kernel, last, steps),
        out_shape=out_shape,
        in_specs=[SMEM] + [ANY] * (4 + len(halos)),
        out_specs=(VMEM,) * len(out_shape),
        scratch_shapes=[
            pltpu.VMEM((2, extended, tiles, rows + 16, 128), jnp.float32),
            pltpu.VMEM((extended, rows, cols), jnp.float32),
            pltpu.VMEM((3, extended, rows, cols), jnp.float32),
            pltpu.VMEM((extended, rows, cols), jnp.float32),
            pltpu.SemaphoreType.DMA((tiles + 5,)),
            pltpu.SemaphoreType.DMA((2 * (tiles + 5),)),
        ],
        compiler_params=PARAMS,
        name="fine_last" if last else "fine_first",
    )(slab, adj, force, vel, upt, *halos)


def half_step(field, coef):
    depth = len(field)
    stepped = []
    ahead = [pltpu.roll(c, c.shape[1] - 1, 1) for c in field]
    behind = [pltpu.roll(c, 1, 1) for c in field]
    for z in range(depth):
        c = field[z]
        total = coef[0, z] * c
        if z + 1 < depth:
            total += coef[1, z] * field[z + 1]
        if z:
            total += coef[2, z] * field[z - 1]
        other = coef[3, z] * pltpu.roll(c, c.shape[0] - 1, 0) + coef[4, z] * pltpu.roll(c, 1, 0)
        total = (total + other) + (coef[5, z] * ahead[z] + coef[6, z] * behind[z])
        stepped.append(total)
    return stepped


def place(ref, slab, own, others):
    depth = own.shape[-3]
    for flip, part in enumerate((own,) + tuple(others)):
        ref[pl.ds(lax.bitwise_xor(slab, flip) * depth, depth)] = part


def prepare_kernel(slab_ref, own, one, two, three, coef, stepped, whole):
    slab = slab_ref[0]
    depth = own.shape[0] // 5
    for flip, ref in enumerate((own, one, two, three)):
        for part in range(5):
            first = lax.bitwise_xor(slab, flip) * depth
            whole[part, pl.ds(first, depth)] = ref[pl.ds(part * depth, depth)]
    full = whole.shape[1:]
    center = (1.0 - 6.0 * DIFFUSION_COARSE) - 4.0 * whole[4]
    for dim in range(3):
        v = whole[1 + dim]
        center -= jnp.abs(v)
        place_in = lax.broadcasted_iota(jnp.int32, full, dim)
        plus = DIFFUSION_COARSE + jnp.maximum(v, 0.0)
        minus = DIFFUSION_COARSE - jnp.minimum(v, 0.0)
        coef[1 + 2 * dim] = jnp.where(place_in == full[dim] - 1, 0.0, plus)
        coef[2 + 2 * dim] = jnp.where(place_in == 0, 0.0, minus)
    coef[0] = center
    field = [whole[0, z] for z in range(full[0])]
    field = half_step(half_step(field, coef), coef)
    for z in range(full[0]):
        stepped[z] = field[z]


def prepare(slab, parts):
    depth5, rows, cols = parts[0].shape
    full = (4 * depth5 // 5, rows, cols)
    return pl.pallas_call(
        prepare_kernel,
        out_shape=(f32(7, *full), f32(*full)),
        in_specs=[SMEM] + [VMEM] * 4,
        out_specs=(VMEM, VMEM),
        scratch_shapes=[pltpu.VMEM((5,) + full, jnp.float32)],
        compiler_params=PARAMS,
        name="prepare",
    )(slab, *parts)


def start_kernel(place_ref, own, one, two, three, stepped, begun, whole):
    place(whole, place_ref[0], own[...], (one[...], two[...], three[...]))
    kept = jnp.where(place_ref[1] == 1, 0.0, 1.0)
    begun[...] = whole[...] - kept * stepped[...]


def start_sweep(where, parts, stepped):
    return pl.pallas_call(
        start_kernel,
        out_shape=(f32(*stepped.shape), f32(*stepped.shape)),
        in_specs=[SMEM] + [VMEM] * 5,
        out_specs=(VMEM, VMEM),
        compiler_params=PARAMS,
        name="start_sweep",
    )(where, *parts, stepped)


def chain_kernel(distance, coef, *refs):
    *terms, out = refs
    depth = out.shape[0]
    field = [terms[0][z] for z in range(depth)]
    for term in terms[1:]:

        def body(_, c):
            return tuple(half_step(half_step(c, coef), coef))

        field = lax.fori_loop(0, distance, body, tuple(field))
        field = [field[z] + term[z] for z in range(depth)]
    for z in range(depth):
        out[z] = field[z]


def chain(distance, coef, terms):
    return pl.pallas_call(
        functools.partial(chain_kernel, distance),
        out_shape=f32(*terms[0].shape),
        in_specs=[VMEM] * (1 + len(terms)),
        out_specs=VMEM,
        compiler_params=PARAMS,
        name="chain",
    )(coef, *terms)


def correct_kernel(slab_ref, prop, coarse_new, coarse_prop, out):
    depth, rows, cols = prop.shape
    count = depth // 4
    first = slab_ref[0] * count
    part = coarse_new[pl.ds(first, count)] - coarse_prop[pl.ds(first, count)]
    flat = part.reshape(count * rows // 4, cols // 4)
    fine = lax.broadcasted_iota(jnp.int32, (cols // 4, cols), 1)
    coarse = lax.broadcasted_iota(jnp.int32, (cols // 4, cols), 0)
    spread = jnp.where(lax.shift_right_logical(fine, 2) == coarse, 1.0, 0.0)
    across = jnp.dot(flat, spread, precision=HIGH)
    fine = lax.broadcasted_iota(jnp.int32, (count * rows, count * rows // 4), 0)
    coarse = lax.broadcasted_iota(jnp.int32, (count * rows, count * rows // 4), 1)
    spread = jnp.where(lax.shift_right_logical(fine, 2) == coarse, 1.0, 0.0)
    down = jnp.dot(spread, across, precision=HIGH).reshape(count, rows, cols)
    for z in range(depth):
        out[z] = prop[z] + down[z // 4]


def correct(slab, prop, coarse_new, coarse_prop):
    return pl.pallas_call(
        correct_kernel,
        out_shape=f32(*prop.shape),
        in_specs=[SMEM, VMEM, VMEM, VMEM],
        out_specs=VMEM,
        compiler_params=PARAMS,
        name="correct",
    )(slab, prop, coarse_new, coarse_prop)


def per_device(adjoint_end, forcing, velocity, uptake):
    adj, force = adjoint_end[0], forcing[0]
    times, slabs = lax.axis_size("tm"), lax.axis_size("slab")
    slab_no, time_no = lax.axis_index("slab"), lax.axis_index("tm")
    slab = slab_no.astype(jnp.int32).reshape(1)

    def send(array, pairs):
        route = [(t0 * slabs + s0, t1 * slabs + s1) for (t0, s0), (t1, s1) in pairs]
        return lax.ppermute(array, AXES, route)

    def flipped(array, flip):
        return send(array, [((t, s ^ flip), (t, s)) for t in range(times) for s in range(slabs)])

    def to_next_chip(array, shift=0):
        pairs = [(1, 2), (2, 1)]
        return send(
            array, [((t, a), ((t + shift) % times, b)) for t in range(times) for a, b in pairs]
        )

    def gathered(array):
        return [array] + [flipped(array, flip) for flip in (1, 2, 3)]

    chip_pack, near_pack, vel_pack = pack(slab, adj, force, velocity, uptake)
    near = to_next_chip(near_pack)
    near_vel = to_next_chip(vel_pack, times // 2)
    chip = flipped(chip_pack, 1)
    restricted = restrict_inputs(adj, velocity, uptake)
    coef, stepped = prepare(slab, gathered(restricted))

    halves = STEPS // 2
    adj, chip_send, near_send = fine(
        slab, adj, force, velocity, uptake, (chip, near, near_vel), False, halves
    )
    near_adj = to_next_chip(near_send)
    chip_adj = flipped(chip_send, 1)
    prop, coarse_part = fine(
        slab,
        adj,
        force,
        velocity,
        uptake,
        (chip_adj, near_adj, chip, near, near_vel),
        True,
        STEPS - halves,
    )
    at_end = (time_no == times - 1).astype(jnp.int32).reshape(1)
    where = jnp.concatenate([slab, at_end])
    field, coarse_prop = start_sweep(where, gathered(coarse_part), stepped)

    distance = 1
    while distance < times:
        terms = [field]
        for hops in range(distance, min(4 * distance, times), distance):
            terms.insert(
                0,
                send(
                    field, [((t + hops, s), (t, s)) for t in range(times - hops) for s in range(slabs)]
                ),
            )
        field = chain(distance, coef, terms)
        distance *= 4
    corrected = correct(slab, prop, field, coarse_prop)
    return corrected[None], field[None]


def solution(mesh):
    in_specs = (
        P("tm", "slab", None, None),
        P("tm", "slab", None, None),
        P(None, "slab", None, None),
        P("slab", None, None),
    )
    out_specs = (P("tm", "slab", None, None), P("tm", None, None, None))
    return jax.shard_map(
        per_device, mesh=mesh, in_specs=in_specs, out_specs=out_specs, check_vma=False
    )
```

time: 981 us -> 129 us (0.13)
  the two profiles are of different devices: /device:TPU:24 before, /device:TPU:230 now
where the time goes in v1:
time: 129 us; the launch traced here: 128 us
  starting transfers between devices  50.3 us (39%)
  Pallas kernels  35.9 us (28%)
  waiting for transfers between devices  30.8 us (24%)
  local copies, waits for them, and re-layouts  10.3 us (8%)
    ppermute x20, starting transfers between devices, send(): return lax.ppermute(array, AXES, route)  50.3 us
    ppermute x20, waiting for transfers between devices, send(): return lax.ppermute(array, AXES, route)  30.8 us
    pallas_call x2, Pallas kernels, fine(): pl.pallas_call(functools.partial(fine_kernel, last, steps), out_shape=out...  19.2 us
    pallas_call x3, Pallas kernels, chain(): pl.pallas_call(functools.partial(chain_kernel, distance), out_shape=f32(*...  11 us
    unnamed x28, local copies, waits for them, and re-layouts  10.3 us
    pallas_call x1, Pallas kernels, pack(): pl.pallas_call(pack_kernel, out_shape=(f32(WIDE + 5 * thin, rows, cols),...  2.69 us
  transfers between devices with their start and end apart: 20, of which 9 were waited for; matrix products, arithmetic and copies ran while one was open for 0% of the time, Pallas kernels for 8%

profile of v1, /device:TPU:230, one launch (start us, length us, event | category | flops | bytes accessed | tf_op | source)
XLA Modules:
  0.0 128.4 jit_solution(14987300467798287135)
XLA Ops:
  5.2 2.7 %pack.1 = (f32[19,32,512]{2,1,0:T(8,128)S(1)}, f32[10,32,512]{2,1,0:T(8,128)S(1)}, f32[9,32,512]{2,1,0:T(8,128)S(1)}) custom-call(s32[1]{0:T(128)} %bitcast.slab_ref, f32[8,32,512]{2,1,0:T(8,128)S(1)} %bitcast.9, f32[8,32,512]{2,1,0:T(8,128)S(1)} %bitcast.6, f32[3,8,32,512]{3,2,1,0:T(8,128)S(1)} %copy-done, f32[8,32,512]{2,1,0:T(8,128)S(1)} %copy-done.2), custom_call_target="tpu_custom_call" | custom-call | tf_op jit(solution)/shard_map/pack/pallas_call | solution.py:63
  10.9 9.8 %fine_first.1 = (f32[8,32,512]{2,1,0:T(8,128)S(1)}, f32[4,32,512]{2,1,0:T(8,128)}, f32[4,32,512]{2,1,0:T(8,128)}) custom-call(s32[1]{0:T(128)} %bitcast.slab_ref, f32[8,32,512]{2,1,0:T(8,128)S(1)} %bitcast.10, f32[8,32,512]{2,1,0:T(8,128)S(1)} %bitcast.7, f32[3,8,32,512]{3,2,1,0:T(8,128)} %vel.7, f32[8,32,512]{2,1,0:T(8,128)S(1)} %copy-done.3, ...), custom_call_target="tpu_custom_call" | custom-call | tf_op jit(solution)/shard_map/fine_first/pallas_call | solution.py:310
  21.5 15.8 %collective-permute-start.3 = (f32[4,32,512]{2,1,0:T(8,128)}, f32[4,32,512]{2,1,0:T(8,128)}, u32[]{:S(2)}, u32[]{:S(2)}) collective-permute-start(f32[4,32,512]{2,1,0:T(8,128)} %get-tuple-element.18), channel_id=1, source_target_pairs={{1,0},{0,1},{3,2},{2,3},{5,4},{4,5},{7,6},{6,7},{9,8},{8,9},{11,10... | collective-permute-start | bytes 786440 | tf_op jit(solution)/shard_map/ppermute | solution.py:470
  40.5 1.7 %collective-permute-start.6 = (f32[10,8,128]{2,1,0:T(8,128)S(1)}, f32[10,8,128]{2,1,0:T(8,128)S(1)}, u32[]{:S(2)}, u32[]{:S(2)}) collective-permute-start(f32[10,8,128]{2,1,0:T(8,128)S(1)} %restrict.1.own), channel_id=1, source_target_pairs={{2,0},{3,1},{0,2},{1,3},{6,4},{7,5},{4,6},{5,7},{10,8},{11,9},{8,1... | collective-permute-start | bytes 122888 | tf_op jit(solution)/shard_map/ppermute | solution.py:470
  46.5 9.3 %fine_last.1 = (f32[8,32,512]{2,1,0:T(8,128)S(1)}, f32[2,8,128]{2,1,0:T(8,128)S(1)}) custom-call(s32[1]{0:T(128)} %bitcast.slab_ref, f32[8,32,512]{2,1,0:T(8,128)S(1)} %copy-done.12, f32[8,32,512]{2,1,0:T(8,128)S(1)} %bitcast.8, f32[3,8,32,512]{3,2,1,0:T(8,128)} %vel.7, f32[8,32,512]{2,1,0:T(8,128)S(1)} %copy-done.3, ...), custom_call_target="tpu_custom_call" | custom-call | tf_op jit(solution)/shard_map/fine_last/pallas_call | solution.py:310
  55.9 1.8 %collective-permute-start.10 = (f32[2,8,128]{2,1,0:T(8,128)S(1)}, f32[2,8,128]{2,1,0:T(8,128)S(1)}, u32[]{:S(2)}, u32[]{:S(2)}) collective-permute-start(f32[2,8,128]{2,1,0:T(8,128)S(1)} %get-tuple-element.22.own), channel_id=1, source_target_pairs={{3,0},{2,1},{1,2},{0,3},{7,4},{6,5},{5,6},{4,7},{11,8},{10,9},{9,1... | collective-permute-start | bytes 24584 | tf_op jit(solution)/shard_map/ppermute | solution.py:470
  57.6 4.8 %collective-permute-start.8 = (f32[2,8,128]{2,1,0:T(8,128)S(1)}, f32[2,8,128]{2,1,0:T(8,128)S(1)}, u32[]{:S(2)}, u32[]{:S(2)}) collective-permute-start(f32[2,8,128]{2,1,0:T(8,128)S(1)} %get-tuple-element.22.own), channel_id=1, source_target_pairs={{1,0},{0,1},{3,2},{2,3},{5,4},{4,5},{7,6},{6,7},{9,8},{8,9},{11,10... | collective-permute-start | bytes 24584 | tf_op jit(solution)/shard_map/ppermute | solution.py:470
  62.5 1.5 %collective-permute-start.9 = (f32[2,8,128]{2,1,0:T(8,128)S(1)}, f32[2,8,128]{2,1,0:T(8,128)S(1)}, u32[]{:S(2)}, u32[]{:S(2)}) collective-permute-start(f32[2,8,128]{2,1,0:T(8,128)S(1)} %get-tuple-element.22.own), channel_id=1, source_target_pairs={{2,0},{3,1},{0,2},{1,3},{6,4},{7,5},{4,6},{5,7},{10,8},{11,9},{8,1... | collective-permute-start | bytes 24584 | tf_op jit(solution)/shard_map/ppermute | solution.py:470
  64.3 1.8 %collective-permute-done.9.two = f32[2,8,128]{2,1,0:T(8,128)S(1)} collective-permute-done((f32[2,8,128]{2,1,0:T(8,128)S(1)}, f32[2,8,128]{2,1,0:T(8,128)S(1)}, u32[]{:S(2)}, u32[]{:S(2)}) %collective-permute-start.9) | collective-permute-done | bytes 8224 | tf_op jit(solution)/shard_map/ppermute | solution.py:470
  66.7 3.8 %collective-permute-start.11 = (f32[8,8,128]{2,1,0:T(8,128)S(1)}, f32[8,8,128]{2,1,0:T(8,128)S(1)}, u32[]{:S(2)}, u32[]{:S(2)}) collective-permute-start(f32[8,8,128]{2,1,0:T(8,128)S(1)} %get-tuple-element.24.refs_3_), channel_id=1, source_target_pairs={{12,0},{13,1},{14,2},{15,3},{16,4},{17,5},{18,6},{19,7},{20,8},{21... | collective-permute-start | bytes 98312 | tf_op jit(solution)/shard_map/ppermute | solution.py:470
  70.5 1.9 %collective-permute-start.12 = (f32[8,8,128]{2,1,0:T(8,128)S(1)}, f32[8,8,128]{2,1,0:T(8,128)S(1)}, u32[]{:S(2)}, u32[]{:S(2)}) collective-permute-start(f32[8,8,128]{2,1,0:T(8,128)S(1)} %get-tuple-element.24.refs_3_), channel_id=1, source_target_pairs={{8,0},{9,1},{10,2},{11,3},{12,4},{13,5},{14,6},{15,7},{16,8},{17,9... | collective-permute-start | bytes 98312 | tf_op jit(solution)/shard_map/ppermute | solution.py:470
  72.4 2.5 %collective-permute-start.13 = (f32[8,8,128]{2,1,0:T(8,128)S(1)}, f32[8,8,128]{2,1,0:T(8,128)S(1)}, u32[]{:S(2)}, u32[]{:S(2)}) collective-permute-start(f32[8,8,128]{2,1,0:T(8,128)S(1)} %get-tuple-element.24.refs_3_), channel_id=1, source_target_pairs={{4,0},{5,1},{6,2},{7,3},{8,4},{9,5},{10,6},{11,7},{12,8},{13,9},{1... | collective-permute-start | bytes 98312 | tf_op jit(solution)/shard_map/ppermute | solution.py:470
  74.9 5.1 %collective-permute-done.11.refs_0_ = f32[8,8,128]{2,1,0:T(8,128)S(1)} collective-permute-done((f32[8,8,128]{2,1,0:T(8,128)S(1)}, f32[8,8,128]{2,1,0:T(8,128)S(1)}, u32[]{:S(2)}, u32[]{:S(2)}) %collective-permute-start.11) | collective-permute-done | bytes 32800 | tf_op jit(solution)/shard_map/ppermute | solution.py:470
  80.0 3.6 %collective-permute-done.12.refs_1_ = f32[8,8,128]{2,1,0:T(8,128)S(1)} collective-permute-done((f32[8,8,128]{2,1,0:T(8,128)S(1)}, f32[8,8,128]{2,1,0:T(8,128)S(1)}, u32[]{:S(2)}, u32[]{:S(2)}) %collective-permute-start.12) | collective-permute-done | bytes 32800 | tf_op jit(solution)/shard_map/ppermute | solution.py:470
  84.5 2.7 %collective-permute-start.14 = (f32[8,8,128]{2,1,0:T(8,128)S(1)}, f32[8,8,128]{2,1,0:T(8,128)S(1)}, u32[]{:S(2)}, u32[]{:S(2)}) collective-permute-start(f32[8,8,128]{2,1,0:T(8,128)S(1)} %chain.3.refs_3_), channel_id=1, source_target_pairs={{48,0},{49,1},{50,2},{51,3},{52,4},{53,5},{54,6},{55,7},{56,8},{57... | collective-permute-start | bytes 98312 | tf_op jit(solution)/shard_map/ppermute | solution.py:470
  87.1 2.4 %collective-permute-start.15 = (f32[8,8,128]{2,1,0:T(8,128)S(1)}, f32[8,8,128]{2,1,0:T(8,128)S(1)}, u32[]{:S(2)}, u32[]{:S(2)}) collective-permute-start(f32[8,8,128]{2,1,0:T(8,128)S(1)} %chain.3.refs_3_), channel_id=1, source_target_pairs={{32,0},{33,1},{34,2},{35,3},{36,4},{37,5},{38,6},{39,7},{40,8},{41... | collective-permute-start | bytes 98312 | tf_op jit(solution)/shard_map/ppermute | solution.py:470
  89.6 3.8 %collective-permute-start.16 = (f32[8,8,128]{2,1,0:T(8,128)S(1)}, f32[8,8,128]{2,1,0:T(8,128)S(1)}, u32[]{:S(2)}, u32[]{:S(2)}) collective-permute-start(f32[8,8,128]{2,1,0:T(8,128)S(1)} %chain.3.refs_3_), channel_id=1, source_target_pairs={{16,0},{17,1},{18,2},{19,3},{20,4},{21,5},{22,6},{23,7},{24,8},{25... | collective-permute-start | bytes 98312 | tf_op jit(solution)/shard_map/ppermute | solution.py:470
  93.4 5.7 %collective-permute-done.14.refs_0_ = f32[8,8,128]{2,1,0:T(8,128)S(1)} collective-permute-done((f32[8,8,128]{2,1,0:T(8,128)S(1)}, f32[8,8,128]{2,1,0:T(8,128)S(1)}, u32[]{:S(2)}, u32[]{:S(2)}) %collective-permute-start.14) | collective-permute-done | bytes 32800 | tf_op jit(solution)/shard_map/ppermute | solution.py:470
  99.1 5.1 %collective-permute-done.16.refs_2_ = f32[8,8,128]{2,1,0:T(8,128)S(1)} collective-permute-done((f32[8,8,128]{2,1,0:T(8,128)S(1)}, f32[8,8,128]{2,1,0:T(8,128)S(1)}, u32[]{:S(2)}, u32[]{:S(2)}) %collective-permute-start.16) | collective-permute-done | bytes 32800 | tf_op jit(solution)/shard_map/ppermute | solution.py:470
  104.2 2.0 %chain.4.refs_3_ = f32[8,8,128]{2,1,0:T(8,128)S(1)} custom-call(f32[7,8,8,128]{3,2,1,0:T(8,128)S(1)} %get-tuple-element.21.coef, f32[8,8,128]{2,1,0:T(8,128)S(1)} %collective-permute-done.14.refs_0_, f32[8,8,128]{2,1,0:T(8,128)S(1)} %collective-permute-done.15.refs_1_, f32[8,8,128]{2,1,0:T(8,128)S(1)} %collective-permute-done.16.refs_2_, ...), custom_call_target="tpu_custom_call" | custom-call | tf_op jit(solution)/shard_map/chain/pallas_call | solution.py:423
  108.1 1.9 %collective-permute-start.19 = (f32[8,8,128]{2,1,0:T(8,128)S(1)}, f32[8,8,128]{2,1,0:T(8,128)S(1)}, u32[]{:S(2)}, u32[]{:S(2)}) collective-permute-start(f32[8,8,128]{2,1,0:T(8,128)S(1)} %chain.4.refs_3_), channel_id=1, source_target_pairs={{64,0},{65,1},{66,2},{67,3},{68,4},{69,5},{70,6},{71,7},{72,8},{73... | collective-permute-start | bytes 98312 | tf_op jit(solution)/shard_map/ppermute | solution.py:470
  110.1 4.1 %collective-permute-done.18.refs_1_ = f32[8,8,128]{2,1,0:T(8,128)S(1)} collective-permute-done((f32[8,8,128]{2,1,0:T(8,128)S(1)}, f32[8,8,128]{2,1,0:T(8,128)S(1)}, u32[]{:S(2)}, u32[]{:S(2)}) %collective-permute-start.18) | collective-permute-done | bytes 32800 | tf_op jit(solution)/shard_map/ppermute | solution.py:470
  114.1 3.7 %collective-permute-done.19.refs_2_ = f32[8,8,128]{2,1,0:T(8,128)S(1)} collective-permute-done((f32[8,8,128]{2,1,0:T(8,128)S(1)}, f32[8,8,128]{2,1,0:T(8,128)S(1)}, u32[]{:S(2)}, u32[]{:S(2)}) %collective-permute-start.19) | collective-permute-done | bytes 32800 | tf_op jit(solution)/shard_map/ppermute | solution.py:470
  117.8 8.6 %chain.5.coarse_new = f32[8,8,128]{2,1,0:T(8,128)} custom-call(f32[7,8,8,128]{3,2,1,0:T(8,128)S(1)} %get-tuple-element.21.coef, f32[8,8,128]{2,1,0:T(8,128)S(1)} %collective-permute-done.17.refs_0_, f32[8,8,128]{2,1,0:T(8,128)S(1)} %collective-permute-done.18.refs_1_, f32[8,8,128]{2,1,0:T(8,128)S(1)} %collective-permute-done.19.refs_2_, ...), custom_call_target="tpu_custom_call" | custom-call | tf_op jit(solution)/shard_map/chain/pallas_call | solution.py:423
  (55 shorter events, 21.3 us)
Async XLA Ops:
  5.2 5.7 %copy-start.3 = (f32[8,32,512]{2,1,0:T(8,128)S(1)}, f32[8,32,512]{2,1,0:T(8,128)}, u32[]{:S(2)}) copy-start(f32[8,32,512]{2,1,0:T(8,128)} %upt.7) | copy-start | bytes 1572868
  7.9 3.0 %collective-permute-start = (f32[19,32,512]{2,1,0:T(8,128)S(1)}, f32[19,32,512]{2,1,0:T(8,128)S(1)}, u32[]{:S(2)}, u32[]{:S(2)}) collective-permute-start(f32[19,32,512]{2,1,0:T(8,128)S(1)} %get-tuple-element.14), channel_id=1, source_target_pairs={{1,0},{0,1},{3,2},{2,3},{5,4},{4,5},{7,6},{6,7},{9,8},{8,9},{11,10... | collective-permute-start | bytes 3735560 | tf_op jit(solution)/shard_map/ppermute | solution.py:470
  8.0 1.6 %collective-permute-start.1 = (f32[10,32,512]{2,1,0:T(8,128)S(1)}, f32[10,32,512]{2,1,0:T(8,128)S(1)}, u32[]{:S(2)}, u32[]{:S(2)}) collective-permute-start(f32[10,32,512]{2,1,0:T(8,128)S(1)} %get-tuple-element.15), channel_id=1, source_target_pairs={{1,2},{2,1},{5,6},{6,5},{9,10},{10,9},{13,14},{14,13},{17,18},{18,... | collective-permute-start | bytes 1966088 | tf_op jit(solution)/shard_map/ppermute | solution.py:470
  8.7 30.1 %copy-start.1 = (f32[3,8,32,512]{3,2,1,0:T(8,128)S(1)}, f32[3,8,32,512]{3,2,1,0:T(8,128)}, u32[]{:S(2)}) copy-start(f32[3,8,32,512]{3,2,1,0:T(8,128)} %vel.7) | copy-start | bytes 4718596
  8.7 0.8 collective-permute-start.2
  9.5 11.2 %copy-start.9 = (f32[9,32,512]{2,1,0:T(8,128)}, f32[9,32,512]{2,1,0:T(8,128)S(1)}, u32[]{:S(2)}) copy-start(f32[9,32,512]{2,1,0:T(8,128)S(1)} %collective-permute-done.2.refs_2_.refs_4_) | copy-start | bytes 1769476
  9.6 11.2 %copy-start.7 = (f32[10,32,512]{2,1,0:T(8,128)}, f32[10,32,512]{2,1,0:T(8,128)S(1)}, u32[]{:S(2)}) copy-start(f32[10,32,512]{2,1,0:T(8,128)S(1)} %collective-permute-done.1.refs_1_.refs_3_) | copy-start | bytes 1966084
  21.5 20.7 %collective-permute-start.3 = (f32[4,32,512]{2,1,0:T(8,128)}, f32[4,32,512]{2,1,0:T(8,128)}, u32[]{:S(2)}, u32[]{:S(2)}) collective-permute-start(f32[4,32,512]{2,1,0:T(8,128)} %get-tuple-element.18), channel_id=1, source_target_pairs={{1,0},{0,1},{3,2},{2,3},{5,4},{4,5},{7,6},{6,7},{9,8},{8,9},{11,10... | collective-permute-start | bytes 786440 | tf_op jit(solution)/shard_map/ppermute | solution.py:470
  37.4 4.9 %collective-permute-start.4 = (f32[4,32,512]{2,1,0:T(8,128)}, f32[4,32,512]{2,1,0:T(8,128)}, u32[]{:S(2)}, u32[]{:S(2)}) collective-permute-start(f32[4,32,512]{2,1,0:T(8,128)} %get-tuple-element.19), channel_id=1, source_target_pairs={{1,2},{2,1},{5,6},{6,5},{9,10},{10,9},{13,14},{14,13},{17,18},{18,... | collective-permute-start | bytes 786440 | tf_op jit(solution)/shard_map/ppermute | solution.py:470
  39.9 22.6 %collective-permute-start.5 = (f32[10,8,128]{2,1,0:T(8,128)S(1)}, f32[10,8,128]{2,1,0:T(8,128)S(1)}, u32[]{:S(2)}, u32[]{:S(2)}) collective-permute-start(f32[10,8,128]{2,1,0:T(8,128)S(1)} %restrict.1.own), channel_id=1, source_target_pairs={{1,0},{0,1},{3,2},{2,3},{5,4},{4,5},{7,6},{6,7},{9,8},{8,9},{11,10... | collective-permute-start | bytes 122888 | tf_op jit(solution)/shard_map/ppermute | solution.py:470
  40.5 23.6 %collective-permute-start.6 = (f32[10,8,128]{2,1,0:T(8,128)S(1)}, f32[10,8,128]{2,1,0:T(8,128)S(1)}, u32[]{:S(2)}, u32[]{:S(2)}) collective-permute-start(f32[10,8,128]{2,1,0:T(8,128)S(1)} %restrict.1.own), channel_id=1, source_target_pairs={{2,0},{3,1},{0,2},{1,3},{6,4},{7,5},{4,6},{5,7},{10,8},{11,9},{8,1... | collective-permute-start | bytes 122888 | tf_op jit(solution)/shard_map/ppermute | solution.py:470
  42.2 21.9 %collective-permute-start.7 = (f32[10,8,128]{2,1,0:T(8,128)S(1)}, f32[10,8,128]{2,1,0:T(8,128)S(1)}, u32[]{:S(2)}, u32[]{:S(2)}) collective-permute-start(f32[10,8,128]{2,1,0:T(8,128)S(1)} %restrict.1.own), channel_id=1, source_target_pairs={{3,0},{2,1},{1,2},{0,3},{7,4},{6,5},{5,6},{4,7},{11,8},{10,9},{9,1... | collective-permute-start | bytes 122888 | tf_op jit(solution)/shard_map/ppermute | solution.py:470
  55.9 8.4 %collective-permute-start.10 = (f32[2,8,128]{2,1,0:T(8,128)S(1)}, f32[2,8,128]{2,1,0:T(8,128)S(1)}, u32[]{:S(2)}, u32[]{:S(2)}) collective-permute-start(f32[2,8,128]{2,1,0:T(8,128)S(1)} %get-tuple-element.22.own), channel_id=1, source_target_pairs={{3,0},{2,1},{1,2},{0,3},{7,4},{6,5},{5,6},{4,7},{11,8},{10,9},{9,1... | collective-permute-start | bytes 24584 | tf_op jit(solution)/shard_map/ppermute | solution.py:470
  57.6 6.7 %collective-permute-start.8 = (f32[2,8,128]{2,1,0:T(8,128)S(1)}, f32[2,8,128]{2,1,0:T(8,128)S(1)}, u32[]{:S(2)}, u32[]{:S(2)}) collective-permute-start(f32[2,8,128]{2,1,0:T(8,128)S(1)} %get-tuple-element.22.own), channel_id=1, source_target_pairs={{1,0},{0,1},{3,2},{2,3},{5,4},{4,5},{7,6},{6,7},{9,8},{8,9},{11,10... | collective-permute-start | bytes 24584 | tf_op jit(solution)/shard_map/ppermute | solution.py:470
  62.5 3.7 %collective-permute-start.9 = (f32[2,8,128]{2,1,0:T(8,128)S(1)}, f32[2,8,128]{2,1,0:T(8,128)S(1)}, u32[]{:S(2)}, u32[]{:S(2)}) collective-permute-start(f32[2,8,128]{2,1,0:T(8,128)S(1)} %get-tuple-element.22.own), channel_id=1, source_target_pairs={{2,0},{3,1},{0,2},{1,3},{6,4},{7,5},{4,6},{5,7},{10,8},{11,9},{8,1... | collective-permute-start | bytes 24584 | tf_op jit(solution)/shard_map/ppermute | solution.py:470
  66.7 13.3 %collective-permute-start.11 = (f32[8,8,128]{2,1,0:T(8,128)S(1)}, f32[8,8,128]{2,1,0:T(8,128)S(1)}, u32[]{:S(2)}, u32[]{:S(2)}) collective-permute-start(f32[8,8,128]{2,1,0:T(8,128)S(1)} %get-tuple-element.24.refs_3_), channel_id=1, source_target_pairs={{12,0},{13,1},{14,2},{15,3},{16,4},{17,5},{18,6},{19,7},{20,8},{21... | collective-permute-start | bytes 98312 | tf_op jit(solution)/shard_map/ppermute | solution.py:470
  70.5 13.1 %collective-permute-start.12 = (f32[8,8,128]{2,1,0:T(8,128)S(1)}, f32[8,8,128]{2,1,0:T(8,128)S(1)}, u32[]{:S(2)}, u32[]{:S(2)}) collective-permute-start(f32[8,8,128]{2,1,0:T(8,128)S(1)} %get-tuple-element.24.refs_3_), channel_id=1, source_target_pairs={{8,0},{9,1},{10,2},{11,3},{12,4},{13,5},{14,6},{15,7},{16,8},{17,9... | collective-permute-start | bytes 98312 | tf_op jit(solution)/shard_map/ppermute | solution.py:470
  72.4 11.5 %collective-permute-start.13 = (f32[8,8,128]{2,1,0:T(8,128)S(1)}, f32[8,8,128]{2,1,0:T(8,128)S(1)}, u32[]{:S(2)}, u32[]{:S(2)}) collective-permute-start(f32[8,8,128]{2,1,0:T(8,128)S(1)} %get-tuple-element.24.refs_3_), channel_id=1, source_target_pairs={{4,0},{5,1},{6,2},{7,3},{8,4},{9,5},{10,6},{11,7},{12,8},{13,9},{1... | collective-permute-start | bytes 98312 | tf_op jit(solution)/shard_map/ppermute | solution.py:470
  84.5 14.6 %collective-permute-start.14 = (f32[8,8,128]{2,1,0:T(8,128)S(1)}, f32[8,8,128]{2,1,0:T(8,128)S(1)}, u32[]{:S(2)}, u32[]{:S(2)}) collective-permute-start(f32[8,8,128]{2,1,0:T(8,128)S(1)} %chain.3.refs_3_), channel_id=1, source_target_pairs={{48,0},{49,1},{50,2},{51,3},{52,4},{53,5},{54,6},{55,7},{56,8},{57... | collective-permute-start | bytes 98312 | tf_op jit(solution)/shard_map/ppermute | solution.py:470
  87.1 12.0 %collective-permute-start.15 = (f32[8,8,128]{2,1,0:T(8,128)S(1)}, f32[8,8,128]{2,1,0:T(8,128)S(1)}, u32[]{:S(2)}, u32[]{:S(2)}) collective-permute-start(f32[8,8,128]{2,1,0:T(8,128)S(1)} %chain.3.refs_3_), channel_id=1, source_target_pairs={{32,0},{33,1},{34,2},{35,3},{36,4},{37,5},{38,6},{39,7},{40,8},{41... | collective-permute-start | bytes 98312 | tf_op jit(solution)/shard_map/ppermute | solution.py:470
  89.6 14.6 %collective-permute-start.16 = (f32[8,8,128]{2,1,0:T(8,128)S(1)}, f32[8,8,128]{2,1,0:T(8,128)S(1)}, u32[]{:S(2)}, u32[]{:S(2)}) collective-permute-start(f32[8,8,128]{2,1,0:T(8,128)S(1)} %chain.3.refs_3_), channel_id=1, source_target_pairs={{16,0},{17,1},{18,2},{19,3},{20,4},{21,5},{22,6},{23,7},{24,8},{25... | collective-permute-start | bytes 98312 | tf_op jit(solution)/shard_map/ppermute | solution.py:470
  106.2 3.9 %collective-permute-start.17 = (f32[8,8,128]{2,1,0:T(8,128)S(1)}, f32[8,8,128]{2,1,0:T(8,128)S(1)}, u32[]{:S(2)}, u32[]{:S(2)}) collective-permute-start(f32[8,8,128]{2,1,0:T(8,128)S(1)} %chain.4.refs_3_), channel_id=1, source_target_pairs={{192,0},{193,1},{194,2},{195,3},{196,4},{197,5},{198,6},{199,7},{2... | collective-permute-start | bytes 98312 | tf_op jit(solution)/shard_map/ppermute | solution.py:470
  106.8 7.3 %collective-permute-start.18 = (f32[8,8,128]{2,1,0:T(8,128)S(1)}, f32[8,8,128]{2,1,0:T(8,128)S(1)}, u32[]{:S(2)}, u32[]{:S(2)}) collective-permute-start(f32[8,8,128]{2,1,0:T(8,128)S(1)} %chain.4.refs_3_), channel_id=1, source_target_pairs={{128,0},{129,1},{130,2},{131,3},{132,4},{133,5},{134,6},{135,7},{1... | collective-permute-start | bytes 98312 | tf_op jit(solution)/shard_map/ppermute | solution.py:470
  108.1 9.7 %collective-permute-start.19 = (f32[8,8,128]{2,1,0:T(8,128)S(1)}, f32[8,8,128]{2,1,0:T(8,128)S(1)}, u32[]{:S(2)}, u32[]{:S(2)}) collective-permute-start(f32[8,8,128]{2,1,0:T(8,128)S(1)} %chain.4.refs_3_), channel_id=1, source_target_pairs={{64,0},{65,1},{66,2},{67,3},{68,4},{69,5},{70,6},{71,7},{72,8},{73... | collective-permute-start | bytes 98312 | tf_op jit(solution)/shard_map/ppermute | solution.py:470
  (10 other events, 10.3 us)

commit v2 on v0

v2 whole, which is shorter than its diff:
```python
import functools

import jax
import jax.numpy as jnp
from jax import lax
from jax.experimental import pallas as pl
from jax.experimental.pallas import tpu as pltpu
from jax.sharding import PartitionSpec as P

STEPS = 8
WIDE = 4
THIN = WIDE - 1
DEPTH = 8
AXES = ("tm", "slab")
DIFFUSION_FINE = 0.15
DIFFUSION_COARSE = 0.0375
HIGH = lax.Precision.HIGHEST
HBM = pl.BlockSpec(memory_space=pltpu.HBM)
SMEM = pl.BlockSpec(memory_space=pltpu.SMEM)
VMEM = pl.BlockSpec(memory_space=pltpu.VMEM)
PARAMS = pltpu.CompilerParams(vmem_limit_bytes=24 * 2**20)


def f32(*shape):
    return jax.ShapeDtypeStruct(shape, jnp.float32)


def call(kernel, name, outs, in_specs, args, scratch=(), out_specs=None):
    return pl.pallas_call(
        kernel,
        out_shape=outs,
        in_specs=in_specs,
        out_specs=out_specs or ((VMEM,) * len(outs) if isinstance(outs, tuple) else VMEM),
        scratch_shapes=list(scratch),
        compiler_params=PARAMS,
        name=name,
    )(*args)


def pack_kernel(where, adj, force, vel, upt, chip_out, near_out, vel_out, sem):
    odd = lax.rem(where[0], 2)
    copies = []

    def add(src, dst):
        copies.append(pltpu.make_async_copy(src, dst, sem.at[len(copies)]))

    def z(c):
        return jnp.where(odd == 1, c, DEPTH - 1 - c)

    for i in range(WIDE):
        add(adj.at[z(DEPTH - WIDE + i)], near_out.at[i])
    for i in range(THIN):
        c = z(DEPTH - THIN + i)
        add(force.at[c], near_out.at[WIDE + i])
        add(upt.at[c], near_out.at[WIDE + THIN + i])
        for part in range(3):
            add(vel.at[part, c], vel_out.at[part * THIN + i])
    for i in range(WIDE):
        add(adj.at[z(i)], chip_out.at[i])
    for i in range(THIN):
        c = z(i)
        add(force.at[c], chip_out.at[WIDE + i])
        add(upt.at[c], chip_out.at[WIDE + THIN + i])
        for part in range(3):
            add(vel.at[part, c], chip_out.at[WIDE + (2 + part) * THIN + i])
    for copy in copies:
        copy.start()
    for copy in copies:
        copy.wait()


def pack(where, adj, force, vel, upt):
    _, rows, cols = adj.shape
    return call(
        pack_kernel,
        "pack",
        (
            f32(WIDE + 5 * THIN, rows, cols),
            f32(WIDE + 2 * THIN, rows, cols),
            f32(3 * THIN, rows, cols),
        ),
        [SMEM] + [HBM] * 4,
        (where, adj, force, vel, upt),
        [pltpu.SemaphoreType.DMA((2 * (WIDE + 5 * THIN),))],
    )


def groups_of_four(rows, cols, value):
    i = lax.broadcasted_iota(jnp.int32, (rows, cols), 0)
    j = lax.broadcasted_iota(jnp.int32, (rows, cols), 1)
    if rows > cols:
        i = lax.shift_right_logical(i, 2)
    else:
        j = lax.shift_right_logical(j, 2)
    return jnp.where(i == j, value, 0.0)


def restrict_summed(summed):
    rows, cols = summed.shape
    down = jnp.dot(groups_of_four(rows // 4, rows, 1.0), summed, precision=HIGH)
    return jnp.dot(down, groups_of_four(cols, cols // 4, 1.0 / 64.0), precision=HIGH)


def restrict_kernel(adj, vel, upt, out):
    sums = []
    for read in (
        lambda z: adj[z],
        lambda z: vel[0, z],
        lambda z: vel[1, z],
        lambda z: vel[2, z],
        lambda z: upt[z],
    ):
        for z in range(0, DEPTH, 4):
            sums.append((read(z) + read(z + 1)) + (read(z + 2) + read(z + 3)))
    stacked = jnp.concatenate(sums, axis=0)
    out[...] = restrict_summed(stacked).reshape(out.shape)


def restrict_inputs(adj, vel, upt):
    depth, rows, cols = adj.shape
    return call(
        restrict_kernel,
        "restrict",
        f32(5 * depth // 4, rows // 4, cols // 4),
        [VMEM] * 3,
        (adj, vel, upt),
    )


def layer_step(state, now, i, coefs, sign, put):
    tiles, rows = state.shape[2], state.shape[3] - 16
    lane = lax.broadcasted_iota(jnp.int32, (8, 128), 1)
    first_lane, last_lane = lane == 0, lane == 127
    zero = jnp.zeros((8, 128), jnp.float32)
    for block in range(rows // 8):
        y = 8 + 8 * block
        mid = [state[now, i, t, pl.ds(y, 8)] for t in range(tiles)]
        ahead = [pltpu.roll(m, 127, 1) for m in mid]
        behind = [pltpu.roll(m, 1, 1) for m in mid]
        for t in range(tiles):
            xp = jnp.where(last_lane, ahead[t + 1] if t + 1 < tiles else zero, ahead[t])
            xm = jnp.where(first_lane, behind[t - 1] if t else zero, behind[t])
            zp = state[now, i + 1, t, pl.ds(y, 8)]
            zm = state[now, i - 1, t, pl.ds(y, 8)]
            yp = state[now, i, t, pl.ds(y + 1, 8)]
            ym = state[now, i, t, pl.ds(y - 1, 8)]
            at = (pl.ds(8 * block, 8), pl.ds(128 * t, 128))
            force, upt, vz, vy, vx = (ref[index + at] for ref, index in coefs)
            spread = ((zp + zm) + (yp + ym)) + (xp + xm)
            carried = vz * (sign * (zp - zm)) + vy * (yp - ym) + vx * (xp - xm)
            kept = ((1.0 - 6.0 * DIFFUSION_FINE) - upt) * mid[t]
            put(block, t, (DIFFUSION_FINE * spread + 0.5 * carried) + (kept + force))


def zero_pads(state):
    count, layers, tiles, rows, lanes = state.shape
    for edge in (0, rows - 8):
        state[:, :, :, pl.ds(edge, 8)] = jnp.zeros((count, layers, tiles, 8, lanes), jnp.float32)


def put_layer(state, which, i, value):
    rows = value.shape[0]
    for t in range(state.shape[2]):
        state[which, i, t, pl.ds(8, rows)] = value[:, 128 * t : 128 * (t + 1)]


def own_coefs(odd, force, vel, upt, c):
    z = jnp.where(odd == 1, c, DEPTH - 1 - c)
    return [(force, (z,)), (upt, (z,)), (vel, (0, z)), (vel, (1, z)), (vel, (2, z))]


def inner_kernel(last, where, force, vel, upt, chip_part, near_part, halo, chip, *refs):
    if last:
        edge, out, coarse, state = refs
    else:
        edge, out, state = refs
    odd = lax.rem(where[0], 2)
    sign = jnp.where(odd == 1, 1.0, -1.0)
    zero_pads(state)
    for h in range(1, WIDE + 1):
        put_layer(state, 0, WIDE - h, halo[h - 1])
    for c in range(DEPTH):
        value = chip_part[c] if c < WIDE else near_part[c - WIDE]
        put_layer(state, 0, WIDE + c, value)
        if c >= DEPTH - 2:
            edge[0, c - (DEPTH - 2)] = value
    for step in range(1, WIDE + 1):
        now, later = (step - 1) % 2, step % 2
        for c in range(step - WIDE, DEPTH - step):
            if c < 0:
                i = -c - 1
                coefs = [(chip, (WIDE + part * THIN + i,)) for part in range(5)]
            else:
                coefs = own_coefs(odd, force, vel, upt, c)

            def put(block, t, value, c=c, step=step, later=later):
                at = (pl.ds(8 * block, 8), pl.ds(128 * t, 128))
                if step == WIDE:
                    out[(c,) + at] = value
                    return
                state[later, WIDE + c, t, pl.ds(8 + 8 * block, 8)] = value
                if c >= DEPTH - 2 - step:
                    edge[(step, c - (DEPTH - 2 - step)) + at] = value

            layer_step(state, now, WIDE + c, coefs, sign, put)
    if last:
        coarse[...] = restrict_summed((out[0] + out[1]) + (out[2] + out[3]))


def inner(last, where, force, vel, upt, chip_part, near_part, halo, chip):
    _, rows, cols = force.shape
    outs = (f32(WIDE, 2, rows, cols), f32(WIDE, rows, cols))
    if last:
        outs += (f32(rows // 4, cols // 4),)
    return call(
        functools.partial(inner_kernel, last),
        "inner_last" if last else "inner_first",
        outs,
        [SMEM] + [VMEM] * 7,
        (where, force, vel, upt, chip_part, near_part, halo, chip),
        [pltpu.VMEM((2, DEPTH + WIDE, cols // 128, rows + 16, 128), jnp.float32)],
    )


def wedge_kernel(last, where, force, vel, upt, edge, halo, near, near_vel, *refs):
    if last:
        coarse_chip, stepped, out, begun, coarse, state = refs
    else:
        out, state = refs
    slab = where[0]
    odd = lax.rem(slab, 2)
    sign = jnp.where(odd == 1, 1.0, -1.0)
    alive = jnp.where(jnp.logical_or(slab == 1, slab == 2), 1.0, 0.0)
    zero_pads(state)
    for h in range(1, WIDE + 1):
        put_layer(state, 0, 1 + h, halo[WIDE - h])
    for step in range(1, WIDE + 1):
        now, later = (step - 1) % 2, step % 2
        for i in range(2):
            put_layer(state, now, i, edge[step - 1, i])
        for j in range(WIDE):
            c = DEPTH - step + j
            if c < DEPTH:
                coefs = own_coefs(odd, force, vel, upt, c)
            else:
                i = THIN - 1 - (c - DEPTH)
                coefs = [(near, (WIDE + i,)), (near, (WIDE + THIN + i,))]
                coefs += [(near_vel, (part * THIN + i,)) for part in range(3)]

            def put(block, t, value, c=c, j=j, step=step, later=later):
                if c >= DEPTH:
                    value = value * alive
                if step == WIDE:
                    out[j, pl.ds(8 * block, 8), pl.ds(128 * t, 128)] = value
                else:
                    state[later, 2 + j, t, pl.ds(8 + 8 * block, 8)] = value

            layer_step(state, now, 1 + j, coefs, sign, put)
    if last:
        near_coarse = restrict_summed((out[0] + out[1]) + (out[2] + out[3]))
        chip_coarse = coarse_chip[...]
        coarse[0] = jnp.where(odd == 1, chip_coarse, near_coarse)
        coarse[1] = jnp.where(odd == 1, near_coarse, chip_coarse)
        kept = jnp.where(where[1] == 1, 0.0, 1.0)
        part = coarse[...] - kept * stepped[pl.ds(2 * slab, 2)]
        for copy in range(begun.shape[0]):
            begun[copy] = part


def wedge(last, where, force, vel, upt, edge, halo, near, near_vel, more=(), copies=0):
    _, rows, cols = force.shape
    outs = (f32(WIDE, rows, cols),)
    if last:
        outs += (f32(copies, 2, rows // 4, cols // 4), f32(2, rows // 4, cols // 4))
    return call(
        functools.partial(wedge_kernel, last),
        "wedge_last" if last else "wedge_first",
        outs,
        [SMEM] + [VMEM] * (7 + len(more)),
        (where, force, vel, upt, edge, halo, near, near_vel) + more,
        [pltpu.VMEM((2, WIDE + 2, cols // 128, rows + 16, 128), jnp.float32)],
    )


NEIGHBOURS = ((0, 0, 0), (1, 0, 0), (-1, 0, 0), (0, 1, 0), (0, -1, 0), (0, 0, 1), (0, 0, -1))
STENCIL = sorted({tuple(a + b for a, b in zip(p, q)) for p in NEIGHBOURS for q in NEIGHBOURS})


def shifted(field, offset):
    dz, dy, dx = offset
    if dz:
        field = jnp.concatenate([field[dz:], field[:dz]], axis=0)
    for axis, by in ((1, dy), (2, dx)):
        if by:
            size = field.shape[axis]
            field = pltpu.roll(field, (size - by) % size, axis)
    return field


def coarse_step(field, coef):
    depth = len(field)
    rows, cols = field[0].shape
    moved = {0: field}
    for dy in (-2, -1, 1, 2):
        moved[dy] = [pltpu.roll(c, (rows - dy) % rows, 0) for c in field]

    def part(dx, z):
        total = None
        for k, offset in enumerate(STENCIL):
            if offset[2] != dx or not 0 <= z + offset[0] < depth:
                continue
            term = coef[k, z] * moved[offset[1]][z + offset[0]]
            total = term if total is None else total + term
        return total

    sides = []
    for z in range(depth):
        sides.append([pltpu.roll(part(dx, z), (cols - dx) % cols, 1) for dx in (-2, 2, -1, 1)])
    return [part(0, z) + ((s[0] + s[1]) + (s[2] + s[3])) for z, s in enumerate(sides)]


def steps(field, coef, count):
    def body(_, layers):
        return tuple(coarse_step(coarse_step(list(layers), coef), coef))

    if count >= 2:
        field = lax.fori_loop(0, count // 2, body, tuple(field))
    if count % 2:
        field = coarse_step(list(field), coef)
    return list(field)


def prepare_kernel(where, own, one, two, three, coef, stepped, whole):
    slab = where[0]
    depth = own.shape[0] // 5
    for flip, ref in enumerate((own, one, two, three)):
        first = lax.bitwise_xor(slab, flip) * depth
        for part in range(5):
            whole[part, pl.ds(first, depth)] = ref[pl.ds(part * depth, depth)]
    full = whole.shape[1:]
    half = {NEIGHBOURS[0]: (1.0 - 6.0 * DIFFUSION_COARSE) - 4.0 * whole[4]}
    for dim in range(3):
        v = whole[1 + dim]
        half[NEIGHBOURS[0]] -= jnp.abs(v)
        at = lax.broadcasted_iota(jnp.int32, full, dim)
        plus = DIFFUSION_COARSE + jnp.maximum(v, 0.0)
        minus = DIFFUSION_COARSE - jnp.minimum(v, 0.0)
        half[NEIGHBOURS[1 + 2 * dim]] = jnp.where(at == full[dim] - 1, 0.0, plus)
        half[NEIGHBOURS[2 + 2 * dim]] = jnp.where(at == 0, 0.0, minus)
    both = {}
    for p in NEIGHBOURS:
        for q in NEIGHBOURS:
            offset = tuple(a + b for a, b in zip(p, q))
            term = half[p] * shifted(half[q], p)
            both[offset] = both[offset] + term if offset in both else term
    for k, offset in enumerate(STENCIL):
        coef[k] = shifted(both[offset], (0, 0, -offset[2]))
    field = coarse_step([whole[0, z] for z in range(full[0])], coef)
    for z in range(full[0]):
        stepped[z] = field[z]


def prepare(where, parts):
    depth5, rows, cols = parts[0].shape
    full = (4 * depth5 // 5, rows, cols)
    return call(
        prepare_kernel,
        "prepare",
        (f32(len(STENCIL), *full), f32(*full)),
        [SMEM] + [VMEM] * 4,
        (where, *parts),
        [pltpu.VMEM((5,) + full, jnp.float32)],
    )


def outer_kernel(inner_count, where, coef, own, one, two, three, out, whole):
    slab, group, place = where[0], where[2], where[3]
    count, part_depth = own.shape[:2]
    depth = whole.shape[1]
    for flip, ref in enumerate((own, one, two, three)):
        first = lax.bitwise_xor(slab, flip) * part_depth
        for r in range(count):
            whole[r, pl.ds(first, part_depth)] = ref[r]

    def body(i, layers):
        r = count - 2 - i
        layers = steps(layers, coef, inner_count)
        return tuple(layers[z] + whole[r, z] for z in range(depth))

    later = jnp.where(group == count - 1, 0.0, 1.0)
    field = tuple(later * whole[count - 1, z] for z in range(depth))
    without = lax.fori_loop(0, count - 2 - group, body, field)
    stepped = steps(without, coef, inner_count)
    for z in range(depth):
        with_own = stepped[z] + whole[group, z]
        for target in range(out.shape[0]):
            out[target, z] = jnp.where(place >= target, with_own, without[z])


def outer(inner_count, where, coef, parts):
    full = coef.shape[1:]
    count = parts[0].shape[0]
    return call(
        functools.partial(outer_kernel, inner_count),
        "outer",
        f32(inner_count, *full),
        [SMEM] + [VMEM] * 5,
        (where, coef, *parts),
        [pltpu.VMEM((count,) + full, jnp.float32)],
    )


def finish_kernel(where, coef, terms, coarse, chip_part, near_part, corrected, coarse_new):
    slab, place = where[0], where[3]
    odd = lax.rem(slab, 2)
    count, depth = terms.shape[:2]

    def term(j):
        return terms.at[lax.rem(place + j, count)]

    field = [term(count - 1)[z] for z in range(depth)]

    def body(i, layers):
        stepped = coarse_step(list(layers), coef)
        added = term(count - 2 - i)
        return tuple(stepped[z] + added[z] for z in range(depth))

    field = lax.fori_loop(0, count - 1, body, tuple(field))
    for z in range(depth):
        coarse_new[z] = field[z]
    part = coarse_new[pl.ds(2 * slab, 2)] - coarse[...]
    rows, cols = chip_part.shape[1:]
    flat = part.reshape(rows // 2, cols // 4)
    down = jnp.dot(groups_of_four(2 * rows, rows // 2, 1.0), flat, precision=HIGH)
    fine = jnp.dot(down, groups_of_four(cols // 4, cols, 1.0), precision=HIGH)
    lower, upper = fine[:rows], fine[rows:]
    for i in range(WIDE):
        z = jnp.where(odd == 1, i, DEPTH - 1 - i)
        corrected[z] = chip_part[i] + jnp.where(odd == 1, lower, upper)
        z = jnp.where(odd == 1, WIDE + i, DEPTH - 1 - WIDE - i)
        corrected[z] = near_part[i] + jnp.where(odd == 1, upper, lower)


def finish(where, coef, terms, coarse, chip_part, near_part):
    _, rows, cols = chip_part.shape
    return call(
        finish_kernel,
        "finish",
        (f32(DEPTH, rows, cols), f32(*terms.shape[1:])),
        [SMEM] + [VMEM] * 5,
        (where, coef, terms, coarse, chip_part, near_part),
    )


def per_device(adjoint_end, forcing, velocity, uptake):
    adj, force = adjoint_end[0], forcing[0]
    times, slabs = lax.axis_size("tm"), lax.axis_size("slab")
    slab, time = lax.axis_index("slab"), lax.axis_index("tm")
    inner_count = 8 if times >= 16 else 2
    outer_count = times // inner_count
    where = jnp.stack([slab, time == times - 1, time // inner_count, time % inner_count])
    where = where.astype(jnp.int32)

    def send(array, pairs):
        route = [(t0 * slabs + s0, t1 * slabs + s1) for (t0, s0), (t1, s1) in pairs]
        return lax.ppermute(array, AXES, route)

    def flipped(array, flip):
        return send(array, [((t, s ^ flip), (t, s)) for t in range(times) for s in range(slabs)])

    def to_next_chip(array, shift=0):
        pairs = [(1, 2), (2, 1)]
        return send(
            array, [((t, a), ((t + shift) % times, b)) for t in range(times) for a, b in pairs]
        )

    def gathered(array):
        return [array] + [flipped(array, flip) for flip in (1, 2, 3)]

    own = (force, velocity, uptake)
    chip_pack, near_pack, vel_pack = pack(where, adj, force, velocity, uptake)
    near = to_next_chip(near_pack)
    near_vel = to_next_chip(vel_pack, times // 2)
    chip = flipped(chip_pack, 1)
    edge, chip_part = inner(False, where, *own, chip_pack, near_pack, chip, chip)
    chip_halo = flipped(chip_part, 1)
    restricted = restrict_inputs(adj, velocity, uptake)
    near, near_vel, restricted, edge = lax.optimization_barrier((near, near_vel, restricted, edge))
    (near_part,) = wedge(False, where, *own, edge, near, near, near_vel)
    near_halo = to_next_chip(near_part)
    edge, chip_part, coarse_chip = inner(True, where, *own, chip_part, near_part, chip_halo, chip)
    coef, stepped = prepare(where, gathered(restricted))
    near_halo, edge, coef, stepped = lax.optimization_barrier((near_halo, edge, coef, stepped))
    near_part, begun, coarse = wedge(
        True, where, *own, edge, near_halo, near, near_vel, (coarse_chip, stepped), outer_count
    )

    across = [[g * inner_count + i for g in range(outer_count)] for i in range(inner_count)]
    within = [[g * inner_count + i for i in range(inner_count)] for g in range(outer_count)]
    begun = lax.all_to_all(begun, "tm", 0, 0, axis_index_groups=across)
    terms = outer(inner_count, where, coef, gathered(begun))
    terms = lax.all_to_all(terms, "tm", 0, 0, axis_index_groups=within)
    corrected, coarse_new = finish(where, coef, terms, coarse, chip_part, near_part)
    return corrected[None], coarse_new[None]


def solution(mesh):
    in_specs = (
        P("tm", "slab", None, None),
        P("tm", "slab", None, None),
        P(None, "slab", None, None),
        P("slab", None, None),
    )
    out_specs = (P("tm", "slab", None, None), P("tm", None, None, None))
    return jax.shard_map(
        per_device, mesh=mesh, in_specs=in_specs, out_specs=out_specs, check_vma=False
    )
```

time: 981 us -> 89.5 us (0.09)
  the two profiles are of different devices: /device:TPU:24 before, /device:TPU:1 now
where the time goes in v2:
time: 89.5 us; the launch traced here: 88.3 us
  blocking collectives  29.1 us (33%)
  Pallas kernels  23.9 us (27%)
  starting transfers between devices  16.7 us (19%)
  waiting for transfers between devices  13.2 us (15%)
  local copies, waits for them, and re-layouts  4.55 us (5%)
    pallas_call x9, Pallas kernels, call(): pl.pallas_call(kernel, out_shape=outs, in_specs=in_specs, out_specs=out_s...  23.9 us
    all_to_all x1, blocking collectives, per_device(): terms = lax.all_to_all(terms, 'tm', 0, 0, axis_index_groups=within)  17.7 us
    ppermute x11, starting transfers between devices, send(): return lax.ppermute(array, AXES, route)  16.7 us
    ppermute x11, waiting for transfers between devices, send(): return lax.ppermute(array, AXES, route)  13.2 us
    all_to_all x1, blocking collectives, per_device(): begun = lax.all_to_all(begun, 'tm', 0, 0, axis_index_groups=across)  11.4 us
    unnamed x14, local copies, waits for them, and re-layouts  4.55 us
  transfers between devices with their start and end apart: 11, of which 5 were waited for; matrix products, arithmetic and copies ran while one was open for 0% of the time, Pallas kernels for 10%

profile of v2, /device:TPU:1, one launch (start us, length us, event | category | flops | bytes accessed | tf_op | source)
XLA Modules:
  0.0 88.3 jit_solution(12104293042725297196)
XLA Ops:
  0.7 1.4 %copy-done = f32[3,8,32,512]{3,2,1,0:T(8,128)S(1)} copy-done((f32[3,8,32,512]{3,2,1,0:T(8,128)S(1)}, f32[3,8,32,512]{3,2,1,0:T(8,128)}, u32[]{:S(2)}) %copy-start) | copy-done | bytes 1572888
  2.1 1.0 %copy-done.2 = f32[8,32,512]{2,1,0:T(8,128)S(1)} copy-done((f32[8,32,512]{2,1,0:T(8,128)S(1)}, f32[8,32,512]{2,1,0:T(8,128)}, u32[]{:S(2)}) %copy-start.2) | copy-done | bytes 524312
  3.2 1.0 %copy-done.4 = f32[1,8,32,512]{3,2,1,0:T(8,128)S(1)} copy-done((f32[1,8,32,512]{3,2,1,0:T(8,128)S(1)}, f32[1,8,32,512]{3,2,1,0:T(8,128)}, u32[]{:S(2)}) %copy-start.4) | copy-done | bytes 524312
  4.2 1.0 %copy-done.6 = f32[1,8,32,512]{3,2,1,0:T(8,128)S(1)} copy-done((f32[1,8,32,512]{3,2,1,0:T(8,128)S(1)}, f32[1,8,32,512]{3,2,1,0:T(8,128)}, u32[]{:S(2)}) %copy-start.6) | copy-done | bytes 524312
  5.3 4.2 %pack.1 = (f32[19,32,512]{2,1,0:T(8,128)S(1)}, f32[10,32,512]{2,1,0:T(8,128)S(1)}, f32[9,32,512]{2,1,0:T(8,128)S(1)}) custom-call(s32[4]{0:T(128)S(1)} %pad_add_fusion.where, f32[8,32,512]{2,1,0:T(8,128)S(1)} %bitcast.13, f32[8,32,512]{2,1,0:T(8,128)S(1)} %bitcast.8, f32[3,8,32,512]{3,2,1,0:T(8,128)S(1)} %copy-done, f32[8,32,512]{2,1,0:T(8,128)S(1)} %copy-done.2), custom_call_target="tpu_custom_call" | custom-call | tf_op jit(solution)/shard_map/pack/pallas_call | solution.py:29
  9.4 3.3 %collective-permute-start.2 = (f32[19,32,512]{2,1,0:T(8,128)S(1)}, f32[19,32,512]{2,1,0:T(8,128)S(1)}, u32[]{:S(2)}, u32[]{:S(2)}) collective-permute-start(f32[19,32,512]{2,1,0:T(8,128)S(1)} %get-tuple-element.27.chip_part), channel_id=1, source_target_pairs={{1,0},{0,1},{3,2},{2,3},{5,4},{4,5},{7,6},{6,7},{9,8},{8,9},{11,10... | collective-permute-start | bytes 3735560 | tf_op jit(solution)/shard_map/ppermute | solution.py:466
  12.8 1.9 %collective-permute-start = (f32[10,32,512]{2,1,0:T(8,128)S(1)}, f32[10,32,512]{2,1,0:T(8,128)S(1)}, u32[]{:S(2)}, u32[]{:S(2)}) collective-permute-start(f32[10,32,512]{2,1,0:T(8,128)S(1)} %get-tuple-element.25.near_part), channel_id=1, source_target_pairs={{1,2},{2,1},{5,6},{6,5},{9,10},{10,9},{13,14},{14,13},{17,18},{18,... | collective-permute-start | bytes 1966088 | tf_op jit(solution)/shard_map/ppermute | solution.py:466
  14.7 3.8 %collective-permute-start.1 = (f32[9,32,512]{2,1,0:T(8,128)S(1)}, f32[9,32,512]{2,1,0:T(8,128)S(1)}, u32[]{:S(2)}, u32[]{:S(2)}) collective-permute-start(f32[9,32,512]{2,1,0:T(8,128)S(1)} %get-tuple-element.26), channel_id=1, source_target_pairs={{1,130},{2,129},{5,134},{6,133},{9,138},{10,137},{13,142},{14,141}... | collective-permute-start | bytes 1769480 | tf_op jit(solution)/shard_map/ppermute | solution.py:466
  19.4 2.3 %inner_first.1 = (f32[4,2,32,512]{3,2,1,0:T(8,128)S(1)}, f32[4,32,512]{2,1,0:T(8,128)S(1)}) custom-call(s32[4]{0:T(128)S(1)} %pad_add_fusion.where, f32[8,32,512]{2,1,0:T(8,128)S(1)} %bitcast.9, f32[3,8,32,512]{3,2,1,0:T(8,128)S(1)} %copy-done.1, f32[8,32,512]{2,1,0:T(8,128)S(1)} %copy-done.3, f32[19,32,512]{2,1,0:T(8,128)S(1)} %get-tuple-element.27.chip_part, ...), custom_call_target="tpu_custom_call" | custom-call | tf_op jit(solution)/shard_map/inner_first/pallas_call | solution.py:29
  21.8 5.5 %collective-permute-done.1.near_vel = f32[9,32,512]{2,1,0:T(8,128)S(1)} collective-permute-done((f32[9,32,512]{2,1,0:T(8,128)S(1)}, f32[9,32,512]{2,1,0:T(8,128)S(1)}, u32[]{:S(2)}, u32[]{:S(2)}) %collective-permute-start.1) | collective-permute-done | bytes 589856 | tf_op jit(solution)/shard_map/ppermute | solution.py:466
  27.3 1.6 %wedge_first.1.near_part = f32[4,32,512]{2,1,0:T(8,128)S(1)} custom-call(s32[4]{0:T(128)S(1)} %pad_add_fusion.where, f32[8,32,512]{2,1,0:T(8,128)S(1)} %bitcast.10, f32[3,8,32,512]{3,2,1,0:T(8,128)S(1)} %copy-done.1, f32[8,32,512]{2,1,0:T(8,128)S(1)} %copy-done.3, f32[4,2,32,512]{3,2,1,0:T(8,128)S(1)} %get-tuple-element.29.edge, ...), custom_call_target="tpu_custom_call" | custom-call | tf_op jit(solution)/shard_map/wedge_first/pallas_call | solution.py:29
  28.8 2.4 %collective-permute-start.3 = (f32[4,32,512]{2,1,0:T(8,128)S(1)}, f32[4,32,512]{2,1,0:T(8,128)S(1)}, u32[]{:S(2)}, u32[]{:S(2)}) collective-permute-start(f32[4,32,512]{2,1,0:T(8,128)S(1)} %wedge_first.1.near_part), channel_id=1, source_target_pairs={{1,2},{2,1},{5,6},{6,5},{9,10},{10,9},{13,14},{14,13},{17,18},{18,... | collective-permute-start | bytes 786440 | tf_op jit(solution)/shard_map/ppermute | solution.py:466
  31.4 1.3 %collective-permute-start.6 = (f32[10,8,128]{2,1,0:T(8,128)S(1)}, f32[10,8,128]{2,1,0:T(8,128)S(1)}, u32[]{:S(2)}, u32[]{:S(2)}) collective-permute-start(f32[10,8,128]{2,1,0:T(8,128)S(1)} %restrict.1.own), channel_id=1, source_target_pairs={{2,0},{3,1},{0,2},{1,3},{6,4},{7,5},{4,6},{5,7},{10,8},{11,9},{8,1... | collective-permute-start | bytes 122888 | tf_op jit(solution)/shard_map/ppermute | solution.py:466
  33.5 2.4 %collective-permute-done.6.two = f32[10,8,128]{2,1,0:T(8,128)S(1)} collective-permute-done((f32[10,8,128]{2,1,0:T(8,128)S(1)}, f32[10,8,128]{2,1,0:T(8,128)S(1)}, u32[]{:S(2)}, u32[]{:S(2)}) %collective-permute-start.6) | collective-permute-done | bytes 40992 | tf_op jit(solution)/shard_map/ppermute | solution.py:466
  35.9 2.4 %collective-permute-done.7.three = f32[10,8,128]{2,1,0:T(8,128)S(1)} collective-permute-done((f32[10,8,128]{2,1,0:T(8,128)S(1)}, f32[10,8,128]{2,1,0:T(8,128)S(1)}, u32[]{:S(2)}, u32[]{:S(2)}) %collective-permute-start.7) | collective-permute-done | bytes 40992 | tf_op jit(solution)/shard_map/ppermute | solution.py:466
  38.3 1.0 %prepare.1 = (f32[25,8,8,128]{3,2,1,0:T(8,128)S(1)}, f32[8,8,128]{2,1,0:T(8,128)S(1)}) custom-call(s32[4]{0:T(128)S(1)} %pad_add_fusion.where, f32[10,8,128]{2,1,0:T(8,128)S(1)} %restrict.1.own, f32[10,8,128]{2,1,0:T(8,128)S(1)} %collective-permute-done.5.one, f32[10,8,128]{2,1,0:T(8,128)S(1)} %collective-permute-done.6.two, ...), custom_call_target="tpu_custom_call" | custom-call | tf_op jit(solution)/shard_map/prepare/pallas_call | solution.py:29
  39.3 2.7 %inner_last.1 = (f32[4,2,32,512]{3,2,1,0:T(8,128)S(1)}, f32[4,32,512]{2,1,0:T(8,128)S(1)}, f32[8,128]{1,0:T(8,128)S(1)}) custom-call(s32[4]{0:T(128)S(1)} %pad_add_fusion.where, f32[8,32,512]{2,1,0:T(8,128)S(1)} %bitcast.11, f32[3,8,32,512]{3,2,1,0:T(8,128)S(1)} %copy-done.1, f32[8,32,512]{2,1,0:T(8,128)S(1)} %copy-done.3, ...), custom_call_target="tpu_custom_call" | custom-call | tf_op jit(solution)/shard_map/inner_last/pallas_call | solution.py:29
  42.0 1.9 %wedge_last.1 = (f32[4,32,512]{2,1,0:T(8,128)S(1)}, f32[8,2,8,128]{3,2,1,0:T(8,128)S(1)}, f32[2,8,128]{2,1,0:T(8,128)S(1)}) custom-call(s32[4]{0:T(128)S(1)} %pad_add_fusion.where, f32[8,32,512]{2,1,0:T(8,128)S(1)} %bitcast.12, f32[3,8,32,512]{3,2,1,0:T(8,128)S(1)} %copy-done.1, f32[8,32,512]{2,1,0:T(8,128)S(1)} %copy-done.3, ...), custom_call_target="tpu_custom_call" | custom-call | tf_op jit(solution)/shard_map/wedge_last/pallas_call | solution.py:29
  44.0 11.4 %all_to_all.10.own = f32[8,2,8,128]{3,2,1,0:T(8,128)S(1)} all-to-all(f32[8,2,8,128]{3,2,1,0:T(8,128)S(1)} %get-tuple-element.42), channel_id=1, replica_groups={{0,32,64,96,128,160,192,224},{4,36,68,100,132,164,196,228},{8,40,72,104..., dimensions={0} | all-to-all | bytes 131072 | tf_op jit(solution)/shard_map/all_to_all | solution.py:500
  55.4 2.6 %collective-permute-start.10 = (f32[8,2,8,128]{3,2,1,0:T(8,128)S(1)}, f32[8,2,8,128]{3,2,1,0:T(8,128)S(1)}, u32[]{:S(2)}, u32[]{:S(2)}) collective-permute-start(f32[8,2,8,128]{3,2,1,0:T(8,128)S(1)} %all_to_all.10.own), channel_id=1, source_target_pairs={{3,0},{2,1},{1,2},{0,3},{7,4},{6,5},{5,6},{4,7},{11,8},{10,9},{9,1... | collective-permute-start | bytes 196616 | tf_op jit(solution)/shard_map/ppermute | solution.py:466
  58.4 2.3 %collective-permute-done.10.three = f32[8,2,8,128]{3,2,1,0:T(8,128)S(1)} collective-permute-done((f32[8,2,8,128]{3,2,1,0:T(8,128)S(1)}, f32[8,2,8,128]{3,2,1,0:T(8,128)S(1)}, u32[]{:S(2)}, u32[]{:S(2)}) %collective-permute-start.10) | collective-permute-done | bytes 65568 | tf_op jit(solution)/shard_map/ppermute | solution.py:466
  61.3 6.8 %outer.1 = f32[8,8,8,128]{3,2,1,0:T(8,128)S(1)} custom-call(s32[4]{0:T(128)S(1)} %pad_add_fusion.where, f32[25,8,8,128]{3,2,1,0:T(8,128)S(1)} %get-tuple-element.37.coef, f32[8,2,8,128]{3,2,1,0:T(8,128)S(1)} %all_to_all.10.own, f32[8,2,8,128]{3,2,1,0:T(8,128)S(1)} %collective-permute-done.8.one, f32[8,2,8,128]{3,2,1,0:T(8,128)S(1)} %collective-permute-done.9.two, ...), custom_call_target="tpu_custom_call" | custom-call | tf_op jit(solution)/shard_map/outer/pallas_call | solution.py:29
  68.0 17.7 %all_to_all.11.terms = f32[8,8,8,128]{3,2,1,0:T(8,128)S(1)} all-to-all(f32[8,8,8,128]{3,2,1,0:T(8,128)S(1)} %outer.1), channel_id=1, replica_groups={{0,4,8,12,16,20,24,28},{32,36,40,44,48,52,56,60},{64,68,72,76,80,84,88,..., dimensions={0} | all-to-all | bytes 524288 | tf_op jit(solution)/shard_map/all_to_all | solution.py:502
  85.7 2.6 %finish.1 = (f32[8,32,512]{2,1,0:T(8,128)}, f32[8,8,128]{2,1,0:T(8,128)}) custom-call(s32[4]{0:T(128)S(1)} %pad_add_fusion.where, f32[25,8,8,128]{3,2,1,0:T(8,128)S(1)} %get-tuple-element.37.coef, f32[8,8,8,128]{3,2,1,0:T(8,128)S(1)} %all_to_all.11.terms, f32[2,8,128]{2,1,0:T(8,128)S(1)} %get-tuple-element.43.coarse, ...), custom_call_target="tpu_custom_call" | custom-call | tf_op jit(solution)/shard_map/finish/pallas_call | solution.py:29
  (24 shorter events, 3.0 us)
Async XLA Ops:
  0.7 1.4 %copy-start = (f32[3,8,32,512]{3,2,1,0:T(8,128)S(1)}, f32[3,8,32,512]{3,2,1,0:T(8,128)}, u32[]{:S(2)}) copy-start(f32[3,8,32,512]{3,2,1,0:T(8,128)} %vel.11) | copy-start | bytes 4718596
  2.1 1.0 %copy-start.2 = (f32[8,32,512]{2,1,0:T(8,128)S(1)}, f32[8,32,512]{2,1,0:T(8,128)}, u32[]{:S(2)}) copy-start(f32[8,32,512]{2,1,0:T(8,128)} %upt.11) | copy-start | bytes 1572868
  3.2 1.0 %copy-start.4 = (f32[1,8,32,512]{3,2,1,0:T(8,128)S(1)}, f32[1,8,32,512]{3,2,1,0:T(8,128)}, u32[]{:S(2)}) copy-start(f32[1,8,32,512]{3,2,1,0:T(8,128)} %param.5) | copy-start | bytes 1572868
  4.2 1.0 %copy-start.6 = (f32[1,8,32,512]{3,2,1,0:T(8,128)S(1)}, f32[1,8,32,512]{3,2,1,0:T(8,128)}, u32[]{:S(2)}) copy-start(f32[1,8,32,512]{3,2,1,0:T(8,128)} %param.4) | copy-start | bytes 1572868
  9.4 9.9 %collective-permute-start.2 = (f32[19,32,512]{2,1,0:T(8,128)S(1)}, f32[19,32,512]{2,1,0:T(8,128)S(1)}, u32[]{:S(2)}, u32[]{:S(2)}) collective-permute-start(f32[19,32,512]{2,1,0:T(8,128)S(1)} %get-tuple-element.27.chip_part), channel_id=1, source_target_pairs={{1,0},{0,1},{3,2},{2,3},{5,4},{4,5},{7,6},{6,7},{9,8},{8,9},{11,10... | collective-permute-start | bytes 3735560 | tf_op jit(solution)/shard_map/ppermute | solution.py:466
  12.8 14.5 %collective-permute-start = (f32[10,32,512]{2,1,0:T(8,128)S(1)}, f32[10,32,512]{2,1,0:T(8,128)S(1)}, u32[]{:S(2)}, u32[]{:S(2)}) collective-permute-start(f32[10,32,512]{2,1,0:T(8,128)S(1)} %get-tuple-element.25.near_part), channel_id=1, source_target_pairs={{1,2},{2,1},{5,6},{6,5},{9,10},{10,9},{13,14},{14,13},{17,18},{18,... | collective-permute-start | bytes 1966088 | tf_op jit(solution)/shard_map/ppermute | solution.py:466
  14.7 4.7 %copy-start.1 = (f32[3,8,32,512]{3,2,1,0:T(8,128)S(1)}, f32[3,8,32,512]{3,2,1,0:T(8,128)}, u32[]{:S(2)}) copy-start(f32[3,8,32,512]{3,2,1,0:T(8,128)} %vel.11) | copy-start | bytes 4718596
  14.7 4.7 %copy-start.3 = (f32[8,32,512]{2,1,0:T(8,128)S(1)}, f32[8,32,512]{2,1,0:T(8,128)}, u32[]{:S(2)}) copy-start(f32[8,32,512]{2,1,0:T(8,128)} %upt.11) | copy-start | bytes 1572868
  14.7 4.7 %copy-start.5 = (f32[1,8,32,512]{3,2,1,0:T(8,128)S(1)}, f32[1,8,32,512]{3,2,1,0:T(8,128)}, u32[]{:S(2)}) copy-start(f32[1,8,32,512]{3,2,1,0:T(8,128)} %param.5) | copy-start | bytes 1572868
  14.7 12.5 %collective-permute-start.1 = (f32[9,32,512]{2,1,0:T(8,128)S(1)}, f32[9,32,512]{2,1,0:T(8,128)S(1)}, u32[]{:S(2)}, u32[]{:S(2)}) collective-permute-start(f32[9,32,512]{2,1,0:T(8,128)S(1)} %get-tuple-element.26), channel_id=1, source_target_pairs={{1,130},{2,129},{5,134},{6,133},{9,138},{10,137},{13,142},{14,141}... | collective-permute-start | bytes 1769480 | tf_op jit(solution)/shard_map/ppermute | solution.py:466
  27.3 12.0 %collective-permute-start.4 = (f32[4,32,512]{2,1,0:T(8,128)S(1)}, f32[4,32,512]{2,1,0:T(8,128)S(1)}, u32[]{:S(2)}, u32[]{:S(2)}) collective-permute-start(f32[4,32,512]{2,1,0:T(8,128)S(1)} %get-tuple-element.32.chip_part), channel_id=1, source_target_pairs={{1,0},{0,1},{3,2},{2,3},{5,4},{4,5},{7,6},{6,7},{9,8},{8,9},{11,10... | collective-permute-start | bytes 786440 | tf_op jit(solution)/shard_map/ppermute | solution.py:466
  28.8 13.2 %collective-permute-start.3 = (f32[4,32,512]{2,1,0:T(8,128)S(1)}, f32[4,32,512]{2,1,0:T(8,128)S(1)}, u32[]{:S(2)}, u32[]{:S(2)}) collective-permute-start(f32[4,32,512]{2,1,0:T(8,128)S(1)} %wedge_first.1.near_part), channel_id=1, source_target_pairs={{1,2},{2,1},{5,6},{6,5},{9,10},{10,9},{13,14},{14,13},{17,18},{18,... | collective-permute-start | bytes 786440 | tf_op jit(solution)/shard_map/ppermute | solution.py:466
  31.3 2.2 %collective-permute-start.5 = (f32[10,8,128]{2,1,0:T(8,128)S(1)}, f32[10,8,128]{2,1,0:T(8,128)S(1)}, u32[]{:S(2)}, u32[]{:S(2)}) collective-permute-start(f32[10,8,128]{2,1,0:T(8,128)S(1)} %restrict.1.own), channel_id=1, source_target_pairs={{1,0},{0,1},{3,2},{2,3},{5,4},{4,5},{7,6},{6,7},{9,8},{8,9},{11,10... | collective-permute-start | bytes 122888 | tf_op jit(solution)/shard_map/ppermute | solution.py:466
  31.4 4.5 %collective-permute-start.6 = (f32[10,8,128]{2,1,0:T(8,128)S(1)}, f32[10,8,128]{2,1,0:T(8,128)S(1)}, u32[]{:S(2)}, u32[]{:S(2)}) collective-permute-start(f32[10,8,128]{2,1,0:T(8,128)S(1)} %restrict.1.own), channel_id=1, source_target_pairs={{2,0},{3,1},{0,2},{1,3},{6,4},{7,5},{4,6},{5,7},{10,8},{11,9},{8,1... | collective-permute-start | bytes 122888 | tf_op jit(solution)/shard_map/ppermute | solution.py:466
  32.7 5.6 %collective-permute-start.7 = (f32[10,8,128]{2,1,0:T(8,128)S(1)}, f32[10,8,128]{2,1,0:T(8,128)S(1)}, u32[]{:S(2)}, u32[]{:S(2)}) collective-permute-start(f32[10,8,128]{2,1,0:T(8,128)S(1)} %restrict.1.own), channel_id=1, source_target_pairs={{3,0},{2,1},{1,2},{0,3},{7,4},{6,5},{5,6},{4,7},{11,8},{10,9},{9,1... | collective-permute-start | bytes 122888 | tf_op jit(solution)/shard_map/ppermute | solution.py:466
  55.4 5.3 %collective-permute-start.10 = (f32[8,2,8,128]{3,2,1,0:T(8,128)S(1)}, f32[8,2,8,128]{3,2,1,0:T(8,128)S(1)}, u32[]{:S(2)}, u32[]{:S(2)}) collective-permute-start(f32[8,2,8,128]{3,2,1,0:T(8,128)S(1)} %all_to_all.10.own), channel_id=1, source_target_pairs={{3,0},{2,1},{1,2},{0,3},{7,4},{6,5},{5,6},{4,7},{11,8},{10,9},{9,1... | collective-permute-start | bytes 196616 | tf_op jit(solution)/shard_map/ppermute | solution.py:466
  57.9 2.8 %collective-permute-start.8 = (f32[8,2,8,128]{3,2,1,0:T(8,128)S(1)}, f32[8,2,8,128]{3,2,1,0:T(8,128)S(1)}, u32[]{:S(2)}, u32[]{:S(2)}) collective-permute-start(f32[8,2,8,128]{3,2,1,0:T(8,128)S(1)} %all_to_all.10.own), channel_id=1, source_target_pairs={{1,0},{0,1},{3,2},{2,3},{5,4},{4,5},{7,6},{6,7},{9,8},{8,9},{11,10... | collective-permute-start | bytes 196616 | tf_op jit(solution)/shard_map/ppermute | solution.py:466
  57.9 3.3 %collective-permute-start.9 = (f32[8,2,8,128]{3,2,1,0:T(8,128)S(1)}, f32[8,2,8,128]{3,2,1,0:T(8,128)S(1)}, u32[]{:S(2)}, u32[]{:S(2)}) collective-permute-start(f32[8,2,8,128]{3,2,1,0:T(8,128)S(1)} %all_to_all.10.own), channel_id=1, source_target_pairs={{2,0},{3,1},{0,2},{1,3},{6,4},{7,5},{4,6},{5,7},{10,8},{11,9},{8,1... | collective-permute-start | bytes 196616 | tf_op jit(solution)/shard_map/ppermute | solution.py:466

commit v3 on v2

--- a/solution.py
+++ b/solution.py
@@ -37,51 +37,46 @@
     )(*args)
 
 
-def pack_kernel(where, adj, force, vel, upt, chip_out, near_out, vel_out, sem):
+def pack_kernel(first, counts, where, adj, force, vel, upt, *refs):
+    *outs, sem = refs[-1 - len(counts) :]
+    places = [out.at[i] for out, count in zip(outs, counts) for i in range(count)]
     odd = lax.rem(where[0], 2)
     copies = []
 
-    def add(src, dst):
-        copies.append(pltpu.make_async_copy(src, dst, sem.at[len(copies)]))
+    def add(src):
+        at = len(copies)
+        copies.append(pltpu.make_async_copy(src, places[at], sem.at[at]))
 
     def z(c):
         return jnp.where(odd == 1, c, DEPTH - 1 - c)
 
     for i in range(WIDE):
-        add(adj.at[z(DEPTH - WIDE + i)], near_out.at[i])
-    for i in range(THIN):
-        c = z(DEPTH - THIN + i)
-        add(force.at[c], near_out.at[WIDE + i])
-        add(upt.at[c], near_out.at[WIDE + THIN + i])
-        for part in range(3):
-            add(vel.at[part, c], vel_out.at[part * THIN + i])
-    for i in range(WIDE):
-        add(adj.at[z(i)], chip_out.at[i])
-    for i in range(THIN):
-        c = z(i)
-        add(force.at[c], chip_out.at[WIDE + i])
-        add(upt.at[c], chip_out.at[WIDE + THIN + i])
-        for part in range(3):
-            add(vel.at[part, c], chip_out.at[WIDE + (2 + part) * THIN + i])
+        add(adj.at[z(first + i)])
+    inner_first = first + 1 if first else 0
+    layers = [z(inner_first + i) for i in range(THIN)]
+    for c in layers:
+        add(force.at[c])
+    for c in layers:
+        add(upt.at[c])
+    for part in range(3):
+        for c in layers:
+            add(vel.at[part, c])
     for copy in copies:
         copy.start()
     for copy in copies:
         copy.wait()
 
 
-def pack(where, adj, force, vel, upt):
+def pack(first, counts, where, adj, force, vel, upt, after=()):
     _, rows, cols = adj.shape
-    return call(
-        pack_kernel,
+    arrays = [pltpu.with_memory_space_constraint(x, pltpu.HBM) for x in (adj, force, vel, upt)]
+    return call(
+        functools.partial(pack_kernel, first, counts),
         "pack",
-        (
-            f32(WIDE + 5 * THIN, rows, cols),
-            f32(WIDE + 2 * THIN, rows, cols),
-            f32(3 * THIN, rows, cols),
-        ),
-        [SMEM] + [HBM] * 4,
-        (where, adj, force, vel, upt),
-        [pltpu.SemaphoreType.DMA((2 * (WIDE + 5 * THIN),))],
+        tuple(f32(count, rows, cols) for count in counts),
+        [SMEM] + [HBM] * (4 + len(after)),
+        (where, *arrays, *after),
+        [pltpu.SemaphoreType.DMA((WIDE + 5 * THIN,))],
     )
 
 
@@ -330,10 +325,12 @@
     return list(field)
 
 
-def prepare_kernel(where, own, one, two, three, coef, stepped, whole):
+def prepare_kernel(where, own, one, pair, coef, stepped, whole):
     slab = where[0]
-    depth = own.shape[0] // 5
-    for flip, ref in enumerate((own, one, two, three)):
+    size = own.shape[0]
+    depth = size // 5
+    parts = (own, one, pair.at[pl.ds(0, size)], pair.at[pl.ds(size, size)])
+    for flip, ref in enumerate(parts):
         first = lax.bitwise_xor(slab, flip) * depth
         for part in range(5):
             whole[part, pl.ds(first, depth)] = ref[pl.ds(part * depth, depth)]
@@ -367,17 +364,19 @@
         prepare_kernel,
         "prepare",
         (f32(len(STENCIL), *full), f32(*full)),
-        [SMEM] + [VMEM] * 4,
+        [SMEM] + [VMEM] * 3,
         (where, *parts),
         [pltpu.VMEM((5,) + full, jnp.float32)],
     )
 
 
-def outer_kernel(inner_count, where, coef, own, one, two, three, out, whole):
+def outer_kernel(inner_count, where, coef, own, one, pair, mine, *refs):
+    *outs, whole = refs
     slab, group, place = where[0], where[2], where[3]
     count, part_depth = own.shape[:2]
     depth = whole.shape[1]
-    for flip, ref in enumerate((own, one, two, three)):
+    parts = (own, one, pair.at[pl.ds(0, count)], pair.at[pl.ds(count, count)])
+    for flip, ref in enumerate(parts):
         first = lax.bitwise_xor(slab, flip) * part_depth
         for r in range(count):
             whole[r, pl.ds(first, part_depth)] = ref[r]
@@ -391,41 +390,52 @@
     field = tuple(later * whole[count - 1, z] for z in range(depth))
     without = lax.fori_loop(0, count - 2 - group, body, field)
     stepped = steps(without, coef, inner_count)
+    core = lax.rem(slab, 2)
     for z in range(depth):
         with_own = stepped[z] + whole[group, z]
-        for target in range(out.shape[0]):
-            out[target, z] = jnp.where(place >= target, with_own, without[z])
-
-
-def outer(inner_count, where, coef, parts):
+        mine[z] = with_own
+        for out, hops in zip(outs, distances(inner_count)):
+            before = jnp.where(core == 0, place >= hops, place + hops >= inner_count)
+            out[z] = jnp.where(before, with_own, without[z])
+
+
+def distances(count):
+    return range(count // 2, 0, -1)
+
+
+def outer(inner_count, where, coef, own, one, pair):
     full = coef.shape[1:]
-    count = parts[0].shape[0]
+    count = own.shape[0]
     return call(
         functools.partial(outer_kernel, inner_count),
         "outer",
-        f32(inner_count, *full),
-        [SMEM] + [VMEM] * 5,
-        (where, coef, *parts),
+        tuple(f32(*full) for _ in range(1 + inner_count // 2)),
+        [SMEM] + [VMEM] * 4,
+        (where, coef, own, one, pair),
         [pltpu.VMEM((count,) + full, jnp.float32)],
     )
 
 
-def finish_kernel(where, coef, terms, coarse, chip_part, near_part, corrected, coarse_new):
-    slab, place = where[0], where[3]
+def finish_kernel(inner_count, where, coef, mine, *refs):
+    half = inner_count // 2
+    here, there = refs[:half], refs[half : 2 * half]
+    coarse, chip_part, near_part, corrected, coarse_new, terms = refs[2 * half :]
+    slab = where[0]
     odd = lax.rem(slab, 2)
-    count, depth = terms.shape[:2]
-
-    def term(j):
-        return terms.at[lax.rem(place + j, count)]
-
-    field = [term(count - 1)[z] for z in range(depth)]
+    depth = mine.shape[0]
+    terms[0] = mine[...]
+    for k, hops in enumerate(distances(inner_count)):
+        mine_now, other_now = here[k][...], there[k][...]
+        terms[hops] = jnp.where(odd == 0, mine_now, other_now)
+        if hops < half:
+            terms[inner_count - hops] = jnp.where(odd == 0, other_now, mine_now)
 
     def body(i, layers):
         stepped = coarse_step(list(layers), coef)
-        added = term(count - 2 - i)
-        return tuple(stepped[z] + added[z] for z in range(depth))
-
-    field = lax.fori_loop(0, count - 1, body, tuple(field))
+        return tuple(stepped[z] + terms[inner_count - 2 - i, z] for z in range(depth))
+
+    field = tuple(terms[inner_count - 1, z] for z in range(depth))
+    field = lax.fori_loop(0, inner_count - 1, body, field)
     for z in range(depth):
         coarse_new[z] = field[z]
     part = coarse_new[pl.ds(2 * slab, 2)] - coarse[...]
@@ -441,14 +451,16 @@
         corrected[z] = near_part[i] + jnp.where(odd == 1, upper, lower)
 
 
-def finish(where, coef, terms, coarse, chip_part, near_part):
+def finish(inner_count, where, coef, mine, here, there, coarse, chip_part, near_part):
     _, rows, cols = chip_part.shape
-    return call(
-        finish_kernel,
+    args = (coef, mine, *here, *there, coarse, chip_part, near_part)
+    return call(
+        functools.partial(finish_kernel, inner_count),
         "finish",
-        (f32(DEPTH, rows, cols), f32(*terms.shape[1:])),
-        [SMEM] + [VMEM] * 5,
-        (where, coef, terms, coarse, chip_part, near_part),
+        (f32(DEPTH, rows, cols), f32(*mine.shape)),
+        [SMEM] + [VMEM] * len(args),
+        (where, *args),
+        [pltpu.VMEM((inner_count,) + mine.shape, jnp.float32)],
     )
 
 
@@ -475,32 +487,51 @@
         )
 
     def gathered(array):
-        return [array] + [flipped(array, flip) for flip in (1, 2, 3)]
+        one = flipped(array, 1)
+        return array, one, flipped(jnp.concatenate([array, one]), 2)
+
+    def within_group(array, hops):
+        pairs = []
+        for t in range(times):
+            group, place = divmod(t, inner_count)
+            for s in range(slabs):
+                if s % 2 and hops == inner_count // 2:
+                    continue
+                target = (place + hops if s % 2 else place - hops) % inner_count
+                pairs.append(((t, s), (group * inner_count + target, s)))
+        return send(array, pairs)
 
     own = (force, velocity, uptake)
-    chip_pack, near_pack, vel_pack = pack(where, adj, force, velocity, uptake)
+    near_pack, vel_pack = pack(
+        DEPTH - WIDE, (WIDE + 2 * THIN, 3 * THIN), where, adj, force, velocity, uptake
+    )
     near = to_next_chip(near_pack)
     near_vel = to_next_chip(vel_pack, times // 2)
+    (chip_pack,) = pack(
+        0, (WIDE + 5 * THIN,), where, adj, force, velocity, uptake, (near_pack, vel_pack)
+    )
     chip = flipped(chip_pack, 1)
+    restricted = gathered(restrict_inputs(adj, velocity, uptake))
     edge, chip_part = inner(False, where, *own, chip_pack, near_pack, chip, chip)
     chip_halo = flipped(chip_part, 1)
-    restricted = restrict_inputs(adj, velocity, uptake)
     near, near_vel, restricted, edge = lax.optimization_barrier((near, near_vel, restricted, edge))
     (near_part,) = wedge(False, where, *own, edge, near, near, near_vel)
     near_halo = to_next_chip(near_part)
     edge, chip_part, coarse_chip = inner(True, where, *own, chip_part, near_part, chip_halo, chip)
-    coef, stepped = prepare(where, gathered(restricted))
+    coef, stepped = prepare(where, restricted)
     near_halo, edge, coef, stepped = lax.optimization_barrier((near_halo, edge, coef, stepped))
     near_part, begun, coarse = wedge(
         True, where, *own, edge, near_halo, near, near_vel, (coarse_chip, stepped), outer_count
     )
 
     across = [[g * inner_count + i for g in range(outer_count)] for i in range(inner_count)]
-    within = [[g * inner_count + i for i in range(inner_count)] for g in range(outer_count)]
     begun = lax.all_to_all(begun, "tm", 0, 0, axis_index_groups=across)
-    terms = outer(inner_count, where, coef, gathered(begun))
-    terms = lax.all_to_all(terms, "tm", 0, 0, axis_index_groups=within)
-    corrected, coarse_new = finish(where, coef, terms, coarse, chip_part, near_part)
+    mine, *messages = outer(inner_count, where, coef, *gathered(begun))
+    here = [within_group(m, hops) for m, hops in zip(messages, distances(inner_count))]
+    there = [flipped(h, 1) for h in here]
+    corrected, coarse_new = finish(
+        inner_count, where, coef, mine, here, there, coarse, chip_part, near_part
+    )
     return corrected[None], coarse_new[None]
 
 

time: 89.5 us -> 81.6 us (0.912); the launches traced: 88.3 us -> 81.3 us
  blocking collectives: 29.1 us -> 11.4 us
  starting transfers between devices: 16.7 us -> 32.6 us
  local copies, waits for them, and re-layouts: 4.55 us -> 0.03 us
    all_to_all x1 -> x0, blocking collectives: 17.7 us -> none  [per_device(): terms = lax.all_to_all(terms, 'tm', 0, 0, axis_index_groups=within)]
    ppermute x11 -> x17, starting transfers between devices: 16.7 us -> 32.6 us  [send(): return lax.ppermute(array, AXES, route)]
    unnamed x14 -> x8, local copies, waits for them, and re-layouts: 4.55 us -> 0.03 us
    ppermute x11 -> x17, waiting for transfers between devices: 13.2 us -> 12.4 us  [send(): return lax.ppermute(array, AXES, route)]
    pallas_call x9 -> x10, Pallas kernels: 23.9 us -> 24 us  [call(): pl.pallas_call(kernel, out_shape=outs, in_specs=in_specs, out_specs=out_s...]
  transfers between devices with their start and end apart: 11 -> 17, of which waited for: 5 -> 7; matrix products, arithmetic and copies ran while one was open for 0% -> 0% of each run, Pallas kernels for 10% -> 10%
where the time goes in v3:
time: 81.6 us; the launch traced here: 81.3 us
  starting transfers between devices  32.6 us (40%)
  Pallas kernels  24 us (29%)
  waiting for transfers between devices  12.4 us (15%)
  blocking collectives  11.4 us (14%)
  between operations  0.83 us (1%)
    ppermute x17, starting transfers between devices, send(): return lax.ppermute(array, AXES, route)  32.6 us
    pallas_call x10, Pallas kernels, call(): pl.pallas_call(kernel, out_shape=outs, in_specs=in_specs, out_specs=out_s...  24 us
    ppermute x17, waiting for transfers between devices, send(): return lax.ppermute(array, AXES, route)  12.4 us
    all_to_all x1, blocking collectives, per_device(): begun = lax.all_to_all(begun, 'tm', 0, 0, axis_index_groups=across)  11.4 us
  transfers between devices with their start and end apart: 17, of which 7 were waited for; matrix products, arithmetic and copies ran while one was open for 0% of the time, Pallas kernels for 10%

profile of v3, /device:TPU:1, one launch (start us, length us, event | category | flops | bytes accessed | tf_op | source)
XLA Modules:
  0.0 81.3 jit_solution(16092642794776289653)
XLA Ops:
  0.7 2.0 %pack.2 = (f32[10,32,512]{2,1,0:T(8,128)S(1)}, f32[9,32,512]{2,1,0:T(8,128)S(1)}) custom-call(s32[4]{0:T(128)S(1)} %pad_add_fusion.where, f32[8,32,512]{2,1,0:T(8,128)} %bitcast.14, f32[8,32,512]{2,1,0:T(8,128)} %bitcast.8, f32[3,8,32,512]{3,2,1,0:T(8,128)} %vel.13, f32[8,32,512]{2,1,0:T(8,128)} %upt.13), custom_call_target="tpu_custom_call" | custom-call | tf_op jit(solution)/shard_map/pack/pallas_call | solution.py:29
  2.8 2.2 %pack.3.chip_part = f32[19,32,512]{2,1,0:T(8,128)S(1)} custom-call(s32[4]{0:T(128)S(1)} %pad_add_fusion.where, f32[8,32,512]{2,1,0:T(8,128)} %bitcast.15, f32[8,32,512]{2,1,0:T(8,128)} %bitcast.9, f32[3,8,32,512]{3,2,1,0:T(8,128)} %vel.13, f32[8,32,512]{2,1,0:T(8,128)} %upt.13, f32[10,32,512]{2,1,0:T(8,128)S(1)} %get-tuple-element.31.refs_0_.near_part, ...), custom_call_target="tpu_custom_call" | custom-call | tf_op jit(solution)/shard_map/pack/pallas_call | solution.py:29
  5.0 3.3 %collective-permute-start.4 = (f32[19,32,512]{2,1,0:T(8,128)S(1)}, f32[19,32,512]{2,1,0:T(8,128)S(1)}, u32[]{:S(2)}, u32[]{:S(2)}) collective-permute-start(f32[19,32,512]{2,1,0:T(8,128)S(1)} %pack.3.chip_part), channel_id=1, source_target_pairs={{1,0},{0,1},{3,2},{2,3},{5,4},{4,5},{7,6},{6,7},{9,8},{8,9},{11,10... | collective-permute-start | bytes 3735560 | tf_op jit(solution)/shard_map/ppermute | solution.py:478
  8.3 1.9 %collective-permute-start = (f32[10,32,512]{2,1,0:T(8,128)S(1)}, f32[10,32,512]{2,1,0:T(8,128)S(1)}, u32[]{:S(2)}, u32[]{:S(2)}) collective-permute-start(f32[10,32,512]{2,1,0:T(8,128)S(1)} %get-tuple-element.31.refs_0_.near_part), channel_id=1, source_target_pairs={{1,2},{2,1},{5,6},{6,5},{9,10},{10,9},{13,14},{14,13},{17,18},{18,... | collective-permute-start | bytes 1966088 | tf_op jit(solution)/shard_map/ppermute | solution.py:478
  10.3 3.6 %collective-permute-start.1 = (f32[9,32,512]{2,1,0:T(8,128)S(1)}, f32[9,32,512]{2,1,0:T(8,128)S(1)}, u32[]{:S(2)}, u32[]{:S(2)}) collective-permute-start(f32[9,32,512]{2,1,0:T(8,128)S(1)} %get-tuple-element.32.refs_1_), channel_id=1, source_target_pairs={{1,130},{2,129},{5,134},{6,133},{9,138},{10,137},{13,142},{14,141}... | collective-permute-start | bytes 1769480 | tf_op jit(solution)/shard_map/ppermute | solution.py:478
  14.9 1.2 %collective-permute-done.2.one = f32[10,8,128]{2,1,0:T(8,128)S(1)} collective-permute-done((f32[10,8,128]{2,1,0:T(8,128)S(1)}, f32[10,8,128]{2,1,0:T(8,128)S(1)}, u32[]{:S(2)}, u32[]{:S(2)}) %collective-permute-start.2) | collective-permute-done | bytes 40992 | tf_op jit(solution)/shard_map/ppermute | solution.py:478
  16.4 2.3 %inner_first.1 = (f32[4,2,32,512]{3,2,1,0:T(8,128)S(1)}, f32[4,32,512]{2,1,0:T(8,128)S(1)}) custom-call(s32[4]{0:T(128)S(1)} %pad_add_fusion.where, f32[8,32,512]{2,1,0:T(8,128)S(1)} %bitcast.10, f32[3,8,32,512]{3,2,1,0:T(8,128)S(1)} %copy-done, f32[8,32,512]{2,1,0:T(8,128)S(1)} %copy-done.1, f32[19,32,512]{2,1,0:T(8,128)S(1)} %pack.3.chip_part, ...), custom_call_target="tpu_custom_call" | custom-call | tf_op jit(solution)/shard_map/inner_first/pallas_call | solution.py:29
  18.7 1.7 %collective-permute-done.3.pair = f32[20,8,128]{2,1,0:T(8,128)S(1)} collective-permute-done((f32[20,8,128]{2,1,0:T(8,128)S(1)}, f32[20,8,128]{2,1,0:T(8,128)S(1)}, u32[]{:S(2)}, u32[]{:S(2)}) %collective-permute-start.3) | collective-permute-done | bytes 81952 | tf_op jit(solution)/shard_map/ppermute | solution.py:478
  20.4 2.3 %collective-permute-done.1.near_vel = f32[9,32,512]{2,1,0:T(8,128)S(1)} collective-permute-done((f32[9,32,512]{2,1,0:T(8,128)S(1)}, f32[9,32,512]{2,1,0:T(8,128)S(1)}, u32[]{:S(2)}, u32[]{:S(2)}) %collective-permute-start.1) | collective-permute-done | bytes 589856 | tf_op jit(solution)/shard_map/ppermute | solution.py:478
  22.7 1.6 %wedge_first.1.near_part = f32[4,32,512]{2,1,0:T(8,128)S(1)} custom-call(s32[4]{0:T(128)S(1)} %pad_add_fusion.where, f32[8,32,512]{2,1,0:T(8,128)S(1)} %bitcast.11, f32[3,8,32,512]{3,2,1,0:T(8,128)S(1)} %copy-done, f32[8,32,512]{2,1,0:T(8,128)S(1)} %copy-done.1, f32[4,2,32,512]{3,2,1,0:T(8,128)S(1)} %get-tuple-element.34.edge, ...), custom_call_target="tpu_custom_call" | custom-call | tf_op jit(solution)/shard_map/wedge_first/pallas_call | solution.py:29
  24.2 2.4 %collective-permute-start.5 = (f32[4,32,512]{2,1,0:T(8,128)S(1)}, f32[4,32,512]{2,1,0:T(8,128)S(1)}, u32[]{:S(2)}, u32[]{:S(2)}) collective-permute-start(f32[4,32,512]{2,1,0:T(8,128)S(1)} %wedge_first.1.near_part), channel_id=1, source_target_pairs={{1,2},{2,1},{5,6},{6,5},{9,10},{10,9},{13,14},{14,13},{17,18},{18,... | collective-permute-start | bytes 786440 | tf_op jit(solution)/shard_map/ppermute | solution.py:478
  27.7 2.7 %inner_last.1 = (f32[4,2,32,512]{3,2,1,0:T(8,128)S(1)}, f32[4,32,512]{2,1,0:T(8,128)S(1)}, f32[8,128]{1,0:T(8,128)S(1)}) custom-call(s32[4]{0:T(128)S(1)} %pad_add_fusion.where, f32[8,32,512]{2,1,0:T(8,128)S(1)} %bitcast.12, f32[3,8,32,512]{3,2,1,0:T(8,128)S(1)} %copy-done, f32[8,32,512]{2,1,0:T(8,128)S(1)} %copy-done.1, ...), custom_call_target="tpu_custom_call" | custom-call | tf_op jit(solution)/shard_map/inner_last/pallas_call | solution.py:29
  30.4 1.5 %collective-permute-done.5.halo = f32[4,32,512]{2,1,0:T(8,128)S(1)} collective-permute-done((f32[4,32,512]{2,1,0:T(8,128)S(1)}, f32[4,32,512]{2,1,0:T(8,128)S(1)}, u32[]{:S(2)}, u32[]{:S(2)}) %collective-permute-start.5) | collective-permute-done | bytes 262176 | tf_op jit(solution)/shard_map/ppermute | solution.py:478
  31.9 1.9 %wedge_last.1 = (f32[4,32,512]{2,1,0:T(8,128)S(1)}, f32[8,2,8,128]{3,2,1,0:T(8,128)S(1)}, f32[2,8,128]{2,1,0:T(8,128)S(1)}) custom-call(s32[4]{0:T(128)S(1)} %pad_add_fusion.where, f32[8,32,512]{2,1,0:T(8,128)S(1)} %bitcast.13, f32[3,8,32,512]{3,2,1,0:T(8,128)S(1)} %copy-done, f32[8,32,512]{2,1,0:T(8,128)S(1)} %copy-done.1, ...), custom_call_target="tpu_custom_call" | custom-call | tf_op jit(solution)/shard_map/wedge_last/pallas_call | solution.py:29
  33.9 11.4 %all_to_all.5.own = f32[8,2,8,128]{3,2,1,0:T(8,128)S(1)} all-to-all(f32[8,2,8,128]{3,2,1,0:T(8,128)S(1)} %get-tuple-element.49), channel_id=1, replica_groups={{0,32,64,96,128,160,192,224},{4,36,68,100,132,164,196,228},{8,40,72,104..., dimensions={0} | all-to-all | bytes 131072 | tf_op jit(solution)/shard_map/all_to_all | solution.py:528
  45.3 1.3 %collective-permute-done.7.one = f32[8,2,8,128]{3,2,1,0:T(8,128)S(1)} collective-permute-done((f32[8,2,8,128]{3,2,1,0:T(8,128)S(1)}, f32[8,2,8,128]{3,2,1,0:T(8,128)S(1)}, u32[]{:S(2)}, u32[]{:S(2)}) %collective-permute-start.7) | collective-permute-done | bytes 65568 | tf_op jit(solution)/shard_map/ppermute | solution.py:478
  46.6 2.4 %collective-permute-start.8 = (f32[16,2,8,128]{3,2,1,0:T(8,128)S(1)}, f32[16,2,8,128]{3,2,1,0:T(8,128)S(1)}, u32[]{:S(2)}, u32[]{:S(2)}) collective-permute-start(f32[16,2,8,128]{3,2,1,0:T(8,128)S(1)} %pad_maximum_fusion), channel_id=1, source_target_pairs={{2,0},{3,1},{0,2},{1,3},{6,4},{7,5},{4,6},{5,7},{10,8},{11,9},{8,1... | collective-permute-start | bytes 393224 | tf_op jit(solution)/shard_map/ppermute | solution.py:478
  49.0 3.6 %collective-permute-done.8.pair = f32[16,2,8,128]{3,2,1,0:T(8,128)S(1)} collective-permute-done((f32[16,2,8,128]{3,2,1,0:T(8,128)S(1)}, f32[16,2,8,128]{3,2,1,0:T(8,128)S(1)}, u32[]{:S(2)}, u32[]{:S(2)}) %collective-permute-start.8) | collective-permute-done | bytes 131104 | tf_op jit(solution)/shard_map/ppermute | solution.py:478
  52.5 6.7 %outer.1 = (f32[8,8,128]{2,1,0:T(8,128)S(1)}, f32[8,8,128]{2,1,0:T(8,128)S(1)}, f32[8,8,128]{2,1,0:T(8,128)S(1)}, f32[8,8,128]{2,1,0:T(8,128)S(1)}, f32[8,8,128]{2,1,0:T(8,128)S(1)}) custom-call(s32[4]{0:T(128)S(1)} %pad_add_fusion.where, f32[25,8,8,128]{3,2,1,0:T(8,128)S(1)} %get-tuple-element.44.coef, f32[8,2,8,128]{3,2,1,0:T(8,128)S(1)} %all_to_all.5.own, ...), custom_call_target="tpu_custom_call" | custom-call | tf_op jit(solution)/shard_map/outer/pallas_call | solution.py:29
  60.0 4.4 %collective-permute-start.10 = (f32[8,8,128]{2,1,0:T(8,128)S(1)}, f32[8,8,128]{2,1,0:T(8,128)S(1)}, u32[]{:S(2)}, u32[]{:S(2)}) collective-permute-start(f32[8,8,128]{2,1,0:T(8,128)S(1)} %get-tuple-element.52), channel_id=1, source_target_pairs={{0,20},{1,13},{2,22},{3,15},{4,24},{5,17},{6,26},{7,19},{8,28},{9,... | collective-permute-start | bytes 98312 | tf_op jit(solution)/shard_map/ppermute | solution.py:478
  64.4 3.3 %collective-permute-start.11 = (f32[8,8,128]{2,1,0:T(8,128)S(1)}, f32[8,8,128]{2,1,0:T(8,128)S(1)}, u32[]{:S(2)}, u32[]{:S(2)}) collective-permute-start(f32[8,8,128]{2,1,0:T(8,128)S(1)} %get-tuple-element.53), channel_id=1, source_target_pairs={{0,24},{1,9},{2,26},{3,11},{4,28},{5,13},{6,30},{7,15},{8,0},{9,17... | collective-permute-start | bytes 98312 | tf_op jit(solution)/shard_map/ppermute | solution.py:478
  68.4 6.5 %collective-permute-start.13 = (f32[8,8,128]{2,1,0:T(8,128)S(1)}, f32[8,8,128]{2,1,0:T(8,128)S(1)}, u32[]{:S(2)}, u32[]{:S(2)}) collective-permute-start(f32[8,8,128]{2,1,0:T(8,128)S(1)} %collective-permute-done.9.refs_0_), channel_id=1, source_target_pairs={{1,0},{0,1},{3,2},{2,3},{5,4},{4,5},{7,6},{6,7},{9,8},{8,9},{11,10... | collective-permute-start | bytes 98312 | tf_op jit(solution)/shard_map/ppermute | solution.py:478
  75.6 2.3 %collective-permute-start.16 = (f32[8,8,128]{2,1,0:T(8,128)S(1)}, f32[8,8,128]{2,1,0:T(8,128)S(1)}, u32[]{:S(2)}, u32[]{:S(2)}) collective-permute-start(f32[8,8,128]{2,1,0:T(8,128)S(1)} %collective-permute-done.12.refs_3_), channel_id=1, source_target_pairs={{1,0},{0,1},{3,2},{2,3},{5,4},{4,5},{7,6},{6,7},{9,8},{8,9},{11,10... | collective-permute-start | bytes 98312 | tf_op jit(solution)/shard_map/ppermute | solution.py:478
  78.7 2.6 %finish.1 = (f32[8,32,512]{2,1,0:T(8,128)}, f32[8,8,128]{2,1,0:T(8,128)}) custom-call(s32[4]{0:T(128)S(1)} %pad_add_fusion.where, f32[25,8,8,128]{3,2,1,0:T(8,128)S(1)} %get-tuple-element.44.coef, f32[8,8,128]{2,1,0:T(8,128)S(1)} %get-tuple-element.50.mine, f32[8,8,128]{2,1,0:T(8,128)S(1)} %collective-permute-done.9.refs_0_, ...), custom_call_target="tpu_custom_call" | custom-call | tf_op jit(solution)/shard_map/finish/pallas_call | solution.py:29
  (32 shorter events, 5.2 us)
Async XLA Ops:
  2.7 11.2 %copy-start = (f32[3,8,32,512]{3,2,1,0:T(8,128)S(1)}, f32[3,8,32,512]{3,2,1,0:T(8,128)}, u32[]{:S(2)}) copy-start(f32[3,8,32,512]{3,2,1,0:T(8,128)} %vel.13) | copy-start | bytes 4718596
  2.8 11.2 %copy-start.1 = (f32[8,32,512]{2,1,0:T(8,128)S(1)}, f32[8,32,512]{2,1,0:T(8,128)}, u32[]{:S(2)}) copy-start(f32[8,32,512]{2,1,0:T(8,128)} %upt.13) | copy-start | bytes 1572868
  2.8 11.2 %copy-start.3 = (f32[1,8,32,512]{3,2,1,0:T(8,128)S(1)}, f32[1,8,32,512]{3,2,1,0:T(8,128)}, u32[]{:S(2)}) copy-start(f32[1,8,32,512]{3,2,1,0:T(8,128)} %param.4) | copy-start | bytes 1572868
  5.0 11.4 %copy-start.2 = (f32[1,8,32,512]{3,2,1,0:T(8,128)S(1)}, f32[1,8,32,512]{3,2,1,0:T(8,128)}, u32[]{:S(2)}) copy-start(f32[1,8,32,512]{3,2,1,0:T(8,128)} %param.5) | copy-start | bytes 1572868
  5.0 11.3 %collective-permute-start.4 = (f32[19,32,512]{2,1,0:T(8,128)S(1)}, f32[19,32,512]{2,1,0:T(8,128)S(1)}, u32[]{:S(2)}, u32[]{:S(2)}) collective-permute-start(f32[19,32,512]{2,1,0:T(8,128)S(1)} %pack.3.chip_part), channel_id=1, source_target_pairs={{1,0},{0,1},{3,2},{2,3},{5,4},{4,5},{7,6},{6,7},{9,8},{8,9},{11,10... | collective-permute-start | bytes 3735560 | tf_op jit(solution)/shard_map/ppermute | solution.py:478
  8.3 14.3 %collective-permute-start = (f32[10,32,512]{2,1,0:T(8,128)S(1)}, f32[10,32,512]{2,1,0:T(8,128)S(1)}, u32[]{:S(2)}, u32[]{:S(2)}) collective-permute-start(f32[10,32,512]{2,1,0:T(8,128)S(1)} %get-tuple-element.31.refs_0_.near_part), channel_id=1, source_target_pairs={{1,2},{2,1},{5,6},{6,5},{9,10},{10,9},{13,14},{14,13},{17,18},{18,... | collective-permute-start | bytes 1966088 | tf_op jit(solution)/shard_map/ppermute | solution.py:478
  10.3 12.4 %collective-permute-start.1 = (f32[9,32,512]{2,1,0:T(8,128)S(1)}, f32[9,32,512]{2,1,0:T(8,128)S(1)}, u32[]{:S(2)}, u32[]{:S(2)}) collective-permute-start(f32[9,32,512]{2,1,0:T(8,128)S(1)} %get-tuple-element.32.refs_1_), channel_id=1, source_target_pairs={{1,130},{2,129},{5,134},{6,133},{9,138},{10,137},{13,142},{14,141}... | collective-permute-start | bytes 1769480 | tf_op jit(solution)/shard_map/ppermute | solution.py:478
  14.8 1.3 %collective-permute-start.2 = (f32[10,8,128]{2,1,0:T(8,128)S(1)}, f32[10,8,128]{2,1,0:T(8,128)S(1)}, u32[]{:S(2)}, u32[]{:S(2)}) collective-permute-start(f32[10,8,128]{2,1,0:T(8,128)S(1)} %restrict.1.own), channel_id=1, source_target_pairs={{1,0},{0,1},{3,2},{2,3},{5,4},{4,5},{7,6},{6,7},{9,8},{8,9},{11,10... | collective-permute-start | bytes 122888 | tf_op jit(solution)/shard_map/ppermute | solution.py:478
  16.1 4.2 %collective-permute-start.3 = (f32[20,8,128]{2,1,0:T(8,128)S(1)}, f32[20,8,128]{2,1,0:T(8,128)S(1)}, u32[]{:S(2)}, u32[]{:S(2)}) collective-permute-start(f32[20,8,128]{2,1,0:T(8,128)S(1)} %pad_maximum_fusion.1), channel_id=1, source_target_pairs={{2,0},{3,1},{0,2},{1,3},{6,4},{7,5},{4,6},{5,7},{10,8},{11,9},{8,1... | collective-permute-start | bytes 245768 | tf_op jit(solution)/shard_map/ppermute | solution.py:478
  22.7 5.0 %collective-permute-start.6 = (f32[4,32,512]{2,1,0:T(8,128)S(1)}, f32[4,32,512]{2,1,0:T(8,128)S(1)}, u32[]{:S(2)}, u32[]{:S(2)}) collective-permute-start(f32[4,32,512]{2,1,0:T(8,128)S(1)} %get-tuple-element.37.chip_part), channel_id=1, source_target_pairs={{1,0},{0,1},{3,2},{2,3},{5,4},{4,5},{7,6},{6,7},{9,8},{8,9},{11,10... | collective-permute-start | bytes 786440 | tf_op jit(solution)/shard_map/ppermute | solution.py:478
  24.2 7.7 %collective-permute-start.5 = (f32[4,32,512]{2,1,0:T(8,128)S(1)}, f32[4,32,512]{2,1,0:T(8,128)S(1)}, u32[]{:S(2)}, u32[]{:S(2)}) collective-permute-start(f32[4,32,512]{2,1,0:T(8,128)S(1)} %wedge_first.1.near_part), channel_id=1, source_target_pairs={{1,2},{2,1},{5,6},{6,5},{9,10},{10,9},{13,14},{14,13},{17,18},{18,... | collective-permute-start | bytes 786440 | tf_op jit(solution)/shard_map/ppermute | solution.py:478
  45.3 1.3 %collective-permute-start.7 = (f32[8,2,8,128]{3,2,1,0:T(8,128)S(1)}, f32[8,2,8,128]{3,2,1,0:T(8,128)S(1)}, u32[]{:S(2)}, u32[]{:S(2)}) collective-permute-start(f32[8,2,8,128]{3,2,1,0:T(8,128)S(1)} %all_to_all.5.own), channel_id=1, source_target_pairs={{1,0},{0,1},{3,2},{2,3},{5,4},{4,5},{7,6},{6,7},{9,8},{8,9},{11,10... | collective-permute-start | bytes 196616 | tf_op jit(solution)/shard_map/ppermute | solution.py:478
  46.6 6.0 %collective-permute-start.8 = (f32[16,2,8,128]{3,2,1,0:T(8,128)S(1)}, f32[16,2,8,128]{3,2,1,0:T(8,128)S(1)}, u32[]{:S(2)}, u32[]{:S(2)}) collective-permute-start(f32[16,2,8,128]{3,2,1,0:T(8,128)S(1)} %pad_maximum_fusion), channel_id=1, source_target_pairs={{2,0},{3,1},{0,2},{1,3},{6,4},{7,5},{4,6},{5,7},{10,8},{11,9},{8,1... | collective-permute-start | bytes 393224 | tf_op jit(solution)/shard_map/ppermute | solution.py:478
  59.3 9.1 %collective-permute-start.9 = (f32[8,8,128]{2,1,0:T(8,128)S(1)}, f32[8,8,128]{2,1,0:T(8,128)S(1)}, u32[]{:S(2)}, u32[]{:S(2)}) collective-permute-start(f32[8,8,128]{2,1,0:T(8,128)S(1)} %get-tuple-element.51), channel_id=1, source_target_pairs={{0,16},{2,18},{4,20},{6,22},{8,24},{10,26},{12,28},{14,30},{16,0},... | collective-permute-start | bytes 98312 | tf_op jit(solution)/shard_map/ppermute | solution.py:478
  60.0 15.0 %collective-permute-start.10 = (f32[8,8,128]{2,1,0:T(8,128)S(1)}, f32[8,8,128]{2,1,0:T(8,128)S(1)}, u32[]{:S(2)}, u32[]{:S(2)}) collective-permute-start(f32[8,8,128]{2,1,0:T(8,128)S(1)} %get-tuple-element.52), channel_id=1, source_target_pairs={{0,20},{1,13},{2,22},{3,15},{4,24},{5,17},{6,26},{7,19},{8,28},{9,... | collective-permute-start | bytes 98312 | tf_op jit(solution)/shard_map/ppermute | solution.py:478
  64.4 10.8 %collective-permute-start.11 = (f32[8,8,128]{2,1,0:T(8,128)S(1)}, f32[8,8,128]{2,1,0:T(8,128)S(1)}, u32[]{:S(2)}, u32[]{:S(2)}) collective-permute-start(f32[8,8,128]{2,1,0:T(8,128)S(1)} %get-tuple-element.53), channel_id=1, source_target_pairs={{0,24},{1,9},{2,26},{3,11},{4,28},{5,13},{6,30},{7,15},{8,0},{9,17... | collective-permute-start | bytes 98312 | tf_op jit(solution)/shard_map/ppermute | solution.py:478
  67.7 7.9 %collective-permute-start.12 = (f32[8,8,128]{2,1,0:T(8,128)S(1)}, f32[8,8,128]{2,1,0:T(8,128)S(1)}, u32[]{:S(2)}, u32[]{:S(2)}) collective-permute-start(f32[8,8,128]{2,1,0:T(8,128)S(1)} %get-tuple-element.54), channel_id=1, source_target_pairs={{0,28},{1,5},{2,30},{3,7},{4,0},{5,9},{6,2},{7,11},{8,4},{9,13},{1... | collective-permute-start | bytes 98312 | tf_op jit(solution)/shard_map/ppermute | solution.py:478
  68.4 9.4 %collective-permute-start.13 = (f32[8,8,128]{2,1,0:T(8,128)S(1)}, f32[8,8,128]{2,1,0:T(8,128)S(1)}, u32[]{:S(2)}, u32[]{:S(2)}) collective-permute-start(f32[8,8,128]{2,1,0:T(8,128)S(1)} %collective-permute-done.9.refs_0_), channel_id=1, source_target_pairs={{1,0},{0,1},{3,2},{2,3},{5,4},{4,5},{7,6},{6,7},{9,8},{8,9},{11,10... | collective-permute-start | bytes 98312 | tf_op jit(solution)/shard_map/ppermute | solution.py:478
  75.0 2.9 %collective-permute-start.14 = (f32[8,8,128]{2,1,0:T(8,128)S(1)}, f32[8,8,128]{2,1,0:T(8,128)S(1)}, u32[]{:S(2)}, u32[]{:S(2)}) collective-permute-start(f32[8,8,128]{2,1,0:T(8,128)S(1)} %collective-permute-done.10.refs_1_), channel_id=1, source_target_pairs={{1,0},{0,1},{3,2},{2,3},{5,4},{4,5},{7,6},{6,7},{9,8},{8,9},{11,10... | collective-permute-start | bytes 98312 | tf_op jit(solution)/shard_map/ppermute | solution.py:478
  75.1 2.7 %collective-permute-start.15 = (f32[8,8,128]{2,1,0:T(8,128)S(1)}, f32[8,8,128]{2,1,0:T(8,128)S(1)}, u32[]{:S(2)}, u32[]{:S(2)}) collective-permute-start(f32[8,8,128]{2,1,0:T(8,128)S(1)} %collective-permute-done.11.refs_2_), channel_id=1, source_target_pairs={{1,0},{0,1},{3,2},{2,3},{5,4},{4,5},{7,6},{6,7},{9,8},{8,9},{11,10... | collective-permute-start | bytes 98312 | tf_op jit(solution)/shard_map/ppermute | solution.py:478
  75.6 3.2 %collective-permute-start.16 = (f32[8,8,128]{2,1,0:T(8,128)S(1)}, f32[8,8,128]{2,1,0:T(8,128)S(1)}, u32[]{:S(2)}, u32[]{:S(2)}) collective-permute-start(f32[8,8,128]{2,1,0:T(8,128)S(1)} %collective-permute-done.12.refs_3_), channel_id=1, source_target_pairs={{1,0},{0,1},{3,2},{2,3},{5,4},{4,5},{7,6},{6,7},{9,8},{8,9},{11,10... | collective-permute-start | bytes 98312 | tf_op jit(solution)/shard_map/ppermute | solution.py:478

commit v4 on v2

--- a/solution.py
+++ b/solution.py
@@ -37,7 +37,7 @@
     )(*args)
 
 
-def pack_kernel(where, adj, force, vel, upt, chip_out, near_out, vel_out, sem):
+def pack_kernel(where, adj, force, vel, upt, near_out, vel_out, chip_out, sem):
     odd = lax.rem(where[0], 2)
     copies = []
 
@@ -69,19 +69,17 @@
         copy.wait()
 
 
-def pack(where, adj, force, vel, upt):
-    _, rows, cols = adj.shape
+def pack(where, *arrays):
+    _, rows, cols = arrays[0].shape
+    arrays = [pltpu.with_memory_space_constraint(x, pltpu.HBM) for x in arrays]
+    counts = (WIDE + 2 * THIN, 3 * THIN, WIDE + 5 * THIN)
     return call(
         pack_kernel,
         "pack",
-        (
-            f32(WIDE + 5 * THIN, rows, cols),
-            f32(WIDE + 2 * THIN, rows, cols),
-            f32(3 * THIN, rows, cols),
-        ),
+        tuple(f32(count, rows, cols) for count in counts),
         [SMEM] + [HBM] * 4,
-        (where, adj, force, vel, upt),
-        [pltpu.SemaphoreType.DMA((2 * (WIDE + 5 * THIN),))],
+        (where, *arrays),
+        [pltpu.SemaphoreType.DMA((sum(counts),))],
     )
 
 
@@ -330,10 +328,12 @@
     return list(field)
 
 
-def prepare_kernel(where, own, one, two, three, coef, stepped, whole):
+def prepare_kernel(where, own, one, pair, coef, stepped, whole):
     slab = where[0]
-    depth = own.shape[0] // 5
-    for flip, ref in enumerate((own, one, two, three)):
+    size = own.shape[0]
+    depth = size // 5
+    parts = (own, one, pair.at[pl.ds(0, size)], pair.at[pl.ds(size, size)])
+    for flip, ref in enumerate(parts):
         first = lax.bitwise_xor(slab, flip) * depth
         for part in range(5):
             whole[part, pl.ds(first, depth)] = ref[pl.ds(part * depth, depth)]
@@ -367,67 +367,73 @@
         prepare_kernel,
         "prepare",
         (f32(len(STENCIL), *full), f32(*full)),
-        [SMEM] + [VMEM] * 4,
+        [SMEM] + [VMEM] * 3,
         (where, *parts),
         [pltpu.VMEM((5,) + full, jnp.float32)],
     )
 
 
-def outer_kernel(inner_count, where, coef, own, one, two, three, out, whole):
-    slab, group, place = where[0], where[2], where[3]
+def within_kernel(where, coef, own, one, two, three, mine, total, whole):
+    slab, place = where[0], where[3]
     count, part_depth = own.shape[:2]
     depth = whole.shape[1]
     for flip, ref in enumerate((own, one, two, three)):
         first = lax.bitwise_xor(slab, flip) * part_depth
-        for r in range(count):
-            whole[r, pl.ds(first, part_depth)] = ref[r]
+        for t in range(count):
+            whole[t, pl.ds(first, part_depth)] = ref[t]
+
+    def keep(t, layers):
+        @pl.when(t == place)
+        def _():
+            for z in range(depth):
+                mine[z] = layers[z]
 
     def body(i, layers):
-        r = count - 2 - i
-        layers = steps(layers, coef, inner_count)
-        return tuple(layers[z] + whole[r, z] for z in range(depth))
-
-    later = jnp.where(group == count - 1, 0.0, 1.0)
-    field = tuple(later * whole[count - 1, z] for z in range(depth))
-    without = lax.fori_loop(0, count - 2 - group, body, field)
-    stepped = steps(without, coef, inner_count)
-    for z in range(depth):
-        with_own = stepped[z] + whole[group, z]
-        for target in range(out.shape[0]):
-            out[target, z] = jnp.where(place >= target, with_own, without[z])
-
-
-def outer(inner_count, where, coef, parts):
+        t = count - 2 - i
+        layers = coarse_step(list(layers), coef)
+        layers = tuple(layers[z] + whole[t, z] for z in range(depth))
+        keep(t, layers)
+        return layers
+
+    field = tuple(whole[count - 1, z] for z in range(depth))
+    keep(count - 1, field)
+    field = lax.fori_loop(0, count - 1, body, field)
+    for copy in range(total.shape[0]):
+        for z in range(depth):
+            total[copy, z] = field[z]
+
+
+def within(where, coef, parts, copies):
     full = coef.shape[1:]
     count = parts[0].shape[0]
     return call(
-        functools.partial(outer_kernel, inner_count),
-        "outer",
-        f32(inner_count, *full),
+        within_kernel,
+        "within",
+        (f32(*full), f32(copies, *full)),
         [SMEM] + [VMEM] * 5,
         (where, coef, *parts),
         [pltpu.VMEM((count,) + full, jnp.float32)],
     )
 
 
-def finish_kernel(where, coef, terms, coarse, chip_part, near_part, corrected, coarse_new):
-    slab, place = where[0], where[3]
+def finish_kernel(inner_count, where, coef, mine, totals, coarse, chip_part, near_part, *outs):
+    corrected, coarse_new = outs
+    slab, group, place = where[0], where[2], where[3]
     odd = lax.rem(slab, 2)
-    count, depth = terms.shape[:2]
-
-    def term(j):
-        return terms.at[lax.rem(place + j, count)]
-
-    field = [term(count - 1)[z] for z in range(depth)]
+    count, depth = totals.shape[:2]
 
     def body(i, layers):
-        stepped = coarse_step(list(layers), coef)
-        added = term(count - 2 - i)
-        return tuple(stepped[z] + added[z] for z in range(depth))
-
-    field = lax.fori_loop(0, count - 1, body, tuple(field))
+        layers = steps(layers, coef, inner_count)
+        return tuple(layers[z] + totals[count - 2 - i, z] for z in range(depth))
+
+    later = jnp.where(group == count - 1, 0.0, 1.0)
+    field = tuple(later * totals[count - 1, z] for z in range(depth))
+    field = lax.fori_loop(0, count - 2 - group, body, field)
+    field = lax.fori_loop(
+        0, inner_count - place, lambda _, layers: tuple(coarse_step(list(layers), coef)), field
+    )
     for z in range(depth):
-        coarse_new[z] = field[z]
+        coarse_new[z] = field[z] + mine[z]
     part = coarse_new[pl.ds(2 * slab, 2)] - coarse[...]
     rows, cols = chip_part.shape[1:]
     flat = part.reshape(rows // 2, cols // 4)
@@ -441,14 +447,14 @@
         corrected[z] = near_part[i] + jnp.where(odd == 1, upper, lower)
 
 
-def finish(where, coef, terms, coarse, chip_part, near_part):
-    _, rows, cols = chip_part.shape
-    return call(
-        finish_kernel,
+def finish(inner_count, where, *args):
+    _, rows, cols = args[-1].shape
+    return call(
+        functools.partial(finish_kernel, inner_count),
         "finish",
-        (f32(DEPTH, rows, cols), f32(*terms.shape[1:])),
-        [SMEM] + [VMEM] * 5,
-        (where, coef, terms, coarse, chip_part, near_part),
+        (f32(DEPTH, rows, cols), f32(*args[1].shape)),
+        [SMEM] + [VMEM] * len(args),
+        (where, *args),
     )
 
 
@@ -474,33 +480,35 @@
             array, [((t, a), ((t + shift) % times, b)) for t in range(times) for a, b in pairs]
         )
 
-    def gathered(array):
-        return [array] + [flipped(array, flip) for flip in (1, 2, 3)]
-
     own = (force, velocity, uptake)
-    chip_pack, near_pack, vel_pack = pack(where, adj, force, velocity, uptake)
+    near_pack, vel_pack, chip_pack = pack(where, adj, *own)
     near = to_next_chip(near_pack)
     near_vel = to_next_chip(vel_pack, times // 2)
     chip = flipped(chip_pack, 1)
+    restricted = restrict_inputs(adj, velocity, uptake)
+    restricted_one = flipped(restricted, 1)
+    pair = flipped(jnp.concatenate([restricted, restricted_one]), 2)
     edge, chip_part = inner(False, where, *own, chip_pack, near_pack, chip, chip)
     chip_halo = flipped(chip_part, 1)
-    restricted = restrict_inputs(adj, velocity, uptake)
-    near, near_vel, restricted, edge = lax.optimization_barrier((near, near_vel, restricted, edge))
+    near, near_vel, pair, edge = lax.optimization_barrier((near, near_vel, pair, edge))
     (near_part,) = wedge(False, where, *own, edge, near, near, near_vel)
     near_halo = to_next_chip(near_part)
     edge, chip_part, coarse_chip = inner(True, where, *own, chip_part, near_part, chip_halo, chip)
-    coef, stepped = prepare(where, gathered(restricted))
+    coef, stepped = prepare(where, (restricted, restricted_one, pair))
     near_halo, edge, coef, stepped = lax.optimization_barrier((near_halo, edge, coef, stepped))
     near_part, begun, coarse = wedge(
-        True, where, *own, edge, near_halo, near, near_vel, (coarse_chip, stepped), outer_count
-    )
-
-    across = [[g * inner_count + i for g in range(outer_count)] for i in range(inner_count)]
-    within = [[g * inner_count + i for i in range(inner_count)] for g in range(outer_count)]
-    begun = lax.all_to_all(begun, "tm", 0, 0, axis_index_groups=across)
-    terms = outer(inner_count, where, coef, gathered(begun))
-    terms = lax.all_to_all(terms, "tm", 0, 0, axis_index_groups=within)
-    corrected, coarse_new = finish(where, coef, terms, coarse, chip_part, near_part)
+        True, where, *own, edge, near_halo, near, near_vel, (coarse_chip, stepped), inner_count
+    )
+
+    groups = [[g * inner_count + i for i in range(inner_count)] for g in range(outer_count)]
+    begun = lax.all_to_all(begun, "tm", 0, 0, axis_index_groups=groups)
+    parts = [begun] + [flipped(begun, flip) for flip in (1, 2, 3)]
+    mine, total = within(where, coef, parts, outer_count)
+    groups = [list(members) for members in zip(*groups)]
+    totals = lax.all_to_all(total, "tm", 0, 0, axis_index_groups=groups)
+    corrected, coarse_new = finish(
+        inner_count, where, coef, mine, totals, coarse, chip_part, near_part
+    )
     return corrected[None], coarse_new[None]
 
 

time: 89.5 us -> 77.8 us (0.87); the launches traced: 88.3 us -> 77.5 us
  local copies, waits for them, and re-layouts: 4.55 us -> 0.02 us
  waiting for transfers between devices: 13.2 us -> 9.55 us
  starting transfers between devices: 16.7 us -> 14.5 us
  Pallas kernels: 23.9 us -> 22.5 us
  blocking collectives: 29.1 us -> 30.1 us
    unnamed x14 -> x8, local copies, waits for them, and re-layouts: 4.55 us -> 0.02 us
    ppermute x11 -> x10, waiting for transfers between devices: 13.2 us -> 9.55 us  [send(): return lax.ppermute(array, AXES, route)]
    ppermute x11 -> x10, starting transfers between devices: 16.7 us -> 14.5 us  [send(): return lax.ppermute(array, AXES, route)]
    pallas_call x9, Pallas kernels: 23.9 us -> 22.5 us  [call(): pl.pallas_call(kernel, out_shape=outs, in_specs=in_specs, out_specs=out_s...]
    all_to_all x2, blocking collectives: 29.1 us -> 30.1 us  [the longest x1 15.5 us: per_device(): totals = lax.all_to_all(total, 'tm', 0, 0, axis_index_groups=groups)]
  transfers between devices with their start and end apart: 11 -> 10, of which waited for: 5 -> 6; matrix products, arithmetic and copies ran while one was open for 0% -> 0% of each run, Pallas kernels for 10% -> 11%
where the time goes in v4:
time: 77.8 us; the launch traced here: 77.5 us
  blocking collectives  30.1 us (39%)
  Pallas kernels  22.5 us (29%)
  starting transfers between devices  14.5 us (19%)
  waiting for transfers between devices  9.55 us (12%)
    pallas_call x9, Pallas kernels, call(): pl.pallas_call(kernel, out_shape=outs, in_specs=in_specs, out_specs=out_s...  22.5 us
    all_to_all x1, blocking collectives, per_device(): totals = lax.all_to_all(total, 'tm', 0, 0, axis_index_groups=groups)  15.5 us
    all_to_all x1, blocking collectives, per_device(): begun = lax.all_to_all(begun, 'tm', 0, 0, axis_index_groups=groups)  14.7 us
    ppermute x10, starting transfers between devices, send(): return lax.ppermute(array, AXES, route)  14.5 us
    ppermute x10, waiting for transfers between devices, send(): return lax.ppermute(array, AXES, route)  9.55 us
  transfers between devices with their start and end apart: 10, of which 6 were waited for; matrix products, arithmetic and copies ran while one was open for 0% of the time, Pallas kernels for 11%

profile of v4, /device:TPU:1, one launch (start us, length us, event | category | flops | bytes accessed | tf_op | source)
XLA Modules:
  0.0 77.5 jit_solution(7264746736200783633)
XLA Ops:
  0.7 2.8 %pack.1 = (f32[10,32,512]{2,1,0:T(8,128)S(1)}, f32[9,32,512]{2,1,0:T(8,128)S(1)}, f32[19,32,512]{2,1,0:T(8,128)S(1)}) custom-call(s32[4]{0:T(128)S(1)} %pad_add_fusion.where, f32[8,32,512]{2,1,0:T(8,128)} %bitcast.13, f32[8,32,512]{2,1,0:T(8,128)} %bitcast.8, f32[3,8,32,512]{3,2,1,0:T(8,128)} %vel.11, f32[8,32,512]{2,1,0:T(8,128)} %upt.11), custom_call_target="tpu_custom_call" | custom-call | tf_op jit(solution)/shard_map/pack/pallas_call | solution.py:29
  3.5 3.3 %collective-permute-start.4 = (f32[19,32,512]{2,1,0:T(8,128)S(1)}, f32[19,32,512]{2,1,0:T(8,128)S(1)}, u32[]{:S(2)}, u32[]{:S(2)}) collective-permute-start(f32[19,32,512]{2,1,0:T(8,128)S(1)} %get-tuple-element.29.chip_part), channel_id=1, source_target_pairs={{1,0},{0,1},{3,2},{2,3},{5,4},{4,5},{7,6},{6,7},{9,8},{8,9},{11,10... | collective-permute-start | bytes 3735560 | tf_op jit(solution)/shard_map/ppermute | solution.py:472
  6.8 1.9 %collective-permute-start = (f32[10,32,512]{2,1,0:T(8,128)S(1)}, f32[10,32,512]{2,1,0:T(8,128)S(1)}, u32[]{:S(2)}, u32[]{:S(2)}) collective-permute-start(f32[10,32,512]{2,1,0:T(8,128)S(1)} %get-tuple-element.27.near_part), channel_id=1, source_target_pairs={{1,2},{2,1},{5,6},{6,5},{9,10},{10,9},{13,14},{14,13},{17,18},{18,... | collective-permute-start | bytes 1966088 | tf_op jit(solution)/shard_map/ppermute | solution.py:472
  8.8 3.8 %collective-permute-start.1 = (f32[9,32,512]{2,1,0:T(8,128)S(1)}, f32[9,32,512]{2,1,0:T(8,128)S(1)}, u32[]{:S(2)}, u32[]{:S(2)}) collective-permute-start(f32[9,32,512]{2,1,0:T(8,128)S(1)} %get-tuple-element.28), channel_id=1, source_target_pairs={{1,130},{2,129},{5,134},{6,133},{9,138},{10,137},{13,142},{14,141}... | collective-permute-start | bytes 1769480 | tf_op jit(solution)/shard_map/ppermute | solution.py:472
  12.6 0.9 %restrict.1.own = f32[10,8,128]{2,1,0:T(8,128)S(1)} custom-call(f32[8,32,512]{2,1,0:T(8,128)S(1)} %bitcast.14, f32[3,8,32,512]{3,2,1,0:T(8,128)S(1)} %copy-done, f32[8,32,512]{2,1,0:T(8,128)S(1)} %copy-done.1), custom_call_target="tpu_custom_call" | custom-call | tf_op jit(solution)/shard_map/restrict/pallas_call | solution.py:29
  13.6 1.2 %collective-permute-done.2.one = f32[10,8,128]{2,1,0:T(8,128)S(1)} collective-permute-done((f32[10,8,128]{2,1,0:T(8,128)S(1)}, f32[10,8,128]{2,1,0:T(8,128)S(1)}, u32[]{:S(2)}, u32[]{:S(2)}) %collective-permute-start.2) | collective-permute-done | bytes 40992 | tf_op jit(solution)/shard_map/ppermute | solution.py:472
  14.9 2.3 %inner_first.1 = (f32[4,2,32,512]{3,2,1,0:T(8,128)S(1)}, f32[4,32,512]{2,1,0:T(8,128)S(1)}) custom-call(s32[4]{0:T(128)S(1)} %pad_add_fusion.where, f32[8,32,512]{2,1,0:T(8,128)S(1)} %bitcast.9, f32[3,8,32,512]{3,2,1,0:T(8,128)S(1)} %copy-done, f32[8,32,512]{2,1,0:T(8,128)S(1)} %copy-done.1, f32[19,32,512]{2,1,0:T(8,128)S(1)} %get-tuple-element.29.chip_part, ...), custom_call_target="tpu_custom_call" | custom-call | tf_op jit(solution)/shard_map/inner_first/pallas_call | solution.py:29
  17.2 0.7 collective-permute-start.6
  17.9 1.1 %collective-permute-done.3.pair = f32[20,8,128]{2,1,0:T(8,128)S(1)} collective-permute-done((f32[20,8,128]{2,1,0:T(8,128)S(1)}, f32[20,8,128]{2,1,0:T(8,128)S(1)}, u32[]{:S(2)}, u32[]{:S(2)}) %collective-permute-start.3) | collective-permute-done | bytes 81952 | tf_op jit(solution)/shard_map/ppermute | solution.py:472
  19.0 2.3 %collective-permute-done.1.near_vel = f32[9,32,512]{2,1,0:T(8,128)S(1)} collective-permute-done((f32[9,32,512]{2,1,0:T(8,128)S(1)}, f32[9,32,512]{2,1,0:T(8,128)S(1)}, u32[]{:S(2)}, u32[]{:S(2)}) %collective-permute-start.1) | collective-permute-done | bytes 589856 | tf_op jit(solution)/shard_map/ppermute | solution.py:472
  21.3 1.6 %wedge_first.1.near_part = f32[4,32,512]{2,1,0:T(8,128)S(1)} custom-call(s32[4]{0:T(128)S(1)} %pad_add_fusion.where, f32[8,32,512]{2,1,0:T(8,128)S(1)} %bitcast.10, f32[3,8,32,512]{3,2,1,0:T(8,128)S(1)} %copy-done, f32[8,32,512]{2,1,0:T(8,128)S(1)} %copy-done.1, f32[4,2,32,512]{3,2,1,0:T(8,128)S(1)} %get-tuple-element.31.edge, ...), custom_call_target="tpu_custom_call" | custom-call | tf_op jit(solution)/shard_map/wedge_first/pallas_call | solution.py:29
  22.9 2.4 %collective-permute-start.5 = (f32[4,32,512]{2,1,0:T(8,128)S(1)}, f32[4,32,512]{2,1,0:T(8,128)S(1)}, u32[]{:S(2)}, u32[]{:S(2)}) collective-permute-start(f32[4,32,512]{2,1,0:T(8,128)S(1)} %wedge_first.1.near_part), channel_id=1, source_target_pairs={{1,2},{2,1},{5,6},{6,5},{9,10},{10,9},{13,14},{14,13},{17,18},{18,... | collective-permute-start | bytes 786440 | tf_op jit(solution)/shard_map/ppermute | solution.py:472
  25.3 1.0 %prepare.1 = (f32[25,8,8,128]{3,2,1,0:T(8,128)S(1)}, f32[8,8,128]{2,1,0:T(8,128)S(1)}) custom-call(s32[4]{0:T(128)S(1)} %pad_add_fusion.where, f32[10,8,128]{2,1,0:T(8,128)S(1)} %restrict.1.own, f32[10,8,128]{2,1,0:T(8,128)S(1)} %collective-permute-done.2.one, f32[20,8,128]{2,1,0:T(8,128)S(1)} %collective-permute-done.3.pair), custom_call_target="tpu_custom_call" | custom-call | tf_op jit(solution)/shard_map/prepare/pallas_call | solution.py:29
  26.3 2.7 %inner_last.1 = (f32[4,2,32,512]{3,2,1,0:T(8,128)S(1)}, f32[4,32,512]{2,1,0:T(8,128)S(1)}, f32[8,128]{1,0:T(8,128)S(1)}) custom-call(s32[4]{0:T(128)S(1)} %pad_add_fusion.where, f32[8,32,512]{2,1,0:T(8,128)S(1)} %bitcast.11, f32[3,8,32,512]{3,2,1,0:T(8,128)S(1)} %copy-done, f32[8,32,512]{2,1,0:T(8,128)S(1)} %copy-done.1, ...), custom_call_target="tpu_custom_call" | custom-call | tf_op jit(solution)/shard_map/inner_last/pallas_call | solution.py:29
  29.0 1.5 %collective-permute-done.5.halo = f32[4,32,512]{2,1,0:T(8,128)S(1)} collective-permute-done((f32[4,32,512]{2,1,0:T(8,128)S(1)}, f32[4,32,512]{2,1,0:T(8,128)S(1)}, u32[]{:S(2)}, u32[]{:S(2)}) %collective-permute-start.5) | collective-permute-done | bytes 262176 | tf_op jit(solution)/shard_map/ppermute | solution.py:472
  30.6 1.9 %wedge_last.1 = (f32[4,32,512]{2,1,0:T(8,128)S(1)}, f32[8,2,8,128]{3,2,1,0:T(8,128)S(1)}, f32[2,8,128]{2,1,0:T(8,128)S(1)}) custom-call(s32[4]{0:T(128)S(1)} %pad_add_fusion.where, f32[8,32,512]{2,1,0:T(8,128)S(1)} %bitcast.12, f32[3,8,32,512]{3,2,1,0:T(8,128)S(1)} %copy-done, f32[8,32,512]{2,1,0:T(8,128)S(1)} %copy-done.1, ...), custom_call_target="tpu_custom_call" | custom-call | tf_op jit(solution)/shard_map/wedge_last/pallas_call | solution.py:29
  32.5 14.7 %all_to_all.10.own = f32[8,2,8,128]{3,2,1,0:T(8,128)S(1)} all-to-all(f32[8,2,8,128]{3,2,1,0:T(8,128)S(1)} %get-tuple-element.44), channel_id=1, replica_groups={{0,4,8,12,16,20,24,28},{32,36,40,44,48,52,56,60},{64,68,72,76,80,84,88,..., dimensions={0} | all-to-all | bytes 131072 | tf_op jit(solution)/shard_map/all_to_all | solution.py:504
  47.2 1.6 %collective-permute-start.8 = (f32[8,2,8,128]{3,2,1,0:T(8,128)S(1)}, f32[8,2,8,128]{3,2,1,0:T(8,128)S(1)}, u32[]{:S(2)}, u32[]{:S(2)}) collective-permute-start(f32[8,2,8,128]{3,2,1,0:T(8,128)S(1)} %all_to_all.10.own), channel_id=1, source_target_pairs={{2,0},{3,1},{0,2},{1,3},{6,4},{7,5},{4,6},{5,7},{10,8},{11,9},{8,1... | collective-permute-start | bytes 196616 | tf_op jit(solution)/shard_map/ppermute | solution.py:472
  48.7 0.6 collective-permute-start.9
  49.3 1.1 %collective-permute-done.8.two = f32[8,2,8,128]{3,2,1,0:T(8,128)S(1)} collective-permute-done((f32[8,2,8,128]{3,2,1,0:T(8,128)S(1)}, f32[8,2,8,128]{3,2,1,0:T(8,128)S(1)}, u32[]{:S(2)}, u32[]{:S(2)}) %collective-permute-start.8) | collective-permute-done | bytes 65568 | tf_op jit(solution)/shard_map/ppermute | solution.py:472
  50.4 2.3 %collective-permute-done.9.three = f32[8,2,8,128]{3,2,1,0:T(8,128)S(1)} collective-permute-done((f32[8,2,8,128]{3,2,1,0:T(8,128)S(1)}, f32[8,2,8,128]{3,2,1,0:T(8,128)S(1)}, u32[]{:S(2)}, u32[]{:S(2)}) %collective-permute-start.9) | collective-permute-done | bytes 65568 | tf_op jit(solution)/shard_map/ppermute | solution.py:472
  52.7 1.3 %within.1 = (f32[8,8,128]{2,1,0:T(8,128)S(1)}, f32[8,8,8,128]{3,2,1,0:T(8,128)S(1)}) custom-call(s32[4]{0:T(128)S(1)} %pad_add_fusion.where, f32[25,8,8,128]{3,2,1,0:T(8,128)S(1)} %get-tuple-element.39.coef, f32[8,2,8,128]{3,2,1,0:T(8,128)S(1)} %all_to_all.10.own, f32[8,2,8,128]{3,2,1,0:T(8,128)S(1)} %collective-permute-done.7.one, ...), custom_call_target="tpu_custom_call" | custom-call | tf_op jit(solution)/shard_map/within/pallas_call | solution.py:29
  54.1 15.5 %all_to_all.11.totals = f32[8,8,8,128]{3,2,1,0:T(8,128)S(1)} all-to-all(f32[8,8,8,128]{3,2,1,0:T(8,128)S(1)} %get-tuple-element.46), channel_id=1, replica_groups={{0,32,64,96,128,160,192,224},{4,36,68,100,132,164,196,228},{8,40,72,104..., dimensions={0} | all-to-all | bytes 524288 | tf_op jit(solution)/shard_map/all_to_all | solution.py:508
  69.6 8.0 %finish.1 = (f32[8,32,512]{2,1,0:T(8,128)}, f32[8,8,128]{2,1,0:T(8,128)}) custom-call(s32[4]{0:T(128)S(1)} %pad_add_fusion.where, f32[25,8,8,128]{3,2,1,0:T(8,128)S(1)} %get-tuple-element.39.coef, f32[8,8,128]{2,1,0:T(8,128)S(1)} %get-tuple-element.45.mine, f32[8,8,8,128]{3,2,1,0:T(8,128)S(1)} %all_to_all.11.totals, ...), custom_call_target="tpu_custom_call" | custom-call | tf_op jit(solution)/shard_map/finish/pallas_call | solution.py:29
  (17 shorter events, 0.3 us)
Async XLA Ops:
  0.7 11.8 %copy-start = (f32[3,8,32,512]{3,2,1,0:T(8,128)S(1)}, f32[3,8,32,512]{3,2,1,0:T(8,128)}, u32[]{:S(2)}) copy-start(f32[3,8,32,512]{3,2,1,0:T(8,128)} %vel.11) | copy-start | bytes 4718596
  0.7 11.8 %copy-start.1 = (f32[8,32,512]{2,1,0:T(8,128)S(1)}, f32[8,32,512]{2,1,0:T(8,128)}, u32[]{:S(2)}) copy-start(f32[8,32,512]{2,1,0:T(8,128)} %upt.11) | copy-start | bytes 1572868
  0.7 11.8 %copy-start.3 = (f32[1,8,32,512]{3,2,1,0:T(8,128)S(1)}, f32[1,8,32,512]{3,2,1,0:T(8,128)}, u32[]{:S(2)}) copy-start(f32[1,8,32,512]{3,2,1,0:T(8,128)} %param.4) | copy-start | bytes 1572868
  3.5 11.3 %collective-permute-start.4 = (f32[19,32,512]{2,1,0:T(8,128)S(1)}, f32[19,32,512]{2,1,0:T(8,128)S(1)}, u32[]{:S(2)}, u32[]{:S(2)}) collective-permute-start(f32[19,32,512]{2,1,0:T(8,128)S(1)} %get-tuple-element.29.chip_part), channel_id=1, source_target_pairs={{1,0},{0,1},{3,2},{2,3},{5,4},{4,5},{7,6},{6,7},{9,8},{8,9},{11,10... | collective-permute-start | bytes 3735560 | tf_op jit(solution)/shard_map/ppermute | solution.py:472
  6.8 14.5 %collective-permute-start = (f32[10,32,512]{2,1,0:T(8,128)S(1)}, f32[10,32,512]{2,1,0:T(8,128)S(1)}, u32[]{:S(2)}, u32[]{:S(2)}) collective-permute-start(f32[10,32,512]{2,1,0:T(8,128)S(1)} %get-tuple-element.27.near_part), channel_id=1, source_target_pairs={{1,2},{2,1},{5,6},{6,5},{9,10},{10,9},{13,14},{14,13},{17,18},{18,... | collective-permute-start | bytes 1966088 | tf_op jit(solution)/shard_map/ppermute | solution.py:472
  8.8 6.1 %copy-start.2 = (f32[1,8,32,512]{3,2,1,0:T(8,128)S(1)}, f32[1,8,32,512]{3,2,1,0:T(8,128)}, u32[]{:S(2)}) copy-start(f32[1,8,32,512]{3,2,1,0:T(8,128)} %param.5) | copy-start | bytes 1572868
  8.8 12.5 %collective-permute-start.1 = (f32[9,32,512]{2,1,0:T(8,128)S(1)}, f32[9,32,512]{2,1,0:T(8,128)S(1)}, u32[]{:S(2)}, u32[]{:S(2)}) collective-permute-start(f32[9,32,512]{2,1,0:T(8,128)S(1)} %get-tuple-element.28), channel_id=1, source_target_pairs={{1,130},{2,129},{5,134},{6,133},{9,138},{10,137},{13,142},{14,141}... | collective-permute-start | bytes 1769480 | tf_op jit(solution)/shard_map/ppermute | solution.py:472
  13.5 1.3 %collective-permute-start.2 = (f32[10,8,128]{2,1,0:T(8,128)S(1)}, f32[10,8,128]{2,1,0:T(8,128)S(1)}, u32[]{:S(2)}, u32[]{:S(2)}) collective-permute-start(f32[10,8,128]{2,1,0:T(8,128)S(1)} %restrict.1.own), channel_id=1, source_target_pairs={{1,0},{0,1},{3,2},{2,3},{5,4},{4,5},{7,6},{6,7},{9,8},{8,9},{11,10... | collective-permute-start | bytes 122888 | tf_op jit(solution)/shard_map/ppermute | solution.py:472
  14.8 4.2 %collective-permute-start.3 = (f32[20,8,128]{2,1,0:T(8,128)S(1)}, f32[20,8,128]{2,1,0:T(8,128)S(1)}, u32[]{:S(2)}, u32[]{:S(2)}) collective-permute-start(f32[20,8,128]{2,1,0:T(8,128)S(1)} %pad_maximum_fusion), channel_id=1, source_target_pairs={{2,0},{3,1},{0,2},{1,3},{6,4},{7,5},{4,6},{5,7},{10,8},{11,9},{8,1... | collective-permute-start | bytes 245768 | tf_op jit(solution)/shard_map/ppermute | solution.py:472
  17.2 9.1 %collective-permute-start.6 = (f32[4,32,512]{2,1,0:T(8,128)S(1)}, f32[4,32,512]{2,1,0:T(8,128)S(1)}, u32[]{:S(2)}, u32[]{:S(2)}) collective-permute-start(f32[4,32,512]{2,1,0:T(8,128)S(1)} %get-tuple-element.34.chip_part), channel_id=1, source_target_pairs={{1,0},{0,1},{3,2},{2,3},{5,4},{4,5},{7,6},{6,7},{9,8},{8,9},{11,10... | collective-permute-start | bytes 786440 | tf_op jit(solution)/shard_map/ppermute | solution.py:472
  22.9 7.7 %collective-permute-start.5 = (f32[4,32,512]{2,1,0:T(8,128)S(1)}, f32[4,32,512]{2,1,0:T(8,128)S(1)}, u32[]{:S(2)}, u32[]{:S(2)}) collective-permute-start(f32[4,32,512]{2,1,0:T(8,128)S(1)} %wedge_first.1.near_part), channel_id=1, source_target_pairs={{1,2},{2,1},{5,6},{6,5},{9,10},{10,9},{13,14},{14,13},{17,18},{18,... | collective-permute-start | bytes 786440 | tf_op jit(solution)/shard_map/ppermute | solution.py:472
  47.2 2.1 %collective-permute-start.7 = (f32[8,2,8,128]{3,2,1,0:T(8,128)S(1)}, f32[8,2,8,128]{3,2,1,0:T(8,128)S(1)}, u32[]{:S(2)}, u32[]{:S(2)}) collective-permute-start(f32[8,2,8,128]{3,2,1,0:T(8,128)S(1)} %all_to_all.10.own), channel_id=1, source_target_pairs={{1,0},{0,1},{3,2},{2,3},{5,4},{4,5},{7,6},{6,7},{9,8},{8,9},{11,10... | collective-permute-start | bytes 196616 | tf_op jit(solution)/shard_map/ppermute | solution.py:472
  47.2 3.2 %collective-permute-start.8 = (f32[8,2,8,128]{3,2,1,0:T(8,128)S(1)}, f32[8,2,8,128]{3,2,1,0:T(8,128)S(1)}, u32[]{:S(2)}, u32[]{:S(2)}) collective-permute-start(f32[8,2,8,128]{3,2,1,0:T(8,128)S(1)} %all_to_all.10.own), channel_id=1, source_target_pairs={{2,0},{3,1},{0,2},{1,3},{6,4},{7,5},{4,6},{5,7},{10,8},{11,9},{8,1... | collective-permute-start | bytes 196616 | tf_op jit(solution)/shard_map/ppermute | solution.py:472
  48.7 4.0 %collective-permute-start.9 = (f32[8,2,8,128]{3,2,1,0:T(8,128)S(1)}, f32[8,2,8,128]{3,2,1,0:T(8,128)S(1)}, u32[]{:S(2)}, u32[]{:S(2)}) collective-permute-start(f32[8,2,8,128]{3,2,1,0:T(8,128)S(1)} %all_to_all.10.own), channel_id=1, source_target_pairs={{3,0},{2,1},{1,2},{0,3},{7,4},{6,5},{5,6},{4,7},{11,8},{10,9},{9,1... | collective-permute-start | bytes 196616 | tf_op jit(solution)/shard_map/ppermute | solution.py:472

commit v5 on v4

--- a/solution.py
+++ b/solution.py
@@ -5,13 +5,14 @@
 from jax import lax
 from jax.experimental import pallas as pl
 from jax.experimental.pallas import tpu as pltpu
+from jax.sharding import Mesh
 from jax.sharding import PartitionSpec as P
 
 STEPS = 8
 WIDE = 4
 THIN = WIDE - 1
 DEPTH = 8
-AXES = ("tm", "slab")
+AXES = ("group", "place", "chip", "core")
 DIFFUSION_FINE = 0.15
 DIFFUSION_COARSE = 0.0375
 HIGH = lax.Precision.HIGHEST
@@ -373,67 +374,71 @@
     )
 
 
-def within_kernel(where, coef, own, one, two, three, mine, total, whole):
+def outer_kernel(where, coef, own, other, out, whole, ends):
+    slab, group, place = where[0], where[2], where[3]
+    core = lax.rem(slab, 2)
+    targets, half = out.shape[:2]
+    count, depth = whole.shape[:2]
+    chips = own.shape[0] // count
+    part = own.shape[1]
+    for g in range(count):
+        for chip in range(chips):
+            here = 2 * chip + core
+            there = 2 * chip + 1 - core
+            whole[g, pl.ds(here * part, part)] = own[g * chips + chip]
+            whole[g, pl.ds(there * part, part)] = other[g * chips + chip]
+
+    def body(i, layers):
+        layers = steps(layers, coef, targets)
+        return tuple(layers[z] + whole[count - 2 - i, z] for z in range(depth))
+
+    later = jnp.where(group == count - 1, 0.0, 1.0)
+    field = tuple(later * whole[count - 1, z] for z in range(depth))
+    without = lax.fori_loop(0, count - 2 - group, body, field)
+    stepped = steps(without, coef, targets)
+    for z in range(depth):
+        ends[0, z] = stepped[z] + whole[group, z]
+        ends[1, z] = without[z]
+    for target in range(targets):
+        out[target] = ends[jnp.where(place >= target, 0, 1), pl.ds(core * half, half)]
+
+
+def outer(targets, where, coef, own, other):
+    full = coef.shape[1:]
+    depth, rows, cols = full
+    count = own.shape[0] * own.shape[1] * 2 // depth
+    return call(
+        outer_kernel,
+        "outer",
+        f32(targets, depth // 2, rows, cols),
+        [SMEM] + [VMEM] * 3,
+        (where, coef, own, other),
+        [pltpu.VMEM((count,) + full, jnp.float32), pltpu.VMEM((2,) + full, jnp.float32)],
+    )
+
+
+def finish_kernel(where, coef, own, other, coarse, chip_part, near_part, *refs):
+    corrected, coarse_new, whole = refs
     slab, place = where[0], where[3]
-    count, part_depth = own.shape[:2]
-    depth = whole.shape[1]
-    for flip, ref in enumerate((own, one, two, three)):
-        first = lax.bitwise_xor(slab, flip) * part_depth
-        for t in range(count):
-            whole[t, pl.ds(first, part_depth)] = ref[t]
-
-    def keep(t, layers):
-        @pl.when(t == place)
-        def _():
-            for z in range(depth):
-                mine[z] = layers[z]
+    odd = lax.rem(slab, 2)
+    count, depth = whole.shape[:2]
+    half = depth // 2
+    for t in range(count):
+        whole[t, pl.ds(odd * half, half)] = own[t]
+        whole[t, pl.ds((1 - odd) * half, half)] = other[t]
+
+    def term(j):
+        return whole.at[lax.rem(place + j, count)]
 
     def body(i, layers):
-        t = count - 2 - i
-        layers = coarse_step(list(layers), coef)
-        layers = tuple(layers[z] + whole[t, z] for z in range(depth))
-        keep(t, layers)
-        return layers
-
-    field = tuple(whole[count - 1, z] for z in range(depth))
-    keep(count - 1, field)
-    field = lax.fori_loop(0, count - 1, body, field)
-    for copy in range(total.shape[0]):
-        for z in range(depth):
-            total[copy, z] = field[z]
-
-
-def within(where, coef, parts, copies):
-    full = coef.shape[1:]
-    count = parts[0].shape[0]
-    return call(
-        within_kernel,
-        "within",
-        (f32(*full), f32(copies, *full)),
-        [SMEM] + [VMEM] * 5,
-        (where, coef, *parts),
-        [pltpu.VMEM((count,) + full, jnp.float32)],
-    )
-
-
-def finish_kernel(inner_count, where, coef, mine, totals, coarse, chip_part, near_part, *outs):
-    corrected, coarse_new = outs
-    slab, group, place = where[0], where[2], where[3]
-    odd = lax.rem(slab, 2)
-    count, depth = totals.shape[:2]
-
-    def body(i, layers):
-        layers = steps(layers, coef, inner_count)
-        return tuple(layers[z] + totals[count - 2 - i, z] for z in range(depth))
-
-    later = jnp.where(group == count - 1, 0.0, 1.0)
-    field = tuple(later * totals[count - 1, z] for z in range(depth))
-    field = lax.fori_loop(0, count - 2 - group, body, field)
-    field = lax.fori_loop(
-        0, inner_count - place, lambda _, layers: tuple(coarse_step(list(layers), coef)), field
-    )
+        stepped = coarse_step(list(layers), coef)
+        added = term(count - 2 - i)
+        return tuple(stepped[z] + added[z] for z in range(depth))
+
+    first = term(count - 1)
+    field = lax.fori_loop(0, count - 1, body, tuple(first[z] for z in range(depth)))
     for z in range(depth):
-        coarse_new[z] = field[z] + mine[z]
+        coarse_new[z] = field[z]
     part = coarse_new[pl.ds(2 * slab, 2)] - coarse[...]
     rows, cols = chip_part.shape[1:]
     flat = part.reshape(rows // 2, cols // 4)
@@ -447,25 +452,27 @@
         corrected[z] = near_part[i] + jnp.where(odd == 1, upper, lower)
 
 
-def finish(inner_count, where, *args):
+def finish(where, *args):
     _, rows, cols = args[-1].shape
-    return call(
-        functools.partial(finish_kernel, inner_count),
+    full = args[0].shape[1:]
+    return call(
+        finish_kernel,
         "finish",
-        (f32(DEPTH, rows, cols), f32(*args[1].shape)),
+        (f32(DEPTH, rows, cols), f32(*full)),
         [SMEM] + [VMEM] * len(args),
         (where, *args),
+        [pltpu.VMEM(args[1].shape[:1] + full, jnp.float32)],
     )
 
 
 def per_device(adjoint_end, forcing, velocity, uptake):
     adj, force = adjoint_end[0], forcing[0]
-    times, slabs = lax.axis_size("tm"), lax.axis_size("slab")
-    slab, time = lax.axis_index("slab"), lax.axis_index("tm")
-    inner_count = 8 if times >= 16 else 2
-    outer_count = times // inner_count
-    where = jnp.stack([slab, time == times - 1, time // inner_count, time % inner_count])
-    where = where.astype(jnp.int32)
+    groups, places, chips, cores = (lax.axis_size(axis) for axis in AXES)
+    group, place, chip_no, core = (lax.axis_index(axis) for axis in AXES)
+    times, slabs = groups * places, chips * cores
+    slab = chip_no * cores + core
+    last_slice = jnp.logical_and(group == groups - 1, place == places - 1)
+    where = jnp.stack([slab, last_slice.astype(slab.dtype), group, place]).astype(jnp.int32)
 
     def send(array, pairs):
         route = [(t0 * slabs + s0, t1 * slabs + s1) for (t0, s0), (t1, s1) in pairs]
@@ -497,29 +504,27 @@
     coef, stepped = prepare(where, (restricted, restricted_one, pair))
     near_halo, edge, coef, stepped = lax.optimization_barrier((near_halo, edge, coef, stepped))
     near_part, begun, coarse = wedge(
-        True, where, *own, edge, near_halo, near, near_vel, (coarse_chip, stepped), inner_count
-    )
-
-    groups = [[g * inner_count + i for i in range(inner_count)] for g in range(outer_count)]
-    begun = lax.all_to_all(begun, "tm", 0, 0, axis_index_groups=groups)
-    parts = [begun] + [flipped(begun, flip) for flip in (1, 2, 3)]
-    mine, total = within(where, coef, parts, outer_count)
-    groups = [list(members) for members in zip(*groups)]
-    totals = lax.all_to_all(total, "tm", 0, 0, axis_index_groups=groups)
+        True, where, *own, edge, near_halo, near, near_vel, (coarse_chip, stepped), groups * chips
+    )
+
+    begun = lax.all_to_all(begun, ("group", "chip"), 0, 0)
+    terms = outer(places, where, coef, begun, flipped(begun, 1))
+    terms = lax.all_to_all(terms, "place", 0, 0)
     corrected, coarse_new = finish(
-        inner_count, where, coef, mine, totals, coarse, chip_part, near_part
+        where, coef, terms, flipped(terms, 1), coarse, chip_part, near_part
     )
     return corrected[None], coarse_new[None]
 
 
 def solution(mesh):
-    in_specs = (
-        P("tm", "slab", None, None),
-        P("tm", "slab", None, None),
-        P(None, "slab", None, None),
-        P("slab", None, None),
-    )
-    out_specs = (P("tm", "slab", None, None), P("tm", None, None, None))
+    times, slabs = mesh.devices.shape
+    places = 8 if times >= 16 else 2
+    shape = (times // places, places, slabs // 2, 2)
+    time, slab = AXES[:2], AXES[2:]
     return jax.shard_map(
-        per_device, mesh=mesh, in_specs=in_specs, out_specs=out_specs, check_vma=False
-    )
+        per_device,
+        mesh=Mesh(mesh.devices.reshape(shape), AXES),
+        in_specs=(P(time, slab), P(time, slab), P(None, slab), P(slab)),
+        out_specs=(P(time, slab), P(time)),
+        check_vma=False,
+    )

time: 77.8 us -> 75.7 us (0.973)
  blocking collectives: 30.1 us -> 27.6 us
  starting transfers between devices: 14.5 us -> 16.3 us
  waiting for transfers between devices: 9.55 us -> 8.12 us
    all_to_all x2, blocking collectives: 30.1 us -> 27.6 us  [the longest x1 15.9 us: per_device(): terms = lax.all_to_all(terms, 'place', 0, 0)]
    ppermute x10 -> x9, starting transfers between devices: 14.5 us -> 16.3 us  [send(): return lax.ppermute(array, AXES, route)]
    ppermute x10 -> x9, waiting for transfers between devices: 9.55 us -> 8.12 us  [send(): return lax.ppermute(array, AXES, route)]
  transfers between devices with their start and end apart: 10 -> 9, of which waited for: 6 -> 6; matrix products, arithmetic and copies ran while one was open for 0% -> 0% of each run, Pallas kernels for 11% -> 11%
where the time goes in v5:
time: 75.7 us; the launch traced here: 75.4 us
  blocking collectives  27.6 us (36%)
  Pallas kernels  22.6 us (30%)
  starting transfers between devices  16.3 us (22%)
  waiting for transfers between devices  8.12 us (11%)
  between operations  0.76 us (1%)
    pallas_call x9, Pallas kernels, call(): pl.pallas_call(kernel, out_shape=outs, in_specs=in_specs, out_specs=out_s...  22.6 us
    ppermute x9, starting transfers between devices, send(): return lax.ppermute(array, AXES, route)  16.3 us
    all_to_all x1, blocking collectives, per_device(): terms = lax.all_to_all(terms, 'place', 0, 0)  15.9 us
    all_to_all x1, blocking collectives, per_device(): begun = lax.all_to_all(begun, ('group', 'chip'), 0, 0)  11.7 us
    ppermute x9, waiting for transfers between devices, send(): return lax.ppermute(array, AXES, route)  8.12 us
  transfers between devices with their start and end apart: 9, of which 6 were waited for; matrix products, arithmetic and copies ran while one was open for 0% of the time, Pallas kernels for 11%

profile of v5, /device:TPU:1, one launch (start us, length us, event | category | flops | bytes accessed | tf_op | source)
XLA Modules:
  0.0 75.4 jit_solution(1368372786563747695)
XLA Ops:
  0.7 2.8 %pack.1 = (f32[10,32,512]{2,1,0:T(8,128)S(1)}, f32[9,32,512]{2,1,0:T(8,128)S(1)}, f32[19,32,512]{2,1,0:T(8,128)S(1)}) custom-call(s32[4]{0:T(128)S(1)} %pad_add_fusion.where, f32[8,32,512]{2,1,0:T(8,128)} %bitcast.13, f32[8,32,512]{2,1,0:T(8,128)} %bitcast.8, f32[3,8,32,512]{3,2,1,0:T(8,128)} %vel.11, f32[8,32,512]{2,1,0:T(8,128)} %upt.11), custom_call_target="tpu_custom_call" | custom-call | tf_op jit(solution)/shard_map/pack/pallas_call | solution.py:30
  3.5 3.3 %collective-permute-start.4 = (f32[19,32,512]{2,1,0:T(8,128)S(1)}, f32[19,32,512]{2,1,0:T(8,128)S(1)}, u32[]{:S(2)}, u32[]{:S(2)}) collective-permute-start(f32[19,32,512]{2,1,0:T(8,128)S(1)} %get-tuple-element.27.chip_part), channel_id=1, source_target_pairs={{1,0},{0,1},{3,2},{2,3},{5,4},{4,5},{7,6},{6,7},{9,8},{8,9},{11,10... | collective-permute-start | bytes 3735560 | tf_op jit(solution)/shard_map/ppermute | solution.py:479
  6.8 1.9 %collective-permute-start = (f32[10,32,512]{2,1,0:T(8,128)S(1)}, f32[10,32,512]{2,1,0:T(8,128)S(1)}, u32[]{:S(2)}, u32[]{:S(2)}) collective-permute-start(f32[10,32,512]{2,1,0:T(8,128)S(1)} %get-tuple-element.25.near_part), channel_id=1, source_target_pairs={{1,2},{2,1},{5,6},{6,5},{9,10},{10,9},{13,14},{14,13},{17,18},{18,... | collective-permute-start | bytes 1966088 | tf_op jit(solution)/shard_map/ppermute | solution.py:479
  8.8 3.8 %collective-permute-start.1 = (f32[9,32,512]{2,1,0:T(8,128)S(1)}, f32[9,32,512]{2,1,0:T(8,128)S(1)}, u32[]{:S(2)}, u32[]{:S(2)}) collective-permute-start(f32[9,32,512]{2,1,0:T(8,128)S(1)} %get-tuple-element.26), channel_id=1, source_target_pairs={{1,130},{2,129},{5,134},{6,133},{9,138},{10,137},{13,142},{14,141}... | collective-permute-start | bytes 1769480 | tf_op jit(solution)/shard_map/ppermute | solution.py:479
  12.6 0.9 %restrict.1.own = f32[10,8,128]{2,1,0:T(8,128)S(1)} custom-call(f32[8,32,512]{2,1,0:T(8,128)S(1)} %bitcast.14, f32[3,8,32,512]{3,2,1,0:T(8,128)S(1)} %copy-done, f32[8,32,512]{2,1,0:T(8,128)S(1)} %copy-done.1), custom_call_target="tpu_custom_call" | custom-call | tf_op jit(solution)/shard_map/restrict/pallas_call | solution.py:30
  13.6 1.2 %collective-permute-done.2.one = f32[10,8,128]{2,1,0:T(8,128)S(1)} collective-permute-done((f32[10,8,128]{2,1,0:T(8,128)S(1)}, f32[10,8,128]{2,1,0:T(8,128)S(1)}, u32[]{:S(2)}, u32[]{:S(2)}) %collective-permute-start.2) | collective-permute-done | bytes 40992 | tf_op jit(solution)/shard_map/ppermute | solution.py:479
  14.9 2.3 %inner_first.1 = (f32[4,2,32,512]{3,2,1,0:T(8,128)S(1)}, f32[4,32,512]{2,1,0:T(8,128)S(1)}) custom-call(s32[4]{0:T(128)S(1)} %pad_add_fusion.where, f32[8,32,512]{2,1,0:T(8,128)S(1)} %bitcast.9, f32[3,8,32,512]{3,2,1,0:T(8,128)S(1)} %copy-done, f32[8,32,512]{2,1,0:T(8,128)S(1)} %copy-done.1, f32[19,32,512]{2,1,0:T(8,128)S(1)} %get-tuple-element.27.chip_part, ...), custom_call_target="tpu_custom_call" | custom-call | tf_op jit(solution)/shard_map/inner_first/pallas_call | solution.py:30
  17.2 0.7 collective-permute-start.6
  17.9 1.1 %collective-permute-done.3.pair = f32[20,8,128]{2,1,0:T(8,128)S(1)} collective-permute-done((f32[20,8,128]{2,1,0:T(8,128)S(1)}, f32[20,8,128]{2,1,0:T(8,128)S(1)}, u32[]{:S(2)}, u32[]{:S(2)}) %collective-permute-start.3) | collective-permute-done | bytes 81952 | tf_op jit(solution)/shard_map/ppermute | solution.py:479
  19.0 2.3 %collective-permute-done.1.near_vel = f32[9,32,512]{2,1,0:T(8,128)S(1)} collective-permute-done((f32[9,32,512]{2,1,0:T(8,128)S(1)}, f32[9,32,512]{2,1,0:T(8,128)S(1)}, u32[]{:S(2)}, u32[]{:S(2)}) %collective-permute-start.1) | collective-permute-done | bytes 589856 | tf_op jit(solution)/shard_map/ppermute | solution.py:479
  21.3 1.6 %wedge_first.1.near_part = f32[4,32,512]{2,1,0:T(8,128)S(1)} custom-call(s32[4]{0:T(128)S(1)} %pad_add_fusion.where, f32[8,32,512]{2,1,0:T(8,128)S(1)} %bitcast.10, f32[3,8,32,512]{3,2,1,0:T(8,128)S(1)} %copy-done, f32[8,32,512]{2,1,0:T(8,128)S(1)} %copy-done.1, f32[4,2,32,512]{3,2,1,0:T(8,128)S(1)} %get-tuple-element.29.edge, ...), custom_call_target="tpu_custom_call" | custom-call | tf_op jit(solution)/shard_map/wedge_first/pallas_call | solution.py:30
  22.9 2.4 %collective-permute-start.5 = (f32[4,32,512]{2,1,0:T(8,128)S(1)}, f32[4,32,512]{2,1,0:T(8,128)S(1)}, u32[]{:S(2)}, u32[]{:S(2)}) collective-permute-start(f32[4,32,512]{2,1,0:T(8,128)S(1)} %wedge_first.1.near_part), channel_id=1, source_target_pairs={{1,2},{2,1},{5,6},{6,5},{9,10},{10,9},{13,14},{14,13},{17,18},{18,... | collective-permute-start | bytes 786440 | tf_op jit(solution)/shard_map/ppermute | solution.py:479
  25.3 1.0 %prepare.1 = (f32[25,8,8,128]{3,2,1,0:T(8,128)S(1)}, f32[8,8,128]{2,1,0:T(8,128)S(1)}) custom-call(s32[4]{0:T(128)S(1)} %pad_add_fusion.where, f32[10,8,128]{2,1,0:T(8,128)S(1)} %restrict.1.own, f32[10,8,128]{2,1,0:T(8,128)S(1)} %collective-permute-done.2.one, f32[20,8,128]{2,1,0:T(8,128)S(1)} %collective-permute-done.3.pair), custom_call_target="tpu_custom_call" | custom-call | tf_op jit(solution)/shard_map/prepare/pallas_call | solution.py:30
  26.3 2.7 %inner_last.1 = (f32[4,2,32,512]{3,2,1,0:T(8,128)S(1)}, f32[4,32,512]{2,1,0:T(8,128)S(1)}, f32[8,128]{1,0:T(8,128)S(1)}) custom-call(s32[4]{0:T(128)S(1)} %pad_add_fusion.where, f32[8,32,512]{2,1,0:T(8,128)S(1)} %bitcast.11, f32[3,8,32,512]{3,2,1,0:T(8,128)S(1)} %copy-done, f32[8,32,512]{2,1,0:T(8,128)S(1)} %copy-done.1, ...), custom_call_target="tpu_custom_call" | custom-call | tf_op jit(solution)/shard_map/inner_last/pallas_call | solution.py:30
  29.0 1.5 %collective-permute-done.5.halo = f32[4,32,512]{2,1,0:T(8,128)S(1)} collective-permute-done((f32[4,32,512]{2,1,0:T(8,128)S(1)}, f32[4,32,512]{2,1,0:T(8,128)S(1)}, u32[]{:S(2)}, u32[]{:S(2)}) %collective-permute-start.5) | collective-permute-done | bytes 262176 | tf_op jit(solution)/shard_map/ppermute | solution.py:479
  30.6 1.9 %wedge_last.1 = (f32[4,32,512]{2,1,0:T(8,128)S(1)}, f32[16,2,8,128]{3,2,1,0:T(8,128)S(1)}, f32[2,8,128]{2,1,0:T(8,128)S(1)}) custom-call(s32[4]{0:T(128)S(1)} %pad_add_fusion.where, f32[8,32,512]{2,1,0:T(8,128)S(1)} %bitcast.12, f32[3,8,32,512]{3,2,1,0:T(8,128)S(1)} %copy-done, f32[8,32,512]{2,1,0:T(8,128)S(1)} %copy-done.1, ...), custom_call_target="tpu_custom_call" | custom-call | tf_op jit(solution)/shard_map/wedge_last/pallas_call | solution.py:30
  32.5 11.7 %all_to_all.10.own = f32[16,2,8,128]{3,2,1,0:T(8,128)S(1)} all-to-all(f32[16,2,8,128]{3,2,1,0:T(8,128)S(1)} %get-tuple-element.42), channel_id=1, replica_groups=mesh['group'=8,'place'=8,'chip'=2,'core'=2] {'group','chip'}, dimensions={0} | all-to-all | bytes 262144 | tf_op jit(solution)/shard_map/all_to_all | solution.py:510
  44.2 1.9 %collective-permute-start.7 = (f32[16,2,8,128]{3,2,1,0:T(8,128)S(1)}, f32[16,2,8,128]{3,2,1,0:T(8,128)S(1)}, u32[]{:S(2)}, u32[]{:S(2)}) collective-permute-start(f32[16,2,8,128]{3,2,1,0:T(8,128)S(1)} %all_to_all.10.own), channel_id=1, source_target_pairs={{1,0},{0,1},{3,2},{2,3},{5,4},{4,5},{7,6},{6,7},{9,8},{8,9},{11,10... | collective-permute-start | bytes 393224 | tf_op jit(solution)/shard_map/ppermute | solution.py:479
  46.1 1.0 %collective-permute-done.7.other = f32[16,2,8,128]{3,2,1,0:T(8,128)S(1)} collective-permute-done((f32[16,2,8,128]{3,2,1,0:T(8,128)S(1)}, f32[16,2,8,128]{3,2,1,0:T(8,128)S(1)}, u32[]{:S(2)}, u32[]{:S(2)}) %collective-permute-start.7) | collective-permute-done | bytes 131104 | tf_op jit(solution)/shard_map/ppermute | solution.py:479
  47.1 6.8 %outer.1 = f32[8,4,8,128]{3,2,1,0:T(8,128)S(1)} custom-call(s32[4]{0:T(128)S(1)} %pad_add_fusion.where, f32[25,8,8,128]{3,2,1,0:T(8,128)S(1)} %get-tuple-element.37.coef, f32[16,2,8,128]{3,2,1,0:T(8,128)S(1)} %all_to_all.10.own, f32[16,2,8,128]{3,2,1,0:T(8,128)S(1)} %collective-permute-done.7.other), custom_call_target="tpu_custom_call" | custom-call | tf_op jit(solution)/shard_map/outer/pallas_call | solution.py:30
  53.9 15.9 %all_to_all.11.own = f32[8,4,8,128]{3,2,1,0:T(8,128)S(1)} all-to-all(f32[8,4,8,128]{3,2,1,0:T(8,128)S(1)} %outer.1), channel_id=1, replica_groups=mesh['group'=8,'place'=8,'chip'=2,'core'=2] {'place'}, dimensions={0} | all-to-all | bytes 262144 | tf_op jit(solution)/shard_map/all_to_all | solution.py:512
  69.8 2.1 %collective-permute-start.8 = (f32[8,4,8,128]{3,2,1,0:T(8,128)S(1)}, f32[8,4,8,128]{3,2,1,0:T(8,128)S(1)}, u32[]{:S(2)}, u32[]{:S(2)}) collective-permute-start(f32[8,4,8,128]{3,2,1,0:T(8,128)S(1)} %all_to_all.11.own), channel_id=1, source_target_pairs={{1,0},{0,1},{3,2},{2,3},{5,4},{4,5},{7,6},{6,7},{9,8},{8,9},{11,10... | collective-permute-start | bytes 393224 | tf_op jit(solution)/shard_map/ppermute | solution.py:479
  71.9 1.0 %collective-permute-done.8.other = f32[8,4,8,128]{3,2,1,0:T(8,128)S(1)} collective-permute-done((f32[8,4,8,128]{3,2,1,0:T(8,128)S(1)}, f32[8,4,8,128]{3,2,1,0:T(8,128)S(1)}, u32[]{:S(2)}, u32[]{:S(2)}) %collective-permute-start.8) | collective-permute-done | bytes 131104 | tf_op jit(solution)/shard_map/ppermute | solution.py:479
  72.8 2.6 %finish.1 = (f32[8,32,512]{2,1,0:T(8,128)}, f32[8,8,128]{2,1,0:T(8,128)}) custom-call(s32[4]{0:T(128)S(1)} %pad_add_fusion.where, f32[25,8,8,128]{3,2,1,0:T(8,128)S(1)} %get-tuple-element.37.coef, f32[8,4,8,128]{3,2,1,0:T(8,128)S(1)} %all_to_all.11.own, f32[8,4,8,128]{3,2,1,0:T(8,128)S(1)} %collective-permute-done.8.other, ...), custom_call_target="tpu_custom_call" | custom-call | tf_op jit(solution)/shard_map/finish/pallas_call | solution.py:30
  (15 shorter events, 0.3 us)
Async XLA Ops:
  0.7 11.8 %copy-start = (f32[3,8,32,512]{3,2,1,0:T(8,128)S(1)}, f32[3,8,32,512]{3,2,1,0:T(8,128)}, u32[]{:S(2)}) copy-start(f32[3,8,32,512]{3,2,1,0:T(8,128)} %vel.11) | copy-start | bytes 4718596
  0.7 11.8 %copy-start.1 = (f32[8,32,512]{2,1,0:T(8,128)S(1)}, f32[8,32,512]{2,1,0:T(8,128)}, u32[]{:S(2)}) copy-start(f32[8,32,512]{2,1,0:T(8,128)} %upt.11) | copy-start | bytes 1572868
  0.7 11.8 %copy-start.3 = (f32[1,8,32,512]{3,2,1,0:T(8,128)S(1)}, f32[1,8,32,512]{3,2,1,0:T(8,128)}, u32[]{:S(2)}) copy-start(f32[1,8,32,512]{3,2,1,0:T(8,128)} %param.4) | copy-start | bytes 1572868
  3.5 11.3 %collective-permute-start.4 = (f32[19,32,512]{2,1,0:T(8,128)S(1)}, f32[19,32,512]{2,1,0:T(8,128)S(1)}, u32[]{:S(2)}, u32[]{:S(2)}) collective-permute-start(f32[19,32,512]{2,1,0:T(8,128)S(1)} %get-tuple-element.27.chip_part), channel_id=1, source_target_pairs={{1,0},{0,1},{3,2},{2,3},{5,4},{4,5},{7,6},{6,7},{9,8},{8,9},{11,10... | collective-permute-start | bytes 3735560 | tf_op jit(solution)/shard_map/ppermute | solution.py:479
  6.8 14.5 %collective-permute-start = (f32[10,32,512]{2,1,0:T(8,128)S(1)}, f32[10,32,512]{2,1,0:T(8,128)S(1)}, u32[]{:S(2)}, u32[]{:S(2)}) collective-permute-start(f32[10,32,512]{2,1,0:T(8,128)S(1)} %get-tuple-element.25.near_part), channel_id=1, source_target_pairs={{1,2},{2,1},{5,6},{6,5},{9,10},{10,9},{13,14},{14,13},{17,18},{18,... | collective-permute-start | bytes 1966088 | tf_op jit(solution)/shard_map/ppermute | solution.py:479
  8.8 6.1 %copy-start.2 = (f32[1,8,32,512]{3,2,1,0:T(8,128)S(1)}, f32[1,8,32,512]{3,2,1,0:T(8,128)}, u32[]{:S(2)}) copy-start(f32[1,8,32,512]{3,2,1,0:T(8,128)} %param.5) | copy-start | bytes 1572868
  8.8 12.5 %collective-permute-start.1 = (f32[9,32,512]{2,1,0:T(8,128)S(1)}, f32[9,32,512]{2,1,0:T(8,128)S(1)}, u32[]{:S(2)}, u32[]{:S(2)}) collective-permute-start(f32[9,32,512]{2,1,0:T(8,128)S(1)} %get-tuple-element.26), channel_id=1, source_target_pairs={{1,130},{2,129},{5,134},{6,133},{9,138},{10,137},{13,142},{14,141}... | collective-permute-start | bytes 1769480 | tf_op jit(solution)/shard_map/ppermute | solution.py:479
  13.5 1.3 %collective-permute-start.2 = (f32[10,8,128]{2,1,0:T(8,128)S(1)}, f32[10,8,128]{2,1,0:T(8,128)S(1)}, u32[]{:S(2)}, u32[]{:S(2)}) collective-permute-start(f32[10,8,128]{2,1,0:T(8,128)S(1)} %restrict.1.own), channel_id=1, source_target_pairs={{1,0},{0,1},{3,2},{2,3},{5,4},{4,5},{7,6},{6,7},{9,8},{8,9},{11,10... | collective-permute-start | bytes 122888 | tf_op jit(solution)/shard_map/ppermute | solution.py:479
  14.8 4.2 %collective-permute-start.3 = (f32[20,8,128]{2,1,0:T(8,128)S(1)}, f32[20,8,128]{2,1,0:T(8,128)S(1)}, u32[]{:S(2)}, u32[]{:S(2)}) collective-permute-start(f32[20,8,128]{2,1,0:T(8,128)S(1)} %pad_maximum_fusion), channel_id=1, source_target_pairs={{2,0},{3,1},{0,2},{1,3},{6,4},{7,5},{4,6},{5,7},{10,8},{11,9},{8,1... | collective-permute-start | bytes 245768 | tf_op jit(solution)/shard_map/ppermute | solution.py:479
  17.2 9.1 %collective-permute-start.6 = (f32[4,32,512]{2,1,0:T(8,128)S(1)}, f32[4,32,512]{2,1,0:T(8,128)S(1)}, u32[]{:S(2)}, u32[]{:S(2)}) collective-permute-start(f32[4,32,512]{2,1,0:T(8,128)S(1)} %get-tuple-element.32.chip_part), channel_id=1, source_target_pairs={{1,0},{0,1},{3,2},{2,3},{5,4},{4,5},{7,6},{6,7},{9,8},{8,9},{11,10... | collective-permute-start | bytes 786440 | tf_op jit(solution)/shard_map/ppermute | solution.py:479
  22.9 7.7 %collective-permute-start.5 = (f32[4,32,512]{2,1,0:T(8,128)S(1)}, f32[4,32,512]{2,1,0:T(8,128)S(1)}, u32[]{:S(2)}, u32[]{:S(2)}) collective-permute-start(f32[4,32,512]{2,1,0:T(8,128)S(1)} %wedge_first.1.near_part), channel_id=1, source_target_pairs={{1,2},{2,1},{5,6},{6,5},{9,10},{10,9},{13,14},{14,13},{17,18},{18,... | collective-permute-start | bytes 786440 | tf_op jit(solution)/shard_map/ppermute | solution.py:479
  44.2 2.9 %collective-permute-start.7 = (f32[16,2,8,128]{3,2,1,0:T(8,128)S(1)}, f32[16,2,8,128]{3,2,1,0:T(8,128)S(1)}, u32[]{:S(2)}, u32[]{:S(2)}) collective-permute-start(f32[16,2,8,128]{3,2,1,0:T(8,128)S(1)} %all_to_all.10.own), channel_id=1, source_target_pairs={{1,0},{0,1},{3,2},{2,3},{5,4},{4,5},{7,6},{6,7},{9,8},{8,9},{11,10... | collective-permute-start | bytes 393224 | tf_op jit(solution)/shard_map/ppermute | solution.py:479
  69.8 3.1 %collective-permute-start.8 = (f32[8,4,8,128]{3,2,1,0:T(8,128)S(1)}, f32[8,4,8,128]{3,2,1,0:T(8,128)S(1)}, u32[]{:S(2)}, u32[]{:S(2)}) collective-permute-start(f32[8,4,8,128]{3,2,1,0:T(8,128)S(1)} %all_to_all.11.own), channel_id=1, source_target_pairs={{1,0},{0,1},{3,2},{2,3},{5,4},{4,5},{7,6},{6,7},{9,8},{8,9},{11,10... | collective-permute-start | bytes 393224 | tf_op jit(solution)/shard_map/ppermute | solution.py:479

commit v6 on v5

--- a/solution.py
+++ b/solution.py
@@ -12,6 +12,8 @@
 WIDE = 4
 THIN = WIDE - 1
 DEPTH = 8
+CHIP_COUNTS = (WIDE + THIN, 2 * THIN, 2 * THIN)
+NEAR_COUNTS = (WIDE + 2 * THIN, 3 * THIN)
 AXES = ("group", "place", "chip", "core")
 DIFFUSION_FINE = 0.15
 DIFFUSION_COARSE = 0.0375
@@ -35,51 +37,43 @@
         scratch_shapes=list(scratch),
         compiler_params=PARAMS,
         name=name,
+        cost_estimate=pl.CostEstimate(flops=1, bytes_accessed=1, transcendentals=0),
     )(*args)
 
 
-def pack_kernel(where, adj, force, vel, upt, near_out, vel_out, chip_out, sem):
+def pack_kernel(to_chip, where, adj, force, vel, upt, *refs):
+    counts = CHIP_COUNTS if to_chip else NEAR_COUNTS
+    *outs, sem = refs[-1 - len(counts) :]
+    places = [out.at[i] for out, count in zip(outs, counts) for i in range(count)]
     odd = lax.rem(where[0], 2)
-    copies = []
-
-    def add(src, dst):
-        copies.append(pltpu.make_async_copy(src, dst, sem.at[len(copies)]))
 
     def z(c):
         return jnp.where(odd == 1, c, DEPTH - 1 - c)
 
-    for i in range(WIDE):
-        add(adj.at[z(DEPTH - WIDE + i)], near_out.at[i])
-    for i in range(THIN):
-        c = z(DEPTH - THIN + i)
-        add(force.at[c], near_out.at[WIDE + i])
-        add(upt.at[c], near_out.at[WIDE + THIN + i])
-        for part in range(3):
-            add(vel.at[part, c], vel_out.at[part * THIN + i])
-    for i in range(WIDE):
-        add(adj.at[z(i)], chip_out.at[i])
-    for i in range(THIN):
-        c = z(i)
-        add(force.at[c], chip_out.at[WIDE + i])
-        add(upt.at[c], chip_out.at[WIDE + THIN + i])
-        for part in range(3):
-            add(vel.at[part, c], chip_out.at[WIDE + (2 + part) * THIN + i])
+    sources = [adj.at[z(i if to_chip else DEPTH - WIDE + i)] for i in range(WIDE)]
+    layers = [z(i if to_chip else DEPTH - THIN + i) for i in range(THIN)]
+    for ref in (force, upt, vel.at[0], vel.at[1], vel.at[2]):
+        sources += [ref.at[c] for c in layers]
+    copies = [
+        pltpu.make_async_copy(src, dst, sem.at[i])
+        for i, (src, dst) in enumerate(zip(sources, places))
+    ]
     for copy in copies:
         copy.start()
     for copy in copies:
         copy.wait()
 
 
-def pack(where, *arrays):
+def pack(to_chip, where, arrays, after=()):
     _, rows, cols = arrays[0].shape
     arrays = [pltpu.with_memory_space_constraint(x, pltpu.HBM) for x in arrays]
-    counts = (WIDE + 2 * THIN, 3 * THIN, WIDE + 5 * THIN)
-    return call(
-        pack_kernel,
-        "pack",
+    counts = CHIP_COUNTS if to_chip else NEAR_COUNTS
+    return call(
+        functools.partial(pack_kernel, to_chip),
+        "pack_chip" if to_chip else "pack_near",
         tuple(f32(count, rows, cols) for count in counts),
-        [SMEM] + [HBM] * 4,
-        (where, *arrays),
+        [SMEM] + [HBM] * (4 + len(after)),
+        (where, *arrays, *after),
         [pltpu.SemaphoreType.DMA((sum(counts),))],
     )
 
@@ -94,14 +88,24 @@
     return jnp.where(i == j, value, 0.0)
 
 
+def put_tiles(summed, first, value):
+    for t in range(summed.shape[0]):
+        summed[t, pl.ds(first, value.shape[0])] = value[:, 128 * t : 128 * (t + 1)]
+
+
 def restrict_summed(summed):
-    rows, cols = summed.shape
-    down = jnp.dot(groups_of_four(rows // 4, rows, 1.0), summed, precision=HIGH)
-    return jnp.dot(down, groups_of_four(cols, cols // 4, 1.0 / 64.0), precision=HIGH)
-
-
-def restrict_kernel(adj, vel, upt, out):
-    sums = []
+    tiles, rows, lanes = summed.shape
+    down = []
+    for t in range(tiles):
+        parts = [summed[t, pl.ds(k, rows // 4, 4)] for k in range(4)]
+        down.append((parts[0] + parts[1]) + (parts[2] + parts[3]))
+    average = groups_of_four(tiles * lanes, tiles * lanes // 4, 1.0 / 64.0)
+    return jnp.dot(jnp.concatenate(down, axis=1), average, precision=HIGH)
+
+
+def restrict_kernel(adj, vel, upt, out, sums):
+    rows = adj.shape[1]
+    count = 0
     for read in (
         lambda z: adj[z],
         lambda z: vel[0, z],
@@ -110,9 +114,9 @@
         lambda z: upt[z],
     ):
         for z in range(0, DEPTH, 4):
-            sums.append((read(z) + read(z + 1)) + (read(z + 2) + read(z + 3)))
-    stacked = jnp.concatenate(sums, axis=0)
-    out[...] = restrict_summed(stacked).reshape(out.shape)
+            put_tiles(sums, count, (read(z) + read(z + 1)) + (read(z + 2) + read(z + 3)))
+            count += rows
+    out[...] = restrict_summed(sums).reshape(out.shape)
 
 
 def restrict_inputs(adj, vel, upt):
@@ -123,6 +127,7 @@
         f32(5 * depth // 4, rows // 4, cols // 4),
         [VMEM] * 3,
         (adj, vel, upt),
+        [pltpu.VMEM((cols // 128, 5 * depth // 4 * rows, 128), jnp.float32)],
     )
 
 
@@ -168,9 +173,10 @@
     return [(force, (z,)), (upt, (z,)), (vel, (0, z)), (vel, (1, z)), (vel, (2, z))]
 
 
-def inner_kernel(last, where, force, vel, upt, chip_part, near_part, halo, chip, *refs):
+def inner_kernel(last, where, force, vel, upt, chip_part, near_part, halo, *refs):
+    chip_a, chip_b, chip_c, *refs = refs
     if last:
-        edge, out, coarse, state = refs
+        edge, out, coarse, state, summed = refs
     else:
         edge, out, state = refs
     odd = lax.rem(where[0], 2)
@@ -188,7 +194,8 @@
         for c in range(step - WIDE, DEPTH - step):
             if c < 0:
                 i = -c - 1
-                coefs = [(chip, (WIDE + part * THIN + i,)) for part in range(5)]
+                coefs = [(chip_a, (WIDE + i,)), (chip_b, (i,)), (chip_b, (THIN + i,))]
+                coefs += [(chip_c, (i,)), (chip_c, (THIN + i,))]
             else:
                 coefs = own_coefs(odd, force, vel, upt, c)
 
@@ -203,27 +210,30 @@
 
             layer_step(state, now, WIDE + c, coefs, sign, put)
     if last:
-        coarse[...] = restrict_summed((out[0] + out[1]) + (out[2] + out[3]))
+        put_tiles(summed, 0, (out[0] + out[1]) + (out[2] + out[3]))
+        coarse[...] = restrict_summed(summed)
 
 
 def inner(last, where, force, vel, upt, chip_part, near_part, halo, chip):
     _, rows, cols = force.shape
     outs = (f32(WIDE, 2, rows, cols), f32(WIDE, rows, cols))
+    scratch = [pltpu.VMEM((2, DEPTH + WIDE, cols // 128, rows + 16, 128), jnp.float32)]
     if last:
         outs += (f32(rows // 4, cols // 4),)
+        scratch.append(pltpu.VMEM((cols // 128, rows, 128), jnp.float32))
     return call(
         functools.partial(inner_kernel, last),
         "inner_last" if last else "inner_first",
         outs,
-        [SMEM] + [VMEM] * 7,
-        (where, force, vel, upt, chip_part, near_part, halo, chip),
-        [pltpu.VMEM((2, DEPTH + WIDE, cols // 128, rows + 16, 128), jnp.float32)],
+        [SMEM] + [VMEM] * 9,
+        (where, force, vel, upt, chip_part, near_part, halo, *chip),
+        scratch,
     )
 
 
 def wedge_kernel(last, where, force, vel, upt, edge, halo, near, near_vel, *refs):
     if last:
-        coarse_chip, stepped, out, begun, coarse, state = refs
+        coarse_chip, stepped, out, begun, coarse, state, summed = refs
     else:
         out, state = refs
     slab = where[0]
@@ -256,7 +266,8 @@
 
             layer_step(state, now, 1 + j, coefs, sign, put)
     if last:
-        near_coarse = restrict_summed((out[0] + out[1]) + (out[2] + out[3]))
+        put_tiles(summed, 0, (out[0] + out[1]) + (out[2] + out[3]))
+        near_coarse = restrict_summed(summed)
         chip_coarse = coarse_chip[...]
         coarse[0] = jnp.where(odd == 1, chip_coarse, near_coarse)
         coarse[1] = jnp.where(odd == 1, near_coarse, chip_coarse)
@@ -269,15 +280,17 @@
 def wedge(last, where, force, vel, upt, edge, halo, near, near_vel, more=(), copies=0):
     _, rows, cols = force.shape
     outs = (f32(WIDE, rows, cols),)
+    scratch = [pltpu.VMEM((2, WIDE + 2, cols // 128, rows + 16, 128), jnp.float32)]
     if last:
         outs += (f32(copies, 2, rows // 4, cols // 4), f32(2, rows // 4, cols // 4))
+        scratch.append(pltpu.VMEM((cols // 128, rows, 128), jnp.float32))
     return call(
         functools.partial(wedge_kernel, last),
         "wedge_last" if last else "wedge_first",
         outs,
         [SMEM] + [VMEM] * (7 + len(more)),
         (where, force, vel, upt, edge, halo, near, near_vel) + more,
-        [pltpu.VMEM((2, WIDE + 2, cols // 128, rows + 16, 128), jnp.float32)],
+        scratch,
     )
 
 
@@ -316,17 +329,6 @@
     for z in range(depth):
         sides.append([pltpu.roll(part(dx, z), (cols - dx) % cols, 1) for dx in (-2, 2, -1, 1)])
     return [part(0, z) + ((s[0] + s[1]) + (s[2] + s[3])) for z, s in enumerate(sides)]
-
-
-def steps(field, coef, count):
-    def body(_, layers):
-        return tuple(coarse_step(coarse_step(list(layers), coef), coef))
-
-    if count >= 2:
-        field = lax.fori_loop(0, count // 2, body, tuple(field))
-    if count % 2:
-        field = coarse_step(list(field), coef)
-    return list(field)
 
 
 def prepare_kernel(where, own, one, pair, coef, stepped, whole):
@@ -388,17 +390,20 @@
             whole[g, pl.ds(here * part, part)] = own[g * chips + chip]
             whole[g, pl.ds(there * part, part)] = other[g * chips + chip]
 
+    def keep(which, layers):
+        for z in range(depth):
+            ends[which, z] = layers[z]
+
     def body(i, layers):
-        layers = steps(layers, coef, targets)
+        keep(1, layers)
+        layers = list(layers)
+        for _ in range(targets):
+            layers = coarse_step(layers, coef)
         return tuple(layers[z] + whole[count - 2 - i, z] for z in range(depth))
 
-    later = jnp.where(group == count - 1, 0.0, 1.0)
-    field = tuple(later * whole[count - 1, z] for z in range(depth))
-    without = lax.fori_loop(0, count - 2 - group, body, field)
-    stepped = steps(without, coef, targets)
-    for z in range(depth):
-        ends[0, z] = stepped[z] + whole[group, z]
-        ends[1, z] = without[z]
+    ends[1] = jnp.zeros(ends.shape[1:], jnp.float32)
+    field = tuple(whole[count - 1, z] for z in range(depth))
+    keep(0, lax.fori_loop(0, count - 1 - group, body, field))
     for target in range(targets):
         out[target] = ends[jnp.where(place >= target, 0, 1), pl.ds(core * half, half)]
 
@@ -418,7 +423,7 @@
 
 
 def finish_kernel(where, coef, own, other, coarse, chip_part, near_part, *refs):
-    corrected, coarse_new, whole = refs
+    corrected, coarse_new, whole, buffer, down, sem = refs
     slab, place = where[0], where[3]
     odd = lax.rem(slab, 2)
     count, depth = whole.shape[:2]
@@ -439,17 +444,22 @@
     field = lax.fori_loop(0, count - 1, body, tuple(first[z] for z in range(depth)))
     for z in range(depth):
         coarse_new[z] = field[z]
-    part = coarse_new[pl.ds(2 * slab, 2)] - coarse[...]
     rows, cols = chip_part.shape[1:]
-    flat = part.reshape(rows // 2, cols // 4)
-    down = jnp.dot(groups_of_four(2 * rows, rows // 2, 1.0), flat, precision=HIGH)
-    fine = jnp.dot(down, groups_of_four(cols // 4, cols, 1.0), precision=HIGH)
+    part = (coarse_new[pl.ds(2 * slab, 2)] - coarse[...]).reshape(rows // 2, cols // 4)
+    for row in range(rows // 2):
+        down[pl.ds(4 * row, 4)] = jnp.broadcast_to(part[row : row + 1], (4, cols // 4))
+    fine = jnp.dot(down[...], groups_of_four(cols // 4, cols, 1.0), precision=HIGH)
     lower, upper = fine[:rows], fine[rows:]
-    for i in range(WIDE):
-        z = jnp.where(odd == 1, i, DEPTH - 1 - i)
-        corrected[z] = chip_part[i] + jnp.where(odd == 1, lower, upper)
-        z = jnp.where(odd == 1, WIDE + i, DEPTH - 1 - WIDE - i)
-        corrected[z] = near_part[i] + jnp.where(odd == 1, upper, lower)
+    chip_fine = jnp.where(odd == 1, lower, upper)
+    near_fine = jnp.where(odd == 1, upper, lower)
+    copies = []
+    for c in range(DEPTH):
+        buffer[c] = chip_part[c] + chip_fine if c < WIDE else near_part[c - WIDE] + near_fine
+        z = jnp.where(odd == 1, c, DEPTH - 1 - c)
+        copies.append(pltpu.make_async_copy(buffer.at[c], corrected.at[z], sem.at[c]))
+        copies[c].start()
+    for copy in copies:
+        copy.wait()
 
 
 def finish(where, *args):
@@ -461,7 +471,13 @@
         (f32(DEPTH, rows, cols), f32(*full)),
         [SMEM] + [VMEM] * len(args),
         (where, *args),
-        [pltpu.VMEM(args[1].shape[:1] + full, jnp.float32)],
+        [
+            pltpu.VMEM(args[1].shape[:1] + full, jnp.float32),
+            pltpu.VMEM((DEPTH, rows, cols), jnp.float32),
+            pltpu.VMEM((2 * rows, cols // 4), jnp.float32),
+            pltpu.SemaphoreType.DMA((DEPTH,)),
+        ],
+        (HBM, VMEM),
     )
 
 
@@ -488,14 +504,15 @@
         )
 
     own = (force, velocity, uptake)
-    near_pack, vel_pack, chip_pack = pack(where, adj, *own)
+    near_pack, vel_pack = pack(False, where, (adj, *own))
     near = to_next_chip(near_pack)
     near_vel = to_next_chip(vel_pack, times // 2)
-    chip = flipped(chip_pack, 1)
     restricted = restrict_inputs(adj, velocity, uptake)
+    chip_packs = pack(True, where, (adj, *own), ())
+    chip = [flipped(array, 1) for array in chip_packs]
     restricted_one = flipped(restricted, 1)
     pair = flipped(jnp.concatenate([restricted, restricted_one]), 2)
-    edge, chip_part = inner(False, where, *own, chip_pack, near_pack, chip, chip)
+    edge, chip_part = inner(False, where, *own, chip_packs[0], near_pack, chip[0], chip)
     chip_halo = flipped(chip_part, 1)
     near, near_vel, pair, edge = lax.optimization_barrier((near, near_vel, pair, edge))
     (near_part,) = wedge(False, where, *own, edge, near, near, near_vel)

time: 75.7 us -> 74.6 us (0.985)
  waiting for transfers between devices: 8.12 us -> 4.33 us
  starting transfers between devices: 16.3 us -> 18 us
    ppermute x9 -> x11, waiting for transfers between devices: 8.12 us -> 4.33 us  [send(): return lax.ppermute(array, AXES, route)]
    ppermute x9 -> x11, starting transfers between devices: 16.3 us -> 18 us  [send(): return lax.ppermute(array, AXES, route)]
    pallas_call x9 -> x10, Pallas kernels: 22.6 us -> 23.2 us  [call(): pl.pallas_call(kernel, out_shape=outs, in_specs=in_specs, out_specs=out_s...]
  transfers between devices with their start and end apart: 9 -> 11, of which waited for: 6 -> 5; matrix products, arithmetic and copies ran while one was open for 0% -> 0% of each run, Pallas kernels for 11% -> 14%
where the time goes in v6:
time: 74.6 us; the launch traced here: 74.2 us
  blocking collectives  27.8 us (37%)
  Pallas kernels  23.2 us (31%)
  starting transfers between devices  18 us (24%)
  waiting for transfers between devices  4.33 us (6%)
  between operations  0.78 us (1%)
    pallas_call x10, Pallas kernels, call(): pl.pallas_call(kernel, out_shape=outs, in_specs=in_specs, out_specs=out_s...  23.2 us
    ppermute x11, starting transfers between devices, send(): return lax.ppermute(array, AXES, route)  18 us
    all_to_all x1, blocking collectives, per_device(): terms = lax.all_to_all(terms, 'place', 0, 0)  15.9 us
    all_to_all x1, blocking collectives, per_device(): begun = lax.all_to_all(begun, ('group', 'chip'), 0, 0)  11.9 us
    ppermute x11, waiting for transfers between devices, send(): return lax.ppermute(array, AXES, route)  4.33 us
  transfers between devices with their start and end apart: 11, of which 5 were waited for; matrix products, arithmetic and copies ran while one was open for 0% of the time, Pallas kernels for 14%

profile of v6, /device:TPU:1, one launch (start us, length us, event | category | flops | bytes accessed | tf_op | source)
XLA Modules:
  0.0 74.2 jit_solution(2023275251869965803)
XLA Ops:
  0.7 2.0 %pack_near.1 = (f32[10,32,512]{2,1,0:T(8,128)S(1)}, f32[9,32,512]{2,1,0:T(8,128)S(1)}) custom-call(s32[4]{0:T(128)S(1)} %pad_add_fusion.where, f32[8,32,512]{2,1,0:T(8,128)} %bitcast.14, f32[8,32,512]{2,1,0:T(8,128)} %bitcast.8, f32[3,8,32,512]{3,2,1,0:T(8,128)} %vel.13, f32[8,32,512]{2,1,0:T(8,128)} %upt.13), custom_call_target="tpu_custom_call" | custom-call | flops 1 | bytes 1 | tf_op jit(solution)/shard_map/pack_near/pallas_call | solution.py:32
  2.7 4.6 %collective-permute-start = (f32[10,32,512]{2,1,0:T(8,128)S(1)}, f32[10,32,512]{2,1,0:T(8,128)S(1)}, u32[]{:S(2)}, u32[]{:S(2)}) collective-permute-start(f32[10,32,512]{2,1,0:T(8,128)S(1)} %get-tuple-element.27.near_part), channel_id=1, source_target_pairs={{1,2},{2,1},{5,6},{6,5},{9,10},{10,9},{13,14},{14,13},{17,18},{18,... | collective-permute-start | bytes 1966088 | tf_op jit(solution)/shard_map/ppermute | solution.py:495
  7.4 3.7 %collective-permute-start.1 = (f32[9,32,512]{2,1,0:T(8,128)S(1)}, f32[9,32,512]{2,1,0:T(8,128)S(1)}, u32[]{:S(2)}, u32[]{:S(2)}) collective-permute-start(f32[9,32,512]{2,1,0:T(8,128)S(1)} %get-tuple-element.28), channel_id=1, source_target_pairs={{1,130},{2,129},{5,134},{6,133},{9,138},{10,137},{13,142},{14,141}... | collective-permute-start | bytes 1769480 | tf_op jit(solution)/shard_map/ppermute | solution.py:495
  11.0 2.0 %pack_chip.1 = (f32[7,32,512]{2,1,0:T(8,128)S(1)}, f32[6,32,512]{2,1,0:T(8,128)S(1)}, f32[6,32,512]{2,1,0:T(8,128)S(1)}) custom-call(s32[4]{0:T(128)S(1)} %pad_add_fusion.where, f32[8,32,512]{2,1,0:T(8,128)} %bitcast.15, f32[8,32,512]{2,1,0:T(8,128)} %bitcast.9, f32[3,8,32,512]{3,2,1,0:T(8,128)} %vel.13, f32[8,32,512]{2,1,0:T(8,128)} %upt.13), custom_call_target="tpu_custom_call" | custom-call | flops 1 | bytes 1 | tf_op jit(solution)/shard_map/pack_chip/pallas_call | solution.py:32
  13.2 0.5 collective-permute-start.4
  13.7 0.5 restrict.1.own
  14.4 1.2 %collective-permute-done.2.one = f32[10,8,128]{2,1,0:T(8,128)S(1)} collective-permute-done((f32[10,8,128]{2,1,0:T(8,128)S(1)}, f32[10,8,128]{2,1,0:T(8,128)S(1)}, u32[]{:S(2)}, u32[]{:S(2)}) %collective-permute-start.2) | collective-permute-done | bytes 40992 | tf_op jit(solution)/shard_map/ppermute | solution.py:495
  15.8 1.0 %collective-permute-start.3 = (f32[20,8,128]{2,1,0:T(8,128)S(1)}, f32[20,8,128]{2,1,0:T(8,128)S(1)}, u32[]{:S(2)}, u32[]{:S(2)}) collective-permute-start(f32[20,8,128]{2,1,0:T(8,128)S(1)} %pad_maximum_fusion), channel_id=1, source_target_pairs={{2,0},{3,1},{0,2},{1,3},{6,4},{7,5},{4,6},{5,7},{10,8},{11,9},{8,1... | collective-permute-start | bytes 245768 | tf_op jit(solution)/shard_map/ppermute | solution.py:495
  16.8 0.5 collective-permute-done.6.refs_2_
  17.3 2.3 %inner_first.1 = (f32[4,2,32,512]{3,2,1,0:T(8,128)S(1)}, f32[4,32,512]{2,1,0:T(8,128)S(1)}) custom-call(s32[4]{0:T(128)S(1)} %pad_add_fusion.where, f32[8,32,512]{2,1,0:T(8,128)S(1)} %bitcast.10, f32[3,8,32,512]{3,2,1,0:T(8,128)S(1)} %copy-done, f32[8,32,512]{2,1,0:T(8,128)S(1)} %copy-done.1, f32[7,32,512]{2,1,0:T(8,128)S(1)} %get-tuple-element.29.chip_part, ...), custom_call_target="tpu_custom_call" | custom-call | flops 1 | bytes 1 | tf_op jit(solution)/shard_map/inner_first/pallas_call | solution.py:32
  19.9 1.6 %wedge_first.1.near_part = f32[4,32,512]{2,1,0:T(8,128)S(1)} custom-call(s32[4]{0:T(128)S(1)} %pad_add_fusion.where, f32[8,32,512]{2,1,0:T(8,128)S(1)} %bitcast.11, f32[3,8,32,512]{3,2,1,0:T(8,128)S(1)} %copy-done, f32[8,32,512]{2,1,0:T(8,128)S(1)} %copy-done.1, f32[4,2,32,512]{3,2,1,0:T(8,128)S(1)} %get-tuple-element.33.edge, ...), custom_call_target="tpu_custom_call" | custom-call | flops 1 | bytes 1 | tf_op jit(solution)/shard_map/wedge_first/pallas_call | solution.py:32
  21.5 3.5 %collective-permute-start.7 = (f32[4,32,512]{2,1,0:T(8,128)S(1)}, f32[4,32,512]{2,1,0:T(8,128)S(1)}, u32[]{:S(2)}, u32[]{:S(2)}) collective-permute-start(f32[4,32,512]{2,1,0:T(8,128)S(1)} %wedge_first.1.near_part), channel_id=1, source_target_pairs={{1,2},{2,1},{5,6},{6,5},{9,10},{10,9},{13,14},{14,13},{17,18},{18,... | collective-permute-start | bytes 786440 | tf_op jit(solution)/shard_map/ppermute | solution.py:495
  25.0 1.0 %prepare.1 = (f32[25,8,8,128]{3,2,1,0:T(8,128)S(1)}, f32[8,8,128]{2,1,0:T(8,128)S(1)}) custom-call(s32[4]{0:T(128)S(1)} %pad_add_fusion.where, f32[10,8,128]{2,1,0:T(8,128)S(1)} %restrict.1.own, f32[10,8,128]{2,1,0:T(8,128)S(1)} %collective-permute-done.2.one, f32[20,8,128]{2,1,0:T(8,128)S(1)} %collective-permute-done.3.pair), custom_call_target="tpu_custom_call" | custom-call | flops 1 | bytes 1 | tf_op jit(solution)/shard_map/prepare/pallas_call | solution.py:32
  26.0 2.6 %inner_last.1 = (f32[4,2,32,512]{3,2,1,0:T(8,128)S(1)}, f32[4,32,512]{2,1,0:T(8,128)S(1)}, f32[8,128]{1,0:T(8,128)S(1)}) custom-call(s32[4]{0:T(128)S(1)} %pad_add_fusion.where, f32[8,32,512]{2,1,0:T(8,128)S(1)} %bitcast.12, f32[3,8,32,512]{3,2,1,0:T(8,128)S(1)} %copy-done, f32[8,32,512]{2,1,0:T(8,128)S(1)} %copy-done.1, ...), custom_call_target="tpu_custom_call" | custom-call | flops 1 | bytes 1 | tf_op jit(solution)/shard_map/inner_last/pallas_call | solution.py:32
  28.6 0.5 collective-permute-done.7.halo
  29.2 1.9 %wedge_last.1 = (f32[4,32,512]{2,1,0:T(8,128)S(1)}, f32[16,2,8,128]{3,2,1,0:T(8,128)S(1)}, f32[2,8,128]{2,1,0:T(8,128)S(1)}) custom-call(s32[4]{0:T(128)S(1)} %pad_add_fusion.where, f32[8,32,512]{2,1,0:T(8,128)S(1)} %bitcast.13, f32[3,8,32,512]{3,2,1,0:T(8,128)S(1)} %copy-done, f32[8,32,512]{2,1,0:T(8,128)S(1)} %copy-done.1, ...), custom_call_target="tpu_custom_call" | custom-call | flops 1 | bytes 1 | tf_op jit(solution)/shard_map/wedge_last/pallas_call | solution.py:32
  31.1 11.9 %all_to_all.10.own = f32[16,2,8,128]{3,2,1,0:T(8,128)S(1)} all-to-all(f32[16,2,8,128]{3,2,1,0:T(8,128)S(1)} %get-tuple-element.46), channel_id=1, replica_groups=mesh['group'=8,'place'=8,'chip'=2,'core'=2] {'group','chip'}, dimensions={0} | all-to-all | bytes 262144 | tf_op jit(solution)/shard_map/all_to_all | solution.py:527
  43.0 1.9 %collective-permute-start.9 = (f32[16,2,8,128]{3,2,1,0:T(8,128)S(1)}, f32[16,2,8,128]{3,2,1,0:T(8,128)S(1)}, u32[]{:S(2)}, u32[]{:S(2)}) collective-permute-start(f32[16,2,8,128]{3,2,1,0:T(8,128)S(1)} %all_to_all.10.own), channel_id=1, source_target_pairs={{1,0},{0,1},{3,2},{2,3},{5,4},{4,5},{7,6},{6,7},{9,8},{8,9},{11,10... | collective-permute-start | bytes 393224 | tf_op jit(solution)/shard_map/ppermute | solution.py:495
  44.9 1.0 %collective-permute-done.9.other = f32[16,2,8,128]{3,2,1,0:T(8,128)S(1)} collective-permute-done((f32[16,2,8,128]{3,2,1,0:T(8,128)S(1)}, f32[16,2,8,128]{3,2,1,0:T(8,128)S(1)}, u32[]{:S(2)}, u32[]{:S(2)}) %collective-permute-start.9) | collective-permute-done | bytes 131104 | tf_op jit(solution)/shard_map/ppermute | solution.py:495
  45.9 6.3 %outer.1 = f32[8,4,8,128]{3,2,1,0:T(8,128)S(1)} custom-call(s32[4]{0:T(128)S(1)} %pad_add_fusion.where, f32[25,8,8,128]{3,2,1,0:T(8,128)S(1)} %get-tuple-element.41.coef, f32[16,2,8,128]{3,2,1,0:T(8,128)S(1)} %all_to_all.10.own, f32[16,2,8,128]{3,2,1,0:T(8,128)S(1)} %collective-permute-done.9.other), custom_call_target="tpu_custom_call" | custom-call | flops 1 | bytes 1 | tf_op jit(solution)/shard_map/outer/pallas_call | solution.py:32
  52.1 15.9 %all_to_all.11.own = f32[8,4,8,128]{3,2,1,0:T(8,128)S(1)} all-to-all(f32[8,4,8,128]{3,2,1,0:T(8,128)S(1)} %outer.1), channel_id=1, replica_groups=mesh['group'=8,'place'=8,'chip'=2,'core'=2] {'place'}, dimensions={0} | all-to-all | bytes 262144 | tf_op jit(solution)/shard_map/all_to_all | solution.py:529
  68.0 2.1 %collective-permute-start.10 = (f32[8,4,8,128]{3,2,1,0:T(8,128)S(1)}, f32[8,4,8,128]{3,2,1,0:T(8,128)S(1)}, u32[]{:S(2)}, u32[]{:S(2)}) collective-permute-start(f32[8,4,8,128]{3,2,1,0:T(8,128)S(1)} %all_to_all.11.own), channel_id=1, source_target_pairs={{1,0},{0,1},{3,2},{2,3},{5,4},{4,5},{7,6},{6,7},{9,8},{8,9},{11,10... | collective-permute-start | bytes 393224 | tf_op jit(solution)/shard_map/ppermute | solution.py:495
  70.2 1.0 %collective-permute-done.10.other = f32[8,4,8,128]{3,2,1,0:T(8,128)S(1)} collective-permute-done((f32[8,4,8,128]{3,2,1,0:T(8,128)S(1)}, f32[8,4,8,128]{3,2,1,0:T(8,128)S(1)}, u32[]{:S(2)}, u32[]{:S(2)}) %collective-permute-start.10) | collective-permute-done | bytes 131104 | tf_op jit(solution)/shard_map/ppermute | solution.py:495
  71.1 3.1 %finish.1 = (f32[8,32,512]{2,1,0:T(8,128)}, f32[8,8,128]{2,1,0:T(8,128)}) custom-call(s32[4]{0:T(128)S(1)} %pad_add_fusion.where, f32[25,8,8,128]{3,2,1,0:T(8,128)S(1)} %get-tuple-element.41.coef, f32[8,4,8,128]{3,2,1,0:T(8,128)S(1)} %all_to_all.11.own, f32[8,4,8,128]{3,2,1,0:T(8,128)S(1)} %collective-permute-done.10.other, ...), custom_call_target="tpu_custom_call" | custom-call | flops 1 | bytes 1 | tf_op jit(solution)/shard_map/finish/pallas_call | solution.py:32
  (20 shorter events, 0.8 us)
Async XLA Ops:
  2.7 17.2 %collective-permute-start = (f32[10,32,512]{2,1,0:T(8,128)S(1)}, f32[10,32,512]{2,1,0:T(8,128)S(1)}, u32[]{:S(2)}, u32[]{:S(2)}) collective-permute-start(f32[10,32,512]{2,1,0:T(8,128)S(1)} %get-tuple-element.27.near_part), channel_id=1, source_target_pairs={{1,2},{2,1},{5,6},{6,5},{9,10},{10,9},{13,14},{14,13},{17,18},{18,... | collective-permute-start | bytes 1966088 | tf_op jit(solution)/shard_map/ppermute | solution.py:495
  7.3 6.3 %copy-start = (f32[3,8,32,512]{3,2,1,0:T(8,128)S(1)}, f32[3,8,32,512]{3,2,1,0:T(8,128)}, u32[]{:S(2)}) copy-start(f32[3,8,32,512]{3,2,1,0:T(8,128)} %vel.13) | copy-start | bytes 4718596
  7.4 6.3 %copy-start.1 = (f32[8,32,512]{2,1,0:T(8,128)S(1)}, f32[8,32,512]{2,1,0:T(8,128)}, u32[]{:S(2)}) copy-start(f32[8,32,512]{2,1,0:T(8,128)} %upt.13) | copy-start | bytes 1572868
  7.4 6.3 %copy-start.3 = (f32[1,8,32,512]{3,2,1,0:T(8,128)S(1)}, f32[1,8,32,512]{3,2,1,0:T(8,128)}, u32[]{:S(2)}) copy-start(f32[1,8,32,512]{3,2,1,0:T(8,128)} %param.4) | copy-start | bytes 1572868
  7.4 12.5 %collective-permute-start.1 = (f32[9,32,512]{2,1,0:T(8,128)S(1)}, f32[9,32,512]{2,1,0:T(8,128)S(1)}, u32[]{:S(2)}, u32[]{:S(2)}) collective-permute-start(f32[9,32,512]{2,1,0:T(8,128)S(1)} %get-tuple-element.28), channel_id=1, source_target_pairs={{1,130},{2,129},{5,134},{6,133},{9,138},{10,137},{13,142},{14,141}... | collective-permute-start | bytes 1769480 | tf_op jit(solution)/shard_map/ppermute | solution.py:495
  13.1 4.3 %copy-start.2 = (f32[1,8,32,512]{3,2,1,0:T(8,128)S(1)}, f32[1,8,32,512]{3,2,1,0:T(8,128)}, u32[]{:S(2)}) copy-start(f32[1,8,32,512]{3,2,1,0:T(8,128)} %param.5) | copy-start | bytes 1572868
  13.1 2.7 %collective-permute-start.5 = (f32[6,32,512]{2,1,0:T(8,128)S(1)}, f32[6,32,512]{2,1,0:T(8,128)S(1)}, u32[]{:S(2)}, u32[]{:S(2)}) collective-permute-start(f32[6,32,512]{2,1,0:T(8,128)S(1)} %get-tuple-element.30), channel_id=1, source_target_pairs={{1,0},{0,1},{3,2},{2,3},{5,4},{4,5},{7,6},{6,7},{9,8},{8,9},{11,10... | collective-permute-start | bytes 1179656 | tf_op jit(solution)/shard_map/ppermute | solution.py:495
  13.2 4.2 %collective-permute-start.4 = (f32[7,32,512]{2,1,0:T(8,128)S(1)}, f32[7,32,512]{2,1,0:T(8,128)S(1)}, u32[]{:S(2)}, u32[]{:S(2)}) collective-permute-start(f32[7,32,512]{2,1,0:T(8,128)S(1)} %get-tuple-element.29.chip_part), channel_id=1, source_target_pairs={{1,0},{0,1},{3,2},{2,3},{5,4},{4,5},{7,6},{6,7},{9,8},{8,9},{11,10... | collective-permute-start | bytes 1376264 | tf_op jit(solution)/shard_map/ppermute | solution.py:495
  14.2 1.4 %collective-permute-start.2 = (f32[10,8,128]{2,1,0:T(8,128)S(1)}, f32[10,8,128]{2,1,0:T(8,128)S(1)}, u32[]{:S(2)}, u32[]{:S(2)}) collective-permute-start(f32[10,8,128]{2,1,0:T(8,128)S(1)} %restrict.1.own), channel_id=1, source_target_pairs={{1,0},{0,1},{3,2},{2,3},{5,4},{4,5},{7,6},{6,7},{9,8},{8,9},{11,10... | collective-permute-start | bytes 122888 | tf_op jit(solution)/shard_map/ppermute | solution.py:495
  15.6 1.7 %collective-permute-start.6 = (f32[6,32,512]{2,1,0:T(8,128)S(1)}, f32[6,32,512]{2,1,0:T(8,128)S(1)}, u32[]{:S(2)}, u32[]{:S(2)}) collective-permute-start(f32[6,32,512]{2,1,0:T(8,128)S(1)} %get-tuple-element.31), channel_id=1, source_target_pairs={{1,0},{0,1},{3,2},{2,3},{5,4},{4,5},{7,6},{6,7},{9,8},{8,9},{11,10... | collective-permute-start | bytes 1179656 | tf_op jit(solution)/shard_map/ppermute | solution.py:495
  15.8 4.1 %collective-permute-start.3 = (f32[20,8,128]{2,1,0:T(8,128)S(1)}, f32[20,8,128]{2,1,0:T(8,128)S(1)}, u32[]{:S(2)}, u32[]{:S(2)}) collective-permute-start(f32[20,8,128]{2,1,0:T(8,128)S(1)} %pad_maximum_fusion), channel_id=1, source_target_pairs={{2,0},{3,1},{0,2},{1,3},{6,4},{7,5},{4,6},{5,7},{10,8},{11,9},{8,1... | collective-permute-start | bytes 245768 | tf_op jit(solution)/shard_map/ppermute | solution.py:495
  19.7 6.3 %collective-permute-start.8 = (f32[4,32,512]{2,1,0:T(8,128)S(1)}, f32[4,32,512]{2,1,0:T(8,128)S(1)}, u32[]{:S(2)}, u32[]{:S(2)}) collective-permute-start(f32[4,32,512]{2,1,0:T(8,128)S(1)} %get-tuple-element.36.chip_part), channel_id=1, source_target_pairs={{1,0},{0,1},{3,2},{2,3},{5,4},{4,5},{7,6},{6,7},{9,8},{8,9},{11,10... | collective-permute-start | bytes 786440 | tf_op jit(solution)/shard_map/ppermute | solution.py:495
  21.5 7.7 %collective-permute-start.7 = (f32[4,32,512]{2,1,0:T(8,128)S(1)}, f32[4,32,512]{2,1,0:T(8,128)S(1)}, u32[]{:S(2)}, u32[]{:S(2)}) collective-permute-start(f32[4,32,512]{2,1,0:T(8,128)S(1)} %wedge_first.1.near_part), channel_id=1, source_target_pairs={{1,2},{2,1},{5,6},{6,5},{9,10},{10,9},{13,14},{14,13},{17,18},{18,... | collective-permute-start | bytes 786440 | tf_op jit(solution)/shard_map/ppermute | solution.py:495
  43.0 2.9 %collective-permute-start.9 = (f32[16,2,8,128]{3,2,1,0:T(8,128)S(1)}, f32[16,2,8,128]{3,2,1,0:T(8,128)S(1)}, u32[]{:S(2)}, u32[]{:S(2)}) collective-permute-start(f32[16,2,8,128]{3,2,1,0:T(8,128)S(1)} %all_to_all.10.own), channel_id=1, source_target_pairs={{1,0},{0,1},{3,2},{2,3},{5,4},{4,5},{7,6},{6,7},{9,8},{8,9},{11,10... | collective-permute-start | bytes 393224 | tf_op jit(solution)/shard_map/ppermute | solution.py:495
  68.0 3.1 %collective-permute-start.10 = (f32[8,4,8,128]{3,2,1,0:T(8,128)S(1)}, f32[8,4,8,128]{3,2,1,0:T(8,128)S(1)}, u32[]{:S(2)}, u32[]{:S(2)}) collective-permute-start(f32[8,4,8,128]{3,2,1,0:T(8,128)S(1)} %all_to_all.11.own), channel_id=1, source_target_pairs={{1,0},{0,1},{3,2},{2,3},{5,4},{4,5},{7,6},{6,7},{9,8},{8,9},{11,10... | collective-permute-start | bytes 393224 | tf_op jit(solution)/shard_map/ppermute | solution.py:495

commit v7 on v6

--- a/solution.py
+++ b/solution.py
@@ -379,7 +379,7 @@
 def outer_kernel(where, coef, own, other, out, whole, ends):
     slab, group, place = where[0], where[2], where[3]
     core = lax.rem(slab, 2)
-    targets, half = out.shape[:2]
+    targets = out.shape[0]
     count, depth = whole.shape[:2]
     chips = own.shape[0] // count
     part = own.shape[1]
@@ -405,35 +405,31 @@
     field = tuple(whole[count - 1, z] for z in range(depth))
     keep(0, lax.fori_loop(0, count - 1 - group, body, field))
     for target in range(targets):
-        out[target] = ends[jnp.where(place >= target, 0, 1), pl.ds(core * half, half)]
+        out[target] = ends[jnp.where(place >= target, 0, 1)]
 
 
 def outer(targets, where, coef, own, other):
     full = coef.shape[1:]
-    depth, rows, cols = full
+    depth = full[0]
     count = own.shape[0] * own.shape[1] * 2 // depth
     return call(
         outer_kernel,
         "outer",
-        f32(targets, depth // 2, rows, cols),
+        f32(targets, *full),
         [SMEM] + [VMEM] * 3,
         (where, coef, own, other),
         [pltpu.VMEM((count,) + full, jnp.float32), pltpu.VMEM((2,) + full, jnp.float32)],
     )
 
 
-def finish_kernel(where, coef, own, other, coarse, chip_part, near_part, *refs):
-    corrected, coarse_new, whole, buffer, down, sem = refs
+def finish_kernel(where, coef, terms, coarse, chip_part, near_part, *refs):
+    corrected, coarse_new, down = refs
     slab, place = where[0], where[3]
     odd = lax.rem(slab, 2)
-    count, depth = whole.shape[:2]
-    half = depth // 2
-    for t in range(count):
-        whole[t, pl.ds(odd * half, half)] = own[t]
-        whole[t, pl.ds((1 - odd) * half, half)] = other[t]
+    count, depth = terms.shape[:2]
 
     def term(j):
-        return whole.at[lax.rem(place + j, count)]
+        return terms.at[lax.rem(place + j, count)]
 
     def body(i, layers):
         stepped = coarse_step(list(layers), coef)
@@ -452,14 +448,9 @@
     lower, upper = fine[:rows], fine[rows:]
     chip_fine = jnp.where(odd == 1, lower, upper)
     near_fine = jnp.where(odd == 1, upper, lower)
-    copies = []
     for c in range(DEPTH):
-        buffer[c] = chip_part[c] + chip_fine if c < WIDE else near_part[c - WIDE] + near_fine
         z = jnp.where(odd == 1, c, DEPTH - 1 - c)
-        copies.append(pltpu.make_async_copy(buffer.at[c], corrected.at[z], sem.at[c]))
-        copies[c].start()
-    for copy in copies:
-        copy.wait()
+        corrected[z] = chip_part[c] + chip_fine if c < WIDE else near_part[c - WIDE] + near_fine
 
 
 def finish(where, *args):
@@ -471,13 +462,7 @@
         (f32(DEPTH, rows, cols), f32(*full)),
         [SMEM] + [VMEM] * len(args),
         (where, *args),
-        [
-            pltpu.VMEM(args[1].shape[:1] + full, jnp.float32),
-            pltpu.VMEM((DEPTH, rows, cols), jnp.float32),
-            pltpu.VMEM((2 * rows, cols // 4), jnp.float32),
-            pltpu.SemaphoreType.DMA((DEPTH,)),
-        ],
-        (HBM, VMEM),
+        [pltpu.VMEM((2 * rows, cols // 4), jnp.float32)],
     )
 
 
@@ -527,9 +512,7 @@
     begun = lax.all_to_all(begun, ("group", "chip"), 0, 0)
     terms = outer(places, where, coef, begun, flipped(begun, 1))
     terms = lax.all_to_all(terms, "place", 0, 0)
-    corrected, coarse_new = finish(
-        where, coef, terms, flipped(terms, 1), coarse, chip_part, near_part
-    )
+    corrected, coarse_new = finish(where, coef, terms, coarse, chip_part, near_part)
     return corrected[None], coarse_new[None]
 
 

time: 74.6 us -> 74.1 us (level)
  blocking collectives: 27.8 us -> 31 us
  starting transfers between devices: 18 us -> 15.8 us
  waiting for transfers between devices: 4.33 us -> 3.35 us
    all_to_all x1, blocking collectives: 15.9 us -> 19.1 us  [per_device(): terms = lax.all_to_all(terms, 'place', 0, 0)]
    ppermute x11 -> x10, starting transfers between devices: 18 us -> 15.8 us  [send(): return lax.ppermute(array, AXES, route)]
    ppermute x11 -> x10, waiting for transfers between devices: 4.33 us -> 3.35 us  [send(): return lax.ppermute(array, AXES, route)]
  transfers between devices with their start and end apart: 11 -> 10, of which waited for: 5 -> 4; matrix products, arithmetic and copies ran while one was open for 0% -> 0% of each run, Pallas kernels for 14% -> 14%
where the time goes in v7:
time: 74.1 us; the launch traced here: 73.7 us
  blocking collectives  31 us (42%)
  Pallas kernels  22.6 us (30%)
  starting transfers between devices  15.8 us (21%)
  waiting for transfers between devices  3.35 us (5%)
  between operations  0.77 us (1%)
    pallas_call x10, Pallas kernels, call(): pl.pallas_call(kernel, out_shape=outs, in_specs=in_specs, out_specs=out_s...  22.6 us
    all_to_all x1, blocking collectives, per_device(): terms = lax.all_to_all(terms, 'place', 0, 0)  19.1 us
    ppermute x10, starting transfers between devices, send(): return lax.ppermute(array, AXES, route)  15.8 us
    all_to_all x1, blocking collectives, per_device(): begun = lax.all_to_all(begun, ('group', 'chip'), 0, 0)  11.9 us
    ppermute x10, waiting for transfers between devices, send(): return lax.ppermute(array, AXES, route)  3.35 us
  transfers between devices with their start and end apart: 10, of which 4 were waited for; matrix products, arithmetic and copies ran while one was open for 0% of the time, Pallas kernels for 14%

profile of v7, /device:TPU:1, one launch (start us, length us, event | category | flops | bytes accessed | tf_op | source)
XLA Modules:
  0.0 73.7 jit_solution(16770085196935426132)
XLA Ops:
  0.7 2.0 %pack_near.1 = (f32[10,32,512]{2,1,0:T(8,128)S(1)}, f32[9,32,512]{2,1,0:T(8,128)S(1)}) custom-call(s32[4]{0:T(128)S(1)} %pad_add_fusion.where, f32[8,32,512]{2,1,0:T(8,128)} %bitcast.14, f32[8,32,512]{2,1,0:T(8,128)} %bitcast.8, f32[3,8,32,512]{3,2,1,0:T(8,128)} %vel.13, f32[8,32,512]{2,1,0:T(8,128)} %upt.13), custom_call_target="tpu_custom_call" | custom-call | flops 1 | bytes 1 | tf_op jit(solution)/shard_map/pack_near/pallas_call | solution.py:32
  2.7 4.6 %collective-permute-start = (f32[10,32,512]{2,1,0:T(8,128)S(1)}, f32[10,32,512]{2,1,0:T(8,128)S(1)}, u32[]{:S(2)}, u32[]{:S(2)}) collective-permute-start(f32[10,32,512]{2,1,0:T(8,128)S(1)} %get-tuple-element.27.near_part), channel_id=1, source_target_pairs={{1,2},{2,1},{5,6},{6,5},{9,10},{10,9},{13,14},{14,13},{17,18},{18,... | collective-permute-start | bytes 1966088 | tf_op jit(solution)/shard_map/ppermute | solution.py:480
  7.4 3.7 %collective-permute-start.1 = (f32[9,32,512]{2,1,0:T(8,128)S(1)}, f32[9,32,512]{2,1,0:T(8,128)S(1)}, u32[]{:S(2)}, u32[]{:S(2)}) collective-permute-start(f32[9,32,512]{2,1,0:T(8,128)S(1)} %get-tuple-element.28), channel_id=1, source_target_pairs={{1,130},{2,129},{5,134},{6,133},{9,138},{10,137},{13,142},{14,141}... | collective-permute-start | bytes 1769480 | tf_op jit(solution)/shard_map/ppermute | solution.py:480
  11.0 2.0 %pack_chip.1 = (f32[7,32,512]{2,1,0:T(8,128)S(1)}, f32[6,32,512]{2,1,0:T(8,128)S(1)}, f32[6,32,512]{2,1,0:T(8,128)S(1)}) custom-call(s32[4]{0:T(128)S(1)} %pad_add_fusion.where, f32[8,32,512]{2,1,0:T(8,128)} %bitcast.15, f32[8,32,512]{2,1,0:T(8,128)} %bitcast.9, f32[3,8,32,512]{3,2,1,0:T(8,128)} %vel.13, f32[8,32,512]{2,1,0:T(8,128)} %upt.13), custom_call_target="tpu_custom_call" | custom-call | flops 1 | bytes 1 | tf_op jit(solution)/shard_map/pack_chip/pallas_call | solution.py:32
  13.2 0.5 collective-permute-start.4
  13.7 0.5 restrict.1.own
  14.2 0.2 collective-permute-start.2
  14.4 1.2 %collective-permute-done.2.one = f32[10,8,128]{2,1,0:T(8,128)S(1)} collective-permute-done((f32[10,8,128]{2,1,0:T(8,128)S(1)}, f32[10,8,128]{2,1,0:T(8,128)S(1)}, u32[]{:S(2)}, u32[]{:S(2)}) %collective-permute-start.2) | collective-permute-done | bytes 40992 | tf_op jit(solution)/shard_map/ppermute | solution.py:480
  15.8 1.0 %collective-permute-start.3 = (f32[20,8,128]{2,1,0:T(8,128)S(1)}, f32[20,8,128]{2,1,0:T(8,128)S(1)}, u32[]{:S(2)}, u32[]{:S(2)}) collective-permute-start(f32[20,8,128]{2,1,0:T(8,128)S(1)} %pad_maximum_fusion), channel_id=1, source_target_pairs={{2,0},{3,1},{0,2},{1,3},{6,4},{7,5},{4,6},{5,7},{10,8},{11,9},{8,1... | collective-permute-start | bytes 245768 | tf_op jit(solution)/shard_map/ppermute | solution.py:480
  16.8 0.5 collective-permute-done.6.refs_2_
  17.3 2.3 %inner_first.1 = (f32[4,2,32,512]{3,2,1,0:T(8,128)S(1)}, f32[4,32,512]{2,1,0:T(8,128)S(1)}) custom-call(s32[4]{0:T(128)S(1)} %pad_add_fusion.where, f32[8,32,512]{2,1,0:T(8,128)S(1)} %bitcast.10, f32[3,8,32,512]{3,2,1,0:T(8,128)S(1)} %copy-done, f32[8,32,512]{2,1,0:T(8,128)S(1)} %copy-done.1, f32[7,32,512]{2,1,0:T(8,128)S(1)} %get-tuple-element.29.chip_part, ...), custom_call_target="tpu_custom_call" | custom-call | flops 1 | bytes 1 | tf_op jit(solution)/shard_map/inner_first/pallas_call | solution.py:32
  19.7 0.2 collective-permute-start.8
  19.9 1.6 %wedge_first.1.near_part = f32[4,32,512]{2,1,0:T(8,128)S(1)} custom-call(s32[4]{0:T(128)S(1)} %pad_add_fusion.where, f32[8,32,512]{2,1,0:T(8,128)S(1)} %bitcast.11, f32[3,8,32,512]{3,2,1,0:T(8,128)S(1)} %copy-done, f32[8,32,512]{2,1,0:T(8,128)S(1)} %copy-done.1, f32[4,2,32,512]{3,2,1,0:T(8,128)S(1)} %get-tuple-element.33.edge, ...), custom_call_target="tpu_custom_call" | custom-call | flops 1 | bytes 1 | tf_op jit(solution)/shard_map/wedge_first/pallas_call | solution.py:32
  21.5 3.5 %collective-permute-start.7 = (f32[4,32,512]{2,1,0:T(8,128)S(1)}, f32[4,32,512]{2,1,0:T(8,128)S(1)}, u32[]{:S(2)}, u32[]{:S(2)}) collective-permute-start(f32[4,32,512]{2,1,0:T(8,128)S(1)} %wedge_first.1.near_part), channel_id=1, source_target_pairs={{1,2},{2,1},{5,6},{6,5},{9,10},{10,9},{13,14},{14,13},{17,18},{18,... | collective-permute-start | bytes 786440 | tf_op jit(solution)/shard_map/ppermute | solution.py:480
  25.0 1.0 %prepare.1 = (f32[25,8,8,128]{3,2,1,0:T(8,128)S(1)}, f32[8,8,128]{2,1,0:T(8,128)S(1)}) custom-call(s32[4]{0:T(128)S(1)} %pad_add_fusion.where, f32[10,8,128]{2,1,0:T(8,128)S(1)} %restrict.1.own, f32[10,8,128]{2,1,0:T(8,128)S(1)} %collective-permute-done.2.one, f32[20,8,128]{2,1,0:T(8,128)S(1)} %collective-permute-done.3.pair), custom_call_target="tpu_custom_call" | custom-call | flops 1 | bytes 1 | tf_op jit(solution)/shard_map/prepare/pallas_call | solution.py:32
  26.0 2.6 %inner_last.1 = (f32[4,2,32,512]{3,2,1,0:T(8,128)S(1)}, f32[4,32,512]{2,1,0:T(8,128)S(1)}, f32[8,128]{1,0:T(8,128)S(1)}) custom-call(s32[4]{0:T(128)S(1)} %pad_add_fusion.where, f32[8,32,512]{2,1,0:T(8,128)S(1)} %bitcast.12, f32[3,8,32,512]{3,2,1,0:T(8,128)S(1)} %copy-done, f32[8,32,512]{2,1,0:T(8,128)S(1)} %copy-done.1, ...), custom_call_target="tpu_custom_call" | custom-call | flops 1 | bytes 1 | tf_op jit(solution)/shard_map/inner_last/pallas_call | solution.py:32
  28.6 0.5 collective-permute-done.7.halo
  29.2 1.9 %wedge_last.1 = (f32[4,32,512]{2,1,0:T(8,128)S(1)}, f32[16,2,8,128]{3,2,1,0:T(8,128)S(1)}, f32[2,8,128]{2,1,0:T(8,128)S(1)}) custom-call(s32[4]{0:T(128)S(1)} %pad_add_fusion.where, f32[8,32,512]{2,1,0:T(8,128)S(1)} %bitcast.13, f32[3,8,32,512]{3,2,1,0:T(8,128)S(1)} %copy-done, f32[8,32,512]{2,1,0:T(8,128)S(1)} %copy-done.1, ...), custom_call_target="tpu_custom_call" | custom-call | flops 1 | bytes 1 | tf_op jit(solution)/shard_map/wedge_last/pallas_call | solution.py:32
  31.1 11.9 %all_to_all.10.own = f32[16,2,8,128]{3,2,1,0:T(8,128)S(1)} all-to-all(f32[16,2,8,128]{3,2,1,0:T(8,128)S(1)} %get-tuple-element.46), channel_id=1, replica_groups=mesh['group'=8,'place'=8,'chip'=2,'core'=2] {'group','chip'}, dimensions={0} | all-to-all | bytes 262144 | tf_op jit(solution)/shard_map/all_to_all | solution.py:512
  43.0 1.9 %collective-permute-start.9 = (f32[16,2,8,128]{3,2,1,0:T(8,128)S(1)}, f32[16,2,8,128]{3,2,1,0:T(8,128)S(1)}, u32[]{:S(2)}, u32[]{:S(2)}) collective-permute-start(f32[16,2,8,128]{3,2,1,0:T(8,128)S(1)} %all_to_all.10.own), channel_id=1, source_target_pairs={{1,0},{0,1},{3,2},{2,3},{5,4},{4,5},{7,6},{6,7},{9,8},{8,9},{11,10... | collective-permute-start | bytes 393224 | tf_op jit(solution)/shard_map/ppermute | solution.py:480
  44.9 1.0 %collective-permute-done.9.other = f32[16,2,8,128]{3,2,1,0:T(8,128)S(1)} collective-permute-done((f32[16,2,8,128]{3,2,1,0:T(8,128)S(1)}, f32[16,2,8,128]{3,2,1,0:T(8,128)S(1)}, u32[]{:S(2)}, u32[]{:S(2)}) %collective-permute-start.9) | collective-permute-done | bytes 131104 | tf_op jit(solution)/shard_map/ppermute | solution.py:480
  45.9 6.3 %outer.1 = f32[8,8,8,128]{3,2,1,0:T(8,128)S(1)} custom-call(s32[4]{0:T(128)S(1)} %pad_add_fusion.where, f32[25,8,8,128]{3,2,1,0:T(8,128)S(1)} %get-tuple-element.41.coef, f32[16,2,8,128]{3,2,1,0:T(8,128)S(1)} %all_to_all.10.own, f32[16,2,8,128]{3,2,1,0:T(8,128)S(1)} %collective-permute-done.9.other), custom_call_target="tpu_custom_call" | custom-call | flops 1 | bytes 1 | tf_op jit(solution)/shard_map/outer/pallas_call | solution.py:32
  52.2 19.1 %all_to_all.11.terms = f32[8,8,8,128]{3,2,1,0:T(8,128)S(1)} all-to-all(f32[8,8,8,128]{3,2,1,0:T(8,128)S(1)} %outer.1), channel_id=1, replica_groups=mesh['group'=8,'place'=8,'chip'=2,'core'=2] {'place'}, dimensions={0} | all-to-all | bytes 524288 | tf_op jit(solution)/shard_map/all_to_all | solution.py:514
  71.3 2.4 %finish.1 = (f32[8,32,512]{2,1,0:T(8,128)}, f32[8,8,128]{2,1,0:T(8,128)}) custom-call(s32[4]{0:T(128)S(1)} %pad_add_fusion.where, f32[25,8,8,128]{3,2,1,0:T(8,128)S(1)} %get-tuple-element.41.coef, f32[8,8,8,128]{3,2,1,0:T(8,128)S(1)} %all_to_all.11.terms, f32[2,8,128]{2,1,0:T(8,128)S(1)} %get-tuple-element.47.coarse, ...), custom_call_target="tpu_custom_call" | custom-call | flops 1 | bytes 1 | tf_op jit(solution)/shard_map/finish/pallas_call | solution.py:32
  (18 shorter events, 0.4 us)
Async XLA Ops:
  2.7 17.2 %collective-permute-start = (f32[10,32,512]{2,1,0:T(8,128)S(1)}, f32[10,32,512]{2,1,0:T(8,128)S(1)}, u32[]{:S(2)}, u32[]{:S(2)}) collective-permute-start(f32[10,32,512]{2,1,0:T(8,128)S(1)} %get-tuple-element.27.near_part), channel_id=1, source_target_pairs={{1,2},{2,1},{5,6},{6,5},{9,10},{10,9},{13,14},{14,13},{17,18},{18,... | collective-permute-start | bytes 1966088 | tf_op jit(solution)/shard_map/ppermute | solution.py:480
  7.3 6.3 %copy-start = (f32[3,8,32,512]{3,2,1,0:T(8,128)S(1)}, f32[3,8,32,512]{3,2,1,0:T(8,128)}, u32[]{:S(2)}) copy-start(f32[3,8,32,512]{3,2,1,0:T(8,128)} %vel.13) | copy-start | bytes 4718596
  7.4 6.3 %copy-start.1 = (f32[8,32,512]{2,1,0:T(8,128)S(1)}, f32[8,32,512]{2,1,0:T(8,128)}, u32[]{:S(2)}) copy-start(f32[8,32,512]{2,1,0:T(8,128)} %upt.13) | copy-start | bytes 1572868
  7.4 6.3 %copy-start.3 = (f32[1,8,32,512]{3,2,1,0:T(8,128)S(1)}, f32[1,8,32,512]{3,2,1,0:T(8,128)}, u32[]{:S(2)}) copy-start(f32[1,8,32,512]{3,2,1,0:T(8,128)} %param.4) | copy-start | bytes 1572868
  7.4 12.5 %collective-permute-start.1 = (f32[9,32,512]{2,1,0:T(8,128)S(1)}, f32[9,32,512]{2,1,0:T(8,128)S(1)}, u32[]{:S(2)}, u32[]{:S(2)}) collective-permute-start(f32[9,32,512]{2,1,0:T(8,128)S(1)} %get-tuple-element.28), channel_id=1, source_target_pairs={{1,130},{2,129},{5,134},{6,133},{9,138},{10,137},{13,142},{14,141}... | collective-permute-start | bytes 1769480 | tf_op jit(solution)/shard_map/ppermute | solution.py:480
  13.1 4.3 %copy-start.2 = (f32[1,8,32,512]{3,2,1,0:T(8,128)S(1)}, f32[1,8,32,512]{3,2,1,0:T(8,128)}, u32[]{:S(2)}) copy-start(f32[1,8,32,512]{3,2,1,0:T(8,128)} %param.5) | copy-start | bytes 1572868
  13.1 2.7 %collective-permute-start.5 = (f32[6,32,512]{2,1,0:T(8,128)S(1)}, f32[6,32,512]{2,1,0:T(8,128)S(1)}, u32[]{:S(2)}, u32[]{:S(2)}) collective-permute-start(f32[6,32,512]{2,1,0:T(8,128)S(1)} %get-tuple-element.30), channel_id=1, source_target_pairs={{1,0},{0,1},{3,2},{2,3},{5,4},{4,5},{7,6},{6,7},{9,8},{8,9},{11,10... | collective-permute-start | bytes 1179656 | tf_op jit(solution)/shard_map/ppermute | solution.py:480
  13.2 4.2 %collective-permute-start.4 = (f32[7,32,512]{2,1,0:T(8,128)S(1)}, f32[7,32,512]{2,1,0:T(8,128)S(1)}, u32[]{:S(2)}, u32[]{:S(2)}) collective-permute-start(f32[7,32,512]{2,1,0:T(8,128)S(1)} %get-tuple-element.29.chip_part), channel_id=1, source_target_pairs={{1,0},{0,1},{3,2},{2,3},{5,4},{4,5},{7,6},{6,7},{9,8},{8,9},{11,10... | collective-permute-start | bytes 1376264 | tf_op jit(solution)/shard_map/ppermute | solution.py:480
  14.2 1.4 %collective-permute-start.2 = (f32[10,8,128]{2,1,0:T(8,128)S(1)}, f32[10,8,128]{2,1,0:T(8,128)S(1)}, u32[]{:S(2)}, u32[]{:S(2)}) collective-permute-start(f32[10,8,128]{2,1,0:T(8,128)S(1)} %restrict.1.own), channel_id=1, source_target_pairs={{1,0},{0,1},{3,2},{2,3},{5,4},{4,5},{7,6},{6,7},{9,8},{8,9},{11,10... | collective-permute-start | bytes 122888 | tf_op jit(solution)/shard_map/ppermute | solution.py:480
  15.6 1.7 %collective-permute-start.6 = (f32[6,32,512]{2,1,0:T(8,128)S(1)}, f32[6,32,512]{2,1,0:T(8,128)S(1)}, u32[]{:S(2)}, u32[]{:S(2)}) collective-permute-start(f32[6,32,512]{2,1,0:T(8,128)S(1)} %get-tuple-element.31), channel_id=1, source_target_pairs={{1,0},{0,1},{3,2},{2,3},{5,4},{4,5},{7,6},{6,7},{9,8},{8,9},{11,10... | collective-permute-start | bytes 1179656 | tf_op jit(solution)/shard_map/ppermute | solution.py:480
  15.8 4.1 %collective-permute-start.3 = (f32[20,8,128]{2,1,0:T(8,128)S(1)}, f32[20,8,128]{2,1,0:T(8,128)S(1)}, u32[]{:S(2)}, u32[]{:S(2)}) collective-permute-start(f32[20,8,128]{2,1,0:T(8,128)S(1)} %pad_maximum_fusion), channel_id=1, source_target_pairs={{2,0},{3,1},{0,2},{1,3},{6,4},{7,5},{4,6},{5,7},{10,8},{11,9},{8,1... | collective-permute-start | bytes 245768 | tf_op jit(solution)/shard_map/ppermute | solution.py:480
  19.7 6.3 %collective-permute-start.8 = (f32[4,32,512]{2,1,0:T(8,128)S(1)}, f32[4,32,512]{2,1,0:T(8,128)S(1)}, u32[]{:S(2)}, u32[]{:S(2)}) collective-permute-start(f32[4,32,512]{2,1,0:T(8,128)S(1)} %get-tuple-element.36.chip_part), channel_id=1, source_target_pairs={{1,0},{0,1},{3,2},{2,3},{5,4},{4,5},{7,6},{6,7},{9,8},{8,9},{11,10... | collective-permute-start | bytes 786440 | tf_op jit(solution)/shard_map/ppermute | solution.py:480
  21.5 7.7 %collective-permute-start.7 = (f32[4,32,512]{2,1,0:T(8,128)S(1)}, f32[4,32,512]{2,1,0:T(8,128)S(1)}, u32[]{:S(2)}, u32[]{:S(2)}) collective-permute-start(f32[4,32,512]{2,1,0:T(8,128)S(1)} %wedge_first.1.near_part), channel_id=1, source_target_pairs={{1,2},{2,1},{5,6},{6,5},{9,10},{10,9},{13,14},{14,13},{17,18},{18,... | collective-permute-start | bytes 786440 | tf_op jit(solution)/shard_map/ppermute | solution.py:480
  43.0 2.9 %collective-permute-start.9 = (f32[16,2,8,128]{3,2,1,0:T(8,128)S(1)}, f32[16,2,8,128]{3,2,1,0:T(8,128)S(1)}, u32[]{:S(2)}, u32[]{:S(2)}) collective-permute-start(f32[16,2,8,128]{3,2,1,0:T(8,128)S(1)} %all_to_all.10.own), channel_id=1, source_target_pairs={{1,0},{0,1},{3,2},{2,3},{5,4},{4,5},{7,6},{6,7},{9,8},{8,9},{11,10... | collective-permute-start | bytes 393224 | tf_op jit(solution)/shard_map/ppermute | solution.py:480

commit v8 on v6

--- a/solution.py
+++ b/solution.py
@@ -12,8 +12,10 @@
 WIDE = 4
 THIN = WIDE - 1
 DEPTH = 8
-CHIP_COUNTS = (WIDE + THIN, 2 * THIN, 2 * THIN)
-NEAR_COUNTS = (WIDE + 2 * THIN, 3 * THIN)
+CHIP_COUNTS = (7, 6, 6)
+STAIRS = 4
+KNOWN = 2
+SHARED = 3
 AXES = ("group", "place", "chip", "core")
 DIFFUSION_FINE = 0.15
 DIFFUSION_COARSE = 0.0375
@@ -41,40 +43,84 @@
     )(*args)
 
 
-def pack_kernel(to_chip, where, adj, force, vel, upt, *refs):
-    counts = CHIP_COUNTS if to_chip else NEAR_COUNTS
-    *outs, sem = refs[-1 - len(counts) :]
-    places = [out.at[i] for out, count in zip(outs, counts) for i in range(count)]
+def layer_of(odd, c):
+    return jnp.where(odd == 1, c, DEPTH - 1 - c)
+
+
+def pack_kernel(where, adj, force, vel, upt, near, near_rest, *refs):
+    chip, (edge, coefs, state, sem) = refs[: len(CHIP_COUNTS)], refs[len(CHIP_COUNTS) :]
     odd = lax.rem(where[0], 2)
-
-    def z(c):
-        return jnp.where(odd == 1, c, DEPTH - 1 - c)
-
-    sources = [adj.at[z(i if to_chip else DEPTH - WIDE + i)] for i in range(WIDE)]
-    layers = [z(i if to_chip else DEPTH - THIN + i) for i in range(THIN)]
-    for ref in (force, upt, vel.at[0], vel.at[1], vel.at[2]):
-        sources += [ref.at[c] for c in layers]
-    copies = [
-        pltpu.make_async_copy(src, dst, sem.at[i])
-        for i, (src, dst) in enumerate(zip(sources, places))
-    ]
+    sign = jnp.where(odd == 1, 1.0, -1.0)
+    copies = []
+
+    def add(src, dst):
+        copies.append(pltpu.make_async_copy(src, dst, sem.at[len(copies)]))
+
+    for i in range(WIDE):
+        add(adj.at[layer_of(odd, DEPTH - WIDE + i)], edge.at[i])
+    parts = (force, upt, vel.at[0], vel.at[1], vel.at[2])
+    for part, ref in enumerate(parts):
+        add(ref.at[layer_of(odd, DEPTH - 3)], coefs.at[part])
+        for h in range(KNOWN):
+            out, at = near_place(near, near_rest, part, h)
+            add(ref.at[layer_of(odd, DEPTH - 1 - h)], out.at[at])
+    needed = len(copies)
+    sources = [adj.at[layer_of(odd, c)] for c in range(WIDE)]
+    for ref in parts:
+        sources += [ref.at[layer_of(odd, c)] for c in range(THIN)]
+    places = [out.at[i] for out, count in zip(chip, CHIP_COUNTS) for i in range(count)]
+    for src, dst in zip(sources, places):
+        add(src, dst)
     for copy in copies:
         copy.start()
-    for copy in copies:
+    zero_pads(state)
+    for copy in copies[:needed]:
         copy.wait()
-
-
-def pack(to_chip, where, arrays, after=()):
+    for i in range(WIDE):
+        put_layer(state, 0, i, edge[i])
+    near[0] = edge[WIDE - 1]
+    near[1] = edge[WIDE - 2]
+    second = near_coefs(near, near_rest, 1)
+    put_stairs(state, (second, [(coefs, (part,)) for part in range(5)]), sign, near, 0)
+    for copy in copies[needed:]:
+        copy.wait()
+
+
+def near_place(near, near_rest, part, h):
+    at = part * KNOWN + h
+    return (near, STAIRS + at) if at < SHARED else (near_rest, at - SHARED)
+
+
+def near_coefs(near, near_rest, h):
+    places = [near_place(near, near_rest, part, h) for part in range(5)]
+    return [(ref, (at,)) for ref, at in places]
+
+
+def put_stairs(state, coefs, sign, out, first):
+    for which in range(2):
+
+        def put(block, t, value, which=which):
+            out[2 + which, pl.ds(8 * block, 8), pl.ds(128 * t, 128)] = value
+
+        layer_step(state, 0, first + WIDE - 2 - which, coefs[which], sign, put)
+
+
+def pack(where, *arrays):
     _, rows, cols = arrays[0].shape
     arrays = [pltpu.with_memory_space_constraint(x, pltpu.HBM) for x in arrays]
-    counts = CHIP_COUNTS if to_chip else NEAR_COUNTS
-    return call(
-        functools.partial(pack_kernel, to_chip),
-        "pack_chip" if to_chip else "pack_near",
+    counts = (STAIRS + SHARED, 5 * KNOWN - SHARED) + CHIP_COUNTS
+    return call(
+        pack_kernel,
+        "pack",
         tuple(f32(count, rows, cols) for count in counts),
-        [SMEM] + [HBM] * (4 + len(after)),
-        (where, *arrays, *after),
-        [pltpu.SemaphoreType.DMA((sum(counts),))],
+        [SMEM] + [HBM] * 4,
+        (where, *arrays),
+        [
+            pltpu.VMEM((WIDE, rows, cols), jnp.float32),
+            pltpu.VMEM((5, rows, cols), jnp.float32),
+            pltpu.VMEM((1, WIDE, cols // 128, rows + 16, 128), jnp.float32),
+            pltpu.SemaphoreType.DMA((WIDE + 5 * (KNOWN + 1) + sum(CHIP_COUNTS),)),
+        ],
     )
 
 
@@ -169,12 +215,19 @@
 
 
 def own_coefs(odd, force, vel, upt, c):
-    z = jnp.where(odd == 1, c, DEPTH - 1 - c)
+    z = layer_of(odd, c)
     return [(force, (z,)), (upt, (z,)), (vel, (0, z)), (vel, (1, z)), (vel, (2, z))]
 
 
-def inner_kernel(last, where, force, vel, upt, chip_part, near_part, halo, *refs):
-    chip_a, chip_b, chip_c, *refs = refs
+def chip_coefs(halo, i):
+    places = [(ref, at) for ref, count in zip(halo, CHIP_COUNTS) for at in range(count)]
+    return [(ref, (at,)) for ref, at in places[WIDE + i :: THIN]]
+
+
+def inner_kernel(last, where, force, vel, upt, *refs):
+    begin = 2 if last else 1
+    own, halo = refs[:begin], refs[begin]
+    chip, refs = refs[begin + 1 :][: len(CHIP_COUNTS)], refs[begin + 1 + len(CHIP_COUNTS) :]
     if last:
         edge, out, coarse, state, summed = refs
     else:
@@ -185,7 +238,7 @@
     for h in range(1, WIDE + 1):
         put_layer(state, 0, WIDE - h, halo[h - 1])
     for c in range(DEPTH):
-        value = chip_part[c] if c < WIDE else near_part[c - WIDE]
+        value = own[c // WIDE][c % WIDE] if last else own[0][layer_of(odd, c)]
         put_layer(state, 0, WIDE + c, value)
         if c >= DEPTH - 2:
             edge[0, c - (DEPTH - 2)] = value
@@ -194,8 +247,7 @@
         for c in range(step - WIDE, DEPTH - step):
             if c < 0:
                 i = -c - 1
-                coefs = [(chip_a, (WIDE + i,)), (chip_b, (i,)), (chip_b, (THIN + i,))]
-                coefs += [(chip_c, (i,)), (chip_c, (THIN + i,))]
+                coefs = chip_coefs(chip, i)
             else:
                 coefs = own_coefs(odd, force, vel, upt, c)
 
@@ -214,7 +266,7 @@
         coarse[...] = restrict_summed(summed)
 
 
-def inner(last, where, force, vel, upt, chip_part, near_part, halo, chip):
+def inner(last, where, force, vel, upt, own, halo, chip):
     _, rows, cols = force.shape
     outs = (f32(WIDE, 2, rows, cols), f32(WIDE, rows, cols))
     scratch = [pltpu.VMEM((2, DEPTH + WIDE, cols // 128, rows + 16, 128), jnp.float32)]
@@ -225,46 +277,52 @@
         functools.partial(inner_kernel, last),
         "inner_last" if last else "inner_first",
         outs,
-        [SMEM] + [VMEM] * 9,
-        (where, force, vel, upt, chip_part, near_part, halo, *chip),
+        [SMEM] + [VMEM] * (4 + len(own) + len(chip)),
+        (where, force, vel, upt, *own, halo, *chip),
         scratch,
     )
 
 
-def wedge_kernel(last, where, force, vel, upt, edge, halo, near, near_vel, *refs):
+def wedge_kernel(last, where, force, vel, upt, edge, halo, near, near_rest, *refs):
     if last:
         coarse_chip, stepped, out, begun, coarse, state, summed = refs
     else:
-        out, state = refs
+        out, ahead, state = refs
     slab = where[0]
     odd = lax.rem(slab, 2)
     sign = jnp.where(odd == 1, 1.0, -1.0)
     alive = jnp.where(jnp.logical_or(slab == 1, slab == 2), 1.0, 0.0)
     zero_pads(state)
-    for h in range(1, WIDE + 1):
-        put_layer(state, 0, 1 + h, halo[WIDE - h])
+    put_layer(state, 0, 2, halo[0])
+    put_layer(state, 0, 3, halo[1])
     for step in range(1, WIDE + 1):
         now, later = (step - 1) % 2, step % 2
         for i in range(2):
             put_layer(state, now, i, edge[step - 1, i])
-        for j in range(WIDE):
+        if step == 2:
+            put_layer(state, now, 4, halo[2])
+            put_layer(state, now, 5, halo[3])
+        for j in range(2 if step == 1 else WIDE):
             c = DEPTH - step + j
             if c < DEPTH:
                 coefs = own_coefs(odd, force, vel, upt, c)
             else:
-                i = THIN - 1 - (c - DEPTH)
-                coefs = [(near, (WIDE + i,)), (near, (WIDE + THIN + i,))]
-                coefs += [(near_vel, (part * THIN + i,)) for part in range(3)]
+                coefs = near_coefs(near, near_rest, c - DEPTH)
 
             def put(block, t, value, c=c, j=j, step=step, later=later):
                 if c >= DEPTH:
                     value = value * alive
                 if step == WIDE:
                     out[j, pl.ds(8 * block, 8), pl.ds(128 * t, 128)] = value
-                else:
+                if step < WIDE or not last:
                     state[later, 2 + j, t, pl.ds(8 + 8 * block, 8)] = value
 
             layer_step(state, now, 1 + j, coefs, sign, put)
+    if not last:
+        ahead[0] = out[WIDE - 1]
+        ahead[1] = out[WIDE - 2]
+        coefs = [own_coefs(odd, force, vel, upt, c) for c in (DEPTH - 2, DEPTH - 3)]
+        put_stairs(state, coefs, sign, ahead, 2)
     if last:
         put_tiles(summed, 0, (out[0] + out[1]) + (out[2] + out[3]))
         near_coarse = restrict_summed(summed)
@@ -277,9 +335,11 @@
             begun[copy] = part
 
 
-def wedge(last, where, force, vel, upt, edge, halo, near, near_vel, more=(), copies=0):
+def wedge(last, where, force, vel, upt, edge, halo, near, near_rest, more=(), copies=0):
     _, rows, cols = force.shape
     outs = (f32(WIDE, rows, cols),)
+    if not last:
+        outs += (f32(STAIRS, rows, cols),)
     scratch = [pltpu.VMEM((2, WIDE + 2, cols // 128, rows + 16, 128), jnp.float32)]
     if last:
         outs += (f32(copies, 2, rows // 4, cols // 4), f32(2, rows // 4, cols // 4))
@@ -289,7 +349,7 @@
         "wedge_last" if last else "wedge_first",
         outs,
         [SMEM] + [VMEM] * (7 + len(more)),
-        (where, force, vel, upt, edge, halo, near, near_vel) + more,
+        (where, force, vel, upt, edge, halo, near, near_rest) + more,
         scratch,
     )
 
@@ -423,7 +483,7 @@
 
 
 def finish_kernel(where, coef, own, other, coarse, chip_part, near_part, *refs):
-    corrected, coarse_new, whole, buffer, down, sem = refs
+    corrected, coarse_new, whole, down = refs
     slab, place = where[0], where[3]
     odd = lax.rem(slab, 2)
     count, depth = whole.shape[:2]
@@ -452,14 +512,9 @@
     lower, upper = fine[:rows], fine[rows:]
     chip_fine = jnp.where(odd == 1, lower, upper)
     near_fine = jnp.where(odd == 1, upper, lower)
-    copies = []
     for c in range(DEPTH):
-        buffer[c] = chip_part[c] + chip_fine if c < WIDE else near_part[c - WIDE] + near_fine
         z = jnp.where(odd == 1, c, DEPTH - 1 - c)
-        copies.append(pltpu.make_async_copy(buffer.at[c], corrected.at[z], sem.at[c]))
-        copies[c].start()
-    for copy in copies:
-        copy.wait()
+        corrected[z] = chip_part[c] + chip_fine if c < WIDE else near_part[c - WIDE] + near_fine
 
 
 def finish(where, *args):
@@ -473,11 +528,8 @@
         (where, *args),
         [
             pltpu.VMEM(args[1].shape[:1] + full, jnp.float32),
-            pltpu.VMEM((DEPTH, rows, cols), jnp.float32),
             pltpu.VMEM((2 * rows, cols // 4), jnp.float32),
-            pltpu.SemaphoreType.DMA((DEPTH,)),
         ],
-        (HBM, VMEM),
     )
 
 
@@ -504,24 +556,23 @@
         )
 
     own = (force, velocity, uptake)
-    near_pack, vel_pack = pack(False, where, (adj, *own))
+    near_pack, rest_pack, *chip_packs = pack(where, adj, *own)
     near = to_next_chip(near_pack)
-    near_vel = to_next_chip(vel_pack, times // 2)
+    near_rest = to_next_chip(rest_pack, times // 2)
     restricted = restrict_inputs(adj, velocity, uptake)
-    chip_packs = pack(True, where, (adj, *own), ())
     chip = [flipped(array, 1) for array in chip_packs]
     restricted_one = flipped(restricted, 1)
     pair = flipped(jnp.concatenate([restricted, restricted_one]), 2)
-    edge, chip_part = inner(False, where, *own, chip_packs[0], near_pack, chip[0], chip)
+    edge, chip_part = inner(False, where, *own, (adj,), chip[0], chip)
     chip_halo = flipped(chip_part, 1)
-    near, near_vel, pair, edge = lax.optimization_barrier((near, near_vel, pair, edge))
-    (near_part,) = wedge(False, where, *own, edge, near, near, near_vel)
-    near_halo = to_next_chip(near_part)
-    edge, chip_part, coarse_chip = inner(True, where, *own, chip_part, near_part, chip_halo, chip)
+    near, near_rest, pair, edge = lax.optimization_barrier((near, near_rest, pair, edge))
+    near_part, ahead = wedge(False, where, *own, edge, near, near, near_rest)
+    near_halo = to_next_chip(ahead)
+    edge, chip_part, coarse_chip = inner(True, where, *own, (chip_part, near_part), chip_halo, chip)
     coef, stepped = prepare(where, (restricted, restricted_one, pair))
     near_halo, edge, coef, stepped = lax.optimization_barrier((near_halo, edge, coef, stepped))
     near_part, begun, coarse = wedge(
-        True, where, *own, edge, near_halo, near, near_vel, (coarse_chip, stepped), groups * chips
+        True, where, *own, edge, near_halo, near, near_rest, (coarse_chip, stepped), groups * chips
     )
 
     begun = lax.all_to_all(begun, ("group", "chip"), 0, 0)

time: 74.6 us -> 73.5 us (0.985)
  waiting for transfers between devices: 4.33 us -> 6.91 us
  Pallas kernels: 23.2 us -> 21.5 us
  starting transfers between devices: 18 us -> 16.4 us
    ppermute x11, waiting for transfers between devices: 4.33 us -> 6.91 us  [send(): return lax.ppermute(array, AXES, route)]
    pallas_call x10 -> x9, Pallas kernels: 23.2 us -> 21.5 us  [call(): pl.pallas_call(kernel, out_shape=outs, in_specs=in_specs, out_specs=out_s...]
    ppermute x11, starting transfers between devices: 18 us -> 16.4 us  [send(): return lax.ppermute(array, AXES, route)]
  transfers between devices with their start and end apart: 11 -> 11, of which waited for: 5 -> 6; matrix products, arithmetic and copies ran while one was open for 0% -> 0% of each run, Pallas kernels for 14% -> 11%
where the time goes in v8:
time: 73.5 us; the launch traced here: 73.3 us
  blocking collectives  27.6 us (38%)
  Pallas kernels  21.5 us (29%)
  starting transfers between devices  16.4 us (22%)
  waiting for transfers between devices  6.91 us (9%)
  between operations  0.79 us (1%)
    pallas_call x9, Pallas kernels, call(): pl.pallas_call(kernel, out_shape=outs, in_specs=in_specs, out_specs=out_s...  21.5 us
    ppermute x11, starting transfers between devices, send(): return lax.ppermute(array, AXES, route)  16.4 us
    all_to_all x1, blocking collectives, per_device(): terms = lax.all_to_all(terms, 'place', 0, 0)  15.9 us
    all_to_all x1, blocking collectives, per_device(): begun = lax.all_to_all(begun, ('group', 'chip'), 0, 0)  11.7 us
    ppermute x11, waiting for transfers between devices, send(): return lax.ppermute(array, AXES, route)  6.91 us
  transfers between devices with their start and end apart: 11, of which 6 were waited for; matrix products, arithmetic and copies ran while one was open for 0% of the time, Pallas kernels for 11%

profile of v8, /device:TPU:1, one launch (start us, length us, event | category | flops | bytes accessed | tf_op | source)
XLA Modules:
  0.0 73.3 jit_solution(2404870821628860564)
XLA Ops:
  0.7 2.8 %pack.1 = (f32[7,32,512]{2,1,0:T(8,128)S(1)}, f32[7,32,512]{2,1,0:T(8,128)S(1)}, f32[7,32,512]{2,1,0:T(8,128)S(1)}, f32[6,32,512]{2,1,0:T(8,128)S(1)}, f32[6,32,512]{2,1,0:T(8,128)S(1)}) custom-call(s32[4]{0:T(128)S(1)} %pad_add_fusion.where, f32[8,32,512]{2,1,0:T(8,128)} %bitcast.13, f32[8,32,512]{2,1,0:T(8,128)} %bitcast.8, f32[3,8,32,512]{3,2,1,0:T(8,128)} %vel.11, ...), custom_call_target="tpu_custom_call" | custom-call | flops 1 | bytes 1 | tf_op jit(solution)/shard_map/pack/pallas_call | solution.py:34
  3.5 3.3 %collective-permute-start.5 = (f32[6,32,512]{2,1,0:T(8,128)S(1)}, f32[6,32,512]{2,1,0:T(8,128)S(1)}, u32[]{:S(2)}, u32[]{:S(2)}) collective-permute-start(f32[6,32,512]{2,1,0:T(8,128)S(1)} %get-tuple-element.32), channel_id=1, source_target_pairs={{1,0},{0,1},{3,2},{2,3},{5,4},{4,5},{7,6},{6,7},{9,8},{8,9},{11,10... | collective-permute-start | bytes 1179656 | tf_op jit(solution)/shard_map/ppermute | solution.py:547
  7.0 1.9 %collective-permute-start = (f32[7,32,512]{2,1,0:T(8,128)S(1)}, f32[7,32,512]{2,1,0:T(8,128)S(1)}, u32[]{:S(2)}, u32[]{:S(2)}) collective-permute-start(f32[7,32,512]{2,1,0:T(8,128)S(1)} %get-tuple-element.29), channel_id=1, source_target_pairs={{1,2},{2,1},{5,6},{6,5},{9,10},{10,9},{13,14},{14,13},{17,18},{18,... | collective-permute-start | bytes 1376264 | tf_op jit(solution)/shard_map/ppermute | solution.py:547
  8.9 3.6 %collective-permute-start.1 = (f32[7,32,512]{2,1,0:T(8,128)S(1)}, f32[7,32,512]{2,1,0:T(8,128)S(1)}, u32[]{:S(2)}, u32[]{:S(2)}) collective-permute-start(f32[7,32,512]{2,1,0:T(8,128)S(1)} %get-tuple-element.30), channel_id=1, source_target_pairs={{1,130},{2,129},{5,134},{6,133},{9,138},{10,137},{13,142},{14,141}... | collective-permute-start | bytes 1376264 | tf_op jit(solution)/shard_map/ppermute | solution.py:547
  12.5 0.5 restrict.1.own
  13.1 1.2 %collective-permute-done.2.one = f32[10,8,128]{2,1,0:T(8,128)S(1)} collective-permute-done((f32[10,8,128]{2,1,0:T(8,128)S(1)}, f32[10,8,128]{2,1,0:T(8,128)S(1)}, u32[]{:S(2)}, u32[]{:S(2)}) %collective-permute-start.2) | collective-permute-done | bytes 40992 | tf_op jit(solution)/shard_map/ppermute | solution.py:547
  14.5 0.7 %collective-permute-start.3 = (f32[20,8,128]{2,1,0:T(8,128)S(1)}, f32[20,8,128]{2,1,0:T(8,128)S(1)}, u32[]{:S(2)}, u32[]{:S(2)}) collective-permute-start(f32[20,8,128]{2,1,0:T(8,128)S(1)} %pad_maximum_fusion), channel_id=1, source_target_pairs={{2,0},{3,1},{0,2},{1,3},{6,4},{7,5},{4,6},{5,7},{10,8},{11,9},{8,1... | collective-permute-start | bytes 245768 | tf_op jit(solution)/shard_map/ppermute | solution.py:547
  15.3 0.8 %collective-permute-done.6.refs_4_.refs_5_ = f32[6,32,512]{2,1,0:T(8,128)S(1)} collective-permute-done((f32[6,32,512]{2,1,0:T(8,128)S(1)}, f32[6,32,512]{2,1,0:T(8,128)S(1)}, u32[]{:S(2)}, u32[]{:S(2)}) %collective-permute-start.6) | collective-permute-done | bytes 393248 | tf_op jit(solution)/shard_map/ppermute | solution.py:547
  16.1 2.4 %inner_first.1 = (f32[4,2,32,512]{3,2,1,0:T(8,128)S(1)}, f32[4,32,512]{2,1,0:T(8,128)S(1)}) custom-call(s32[4]{0:T(128)S(1)} %pad_add_fusion.where, f32[8,32,512]{2,1,0:T(8,128)S(1)} %bitcast.9, f32[3,8,32,512]{3,2,1,0:T(8,128)S(1)} %copy-done, f32[8,32,512]{2,1,0:T(8,128)S(1)} %copy-done.1, f32[8,32,512]{2,1,0:T(8,128)S(1)} %bitcast.15, ...), custom_call_target="tpu_custom_call" | custom-call | flops 1 | bytes 1 | tf_op jit(solution)/shard_map/inner_first/pallas_call | solution.py:34
  18.5 1.4 %collective-permute-done.1.near_rest = f32[7,32,512]{2,1,0:T(8,128)S(1)} collective-permute-done((f32[7,32,512]{2,1,0:T(8,128)S(1)}, f32[7,32,512]{2,1,0:T(8,128)S(1)}, u32[]{:S(2)}, u32[]{:S(2)}) %collective-permute-start.1) | collective-permute-done | bytes 458784 | tf_op jit(solution)/shard_map/ppermute | solution.py:547
  19.9 1.6 %wedge_first.1 = (f32[4,32,512]{2,1,0:T(8,128)S(1)}, f32[4,32,512]{2,1,0:T(8,128)S(1)}) custom-call(s32[4]{0:T(128)S(1)} %pad_add_fusion.where, f32[8,32,512]{2,1,0:T(8,128)S(1)} %bitcast.10, f32[3,8,32,512]{3,2,1,0:T(8,128)S(1)} %copy-done, f32[8,32,512]{2,1,0:T(8,128)S(1)} %copy-done.1, f32[4,2,32,512]{3,2,1,0:T(8,128)S(1)} %get-tuple-element.35.edge, ...), custom_call_target="tpu_custom_call" | custom-call | flops 1 | bytes 1 | tf_op jit(solution)/shard_map/wedge_first/pallas_call | solution.py:34
  21.5 2.4 %collective-permute-start.7 = (f32[4,32,512]{2,1,0:T(8,128)S(1)}, f32[4,32,512]{2,1,0:T(8,128)S(1)}, u32[]{:S(2)}, u32[]{:S(2)}) collective-permute-start(f32[4,32,512]{2,1,0:T(8,128)S(1)} %get-tuple-element.38), channel_id=1, source_target_pairs={{1,2},{2,1},{5,6},{6,5},{9,10},{10,9},{13,14},{14,13},{17,18},{18,... | collective-permute-start | bytes 786440 | tf_op jit(solution)/shard_map/ppermute | solution.py:547
  23.9 1.0 %prepare.1 = (f32[25,8,8,128]{3,2,1,0:T(8,128)S(1)}, f32[8,8,128]{2,1,0:T(8,128)S(1)}) custom-call(s32[4]{0:T(128)S(1)} %pad_add_fusion.where, f32[10,8,128]{2,1,0:T(8,128)S(1)} %restrict.1.own, f32[10,8,128]{2,1,0:T(8,128)S(1)} %collective-permute-done.2.one, f32[20,8,128]{2,1,0:T(8,128)S(1)} %collective-permute-done.3.pair), custom_call_target="tpu_custom_call" | custom-call | flops 1 | bytes 1 | tf_op jit(solution)/shard_map/prepare/pallas_call | solution.py:34
  24.9 2.7 %inner_last.1 = (f32[4,2,32,512]{3,2,1,0:T(8,128)S(1)}, f32[4,32,512]{2,1,0:T(8,128)S(1)}, f32[8,128]{1,0:T(8,128)S(1)}) custom-call(s32[4]{0:T(128)S(1)} %pad_add_fusion.where, f32[8,32,512]{2,1,0:T(8,128)S(1)} %bitcast.11, f32[3,8,32,512]{3,2,1,0:T(8,128)S(1)} %copy-done, f32[8,32,512]{2,1,0:T(8,128)S(1)} %copy-done.1, ...), custom_call_target="tpu_custom_call" | custom-call | flops 1 | bytes 1 | tf_op jit(solution)/shard_map/inner_last/pallas_call | solution.py:34
  27.6 1.5 %collective-permute-done.7.halo = f32[4,32,512]{2,1,0:T(8,128)S(1)} collective-permute-done((f32[4,32,512]{2,1,0:T(8,128)S(1)}, f32[4,32,512]{2,1,0:T(8,128)S(1)}, u32[]{:S(2)}, u32[]{:S(2)}) %collective-permute-start.7) | collective-permute-done | bytes 262176 | tf_op jit(solution)/shard_map/ppermute | solution.py:547
  29.2 1.8 %wedge_last.1 = (f32[4,32,512]{2,1,0:T(8,128)S(1)}, f32[16,2,8,128]{3,2,1,0:T(8,128)S(1)}, f32[2,8,128]{2,1,0:T(8,128)S(1)}) custom-call(s32[4]{0:T(128)S(1)} %pad_add_fusion.where, f32[8,32,512]{2,1,0:T(8,128)S(1)} %bitcast.12, f32[3,8,32,512]{3,2,1,0:T(8,128)S(1)} %copy-done, f32[8,32,512]{2,1,0:T(8,128)S(1)} %copy-done.1, ...), custom_call_target="tpu_custom_call" | custom-call | flops 1 | bytes 1 | tf_op jit(solution)/shard_map/wedge_last/pallas_call | solution.py:34
  31.0 11.7 %all_to_all.10.own = f32[16,2,8,128]{3,2,1,0:T(8,128)S(1)} all-to-all(f32[16,2,8,128]{3,2,1,0:T(8,128)S(1)} %get-tuple-element.50), channel_id=1, replica_groups=mesh['group'=8,'place'=8,'chip'=2,'core'=2] {'group','chip'}, dimensions={0} | all-to-all | bytes 262144 | tf_op jit(solution)/shard_map/all_to_all | solution.py:578
  42.7 1.9 %collective-permute-start.9 = (f32[16,2,8,128]{3,2,1,0:T(8,128)S(1)}, f32[16,2,8,128]{3,2,1,0:T(8,128)S(1)}, u32[]{:S(2)}, u32[]{:S(2)}) collective-permute-start(f32[16,2,8,128]{3,2,1,0:T(8,128)S(1)} %all_to_all.10.own), channel_id=1, source_target_pairs={{1,0},{0,1},{3,2},{2,3},{5,4},{4,5},{7,6},{6,7},{9,8},{8,9},{11,10... | collective-permute-start | bytes 393224 | tf_op jit(solution)/shard_map/ppermute | solution.py:547
  44.5 1.0 %collective-permute-done.9.other = f32[16,2,8,128]{3,2,1,0:T(8,128)S(1)} collective-permute-done((f32[16,2,8,128]{3,2,1,0:T(8,128)S(1)}, f32[16,2,8,128]{3,2,1,0:T(8,128)S(1)}, u32[]{:S(2)}, u32[]{:S(2)}) %collective-permute-start.9) | collective-permute-done | bytes 131104 | tf_op jit(solution)/shard_map/ppermute | solution.py:547
  45.5 6.3 %outer.1 = f32[8,4,8,128]{3,2,1,0:T(8,128)S(1)} custom-call(s32[4]{0:T(128)S(1)} %pad_add_fusion.where, f32[25,8,8,128]{3,2,1,0:T(8,128)S(1)} %get-tuple-element.45.coef, f32[16,2,8,128]{3,2,1,0:T(8,128)S(1)} %all_to_all.10.own, f32[16,2,8,128]{3,2,1,0:T(8,128)S(1)} %collective-permute-done.9.other), custom_call_target="tpu_custom_call" | custom-call | flops 1 | bytes 1 | tf_op jit(solution)/shard_map/outer/pallas_call | solution.py:34
  51.8 15.9 %all_to_all.11.own = f32[8,4,8,128]{3,2,1,0:T(8,128)S(1)} all-to-all(f32[8,4,8,128]{3,2,1,0:T(8,128)S(1)} %outer.1), channel_id=1, replica_groups=mesh['group'=8,'place'=8,'chip'=2,'core'=2] {'place'}, dimensions={0} | all-to-all | bytes 262144 | tf_op jit(solution)/shard_map/all_to_all | solution.py:580
  67.7 2.1 %collective-permute-start.10 = (f32[8,4,8,128]{3,2,1,0:T(8,128)S(1)}, f32[8,4,8,128]{3,2,1,0:T(8,128)S(1)}, u32[]{:S(2)}, u32[]{:S(2)}) collective-permute-start(f32[8,4,8,128]{3,2,1,0:T(8,128)S(1)} %all_to_all.11.own), channel_id=1, source_target_pairs={{1,0},{0,1},{3,2},{2,3},{5,4},{4,5},{7,6},{6,7},{9,8},{8,9},{11,10... | collective-permute-start | bytes 393224 | tf_op jit(solution)/shard_map/ppermute | solution.py:547
  69.8 1.0 %collective-permute-done.10.other = f32[8,4,8,128]{3,2,1,0:T(8,128)S(1)} collective-permute-done((f32[8,4,8,128]{3,2,1,0:T(8,128)S(1)}, f32[8,4,8,128]{3,2,1,0:T(8,128)S(1)}, u32[]{:S(2)}, u32[]{:S(2)}) %collective-permute-start.10) | collective-permute-done | bytes 131104 | tf_op jit(solution)/shard_map/ppermute | solution.py:547
  70.8 2.4 %finish.1 = (f32[8,32,512]{2,1,0:T(8,128)}, f32[8,8,128]{2,1,0:T(8,128)}) custom-call(s32[4]{0:T(128)S(1)} %pad_add_fusion.where, f32[25,8,8,128]{3,2,1,0:T(8,128)S(1)} %get-tuple-element.45.coef, f32[8,4,8,128]{3,2,1,0:T(8,128)S(1)} %all_to_all.11.own, f32[8,4,8,128]{3,2,1,0:T(8,128)S(1)} %collective-permute-done.10.other, ...), custom_call_target="tpu_custom_call" | custom-call | flops 1 | bytes 1 | tf_op jit(solution)/shard_map/finish/pallas_call | solution.py:34
  (19 shorter events, 0.5 us)
Async XLA Ops:
  0.7 11.8 %copy-start = (f32[3,8,32,512]{3,2,1,0:T(8,128)S(1)}, f32[3,8,32,512]{3,2,1,0:T(8,128)}, u32[]{:S(2)}) copy-start(f32[3,8,32,512]{3,2,1,0:T(8,128)} %vel.11) | copy-start | bytes 4718596
  0.7 11.8 %copy-start.1 = (f32[8,32,512]{2,1,0:T(8,128)S(1)}, f32[8,32,512]{2,1,0:T(8,128)}, u32[]{:S(2)}) copy-start(f32[8,32,512]{2,1,0:T(8,128)} %upt.11) | copy-start | bytes 1572868
  0.7 11.8 %copy-start.3 = (f32[1,8,32,512]{3,2,1,0:T(8,128)S(1)}, f32[1,8,32,512]{3,2,1,0:T(8,128)}, u32[]{:S(2)}) copy-start(f32[1,8,32,512]{3,2,1,0:T(8,128)} %param.4) | copy-start | bytes 1572868
  3.5 12.6 %copy-start.2 = (f32[1,8,32,512]{3,2,1,0:T(8,128)S(1)}, f32[1,8,32,512]{3,2,1,0:T(8,128)}, u32[]{:S(2)}) copy-start(f32[1,8,32,512]{3,2,1,0:T(8,128)} %param.5) | copy-start | bytes 1572868
  3.5 11.0 %collective-permute-start.5 = (f32[6,32,512]{2,1,0:T(8,128)S(1)}, f32[6,32,512]{2,1,0:T(8,128)S(1)}, u32[]{:S(2)}, u32[]{:S(2)}) collective-permute-start(f32[6,32,512]{2,1,0:T(8,128)S(1)} %get-tuple-element.32), channel_id=1, source_target_pairs={{1,0},{0,1},{3,2},{2,3},{5,4},{4,5},{7,6},{6,7},{9,8},{8,9},{11,10... | collective-permute-start | bytes 1179656 | tf_op jit(solution)/shard_map/ppermute | solution.py:547
  6.8 9.2 %collective-permute-start.4 = (f32[7,32,512]{2,1,0:T(8,128)S(1)}, f32[7,32,512]{2,1,0:T(8,128)S(1)}, u32[]{:S(2)}, u32[]{:S(2)}) collective-permute-start(f32[7,32,512]{2,1,0:T(8,128)S(1)} %get-tuple-element.31), channel_id=1, source_target_pairs={{1,0},{0,1},{3,2},{2,3},{5,4},{4,5},{7,6},{6,7},{9,8},{8,9},{11,10... | collective-permute-start | bytes 1376264 | tf_op jit(solution)/shard_map/ppermute | solution.py:547
  7.0 11.6 %collective-permute-start = (f32[7,32,512]{2,1,0:T(8,128)S(1)}, f32[7,32,512]{2,1,0:T(8,128)S(1)}, u32[]{:S(2)}, u32[]{:S(2)}) collective-permute-start(f32[7,32,512]{2,1,0:T(8,128)S(1)} %get-tuple-element.29), channel_id=1, source_target_pairs={{1,2},{2,1},{5,6},{6,5},{9,10},{10,9},{13,14},{14,13},{17,18},{18,... | collective-permute-start | bytes 1376264 | tf_op jit(solution)/shard_map/ppermute | solution.py:547
  8.9 11.0 %collective-permute-start.1 = (f32[7,32,512]{2,1,0:T(8,128)S(1)}, f32[7,32,512]{2,1,0:T(8,128)S(1)}, u32[]{:S(2)}, u32[]{:S(2)}) collective-permute-start(f32[7,32,512]{2,1,0:T(8,128)S(1)} %get-tuple-element.30), channel_id=1, source_target_pairs={{1,130},{2,129},{5,134},{6,133},{9,138},{10,137},{13,142},{14,141}... | collective-permute-start | bytes 1376264 | tf_op jit(solution)/shard_map/ppermute | solution.py:547
  13.0 1.3 %collective-permute-start.2 = (f32[10,8,128]{2,1,0:T(8,128)S(1)}, f32[10,8,128]{2,1,0:T(8,128)S(1)}, u32[]{:S(2)}, u32[]{:S(2)}) collective-permute-start(f32[10,8,128]{2,1,0:T(8,128)S(1)} %restrict.1.own), channel_id=1, source_target_pairs={{1,0},{0,1},{3,2},{2,3},{5,4},{4,5},{7,6},{6,7},{9,8},{8,9},{11,10... | collective-permute-start | bytes 122888 | tf_op jit(solution)/shard_map/ppermute | solution.py:547
  14.3 1.7 %collective-permute-start.6 = (f32[6,32,512]{2,1,0:T(8,128)S(1)}, f32[6,32,512]{2,1,0:T(8,128)S(1)}, u32[]{:S(2)}, u32[]{:S(2)}) collective-permute-start(f32[6,32,512]{2,1,0:T(8,128)S(1)} %get-tuple-element.33), channel_id=1, source_target_pairs={{1,0},{0,1},{3,2},{2,3},{5,4},{4,5},{7,6},{6,7},{9,8},{8,9},{11,10... | collective-permute-start | bytes 1179656 | tf_op jit(solution)/shard_map/ppermute | solution.py:547
  14.5 4.0 %collective-permute-start.3 = (f32[20,8,128]{2,1,0:T(8,128)S(1)}, f32[20,8,128]{2,1,0:T(8,128)S(1)}, u32[]{:S(2)}, u32[]{:S(2)}) collective-permute-start(f32[20,8,128]{2,1,0:T(8,128)S(1)} %pad_maximum_fusion), channel_id=1, source_target_pairs={{2,0},{3,1},{0,2},{1,3},{6,4},{7,5},{4,6},{5,7},{10,8},{11,9},{8,1... | collective-permute-start | bytes 245768 | tf_op jit(solution)/shard_map/ppermute | solution.py:547
  19.9 5.0 %collective-permute-start.8 = (f32[4,32,512]{2,1,0:T(8,128)S(1)}, f32[4,32,512]{2,1,0:T(8,128)S(1)}, u32[]{:S(2)}, u32[]{:S(2)}) collective-permute-start(f32[4,32,512]{2,1,0:T(8,128)S(1)} %get-tuple-element.39.refs_0_), channel_id=1, source_target_pairs={{1,0},{0,1},{3,2},{2,3},{5,4},{4,5},{7,6},{6,7},{9,8},{8,9},{11,10... | collective-permute-start | bytes 786440 | tf_op jit(solution)/shard_map/ppermute | solution.py:547
  21.5 7.7 %collective-permute-start.7 = (f32[4,32,512]{2,1,0:T(8,128)S(1)}, f32[4,32,512]{2,1,0:T(8,128)S(1)}, u32[]{:S(2)}, u32[]{:S(2)}) collective-permute-start(f32[4,32,512]{2,1,0:T(8,128)S(1)} %get-tuple-element.38), channel_id=1, source_target_pairs={{1,2},{2,1},{5,6},{6,5},{9,10},{10,9},{13,14},{14,13},{17,18},{18,... | collective-permute-start | bytes 786440 | tf_op jit(solution)/shard_map/ppermute | solution.py:547
  42.7 2.9 %collective-permute-start.9 = (f32[16,2,8,128]{3,2,1,0:T(8,128)S(1)}, f32[16,2,8,128]{3,2,1,0:T(8,128)S(1)}, u32[]{:S(2)}, u32[]{:S(2)}) collective-permute-start(f32[16,2,8,128]{3,2,1,0:T(8,128)S(1)} %all_to_all.10.own), channel_id=1, source_target_pairs={{1,0},{0,1},{3,2},{2,3},{5,4},{4,5},{7,6},{6,7},{9,8},{8,9},{11,10... | collective-permute-start | bytes 393224 | tf_op jit(solution)/shard_map/ppermute | solution.py:547
  67.7 3.1 %collective-permute-start.10 = (f32[8,4,8,128]{3,2,1,0:T(8,128)S(1)}, f32[8,4,8,128]{3,2,1,0:T(8,128)S(1)}, u32[]{:S(2)}, u32[]{:S(2)}) collective-permute-start(f32[8,4,8,128]{3,2,1,0:T(8,128)S(1)} %all_to_all.11.own), channel_id=1, source_target_pairs={{1,0},{0,1},{3,2},{2,3},{5,4},{4,5},{7,6},{6,7},{9,8},{8,9},{11,10... | collective-permute-start | bytes 393224 | tf_op jit(solution)/shard_map/ppermute | solution.py:547

commit v9 on v8

--- a/solution.py
+++ b/solution.py
@@ -12,10 +12,10 @@
 WIDE = 4
 THIN = WIDE - 1
 DEPTH = 8
-CHIP_COUNTS = (7, 6, 6)
 STAIRS = 4
 KNOWN = 2
-SHARED = 3
+CHIP_COUNTS = (5, 5, 4)
+NEAR_COUNTS = (7, 7)
 AXES = ("group", "place", "chip", "core")
 DIFFUSION_FINE = 0.15
 DIFFUSION_COARSE = 0.0375
@@ -47,71 +47,62 @@
     return jnp.where(odd == 1, c, DEPTH - 1 - c)
 
 
-def pack_kernel(where, adj, force, vel, upt, near, near_rest, *refs):
-    chip, (edge, coefs, state, sem) = refs[: len(CHIP_COUNTS)], refs[len(CHIP_COUNTS) :]
+def places_of(refs, counts):
+    return [(ref, at) for ref, count in zip(refs, counts) for at in range(count)]
+
+
+def halo_coefs(refs, counts, h):
+    places = places_of(refs, counts)[STAIRS + h :: KNOWN]
+    return [(ref, (at,)) for ref, at in places]
+
+
+def pack_kernel(to_chip, where, adj, force, vel, upt, *refs):
+    counts = CHIP_COUNTS if to_chip else NEAR_COUNTS
+    outs, (edge, coefs, state, sem) = refs[: len(counts)], refs[len(counts) :]
+    places = [ref.at[at] for ref, at in places_of(outs, counts)]
     odd = lax.rem(where[0], 2)
-    sign = jnp.where(odd == 1, 1.0, -1.0)
+    sign = jnp.where(odd == 1, 1.0, -1.0) * (1.0 if to_chip else -1.0)
+    layers = [layer_of(odd, i if to_chip else DEPTH - 1 - i) for i in range(WIDE)]
     copies = []
 
     def add(src, dst):
         copies.append(pltpu.make_async_copy(src, dst, sem.at[len(copies)]))
 
     for i in range(WIDE):
-        add(adj.at[layer_of(odd, DEPTH - WIDE + i)], edge.at[i])
-    parts = (force, upt, vel.at[0], vel.at[1], vel.at[2])
-    for part, ref in enumerate(parts):
-        add(ref.at[layer_of(odd, DEPTH - 3)], coefs.at[part])
+        add(adj.at[layers[i]], edge.at[i])
+    for part, ref in enumerate((force, upt, vel.at[0], vel.at[1], vel.at[2])):
         for h in range(KNOWN):
-            out, at = near_place(near, near_rest, part, h)
-            add(ref.at[layer_of(odd, DEPTH - 1 - h)], out.at[at])
-    needed = len(copies)
-    sources = [adj.at[layer_of(odd, c)] for c in range(WIDE)]
-    for ref in parts:
-        sources += [ref.at[layer_of(odd, c)] for c in range(THIN)]
-    places = [out.at[i] for out, count in zip(chip, CHIP_COUNTS) for i in range(count)]
-    for src, dst in zip(sources, places):
-        add(src, dst)
+            add(ref.at[layers[h]], places[STAIRS + part * KNOWN + h])
+        add(ref.at[layers[KNOWN]], coefs.at[part])
     for copy in copies:
         copy.start()
     zero_pads(state)
-    for copy in copies[:needed]:
+    for copy in copies:
         copy.wait()
     for i in range(WIDE):
         put_layer(state, 0, i, edge[i])
-    near[0] = edge[WIDE - 1]
-    near[1] = edge[WIDE - 2]
-    second = near_coefs(near, near_rest, 1)
-    put_stairs(state, (second, [(coefs, (part,)) for part in range(5)]), sign, near, 0)
-    for copy in copies[needed:]:
-        copy.wait()
-
-
-def near_place(near, near_rest, part, h):
-    at = part * KNOWN + h
-    return (near, STAIRS + at) if at < SHARED else (near_rest, at - SHARED)
-
-
-def near_coefs(near, near_rest, h):
-    places = [near_place(near, near_rest, part, h) for part in range(5)]
-    return [(ref, (at,)) for ref, at in places]
-
-
-def put_stairs(state, coefs, sign, out, first):
+    outs[0][0] = edge[0]
+    outs[0][1] = edge[1]
+    third = [(coefs, (part,)) for part in range(5)]
+    put_stairs(state, (halo_coefs(outs, counts, 1), third), sign, outs[0], (1, 2))
+
+
+def put_stairs(state, coefs, sign, out, centers):
     for which in range(2):
 
         def put(block, t, value, which=which):
             out[2 + which, pl.ds(8 * block, 8), pl.ds(128 * t, 128)] = value
 
-        layer_step(state, 0, first + WIDE - 2 - which, coefs[which], sign, put)
-
-
-def pack(where, *arrays):
+        layer_step(state, 0, centers[which], coefs[which], sign, put)
+
+
+def pack(to_chip, where, *arrays):
     _, rows, cols = arrays[0].shape
     arrays = [pltpu.with_memory_space_constraint(x, pltpu.HBM) for x in arrays]
-    counts = (STAIRS + SHARED, 5 * KNOWN - SHARED) + CHIP_COUNTS
-    return call(
-        pack_kernel,
-        "pack",
+    counts = CHIP_COUNTS if to_chip else NEAR_COUNTS
+    return call(
+        functools.partial(pack_kernel, to_chip),
+        "pack_chip" if to_chip else "pack_near",
         tuple(f32(count, rows, cols) for count in counts),
         [SMEM] + [HBM] * 4,
         (where, *arrays),
@@ -119,7 +110,7 @@
             pltpu.VMEM((WIDE, rows, cols), jnp.float32),
             pltpu.VMEM((5, rows, cols), jnp.float32),
             pltpu.VMEM((1, WIDE, cols // 128, rows + 16, 128), jnp.float32),
-            pltpu.SemaphoreType.DMA((WIDE + 5 * (KNOWN + 1) + sum(CHIP_COUNTS),)),
+            pltpu.SemaphoreType.DMA((WIDE + 5 * (KNOWN + 1),)),
         ],
     )
 
@@ -219,11 +210,6 @@
     return [(force, (z,)), (upt, (z,)), (vel, (0, z)), (vel, (1, z)), (vel, (2, z))]
 
 
-def chip_coefs(halo, i):
-    places = [(ref, at) for ref, count in zip(halo, CHIP_COUNTS) for at in range(count)]
-    return [(ref, (at,)) for ref, at in places[WIDE + i :: THIN]]
-
-
 def inner_kernel(last, where, force, vel, upt, *refs):
     begin = 2 if last else 1
     own, halo = refs[:begin], refs[begin]
@@ -231,12 +217,12 @@
     if last:
         edge, out, coarse, state, summed = refs
     else:
-        edge, out, state = refs
+        edge, out, ahead, state = refs
     odd = lax.rem(where[0], 2)
     sign = jnp.where(odd == 1, 1.0, -1.0)
     zero_pads(state)
-    for h in range(1, WIDE + 1):
-        put_layer(state, 0, WIDE - h, halo[h - 1])
+    put_layer(state, 0, WIDE - 1, halo[0])
+    put_layer(state, 0, WIDE - 2, halo[1])
     for c in range(DEPTH):
         value = own[c // WIDE][c % WIDE] if last else own[0][layer_of(odd, c)]
         put_layer(state, 0, WIDE + c, value)
@@ -244,10 +230,12 @@
             edge[0, c - (DEPTH - 2)] = value
     for step in range(1, WIDE + 1):
         now, later = (step - 1) % 2, step % 2
-        for c in range(step - WIDE, DEPTH - step):
+        if step == 2:
+            put_layer(state, now, WIDE - 2, halo[2])
+            put_layer(state, now, WIDE - 3, halo[3])
+        for c in range(-min(step, WIDE - step), DEPTH - step):
             if c < 0:
-                i = -c - 1
-                coefs = chip_coefs(chip, i)
+                coefs = halo_coefs(chip, CHIP_COUNTS, -c - 1)
             else:
                 coefs = own_coefs(odd, force, vel, upt, c)
 
@@ -255,12 +243,17 @@
                 at = (pl.ds(8 * block, 8), pl.ds(128 * t, 128))
                 if step == WIDE:
                     out[(c,) + at] = value
-                    return
-                state[later, WIDE + c, t, pl.ds(8 + 8 * block, 8)] = value
-                if c >= DEPTH - 2 - step:
+                if step < WIDE or not last:
+                    state[later, WIDE + c, t, pl.ds(8 + 8 * block, 8)] = value
+                if step < WIDE and c >= DEPTH - 2 - step:
                     edge[(step, c - (DEPTH - 2 - step)) + at] = value
 
             layer_step(state, now, WIDE + c, coefs, sign, put)
+    if not last:
+        ahead[0] = out[0]
+        ahead[1] = out[1]
+        coefs = [own_coefs(odd, force, vel, upt, c) for c in (1, 2)]
+        put_stairs(state, coefs, sign, ahead, (WIDE + 1, WIDE + 2))
     if last:
         put_tiles(summed, 0, (out[0] + out[1]) + (out[2] + out[3]))
         coarse[...] = restrict_summed(summed)
@@ -269,6 +262,8 @@
 def inner(last, where, force, vel, upt, own, halo, chip):
     _, rows, cols = force.shape
     outs = (f32(WIDE, 2, rows, cols), f32(WIDE, rows, cols))
+    if not last:
+        outs += (f32(STAIRS, rows, cols),)
     scratch = [pltpu.VMEM((2, DEPTH + WIDE, cols // 128, rows + 16, 128), jnp.float32)]
     if last:
         outs += (f32(rows // 4, cols // 4),)
@@ -307,7 +302,7 @@
             if c < DEPTH:
                 coefs = own_coefs(odd, force, vel, upt, c)
             else:
-                coefs = near_coefs(near, near_rest, c - DEPTH)
+                coefs = halo_coefs((near, near_rest), NEAR_COUNTS, c - DEPTH)
 
             def put(block, t, value, c=c, j=j, step=step, later=later):
                 if c >= DEPTH:
@@ -322,7 +317,7 @@
         ahead[0] = out[WIDE - 1]
         ahead[1] = out[WIDE - 2]
         coefs = [own_coefs(odd, force, vel, upt, c) for c in (DEPTH - 2, DEPTH - 3)]
-        put_stairs(state, coefs, sign, ahead, 2)
+        put_stairs(state, coefs, sign, ahead, (WIDE, WIDE - 1))
     if last:
         put_tiles(summed, 0, (out[0] + out[1]) + (out[2] + out[3]))
         near_coarse = restrict_summed(summed)
@@ -556,15 +551,15 @@
         )
 
     own = (force, velocity, uptake)
-    near_pack, rest_pack, *chip_packs = pack(where, adj, *own)
+    near_pack, rest_pack = pack(False, where, adj, *own)
     near = to_next_chip(near_pack)
     near_rest = to_next_chip(rest_pack, times // 2)
     restricted = restrict_inputs(adj, velocity, uptake)
-    chip = [flipped(array, 1) for array in chip_packs]
+    chip = [flipped(array, 1) for array in pack(True, where, adj, *own)]
     restricted_one = flipped(restricted, 1)
     pair = flipped(jnp.concatenate([restricted, restricted_one]), 2)
-    edge, chip_part = inner(False, where, *own, (adj,), chip[0], chip)
-    chip_halo = flipped(chip_part, 1)
+    edge, chip_part, ahead = inner(False, where, *own, (adj,), chip[0], chip)
+    chip_halo = flipped(ahead, 1)
     near, near_rest, pair, edge = lax.optimization_barrier((near, near_rest, pair, edge))
     near_part, ahead = wedge(False, where, *own, edge, near, near, near_rest)
     near_halo = to_next_chip(ahead)

time: 73.5 us -> 73.9 us (level)
  waiting for transfers between devices: 6.91 us -> 3.4 us
  Pallas kernels: 21.5 us -> 23.4 us
  starting transfers between devices: 16.4 us -> 17.9 us
    ppermute x11, waiting for transfers between devices: 6.91 us -> 3.4 us  [send(): return lax.ppermute(array, AXES, route)]
    pallas_call x9 -> x10, Pallas kernels: 21.5 us -> 23.4 us  [call(): pl.pallas_call(kernel, out_shape=outs, in_specs=in_specs, out_specs=out_s...]
    ppermute x11, starting transfers between devices: 16.4 us -> 17.9 us  [send(): return lax.ppermute(array, AXES, route)]
  transfers between devices with their start and end apart: 11 -> 11, of which waited for: 6 -> 5; matrix products, arithmetic and copies ran while one was open for 0% -> 0% of each run, Pallas kernels for 11% -> 14%
where the time goes in v9:
time: 73.9 us; the launch traced here: 73.6 us
  blocking collectives  27.9 us (38%)
  Pallas kernels  23.4 us (32%)
  starting transfers between devices  17.9 us (24%)
  waiting for transfers between devices  3.4 us (5%)
  between operations  0.81 us (1%)
    pallas_call x10, Pallas kernels, call(): pl.pallas_call(kernel, out_shape=outs, in_specs=in_specs, out_specs=out_s...  23.4 us
    ppermute x11, starting transfers between devices, send(): return lax.ppermute(array, AXES, route)  17.9 us
    all_to_all x1, blocking collectives, per_device(): terms = lax.all_to_all(terms, 'place', 0, 0)  15.9 us
    all_to_all x1, blocking collectives, per_device(): begun = lax.all_to_all(begun, ('group', 'chip'), 0, 0)  12 us
    ppermute x11, waiting for transfers between devices, send(): return lax.ppermute(array, AXES, route)  3.4 us
  transfers between devices with their start and end apart: 11, of which 5 were waited for; matrix products, arithmetic and copies ran while one was open for 0% of the time, Pallas kernels for 14%

profile of v9, /device:TPU:1, one launch (start us, length us, event | category | flops | bytes accessed | tf_op | source)
XLA Modules:
  0.0 73.6 jit_solution(14148579852127894233)
XLA Ops:
  0.7 2.4 %pack_near.1 = (f32[7,32,512]{2,1,0:T(8,128)S(1)}, f32[7,32,512]{2,1,0:T(8,128)S(1)}) custom-call(s32[4]{0:T(128)S(1)} %pad_add_fusion.where, f32[8,32,512]{2,1,0:T(8,128)} %bitcast.14, f32[8,32,512]{2,1,0:T(8,128)} %bitcast.8, f32[3,8,32,512]{3,2,1,0:T(8,128)} %vel.13, f32[8,32,512]{2,1,0:T(8,128)} %upt.13), custom_call_target="tpu_custom_call" | custom-call | flops 1 | bytes 1 | tf_op jit(solution)/shard_map/pack_near/pallas_call | solution.py:34
  3.1 4.6 %collective-permute-start = (f32[7,32,512]{2,1,0:T(8,128)S(1)}, f32[7,32,512]{2,1,0:T(8,128)S(1)}, u32[]{:S(2)}, u32[]{:S(2)}) collective-permute-start(f32[7,32,512]{2,1,0:T(8,128)S(1)} %get-tuple-element.30), channel_id=1, source_target_pairs={{1,2},{2,1},{5,6},{6,5},{9,10},{10,9},{13,14},{14,13},{17,18},{18,... | collective-permute-start | bytes 1376264 | tf_op jit(solution)/shard_map/ppermute | solution.py:542
  7.7 3.5 %collective-permute-start.1 = (f32[7,32,512]{2,1,0:T(8,128)S(1)}, f32[7,32,512]{2,1,0:T(8,128)S(1)}, u32[]{:S(2)}, u32[]{:S(2)}) collective-permute-start(f32[7,32,512]{2,1,0:T(8,128)S(1)} %get-tuple-element.31), channel_id=1, source_target_pairs={{1,130},{2,129},{5,134},{6,133},{9,138},{10,137},{13,142},{14,141}... | collective-permute-start | bytes 1376264 | tf_op jit(solution)/shard_map/ppermute | solution.py:542
  11.3 0.5 restrict.1.own
  11.9 2.4 %pack_chip.1 = (f32[5,32,512]{2,1,0:T(8,128)S(1)}, f32[5,32,512]{2,1,0:T(8,128)S(1)}, f32[4,32,512]{2,1,0:T(8,128)S(1)}) custom-call(s32[4]{0:T(128)S(1)} %pad_add_fusion.where, f32[8,32,512]{2,1,0:T(8,128)} %bitcast.15, f32[8,32,512]{2,1,0:T(8,128)} %bitcast.9, f32[3,8,32,512]{3,2,1,0:T(8,128)} %vel.13, f32[8,32,512]{2,1,0:T(8,128)} %upt.13), custom_call_target="tpu_custom_call" | custom-call | flops 1 | bytes 1 | tf_op jit(solution)/shard_map/pack_chip/pallas_call | solution.py:34
  14.4 0.3 collective-permute-start.6
  15.2 0.8 %collective-permute-done.6.refs_4_.refs_5_ = f32[4,32,512]{2,1,0:T(8,128)S(1)} collective-permute-done((f32[4,32,512]{2,1,0:T(8,128)S(1)}, f32[4,32,512]{2,1,0:T(8,128)S(1)}, u32[]{:S(2)}, u32[]{:S(2)}) %collective-permute-start.6) | collective-permute-done | bytes 262176 | tf_op jit(solution)/shard_map/ppermute | solution.py:542
  16.0 0.8 %collective-permute-start.3 = (f32[20,8,128]{2,1,0:T(8,128)S(1)}, f32[20,8,128]{2,1,0:T(8,128)S(1)}, u32[]{:S(2)}, u32[]{:S(2)}) collective-permute-start(f32[20,8,128]{2,1,0:T(8,128)S(1)} %pad_maximum_fusion), channel_id=1, source_target_pairs={{2,0},{3,1},{0,2},{1,3},{6,4},{7,5},{4,6},{5,7},{10,8},{11,9},{8,1... | collective-permute-start | bytes 245768 | tf_op jit(solution)/shard_map/ppermute | solution.py:542
  16.9 2.4 %inner_first.1 = (f32[4,2,32,512]{3,2,1,0:T(8,128)S(1)}, f32[4,32,512]{2,1,0:T(8,128)S(1)}, f32[4,32,512]{2,1,0:T(8,128)S(1)}) custom-call(s32[4]{0:T(128)S(1)} %pad_add_fusion.where, f32[8,32,512]{2,1,0:T(8,128)S(1)} %bitcast.10, f32[3,8,32,512]{3,2,1,0:T(8,128)S(1)} %copy-done.1, f32[8,32,512]{2,1,0:T(8,128)S(1)} %copy-done.3, f32[8,32,512]{2,1,0:T(8,128)S(1)} %bitcast.17, ...), custom_call_target="tpu_custom_call" | custom-call | flops 1 | bytes 1 | tf_op jit(solution)/shard_map/inner_first/pallas_call | solution.py:34
  19.4 0.5 collective-permute-start.8
  19.9 1.6 %wedge_first.1 = (f32[4,32,512]{2,1,0:T(8,128)S(1)}, f32[4,32,512]{2,1,0:T(8,128)S(1)}) custom-call(s32[4]{0:T(128)S(1)} %pad_add_fusion.where, f32[8,32,512]{2,1,0:T(8,128)S(1)} %bitcast.11, f32[3,8,32,512]{3,2,1,0:T(8,128)S(1)} %copy-done.1, f32[8,32,512]{2,1,0:T(8,128)S(1)} %copy-done.3, f32[4,2,32,512]{3,2,1,0:T(8,128)S(1)} %get-tuple-element.36.edge, ...), custom_call_target="tpu_custom_call" | custom-call | flops 1 | bytes 1 | tf_op jit(solution)/shard_map/wedge_first/pallas_call | solution.py:34
  21.5 3.6 %collective-permute-start.7 = (f32[4,32,512]{2,1,0:T(8,128)S(1)}, f32[4,32,512]{2,1,0:T(8,128)S(1)}, u32[]{:S(2)}, u32[]{:S(2)}) collective-permute-start(f32[4,32,512]{2,1,0:T(8,128)S(1)} %get-tuple-element.39), channel_id=1, source_target_pairs={{1,2},{2,1},{5,6},{6,5},{9,10},{10,9},{13,14},{14,13},{17,18},{18,... | collective-permute-start | bytes 786440 | tf_op jit(solution)/shard_map/ppermute | solution.py:542
  25.1 1.0 %prepare.1 = (f32[25,8,8,128]{3,2,1,0:T(8,128)S(1)}, f32[8,8,128]{2,1,0:T(8,128)S(1)}) custom-call(s32[4]{0:T(128)S(1)} %pad_add_fusion.where, f32[10,8,128]{2,1,0:T(8,128)S(1)} %restrict.1.own, f32[10,8,128]{2,1,0:T(8,128)S(1)} %collective-permute-done.2.one, f32[20,8,128]{2,1,0:T(8,128)S(1)} %collective-permute-done.3.pair), custom_call_target="tpu_custom_call" | custom-call | flops 1 | bytes 1 | tf_op jit(solution)/shard_map/prepare/pallas_call | solution.py:34
  26.1 2.6 %inner_last.1 = (f32[4,2,32,512]{3,2,1,0:T(8,128)S(1)}, f32[4,32,512]{2,1,0:T(8,128)S(1)}, f32[8,128]{1,0:T(8,128)S(1)}) custom-call(s32[4]{0:T(128)S(1)} %pad_add_fusion.where, f32[8,32,512]{2,1,0:T(8,128)S(1)} %bitcast.12, f32[3,8,32,512]{3,2,1,0:T(8,128)S(1)} %copy-done.1, f32[8,32,512]{2,1,0:T(8,128)S(1)} %copy-done.3, ...), custom_call_target="tpu_custom_call" | custom-call | flops 1 | bytes 1 | tf_op jit(solution)/shard_map/inner_last/pallas_call | solution.py:34
  28.7 0.5 collective-permute-done.7.halo
  29.2 1.8 %wedge_last.1 = (f32[4,32,512]{2,1,0:T(8,128)S(1)}, f32[16,2,8,128]{3,2,1,0:T(8,128)S(1)}, f32[2,8,128]{2,1,0:T(8,128)S(1)}) custom-call(s32[4]{0:T(128)S(1)} %pad_add_fusion.where, f32[8,32,512]{2,1,0:T(8,128)S(1)} %bitcast.13, f32[3,8,32,512]{3,2,1,0:T(8,128)S(1)} %copy-done.1, f32[8,32,512]{2,1,0:T(8,128)S(1)} %copy-done.3, ...), custom_call_target="tpu_custom_call" | custom-call | flops 1 | bytes 1 | tf_op jit(solution)/shard_map/wedge_last/pallas_call | solution.py:34
  31.0 12.0 %all_to_all.10.own = f32[16,2,8,128]{3,2,1,0:T(8,128)S(1)} all-to-all(f32[16,2,8,128]{3,2,1,0:T(8,128)S(1)} %get-tuple-element.52), channel_id=1, replica_groups=mesh['group'=8,'place'=8,'chip'=2,'core'=2] {'group','chip'}, dimensions={0} | all-to-all | bytes 262144 | tf_op jit(solution)/shard_map/all_to_all | solution.py:573
  43.0 1.9 %collective-permute-start.9 = (f32[16,2,8,128]{3,2,1,0:T(8,128)S(1)}, f32[16,2,8,128]{3,2,1,0:T(8,128)S(1)}, u32[]{:S(2)}, u32[]{:S(2)}) collective-permute-start(f32[16,2,8,128]{3,2,1,0:T(8,128)S(1)} %all_to_all.10.own), channel_id=1, source_target_pairs={{1,0},{0,1},{3,2},{2,3},{5,4},{4,5},{7,6},{6,7},{9,8},{8,9},{11,10... | collective-permute-start | bytes 393224 | tf_op jit(solution)/shard_map/ppermute | solution.py:542
  44.9 1.0 %collective-permute-done.9.other = f32[16,2,8,128]{3,2,1,0:T(8,128)S(1)} collective-permute-done((f32[16,2,8,128]{3,2,1,0:T(8,128)S(1)}, f32[16,2,8,128]{3,2,1,0:T(8,128)S(1)}, u32[]{:S(2)}, u32[]{:S(2)}) %collective-permute-start.9) | collective-permute-done | bytes 131104 | tf_op jit(solution)/shard_map/ppermute | solution.py:542
  45.8 6.3 %outer.1 = f32[8,4,8,128]{3,2,1,0:T(8,128)S(1)} custom-call(s32[4]{0:T(128)S(1)} %pad_add_fusion.where, f32[25,8,8,128]{3,2,1,0:T(8,128)S(1)} %get-tuple-element.47.coef, f32[16,2,8,128]{3,2,1,0:T(8,128)S(1)} %all_to_all.10.own, f32[16,2,8,128]{3,2,1,0:T(8,128)S(1)} %collective-permute-done.9.other), custom_call_target="tpu_custom_call" | custom-call | flops 1 | bytes 1 | tf_op jit(solution)/shard_map/outer/pallas_call | solution.py:34
  52.1 15.9 %all_to_all.11.own = f32[8,4,8,128]{3,2,1,0:T(8,128)S(1)} all-to-all(f32[8,4,8,128]{3,2,1,0:T(8,128)S(1)} %outer.1), channel_id=1, replica_groups=mesh['group'=8,'place'=8,'chip'=2,'core'=2] {'place'}, dimensions={0} | all-to-all | bytes 262144 | tf_op jit(solution)/shard_map/all_to_all | solution.py:575
  68.0 2.1 %collective-permute-start.10 = (f32[8,4,8,128]{3,2,1,0:T(8,128)S(1)}, f32[8,4,8,128]{3,2,1,0:T(8,128)S(1)}, u32[]{:S(2)}, u32[]{:S(2)}) collective-permute-start(f32[8,4,8,128]{3,2,1,0:T(8,128)S(1)} %all_to_all.11.own), channel_id=1, source_target_pairs={{1,0},{0,1},{3,2},{2,3},{5,4},{4,5},{7,6},{6,7},{9,8},{8,9},{11,10... | collective-permute-start | bytes 393224 | tf_op jit(solution)/shard_map/ppermute | solution.py:542
  70.2 1.0 %collective-permute-done.10.other = f32[8,4,8,128]{3,2,1,0:T(8,128)S(1)} collective-permute-done((f32[8,4,8,128]{3,2,1,0:T(8,128)S(1)}, f32[8,4,8,128]{3,2,1,0:T(8,128)S(1)}, u32[]{:S(2)}, u32[]{:S(2)}) %collective-permute-start.10) | collective-permute-done | bytes 131104 | tf_op jit(solution)/shard_map/ppermute | solution.py:542
  71.1 2.4 %finish.1 = (f32[8,32,512]{2,1,0:T(8,128)}, f32[8,8,128]{2,1,0:T(8,128)}) custom-call(s32[4]{0:T(128)S(1)} %pad_add_fusion.where, f32[25,8,8,128]{3,2,1,0:T(8,128)S(1)} %get-tuple-element.47.coef, f32[8,4,8,128]{3,2,1,0:T(8,128)S(1)} %all_to_all.11.own, f32[8,4,8,128]{3,2,1,0:T(8,128)S(1)} %collective-permute-done.10.other, ...), custom_call_target="tpu_custom_call" | custom-call | flops 1 | bytes 1 | tf_op jit(solution)/shard_map/finish/pallas_call | solution.py:34
  (26 shorter events, 0.9 us)
Async XLA Ops:
  0.7 10.6 %copy-start = (f32[3,8,32,512]{3,2,1,0:T(8,128)S(1)}, f32[3,8,32,512]{3,2,1,0:T(8,128)}, u32[]{:S(2)}) copy-start(f32[3,8,32,512]{3,2,1,0:T(8,128)} %vel.13) | copy-start | bytes 4718596
  0.7 10.6 %copy-start.2 = (f32[8,32,512]{2,1,0:T(8,128)S(1)}, f32[8,32,512]{2,1,0:T(8,128)}, u32[]{:S(2)}) copy-start(f32[8,32,512]{2,1,0:T(8,128)} %upt.13) | copy-start | bytes 1572868
  0.7 10.6 %copy-start.5 = (f32[1,8,32,512]{3,2,1,0:T(8,128)S(1)}, f32[1,8,32,512]{3,2,1,0:T(8,128)}, u32[]{:S(2)}) copy-start(f32[1,8,32,512]{3,2,1,0:T(8,128)} %param.4) | copy-start | bytes 1572868
  3.1 16.8 %collective-permute-start = (f32[7,32,512]{2,1,0:T(8,128)S(1)}, f32[7,32,512]{2,1,0:T(8,128)S(1)}, u32[]{:S(2)}, u32[]{:S(2)}) collective-permute-start(f32[7,32,512]{2,1,0:T(8,128)S(1)} %get-tuple-element.30), channel_id=1, source_target_pairs={{1,2},{2,1},{5,6},{6,5},{9,10},{10,9},{13,14},{14,13},{17,18},{18,... | collective-permute-start | bytes 1376264 | tf_op jit(solution)/shard_map/ppermute | solution.py:542
  7.7 12.2 %collective-permute-start.1 = (f32[7,32,512]{2,1,0:T(8,128)S(1)}, f32[7,32,512]{2,1,0:T(8,128)S(1)}, u32[]{:S(2)}, u32[]{:S(2)}) collective-permute-start(f32[7,32,512]{2,1,0:T(8,128)S(1)} %get-tuple-element.31), channel_id=1, source_target_pairs={{1,130},{2,129},{5,134},{6,133},{9,138},{10,137},{13,142},{14,141}... | collective-permute-start | bytes 1376264 | tf_op jit(solution)/shard_map/ppermute | solution.py:542
  11.8 5.1 %copy-start.1 = (f32[3,8,32,512]{3,2,1,0:T(8,128)S(1)}, f32[3,8,32,512]{3,2,1,0:T(8,128)}, u32[]{:S(2)}) copy-start(f32[3,8,32,512]{3,2,1,0:T(8,128)} %vel.13) | copy-start | bytes 4718596
  11.8 5.1 %copy-start.3 = (f32[8,32,512]{2,1,0:T(8,128)S(1)}, f32[8,32,512]{2,1,0:T(8,128)}, u32[]{:S(2)}) copy-start(f32[8,32,512]{2,1,0:T(8,128)} %upt.13) | copy-start | bytes 1572868
  11.8 5.1 %copy-start.4 = (f32[1,8,32,512]{3,2,1,0:T(8,128)S(1)}, f32[1,8,32,512]{3,2,1,0:T(8,128)}, u32[]{:S(2)}) copy-start(f32[1,8,32,512]{3,2,1,0:T(8,128)} %param.5) | copy-start | bytes 1572868
  11.8 5.1 %copy-start.6 = (f32[1,8,32,512]{3,2,1,0:T(8,128)S(1)}, f32[1,8,32,512]{3,2,1,0:T(8,128)}, u32[]{:S(2)}) copy-start(f32[1,8,32,512]{3,2,1,0:T(8,128)} %param.4) | copy-start | bytes 1572868
  11.8 3.1 %collective-permute-start.2 = (f32[10,8,128]{2,1,0:T(8,128)S(1)}, f32[10,8,128]{2,1,0:T(8,128)S(1)}, u32[]{:S(2)}, u32[]{:S(2)}) collective-permute-start(f32[10,8,128]{2,1,0:T(8,128)S(1)} %restrict.1.own), channel_id=1, source_target_pairs={{1,0},{0,1},{3,2},{2,3},{5,4},{4,5},{7,6},{6,7},{9,8},{8,9},{11,10... | collective-permute-start | bytes 122888 | tf_op jit(solution)/shard_map/ppermute | solution.py:542
  14.4 1.6 %collective-permute-start.6 = (f32[4,32,512]{2,1,0:T(8,128)S(1)}, f32[4,32,512]{2,1,0:T(8,128)S(1)}, u32[]{:S(2)}, u32[]{:S(2)}) collective-permute-start(f32[4,32,512]{2,1,0:T(8,128)S(1)} %get-tuple-element.34), channel_id=1, source_target_pairs={{1,0},{0,1},{3,2},{2,3},{5,4},{4,5},{7,6},{6,7},{9,8},{8,9},{11,10... | collective-permute-start | bytes 786440 | tf_op jit(solution)/shard_map/ppermute | solution.py:542
  14.7 2.1 %collective-permute-start.4 = (f32[5,32,512]{2,1,0:T(8,128)S(1)}, f32[5,32,512]{2,1,0:T(8,128)S(1)}, u32[]{:S(2)}, u32[]{:S(2)}) collective-permute-start(f32[5,32,512]{2,1,0:T(8,128)S(1)} %get-tuple-element.32), channel_id=1, source_target_pairs={{1,0},{0,1},{3,2},{2,3},{5,4},{4,5},{7,6},{6,7},{9,8},{8,9},{11,10... | collective-permute-start | bytes 983048 | tf_op jit(solution)/shard_map/ppermute | solution.py:542
  15.0 2.0 %collective-permute-start.5 = (f32[5,32,512]{2,1,0:T(8,128)S(1)}, f32[5,32,512]{2,1,0:T(8,128)S(1)}, u32[]{:S(2)}, u32[]{:S(2)}) collective-permute-start(f32[5,32,512]{2,1,0:T(8,128)S(1)} %get-tuple-element.33), channel_id=1, source_target_pairs={{1,0},{0,1},{3,2},{2,3},{5,4},{4,5},{7,6},{6,7},{9,8},{8,9},{11,10... | collective-permute-start | bytes 983048 | tf_op jit(solution)/shard_map/ppermute | solution.py:542
  16.0 3.9 %collective-permute-start.3 = (f32[20,8,128]{2,1,0:T(8,128)S(1)}, f32[20,8,128]{2,1,0:T(8,128)S(1)}, u32[]{:S(2)}, u32[]{:S(2)}) collective-permute-start(f32[20,8,128]{2,1,0:T(8,128)S(1)} %pad_maximum_fusion), channel_id=1, source_target_pairs={{2,0},{3,1},{0,2},{1,3},{6,4},{7,5},{4,6},{5,7},{10,8},{11,9},{8,1... | collective-permute-start | bytes 245768 | tf_op jit(solution)/shard_map/ppermute | solution.py:542
  19.4 6.7 %collective-permute-start.8 = (f32[4,32,512]{2,1,0:T(8,128)S(1)}, f32[4,32,512]{2,1,0:T(8,128)S(1)}, u32[]{:S(2)}, u32[]{:S(2)}) collective-permute-start(f32[4,32,512]{2,1,0:T(8,128)S(1)} %get-tuple-element.42), channel_id=1, source_target_pairs={{1,0},{0,1},{3,2},{2,3},{5,4},{4,5},{7,6},{6,7},{9,8},{8,9},{11,10... | collective-permute-start | bytes 786440 | tf_op jit(solution)/shard_map/ppermute | solution.py:542
  21.5 7.7 %collective-permute-start.7 = (f32[4,32,512]{2,1,0:T(8,128)S(1)}, f32[4,32,512]{2,1,0:T(8,128)S(1)}, u32[]{:S(2)}, u32[]{:S(2)}) collective-permute-start(f32[4,32,512]{2,1,0:T(8,128)S(1)} %get-tuple-element.39), channel_id=1, source_target_pairs={{1,2},{2,1},{5,6},{6,5},{9,10},{10,9},{13,14},{14,13},{17,18},{18,... | collective-permute-start | bytes 786440 | tf_op jit(solution)/shard_map/ppermute | solution.py:542
  43.0 2.9 %collective-permute-start.9 = (f32[16,2,8,128]{3,2,1,0:T(8,128)S(1)}, f32[16,2,8,128]{3,2,1,0:T(8,128)S(1)}, u32[]{:S(2)}, u32[]{:S(2)}) collective-permute-start(f32[16,2,8,128]{3,2,1,0:T(8,128)S(1)} %all_to_all.10.own), channel_id=1, source_target_pairs={{1,0},{0,1},{3,2},{2,3},{5,4},{4,5},{7,6},{6,7},{9,8},{8,9},{11,10... | collective-permute-start | bytes 393224 | tf_op jit(solution)/shard_map/ppermute | solution.py:542
  68.0 3.1 %collective-permute-start.10 = (f32[8,4,8,128]{3,2,1,0:T(8,128)S(1)}, f32[8,4,8,128]{3,2,1,0:T(8,128)S(1)}, u32[]{:S(2)}, u32[]{:S(2)}) collective-permute-start(f32[8,4,8,128]{3,2,1,0:T(8,128)S(1)} %all_to_all.11.own), channel_id=1, source_target_pairs={{1,0},{0,1},{3,2},{2,3},{5,4},{4,5},{7,6},{6,7},{9,8},{8,9},{11,10... | collective-permute-start | bytes 393224 | tf_op jit(solution)/shard_map/ppermute | solution.py:542

commit v10 on v9

--- a/solution.py
+++ b/solution.py
@@ -56,13 +56,12 @@
     return [(ref, (at,)) for ref, at in places]
 
 
-def pack_kernel(to_chip, where, adj, force, vel, upt, *refs):
-    counts = CHIP_COUNTS if to_chip else NEAR_COUNTS
-    outs, (edge, coefs, state, sem) = refs[: len(counts)], refs[len(counts) :]
-    places = [ref.at[at] for ref, at in places_of(outs, counts)]
+def pack_near_kernel(where, adj, force, vel, upt, *refs):
+    outs, (edge, coefs, state, sem) = refs[: len(NEAR_COUNTS)], refs[len(NEAR_COUNTS) :]
+    places = [ref.at[at] for ref, at in places_of(outs, NEAR_COUNTS)]
     odd = lax.rem(where[0], 2)
-    sign = jnp.where(odd == 1, 1.0, -1.0) * (1.0 if to_chip else -1.0)
-    layers = [layer_of(odd, i if to_chip else DEPTH - 1 - i) for i in range(WIDE)]
+    sign = jnp.where(odd == 1, -1.0, 1.0)
+    layers = [layer_of(odd, DEPTH - 1 - i) for i in range(WIDE)]
     copies = []
 
     def add(src, dst):
@@ -84,7 +83,24 @@
     outs[0][0] = edge[0]
     outs[0][1] = edge[1]
     third = [(coefs, (part,)) for part in range(5)]
-    put_stairs(state, (halo_coefs(outs, counts, 1), third), sign, outs[0], (1, 2))
+    put_stairs(state, (halo_coefs(outs, NEAR_COUNTS, 1), third), sign, outs[0], (1, 2))
+
+
+def pack_chip_kernel(where, adj, force, vel, upt, *refs):
+    *outs, state = refs
+    places = places_of(outs, CHIP_COUNTS)
+    odd = lax.rem(where[0], 2)
+    sign = jnp.where(odd == 1, 1.0, -1.0)
+    zero_pads(state)
+    for c in range(WIDE):
+        put_layer(state, 0, c, adj[layer_of(odd, c)])
+    for c in range(KNOWN):
+        outs[0][c] = adj[layer_of(odd, c)]
+        for part, (src, index) in enumerate(own_coefs(odd, force, vel, upt, c)):
+            dst, at = places[STAIRS + part * KNOWN + c]
+            dst[at] = src[index]
+    coefs = [own_coefs(odd, force, vel, upt, c) for c in (1, 2)]
+    put_stairs(state, coefs, sign, outs[0], (1, 2))
 
 
 def put_stairs(state, coefs, sign, out, centers):
@@ -98,20 +114,23 @@
 
 def pack(to_chip, where, *arrays):
     _, rows, cols = arrays[0].shape
-    arrays = [pltpu.with_memory_space_constraint(x, pltpu.HBM) for x in arrays]
     counts = CHIP_COUNTS if to_chip else NEAR_COUNTS
+    scratch = [pltpu.VMEM((1, WIDE, cols // 128, rows + 16, 128), jnp.float32)]
+    if not to_chip:
+        arrays = [pltpu.with_memory_space_constraint(x, pltpu.HBM) for x in arrays]
+        scratch = [
+            pltpu.VMEM((WIDE, rows, cols), jnp.float32),
+            pltpu.VMEM((5, rows, cols), jnp.float32),
+            *scratch,
+            pltpu.SemaphoreType.DMA((WIDE + 5 * (KNOWN + 1),)),
+        ]
     return call(
-        functools.partial(pack_kernel, to_chip),
+        pack_chip_kernel if to_chip else pack_near_kernel,
         "pack_chip" if to_chip else "pack_near",
         tuple(f32(count, rows, cols) for count in counts),
-        [SMEM] + [HBM] * 4,
+        [SMEM] + [VMEM if to_chip else HBM] * 4,
         (where, *arrays),
-        [
-            pltpu.VMEM((WIDE, rows, cols), jnp.float32),
-            pltpu.VMEM((5, rows, cols), jnp.float32),
-            pltpu.VMEM((1, WIDE, cols // 128, rows + 16, 128), jnp.float32),
-            pltpu.SemaphoreType.DMA((WIDE + 5 * (KNOWN + 1),)),
-        ],
+        scratch,
     )
 
 

time: 73.9 us -> 72.5 us (0.981)
  Pallas kernels: 23.4 us -> 21.8 us
    pallas_call x10, Pallas kernels: 23.4 us -> 21.8 us  [call(): pl.pallas_call(kernel, out_shape=outs, in_specs=in_specs, out_specs=out_s...]
  transfers between devices with their start and end apart: 11 -> 11, of which waited for: 5 -> 5; matrix products, arithmetic and copies ran while one was open for 0% -> 0% of each run, Pallas kernels for 14% -> 12%
where the time goes in v10:
time: 72.5 us; the launch traced here: 72.2 us
  blocking collectives  27.6 us (38%)
  Pallas kernels  21.8 us (30%)
  starting transfers between devices  18.1 us (25%)
  waiting for transfers between devices  3.92 us (5%)
  between operations  0.78 us (1%)
    pallas_call x10, Pallas kernels, call(): pl.pallas_call(kernel, out_shape=outs, in_specs=in_specs, out_specs=out_s...  21.8 us
    ppermute x11, starting transfers between devices, send(): return lax.ppermute(array, AXES, route)  18.1 us
    all_to_all x1, blocking collectives, per_device(): terms = lax.all_to_all(terms, 'place', 0, 0)  15.9 us
    all_to_all x1, blocking collectives, per_device(): begun = lax.all_to_all(begun, ('group', 'chip'), 0, 0)  11.7 us
    ppermute x11, waiting for transfers between devices, send(): return lax.ppermute(array, AXES, route)  3.92 us
  transfers between devices with their start and end apart: 11, of which 5 were waited for; matrix products, arithmetic and copies ran while one was open for 0% of the time, Pallas kernels for 12%

profile of v10, /device:TPU:1, one launch (start us, length us, event | category | flops | bytes accessed | tf_op | source)
XLA Modules:
  0.0 72.2 jit_solution(13141727207427078573)
XLA Ops:
  0.7 2.4 %pack_near.1 = (f32[7,32,512]{2,1,0:T(8,128)S(1)}, f32[7,32,512]{2,1,0:T(8,128)S(1)}) custom-call(s32[4]{0:T(128)S(1)} %pad_add_fusion.where, f32[8,32,512]{2,1,0:T(8,128)} %bitcast.14, f32[8,32,512]{2,1,0:T(8,128)} %bitcast.8, f32[3,8,32,512]{3,2,1,0:T(8,128)} %vel.13, f32[8,32,512]{2,1,0:T(8,128)} %upt.13), custom_call_target="tpu_custom_call" | custom-call | flops 1 | bytes 1 | tf_op jit(solution)/shard_map/pack_near/pallas_call | solution.py:34
  3.1 4.7 %collective-permute-start = (f32[7,32,512]{2,1,0:T(8,128)S(1)}, f32[7,32,512]{2,1,0:T(8,128)S(1)}, u32[]{:S(2)}, u32[]{:S(2)}) collective-permute-start(f32[7,32,512]{2,1,0:T(8,128)S(1)} %get-tuple-element.30), channel_id=1, source_target_pairs={{1,2},{2,1},{5,6},{6,5},{9,10},{10,9},{13,14},{14,13},{17,18},{18,... | collective-permute-start | bytes 1376264 | tf_op jit(solution)/shard_map/ppermute | solution.py:561
  7.9 3.5 %collective-permute-start.1 = (f32[7,32,512]{2,1,0:T(8,128)S(1)}, f32[7,32,512]{2,1,0:T(8,128)S(1)}, u32[]{:S(2)}, u32[]{:S(2)}) collective-permute-start(f32[7,32,512]{2,1,0:T(8,128)S(1)} %get-tuple-element.31), channel_id=1, source_target_pairs={{1,130},{2,129},{5,134},{6,133},{9,138},{10,137},{13,142},{14,141}... | collective-permute-start | bytes 1376264 | tf_op jit(solution)/shard_map/ppermute | solution.py:561
  11.4 0.5 restrict.1.own
  12.1 0.7 %pack_chip.1 = (f32[5,32,512]{2,1,0:T(8,128)S(1)}, f32[5,32,512]{2,1,0:T(8,128)S(1)}, f32[4,32,512]{2,1,0:T(8,128)S(1)}) custom-call(s32[4]{0:T(128)S(1)} %pad_add_fusion.where, f32[8,32,512]{2,1,0:T(8,128)S(1)} %bitcast.16, f32[8,32,512]{2,1,0:T(8,128)S(1)} %bitcast.9, f32[3,8,32,512]{3,2,1,0:T(8,128)S(1)} %copy-done, f32[8,32,512]{2,1,0:T(8,128)S(1)} %copy-done.1), custom_call_target="tpu_custom_call" | custom-call | flops 1 | bytes 1 | tf_op jit(solution)/shard_map/pack_chip/pallas_call | solution.py:34
  12.8 0.6 collective-permute-start.6
  13.9 0.6 collective-permute-done.6.refs_4_.refs_5_
  14.5 0.9 %collective-permute-start.3 = (f32[20,8,128]{2,1,0:T(8,128)S(1)}, f32[20,8,128]{2,1,0:T(8,128)S(1)}, u32[]{:S(2)}, u32[]{:S(2)}) collective-permute-start(f32[20,8,128]{2,1,0:T(8,128)S(1)} %pad_maximum_fusion), channel_id=1, source_target_pairs={{2,0},{3,1},{0,2},{1,3},{6,4},{7,5},{4,6},{5,7},{10,8},{11,9},{8,1... | collective-permute-start | bytes 245768 | tf_op jit(solution)/shard_map/ppermute | solution.py:561
  15.5 2.4 %inner_first.1 = (f32[4,2,32,512]{3,2,1,0:T(8,128)S(1)}, f32[4,32,512]{2,1,0:T(8,128)S(1)}, f32[4,32,512]{2,1,0:T(8,128)S(1)}) custom-call(s32[4]{0:T(128)S(1)} %pad_add_fusion.where, f32[8,32,512]{2,1,0:T(8,128)S(1)} %bitcast.10, f32[3,8,32,512]{3,2,1,0:T(8,128)S(1)} %copy-done, f32[8,32,512]{2,1,0:T(8,128)S(1)} %copy-done.1, f32[8,32,512]{2,1,0:T(8,128)S(1)} %bitcast.17, ...), custom_call_target="tpu_custom_call" | custom-call | flops 1 | bytes 1 | tf_op jit(solution)/shard_map/inner_first/pallas_call | solution.py:34
  17.9 0.5 collective-permute-start.8
  18.9 1.6 %wedge_first.1 = (f32[4,32,512]{2,1,0:T(8,128)S(1)}, f32[4,32,512]{2,1,0:T(8,128)S(1)}) custom-call(s32[4]{0:T(128)S(1)} %pad_add_fusion.where, f32[8,32,512]{2,1,0:T(8,128)S(1)} %bitcast.11, f32[3,8,32,512]{3,2,1,0:T(8,128)S(1)} %copy-done, f32[8,32,512]{2,1,0:T(8,128)S(1)} %copy-done.1, f32[4,2,32,512]{3,2,1,0:T(8,128)S(1)} %get-tuple-element.36.edge, ...), custom_call_target="tpu_custom_call" | custom-call | flops 1 | bytes 1 | tf_op jit(solution)/shard_map/wedge_first/pallas_call | solution.py:34
  20.5 3.2 %collective-permute-start.7 = (f32[4,32,512]{2,1,0:T(8,128)S(1)}, f32[4,32,512]{2,1,0:T(8,128)S(1)}, u32[]{:S(2)}, u32[]{:S(2)}) collective-permute-start(f32[4,32,512]{2,1,0:T(8,128)S(1)} %get-tuple-element.39), channel_id=1, source_target_pairs={{1,2},{2,1},{5,6},{6,5},{9,10},{10,9},{13,14},{14,13},{17,18},{18,... | collective-permute-start | bytes 786440 | tf_op jit(solution)/shard_map/ppermute | solution.py:561
  23.7 1.0 %prepare.1 = (f32[25,8,8,128]{3,2,1,0:T(8,128)S(1)}, f32[8,8,128]{2,1,0:T(8,128)S(1)}) custom-call(s32[4]{0:T(128)S(1)} %pad_add_fusion.where, f32[10,8,128]{2,1,0:T(8,128)S(1)} %restrict.1.own, f32[10,8,128]{2,1,0:T(8,128)S(1)} %collective-permute-done.2.one, f32[20,8,128]{2,1,0:T(8,128)S(1)} %collective-permute-done.3.pair), custom_call_target="tpu_custom_call" | custom-call | flops 1 | bytes 1 | tf_op jit(solution)/shard_map/prepare/pallas_call | solution.py:34
  24.7 2.6 %inner_last.1 = (f32[4,2,32,512]{3,2,1,0:T(8,128)S(1)}, f32[4,32,512]{2,1,0:T(8,128)S(1)}, f32[8,128]{1,0:T(8,128)S(1)}) custom-call(s32[4]{0:T(128)S(1)} %pad_add_fusion.where, f32[8,32,512]{2,1,0:T(8,128)S(1)} %bitcast.12, f32[3,8,32,512]{3,2,1,0:T(8,128)S(1)} %copy-done, f32[8,32,512]{2,1,0:T(8,128)S(1)} %copy-done.1, ...), custom_call_target="tpu_custom_call" | custom-call | flops 1 | bytes 1 | tf_op jit(solution)/shard_map/inner_last/pallas_call | solution.py:34
  27.3 0.8 %collective-permute-done.7.halo = f32[4,32,512]{2,1,0:T(8,128)S(1)} collective-permute-done((f32[4,32,512]{2,1,0:T(8,128)S(1)}, f32[4,32,512]{2,1,0:T(8,128)S(1)}, u32[]{:S(2)}, u32[]{:S(2)}) %collective-permute-start.7) | collective-permute-done | bytes 262176 | tf_op jit(solution)/shard_map/ppermute | solution.py:561
  28.2 1.8 %wedge_last.1 = (f32[4,32,512]{2,1,0:T(8,128)S(1)}, f32[16,2,8,128]{3,2,1,0:T(8,128)S(1)}, f32[2,8,128]{2,1,0:T(8,128)S(1)}) custom-call(s32[4]{0:T(128)S(1)} %pad_add_fusion.where, f32[8,32,512]{2,1,0:T(8,128)S(1)} %bitcast.13, f32[3,8,32,512]{3,2,1,0:T(8,128)S(1)} %copy-done, f32[8,32,512]{2,1,0:T(8,128)S(1)} %copy-done.1, ...), custom_call_target="tpu_custom_call" | custom-call | flops 1 | bytes 1 | tf_op jit(solution)/shard_map/wedge_last/pallas_call | solution.py:34
  30.0 11.7 %all_to_all.10.own = f32[16,2,8,128]{3,2,1,0:T(8,128)S(1)} all-to-all(f32[16,2,8,128]{3,2,1,0:T(8,128)S(1)} %get-tuple-element.52), channel_id=1, replica_groups=mesh['group'=8,'place'=8,'chip'=2,'core'=2] {'group','chip'}, dimensions={0} | all-to-all | bytes 262144 | tf_op jit(solution)/shard_map/all_to_all | solution.py:592
  41.7 1.8 %collective-permute-start.9 = (f32[16,2,8,128]{3,2,1,0:T(8,128)S(1)}, f32[16,2,8,128]{3,2,1,0:T(8,128)S(1)}, u32[]{:S(2)}, u32[]{:S(2)}) collective-permute-start(f32[16,2,8,128]{3,2,1,0:T(8,128)S(1)} %all_to_all.10.own), channel_id=1, source_target_pairs={{1,0},{0,1},{3,2},{2,3},{5,4},{4,5},{7,6},{6,7},{9,8},{8,9},{11,10... | collective-permute-start | bytes 393224 | tf_op jit(solution)/shard_map/ppermute | solution.py:561
  43.5 1.0 %collective-permute-done.9.other = f32[16,2,8,128]{3,2,1,0:T(8,128)S(1)} collective-permute-done((f32[16,2,8,128]{3,2,1,0:T(8,128)S(1)}, f32[16,2,8,128]{3,2,1,0:T(8,128)S(1)}, u32[]{:S(2)}, u32[]{:S(2)}) %collective-permute-start.9) | collective-permute-done | bytes 131104 | tf_op jit(solution)/shard_map/ppermute | solution.py:561
  44.5 6.3 %outer.1 = f32[8,4,8,128]{3,2,1,0:T(8,128)S(1)} custom-call(s32[4]{0:T(128)S(1)} %pad_add_fusion.where, f32[25,8,8,128]{3,2,1,0:T(8,128)S(1)} %get-tuple-element.47.coef, f32[16,2,8,128]{3,2,1,0:T(8,128)S(1)} %all_to_all.10.own, f32[16,2,8,128]{3,2,1,0:T(8,128)S(1)} %collective-permute-done.9.other), custom_call_target="tpu_custom_call" | custom-call | flops 1 | bytes 1 | tf_op jit(solution)/shard_map/outer/pallas_call | solution.py:34
  50.8 15.9 %all_to_all.11.own = f32[8,4,8,128]{3,2,1,0:T(8,128)S(1)} all-to-all(f32[8,4,8,128]{3,2,1,0:T(8,128)S(1)} %outer.1), channel_id=1, replica_groups=mesh['group'=8,'place'=8,'chip'=2,'core'=2] {'place'}, dimensions={0} | all-to-all | bytes 262144 | tf_op jit(solution)/shard_map/all_to_all | solution.py:594
  66.7 2.1 %collective-permute-start.10 = (f32[8,4,8,128]{3,2,1,0:T(8,128)S(1)}, f32[8,4,8,128]{3,2,1,0:T(8,128)S(1)}, u32[]{:S(2)}, u32[]{:S(2)}) collective-permute-start(f32[8,4,8,128]{3,2,1,0:T(8,128)S(1)} %all_to_all.11.own), channel_id=1, source_target_pairs={{1,0},{0,1},{3,2},{2,3},{5,4},{4,5},{7,6},{6,7},{9,8},{8,9},{11,10... | collective-permute-start | bytes 393224 | tf_op jit(solution)/shard_map/ppermute | solution.py:561
  68.8 1.0 %collective-permute-done.10.other = f32[8,4,8,128]{3,2,1,0:T(8,128)S(1)} collective-permute-done((f32[8,4,8,128]{3,2,1,0:T(8,128)S(1)}, f32[8,4,8,128]{3,2,1,0:T(8,128)S(1)}, u32[]{:S(2)}, u32[]{:S(2)}) %collective-permute-start.10) | collective-permute-done | bytes 131104 | tf_op jit(solution)/shard_map/ppermute | solution.py:561
  69.8 2.4 %finish.1 = (f32[8,32,512]{2,1,0:T(8,128)}, f32[8,8,128]{2,1,0:T(8,128)}) custom-call(s32[4]{0:T(128)S(1)} %pad_add_fusion.where, f32[25,8,8,128]{3,2,1,0:T(8,128)S(1)} %get-tuple-element.47.coef, f32[8,4,8,128]{3,2,1,0:T(8,128)S(1)} %all_to_all.11.own, f32[8,4,8,128]{3,2,1,0:T(8,128)S(1)} %collective-permute-done.10.other, ...), custom_call_target="tpu_custom_call" | custom-call | flops 1 | bytes 1 | tf_op jit(solution)/shard_map/finish/pallas_call | solution.py:34
  (20 shorter events, 1.2 us)
Async XLA Ops:
  0.7 10.7 %copy-start = (f32[3,8,32,512]{3,2,1,0:T(8,128)S(1)}, f32[3,8,32,512]{3,2,1,0:T(8,128)}, u32[]{:S(2)}) copy-start(f32[3,8,32,512]{3,2,1,0:T(8,128)} %vel.13) | copy-start | bytes 4718596
  0.7 10.7 %copy-start.1 = (f32[8,32,512]{2,1,0:T(8,128)S(1)}, f32[8,32,512]{2,1,0:T(8,128)}, u32[]{:S(2)}) copy-start(f32[8,32,512]{2,1,0:T(8,128)} %upt.13) | copy-start | bytes 1572868
  0.7 10.7 %copy-start.3 = (f32[1,8,32,512]{3,2,1,0:T(8,128)S(1)}, f32[1,8,32,512]{3,2,1,0:T(8,128)}, u32[]{:S(2)}) copy-start(f32[1,8,32,512]{3,2,1,0:T(8,128)} %param.4) | copy-start | bytes 1572868
  3.1 8.9 %copy-start.2 = (f32[1,8,32,512]{3,2,1,0:T(8,128)S(1)}, f32[1,8,32,512]{3,2,1,0:T(8,128)}, u32[]{:S(2)}) copy-start(f32[1,8,32,512]{3,2,1,0:T(8,128)} %param.5) | copy-start | bytes 1572868
  3.1 15.3 %collective-permute-start = (f32[7,32,512]{2,1,0:T(8,128)S(1)}, f32[7,32,512]{2,1,0:T(8,128)S(1)}, u32[]{:S(2)}, u32[]{:S(2)}) collective-permute-start(f32[7,32,512]{2,1,0:T(8,128)S(1)} %get-tuple-element.30), channel_id=1, source_target_pairs={{1,2},{2,1},{5,6},{6,5},{9,10},{10,9},{13,14},{14,13},{17,18},{18,... | collective-permute-start | bytes 1376264 | tf_op jit(solution)/shard_map/ppermute | solution.py:561
  7.9 11.0 %collective-permute-start.1 = (f32[7,32,512]{2,1,0:T(8,128)S(1)}, f32[7,32,512]{2,1,0:T(8,128)S(1)}, u32[]{:S(2)}, u32[]{:S(2)}) collective-permute-start(f32[7,32,512]{2,1,0:T(8,128)S(1)} %get-tuple-element.31), channel_id=1, source_target_pairs={{1,130},{2,129},{5,134},{6,133},{9,138},{10,137},{13,142},{14,141}... | collective-permute-start | bytes 1376264 | tf_op jit(solution)/shard_map/ppermute | solution.py:561
  11.9 1.5 %collective-permute-start.2 = (f32[10,8,128]{2,1,0:T(8,128)S(1)}, f32[10,8,128]{2,1,0:T(8,128)S(1)}, u32[]{:S(2)}, u32[]{:S(2)}) collective-permute-start(f32[10,8,128]{2,1,0:T(8,128)S(1)} %restrict.1.own), channel_id=1, source_target_pairs={{1,0},{0,1},{3,2},{2,3},{5,4},{4,5},{7,6},{6,7},{9,8},{8,9},{11,10... | collective-permute-start | bytes 122888 | tf_op jit(solution)/shard_map/ppermute | solution.py:561
  12.8 1.7 %collective-permute-start.6 = (f32[4,32,512]{2,1,0:T(8,128)S(1)}, f32[4,32,512]{2,1,0:T(8,128)S(1)}, u32[]{:S(2)}, u32[]{:S(2)}) collective-permute-start(f32[4,32,512]{2,1,0:T(8,128)S(1)} %get-tuple-element.34), channel_id=1, source_target_pairs={{1,0},{0,1},{3,2},{2,3},{5,4},{4,5},{7,6},{6,7},{9,8},{8,9},{11,10... | collective-permute-start | bytes 786440 | tf_op jit(solution)/shard_map/ppermute | solution.py:561
  13.4 2.1 %collective-permute-start.4 = (f32[5,32,512]{2,1,0:T(8,128)S(1)}, f32[5,32,512]{2,1,0:T(8,128)S(1)}, u32[]{:S(2)}, u32[]{:S(2)}) collective-permute-start(f32[5,32,512]{2,1,0:T(8,128)S(1)} %get-tuple-element.32), channel_id=1, source_target_pairs={{1,0},{0,1},{3,2},{2,3},{5,4},{4,5},{7,6},{6,7},{9,8},{8,9},{11,10... | collective-permute-start | bytes 983048 | tf_op jit(solution)/shard_map/ppermute | solution.py:561
  13.5 2.0 %collective-permute-start.5 = (f32[5,32,512]{2,1,0:T(8,128)S(1)}, f32[5,32,512]{2,1,0:T(8,128)S(1)}, u32[]{:S(2)}, u32[]{:S(2)}) collective-permute-start(f32[5,32,512]{2,1,0:T(8,128)S(1)} %get-tuple-element.33), channel_id=1, source_target_pairs={{1,0},{0,1},{3,2},{2,3},{5,4},{4,5},{7,6},{6,7},{9,8},{8,9},{11,10... | collective-permute-start | bytes 983048 | tf_op jit(solution)/shard_map/ppermute | solution.py:561
  14.5 3.9 %collective-permute-start.3 = (f32[20,8,128]{2,1,0:T(8,128)S(1)}, f32[20,8,128]{2,1,0:T(8,128)S(1)}, u32[]{:S(2)}, u32[]{:S(2)}) collective-permute-start(f32[20,8,128]{2,1,0:T(8,128)S(1)} %pad_maximum_fusion), channel_id=1, source_target_pairs={{2,0},{3,1},{0,2},{1,3},{6,4},{7,5},{4,6},{5,7},{10,8},{11,9},{8,1... | collective-permute-start | bytes 245768 | tf_op jit(solution)/shard_map/ppermute | solution.py:561
  17.9 6.8 %collective-permute-start.8 = (f32[4,32,512]{2,1,0:T(8,128)S(1)}, f32[4,32,512]{2,1,0:T(8,128)S(1)}, u32[]{:S(2)}, u32[]{:S(2)}) collective-permute-start(f32[4,32,512]{2,1,0:T(8,128)S(1)} %get-tuple-element.42), channel_id=1, source_target_pairs={{1,0},{0,1},{3,2},{2,3},{5,4},{4,5},{7,6},{6,7},{9,8},{8,9},{11,10... | collective-permute-start | bytes 786440 | tf_op jit(solution)/shard_map/ppermute | solution.py:561
  20.5 7.7 %collective-permute-start.7 = (f32[4,32,512]{2,1,0:T(8,128)S(1)}, f32[4,32,512]{2,1,0:T(8,128)S(1)}, u32[]{:S(2)}, u32[]{:S(2)}) collective-permute-start(f32[4,32,512]{2,1,0:T(8,128)S(1)} %get-tuple-element.39), channel_id=1, source_target_pairs={{1,2},{2,1},{5,6},{6,5},{9,10},{10,9},{13,14},{14,13},{17,18},{18,... | collective-permute-start | bytes 786440 | tf_op jit(solution)/shard_map/ppermute | solution.py:561
  41.7 2.8 %collective-permute-start.9 = (f32[16,2,8,128]{3,2,1,0:T(8,128)S(1)}, f32[16,2,8,128]{3,2,1,0:T(8,128)S(1)}, u32[]{:S(2)}, u32[]{:S(2)}) collective-permute-start(f32[16,2,8,128]{3,2,1,0:T(8,128)S(1)} %all_to_all.10.own), channel_id=1, source_target_pairs={{1,0},{0,1},{3,2},{2,3},{5,4},{4,5},{7,6},{6,7},{9,8},{8,9},{11,10... | collective-permute-start | bytes 393224 | tf_op jit(solution)/shard_map/ppermute | solution.py:561
  66.7 3.1 %collective-permute-start.10 = (f32[8,4,8,128]{3,2,1,0:T(8,128)S(1)}, f32[8,4,8,128]{3,2,1,0:T(8,128)S(1)}, u32[]{:S(2)}, u32[]{:S(2)}) collective-permute-start(f32[8,4,8,128]{3,2,1,0:T(8,128)S(1)} %all_to_all.11.own), channel_id=1, source_target_pairs={{1,0},{0,1},{3,2},{2,3},{5,4},{4,5},{7,6},{6,7},{9,8},{8,9},{11,10... | collective-permute-start | bytes 393224 | tf_op jit(solution)/shard_map/ppermute | solution.py:561

commit v11 on v10

--- a/solution.py
+++ b/solution.py
@@ -15,7 +15,7 @@
 STAIRS = 4
 KNOWN = 2
 CHIP_COUNTS = (5, 5, 4)
-NEAR_COUNTS = (7, 7)
+NEAR_COUNTS = (8, 6)
 AXES = ("group", "place", "chip", "core")
 DIFFUSION_FINE = 0.15
 DIFFUSION_COARSE = 0.0375

time: 72.5 us -> 72.5 us (level)
  waiting for transfers between devices: 3.92 us -> 3.07 us
    ppermute x11, waiting for transfers between devices: 3.92 us -> 3.07 us  [send(): return lax.ppermute(array, AXES, route)]
  transfers between devices with their start and end apart: 11 -> 11, of which waited for: 5 -> 4; matrix products, arithmetic and copies ran while one was open for 0% -> 0% of each run, Pallas kernels for 12% -> 12%
where the time goes in v11:
time: 72.5 us; the launch traced here: 72.2 us
  blocking collectives  27.9 us (38%)
  Pallas kernels  21.7 us (30%)
  starting transfers between devices  18.6 us (26%)
  waiting for transfers between devices  3.07 us (4%)
  between operations  0.78 us (1%)
    pallas_call x10, Pallas kernels, call(): pl.pallas_call(kernel, out_shape=outs, in_specs=in_specs, out_specs=out_s...  21.7 us
    ppermute x11, starting transfers between devices, send(): return lax.ppermute(array, AXES, route)  18.6 us
    all_to_all x1, blocking collectives, per_device(): terms = lax.all_to_all(terms, 'place', 0, 0)  15.9 us
    all_to_all x1, blocking collectives, per_device(): begun = lax.all_to_all(begun, ('group', 'chip'), 0, 0)  12 us
    ppermute x11, waiting for transfers between devices, send(): return lax.ppermute(array, AXES, route)  3.07 us
  transfers between devices with their start and end apart: 11, of which 4 were waited for; matrix products, arithmetic and copies ran while one was open for 0% of the time, Pallas kernels for 12%

profile of v11, /device:TPU:1, one launch (start us, length us, event | category | flops | bytes accessed | tf_op | source)
XLA Modules:
  0.0 72.2 jit_solution(14805182257685387752)
XLA Ops:
  0.7 2.4 %pack_near.1 = (f32[8,32,512]{2,1,0:T(8,128)S(1)}, f32[6,32,512]{2,1,0:T(8,128)S(1)}) custom-call(s32[4]{0:T(128)S(1)} %pad_add_fusion.where, f32[8,32,512]{2,1,0:T(8,128)} %bitcast.14, f32[8,32,512]{2,1,0:T(8,128)} %bitcast.8, f32[3,8,32,512]{3,2,1,0:T(8,128)} %vel.13, f32[8,32,512]{2,1,0:T(8,128)} %upt.13), custom_call_target="tpu_custom_call" | custom-call | flops 1 | bytes 1 | tf_op jit(solution)/shard_map/pack_near/pallas_call | solution.py:34
  3.1 4.7 %collective-permute-start = (f32[8,32,512]{2,1,0:T(8,128)S(1)}, f32[8,32,512]{2,1,0:T(8,128)S(1)}, u32[]{:S(2)}, u32[]{:S(2)}) collective-permute-start(f32[8,32,512]{2,1,0:T(8,128)S(1)} %get-tuple-element.30), channel_id=1, source_target_pairs={{1,2},{2,1},{5,6},{6,5},{9,10},{10,9},{13,14},{14,13},{17,18},{18,... | collective-permute-start | bytes 1572872 | tf_op jit(solution)/shard_map/ppermute | solution.py:561
  7.9 3.5 %collective-permute-start.1 = (f32[6,32,512]{2,1,0:T(8,128)S(1)}, f32[6,32,512]{2,1,0:T(8,128)S(1)}, u32[]{:S(2)}, u32[]{:S(2)}) collective-permute-start(f32[6,32,512]{2,1,0:T(8,128)S(1)} %get-tuple-element.31), channel_id=1, source_target_pairs={{1,130},{2,129},{5,134},{6,133},{9,138},{10,137},{13,142},{14,141}... | collective-permute-start | bytes 1179656 | tf_op jit(solution)/shard_map/ppermute | solution.py:561
  11.4 0.5 restrict.1.own
  12.1 0.7 %pack_chip.1 = (f32[5,32,512]{2,1,0:T(8,128)S(1)}, f32[5,32,512]{2,1,0:T(8,128)S(1)}, f32[4,32,512]{2,1,0:T(8,128)S(1)}) custom-call(s32[4]{0:T(128)S(1)} %pad_add_fusion.where, f32[8,32,512]{2,1,0:T(8,128)S(1)} %bitcast.16, f32[8,32,512]{2,1,0:T(8,128)S(1)} %bitcast.9, f32[3,8,32,512]{3,2,1,0:T(8,128)S(1)} %copy-done, f32[8,32,512]{2,1,0:T(8,128)S(1)} %copy-done.1), custom_call_target="tpu_custom_call" | custom-call | flops 1 | bytes 1 | tf_op jit(solution)/shard_map/pack_chip/pallas_call | solution.py:34
  12.8 0.6 collective-permute-start.6
  13.9 0.6 collective-permute-done.6.refs_4_.refs_5_
  14.5 0.9 %collective-permute-start.3 = (f32[20,8,128]{2,1,0:T(8,128)S(1)}, f32[20,8,128]{2,1,0:T(8,128)S(1)}, u32[]{:S(2)}, u32[]{:S(2)}) collective-permute-start(f32[20,8,128]{2,1,0:T(8,128)S(1)} %pad_maximum_fusion), channel_id=1, source_target_pairs={{2,0},{3,1},{0,2},{1,3},{6,4},{7,5},{4,6},{5,7},{10,8},{11,9},{8,1... | collective-permute-start | bytes 245768 | tf_op jit(solution)/shard_map/ppermute | solution.py:561
  15.5 2.4 %inner_first.1 = (f32[4,2,32,512]{3,2,1,0:T(8,128)S(1)}, f32[4,32,512]{2,1,0:T(8,128)S(1)}, f32[4,32,512]{2,1,0:T(8,128)S(1)}) custom-call(s32[4]{0:T(128)S(1)} %pad_add_fusion.where, f32[8,32,512]{2,1,0:T(8,128)S(1)} %bitcast.10, f32[3,8,32,512]{3,2,1,0:T(8,128)S(1)} %copy-done, f32[8,32,512]{2,1,0:T(8,128)S(1)} %copy-done.1, f32[8,32,512]{2,1,0:T(8,128)S(1)} %bitcast.17, ...), custom_call_target="tpu_custom_call" | custom-call | flops 1 | bytes 1 | tf_op jit(solution)/shard_map/inner_first/pallas_call | solution.py:34
  17.9 0.5 collective-permute-start.8
  18.4 1.6 %wedge_first.1 = (f32[4,32,512]{2,1,0:T(8,128)S(1)}, f32[4,32,512]{2,1,0:T(8,128)S(1)}) custom-call(s32[4]{0:T(128)S(1)} %pad_add_fusion.where, f32[8,32,512]{2,1,0:T(8,128)S(1)} %bitcast.11, f32[3,8,32,512]{3,2,1,0:T(8,128)S(1)} %copy-done, f32[8,32,512]{2,1,0:T(8,128)S(1)} %copy-done.1, f32[4,2,32,512]{3,2,1,0:T(8,128)S(1)} %get-tuple-element.36.edge, ...), custom_call_target="tpu_custom_call" | custom-call | flops 1 | bytes 1 | tf_op jit(solution)/shard_map/wedge_first/pallas_call | solution.py:34
  20.0 3.7 %collective-permute-start.7 = (f32[4,32,512]{2,1,0:T(8,128)S(1)}, f32[4,32,512]{2,1,0:T(8,128)S(1)}, u32[]{:S(2)}, u32[]{:S(2)}) collective-permute-start(f32[4,32,512]{2,1,0:T(8,128)S(1)} %get-tuple-element.39), channel_id=1, source_target_pairs={{1,2},{2,1},{5,6},{6,5},{9,10},{10,9},{13,14},{14,13},{17,18},{18,... | collective-permute-start | bytes 786440 | tf_op jit(solution)/shard_map/ppermute | solution.py:561
  23.7 1.0 %prepare.1 = (f32[25,8,8,128]{3,2,1,0:T(8,128)S(1)}, f32[8,8,128]{2,1,0:T(8,128)S(1)}) custom-call(s32[4]{0:T(128)S(1)} %pad_add_fusion.where, f32[10,8,128]{2,1,0:T(8,128)S(1)} %restrict.1.own, f32[10,8,128]{2,1,0:T(8,128)S(1)} %collective-permute-done.2.one, f32[20,8,128]{2,1,0:T(8,128)S(1)} %collective-permute-done.3.pair), custom_call_target="tpu_custom_call" | custom-call | flops 1 | bytes 1 | tf_op jit(solution)/shard_map/prepare/pallas_call | solution.py:34
  24.7 2.6 %inner_last.1 = (f32[4,2,32,512]{3,2,1,0:T(8,128)S(1)}, f32[4,32,512]{2,1,0:T(8,128)S(1)}, f32[8,128]{1,0:T(8,128)S(1)}) custom-call(s32[4]{0:T(128)S(1)} %pad_add_fusion.where, f32[8,32,512]{2,1,0:T(8,128)S(1)} %bitcast.12, f32[3,8,32,512]{3,2,1,0:T(8,128)S(1)} %copy-done, f32[8,32,512]{2,1,0:T(8,128)S(1)} %copy-done.1, ...), custom_call_target="tpu_custom_call" | custom-call | flops 1 | bytes 1 | tf_op jit(solution)/shard_map/inner_last/pallas_call | solution.py:34
  27.3 0.4 collective-permute-done.7.halo
  27.8 1.8 %wedge_last.1 = (f32[4,32,512]{2,1,0:T(8,128)S(1)}, f32[16,2,8,128]{3,2,1,0:T(8,128)S(1)}, f32[2,8,128]{2,1,0:T(8,128)S(1)}) custom-call(s32[4]{0:T(128)S(1)} %pad_add_fusion.where, f32[8,32,512]{2,1,0:T(8,128)S(1)} %bitcast.13, f32[3,8,32,512]{3,2,1,0:T(8,128)S(1)} %copy-done, f32[8,32,512]{2,1,0:T(8,128)S(1)} %copy-done.1, ...), custom_call_target="tpu_custom_call" | custom-call | flops 1 | bytes 1 | tf_op jit(solution)/shard_map/wedge_last/pallas_call | solution.py:34
  29.6 12.0 %all_to_all.10.own = f32[16,2,8,128]{3,2,1,0:T(8,128)S(1)} all-to-all(f32[16,2,8,128]{3,2,1,0:T(8,128)S(1)} %get-tuple-element.52), channel_id=1, replica_groups=mesh['group'=8,'place'=8,'chip'=2,'core'=2] {'group','chip'}, dimensions={0} | all-to-all | bytes 262144 | tf_op jit(solution)/shard_map/all_to_all | solution.py:592
  41.6 1.9 %collective-permute-start.9 = (f32[16,2,8,128]{3,2,1,0:T(8,128)S(1)}, f32[16,2,8,128]{3,2,1,0:T(8,128)S(1)}, u32[]{:S(2)}, u32[]{:S(2)}) collective-permute-start(f32[16,2,8,128]{3,2,1,0:T(8,128)S(1)} %all_to_all.10.own), channel_id=1, source_target_pairs={{1,0},{0,1},{3,2},{2,3},{5,4},{4,5},{7,6},{6,7},{9,8},{8,9},{11,10... | collective-permute-start | bytes 393224 | tf_op jit(solution)/shard_map/ppermute | solution.py:561
  43.5 1.0 %collective-permute-done.9.other = f32[16,2,8,128]{3,2,1,0:T(8,128)S(1)} collective-permute-done((f32[16,2,8,128]{3,2,1,0:T(8,128)S(1)}, f32[16,2,8,128]{3,2,1,0:T(8,128)S(1)}, u32[]{:S(2)}, u32[]{:S(2)}) %collective-permute-start.9) | collective-permute-done | bytes 131104 | tf_op jit(solution)/shard_map/ppermute | solution.py:561
  44.5 6.3 %outer.1 = f32[8,4,8,128]{3,2,1,0:T(8,128)S(1)} custom-call(s32[4]{0:T(128)S(1)} %pad_add_fusion.where, f32[25,8,8,128]{3,2,1,0:T(8,128)S(1)} %get-tuple-element.47.coef, f32[16,2,8,128]{3,2,1,0:T(8,128)S(1)} %all_to_all.10.own, f32[16,2,8,128]{3,2,1,0:T(8,128)S(1)} %collective-permute-done.9.other), custom_call_target="tpu_custom_call" | custom-call | flops 1 | bytes 1 | tf_op jit(solution)/shard_map/outer/pallas_call | solution.py:34
  50.8 15.9 %all_to_all.11.own = f32[8,4,8,128]{3,2,1,0:T(8,128)S(1)} all-to-all(f32[8,4,8,128]{3,2,1,0:T(8,128)S(1)} %outer.1), channel_id=1, replica_groups=mesh['group'=8,'place'=8,'chip'=2,'core'=2] {'place'}, dimensions={0} | all-to-all | bytes 262144 | tf_op jit(solution)/shard_map/all_to_all | solution.py:594
  66.7 2.1 %collective-permute-start.10 = (f32[8,4,8,128]{3,2,1,0:T(8,128)S(1)}, f32[8,4,8,128]{3,2,1,0:T(8,128)S(1)}, u32[]{:S(2)}, u32[]{:S(2)}) collective-permute-start(f32[8,4,8,128]{3,2,1,0:T(8,128)S(1)} %all_to_all.11.own), channel_id=1, source_target_pairs={{1,0},{0,1},{3,2},{2,3},{5,4},{4,5},{7,6},{6,7},{9,8},{8,9},{11,10... | collective-permute-start | bytes 393224 | tf_op jit(solution)/shard_map/ppermute | solution.py:561
  68.8 1.0 %collective-permute-done.10.other = f32[8,4,8,128]{3,2,1,0:T(8,128)S(1)} collective-permute-done((f32[8,4,8,128]{3,2,1,0:T(8,128)S(1)}, f32[8,4,8,128]{3,2,1,0:T(8,128)S(1)}, u32[]{:S(2)}, u32[]{:S(2)}) %collective-permute-start.10) | collective-permute-done | bytes 131104 | tf_op jit(solution)/shard_map/ppermute | solution.py:561
  69.8 2.4 %finish.1 = (f32[8,32,512]{2,1,0:T(8,128)}, f32[8,8,128]{2,1,0:T(8,128)}) custom-call(s32[4]{0:T(128)S(1)} %pad_add_fusion.where, f32[25,8,8,128]{3,2,1,0:T(8,128)S(1)} %get-tuple-element.47.coef, f32[8,4,8,128]{3,2,1,0:T(8,128)S(1)} %all_to_all.11.own, f32[8,4,8,128]{3,2,1,0:T(8,128)S(1)} %collective-permute-done.10.other, ...), custom_call_target="tpu_custom_call" | custom-call | flops 1 | bytes 1 | tf_op jit(solution)/shard_map/finish/pallas_call | solution.py:34
  (20 shorter events, 0.7 us)
Async XLA Ops:
  0.7 10.7 %copy-start = (f32[3,8,32,512]{3,2,1,0:T(8,128)S(1)}, f32[3,8,32,512]{3,2,1,0:T(8,128)}, u32[]{:S(2)}) copy-start(f32[3,8,32,512]{3,2,1,0:T(8,128)} %vel.13) | copy-start | bytes 4718596
  0.7 10.7 %copy-start.1 = (f32[8,32,512]{2,1,0:T(8,128)S(1)}, f32[8,32,512]{2,1,0:T(8,128)}, u32[]{:S(2)}) copy-start(f32[8,32,512]{2,1,0:T(8,128)} %upt.13) | copy-start | bytes 1572868
  0.7 10.7 %copy-start.3 = (f32[1,8,32,512]{3,2,1,0:T(8,128)S(1)}, f32[1,8,32,512]{3,2,1,0:T(8,128)}, u32[]{:S(2)}) copy-start(f32[1,8,32,512]{3,2,1,0:T(8,128)} %param.4) | copy-start | bytes 1572868
  3.1 8.9 %copy-start.2 = (f32[1,8,32,512]{3,2,1,0:T(8,128)S(1)}, f32[1,8,32,512]{3,2,1,0:T(8,128)}, u32[]{:S(2)}) copy-start(f32[1,8,32,512]{3,2,1,0:T(8,128)} %param.5) | copy-start | bytes 1572868
  3.1 15.3 %collective-permute-start = (f32[8,32,512]{2,1,0:T(8,128)S(1)}, f32[8,32,512]{2,1,0:T(8,128)S(1)}, u32[]{:S(2)}, u32[]{:S(2)}) collective-permute-start(f32[8,32,512]{2,1,0:T(8,128)S(1)} %get-tuple-element.30), channel_id=1, source_target_pairs={{1,2},{2,1},{5,6},{6,5},{9,10},{10,9},{13,14},{14,13},{17,18},{18,... | collective-permute-start | bytes 1572872 | tf_op jit(solution)/shard_map/ppermute | solution.py:561
  7.9 10.6 %collective-permute-start.1 = (f32[6,32,512]{2,1,0:T(8,128)S(1)}, f32[6,32,512]{2,1,0:T(8,128)S(1)}, u32[]{:S(2)}, u32[]{:S(2)}) collective-permute-start(f32[6,32,512]{2,1,0:T(8,128)S(1)} %get-tuple-element.31), channel_id=1, source_target_pairs={{1,130},{2,129},{5,134},{6,133},{9,138},{10,137},{13,142},{14,141}... | collective-permute-start | bytes 1179656 | tf_op jit(solution)/shard_map/ppermute | solution.py:561
  11.9 1.5 %collective-permute-start.2 = (f32[10,8,128]{2,1,0:T(8,128)S(1)}, f32[10,8,128]{2,1,0:T(8,128)S(1)}, u32[]{:S(2)}, u32[]{:S(2)}) collective-permute-start(f32[10,8,128]{2,1,0:T(8,128)S(1)} %restrict.1.own), channel_id=1, source_target_pairs={{1,0},{0,1},{3,2},{2,3},{5,4},{4,5},{7,6},{6,7},{9,8},{8,9},{11,10... | collective-permute-start | bytes 122888 | tf_op jit(solution)/shard_map/ppermute | solution.py:561
  12.8 1.7 %collective-permute-start.6 = (f32[4,32,512]{2,1,0:T(8,128)S(1)}, f32[4,32,512]{2,1,0:T(8,128)S(1)}, u32[]{:S(2)}, u32[]{:S(2)}) collective-permute-start(f32[4,32,512]{2,1,0:T(8,128)S(1)} %get-tuple-element.34), channel_id=1, source_target_pairs={{1,0},{0,1},{3,2},{2,3},{5,4},{4,5},{7,6},{6,7},{9,8},{8,9},{11,10... | collective-permute-start | bytes 786440 | tf_op jit(solution)/shard_map/ppermute | solution.py:561
  13.4 2.1 %collective-permute-start.4 = (f32[5,32,512]{2,1,0:T(8,128)S(1)}, f32[5,32,512]{2,1,0:T(8,128)S(1)}, u32[]{:S(2)}, u32[]{:S(2)}) collective-permute-start(f32[5,32,512]{2,1,0:T(8,128)S(1)} %get-tuple-element.32), channel_id=1, source_target_pairs={{1,0},{0,1},{3,2},{2,3},{5,4},{4,5},{7,6},{6,7},{9,8},{8,9},{11,10... | collective-permute-start | bytes 983048 | tf_op jit(solution)/shard_map/ppermute | solution.py:561
  13.5 2.0 %collective-permute-start.5 = (f32[5,32,512]{2,1,0:T(8,128)S(1)}, f32[5,32,512]{2,1,0:T(8,128)S(1)}, u32[]{:S(2)}, u32[]{:S(2)}) collective-permute-start(f32[5,32,512]{2,1,0:T(8,128)S(1)} %get-tuple-element.33), channel_id=1, source_target_pairs={{1,0},{0,1},{3,2},{2,3},{5,4},{4,5},{7,6},{6,7},{9,8},{8,9},{11,10... | collective-permute-start | bytes 983048 | tf_op jit(solution)/shard_map/ppermute | solution.py:561
  14.5 3.9 %collective-permute-start.3 = (f32[20,8,128]{2,1,0:T(8,128)S(1)}, f32[20,8,128]{2,1,0:T(8,128)S(1)}, u32[]{:S(2)}, u32[]{:S(2)}) collective-permute-start(f32[20,8,128]{2,1,0:T(8,128)S(1)} %pad_maximum_fusion), channel_id=1, source_target_pairs={{2,0},{3,1},{0,2},{1,3},{6,4},{7,5},{4,6},{5,7},{10,8},{11,9},{8,1... | collective-permute-start | bytes 245768 | tf_op jit(solution)/shard_map/ppermute | solution.py:561
  17.9 6.8 %collective-permute-start.8 = (f32[4,32,512]{2,1,0:T(8,128)S(1)}, f32[4,32,512]{2,1,0:T(8,128)S(1)}, u32[]{:S(2)}, u32[]{:S(2)}) collective-permute-start(f32[4,32,512]{2,1,0:T(8,128)S(1)} %get-tuple-element.42), channel_id=1, source_target_pairs={{1,0},{0,1},{3,2},{2,3},{5,4},{4,5},{7,6},{6,7},{9,8},{8,9},{11,10... | collective-permute-start | bytes 786440 | tf_op jit(solution)/shard_map/ppermute | solution.py:561
  20.0 7.7 %collective-permute-start.7 = (f32[4,32,512]{2,1,0:T(8,128)S(1)}, f32[4,32,512]{2,1,0:T(8,128)S(1)}, u32[]{:S(2)}, u32[]{:S(2)}) collective-permute-start(f32[4,32,512]{2,1,0:T(8,128)S(1)} %get-tuple-element.39), channel_id=1, source_target_pairs={{1,2},{2,1},{5,6},{6,5},{9,10},{10,9},{13,14},{14,13},{17,18},{18,... | collective-permute-start | bytes 786440 | tf_op jit(solution)/shard_map/ppermute | solution.py:561
  41.6 2.9 %collective-permute-start.9 = (f32[16,2,8,128]{3,2,1,0:T(8,128)S(1)}, f32[16,2,8,128]{3,2,1,0:T(8,128)S(1)}, u32[]{:S(2)}, u32[]{:S(2)}) collective-permute-start(f32[16,2,8,128]{3,2,1,0:T(8,128)S(1)} %all_to_all.10.own), channel_id=1, source_target_pairs={{1,0},{0,1},{3,2},{2,3},{5,4},{4,5},{7,6},{6,7},{9,8},{8,9},{11,10... | collective-permute-start | bytes 393224 | tf_op jit(solution)/shard_map/ppermute | solution.py:561
  66.7 3.1 %collective-permute-start.10 = (f32[8,4,8,128]{3,2,1,0:T(8,128)S(1)}, f32[8,4,8,128]{3,2,1,0:T(8,128)S(1)}, u32[]{:S(2)}, u32[]{:S(2)}) collective-permute-start(f32[8,4,8,128]{3,2,1,0:T(8,128)S(1)} %all_to_all.11.own), channel_id=1, source_target_pairs={{1,0},{0,1},{3,2},{2,3},{5,4},{4,5},{7,6},{6,7},{9,8},{8,9},{11,10... | collective-permute-start | bytes 393224 | tf_op jit(solution)/shard_map/ppermute | solution.py:561

commit v12 on v10

--- a/solution.py
+++ b/solution.py
@@ -515,7 +515,9 @@
         return tuple(stepped[z] + added[z] for z in range(depth))
 
     first = term(count - 1)
-    field = lax.fori_loop(0, count - 1, body, tuple(first[z] for z in range(depth)))
+    field = tuple(first[z] for z in range(depth))
+    for i in range(count - 1):
+        field = body(i, field)
     for z in range(depth):
         coarse_new[z] = field[z]
     rows, cols = chip_part.shape[1:]

time: 72.5 us -> 72.5 us (level)
  no operation moved by 1% of the time
where the time goes in v12:
time: 72.5 us; the launch traced here: 72.2 us
  blocking collectives  27.6 us (38%)
  Pallas kernels  21.7 us (30%)
  starting transfers between devices  18.1 us (25%)
  waiting for transfers between devices  3.92 us (5%)
  between operations  0.78 us (1%)
    pallas_call x10, Pallas kernels, call(): pl.pallas_call(kernel, out_shape=outs, in_specs=in_specs, out_specs=out_s...  21.7 us
    ppermute x11, starting transfers between devices, send(): return lax.ppermute(array, AXES, route)  18.1 us
    all_to_all x1, blocking collectives, per_device(): terms = lax.all_to_all(terms, 'place', 0, 0)  15.9 us
    all_to_all x1, blocking collectives, per_device(): begun = lax.all_to_all(begun, ('group', 'chip'), 0, 0)  11.7 us
    ppermute x11, waiting for transfers between devices, send(): return lax.ppermute(array, AXES, route)  3.92 us
  transfers between devices with their start and end apart: 11, of which 5 were waited for; matrix products, arithmetic and copies ran while one was open for 0% of the time, Pallas kernels for 12%

profile of v12, /device:TPU:1, one launch (start us, length us, event | category | flops | bytes accessed | tf_op | source)
XLA Modules:
  0.0 72.2 jit_solution(1032026451755732768)
XLA Ops:
  0.7 2.4 %pack_near.1 = (f32[7,32,512]{2,1,0:T(8,128)S(1)}, f32[7,32,512]{2,1,0:T(8,128)S(1)}) custom-call(s32[4]{0:T(128)S(1)} %pad_add_fusion.where, f32[8,32,512]{2,1,0:T(8,128)} %bitcast.14, f32[8,32,512]{2,1,0:T(8,128)} %bitcast.8, f32[3,8,32,512]{3,2,1,0:T(8,128)} %vel.13, f32[8,32,512]{2,1,0:T(8,128)} %upt.13), custom_call_target="tpu_custom_call" | custom-call | flops 1 | bytes 1 | tf_op jit(solution)/shard_map/pack_near/pallas_call | solution.py:34
  3.1 4.7 %collective-permute-start = (f32[7,32,512]{2,1,0:T(8,128)S(1)}, f32[7,32,512]{2,1,0:T(8,128)S(1)}, u32[]{:S(2)}, u32[]{:S(2)}) collective-permute-start(f32[7,32,512]{2,1,0:T(8,128)S(1)} %get-tuple-element.30), channel_id=1, source_target_pairs={{1,2},{2,1},{5,6},{6,5},{9,10},{10,9},{13,14},{14,13},{17,18},{18,... | collective-permute-start | bytes 1376264 | tf_op jit(solution)/shard_map/ppermute | solution.py:563
  7.9 3.5 %collective-permute-start.1 = (f32[7,32,512]{2,1,0:T(8,128)S(1)}, f32[7,32,512]{2,1,0:T(8,128)S(1)}, u32[]{:S(2)}, u32[]{:S(2)}) collective-permute-start(f32[7,32,512]{2,1,0:T(8,128)S(1)} %get-tuple-element.31), channel_id=1, source_target_pairs={{1,130},{2,129},{5,134},{6,133},{9,138},{10,137},{13,142},{14,141}... | collective-permute-start | bytes 1376264 | tf_op jit(solution)/shard_map/ppermute | solution.py:563
  11.4 0.5 restrict.1.own
  12.1 0.7 %pack_chip.1 = (f32[5,32,512]{2,1,0:T(8,128)S(1)}, f32[5,32,512]{2,1,0:T(8,128)S(1)}, f32[4,32,512]{2,1,0:T(8,128)S(1)}) custom-call(s32[4]{0:T(128)S(1)} %pad_add_fusion.where, f32[8,32,512]{2,1,0:T(8,128)S(1)} %bitcast.16, f32[8,32,512]{2,1,0:T(8,128)S(1)} %bitcast.9, f32[3,8,32,512]{3,2,1,0:T(8,128)S(1)} %copy-done, f32[8,32,512]{2,1,0:T(8,128)S(1)} %copy-done.1), custom_call_target="tpu_custom_call" | custom-call | flops 1 | bytes 1 | tf_op jit(solution)/shard_map/pack_chip/pallas_call | solution.py:34
  12.8 0.6 collective-permute-start.6
  13.9 0.6 collective-permute-done.6.refs_4_.refs_5_
  14.5 0.9 %collective-permute-start.3 = (f32[20,8,128]{2,1,0:T(8,128)S(1)}, f32[20,8,128]{2,1,0:T(8,128)S(1)}, u32[]{:S(2)}, u32[]{:S(2)}) collective-permute-start(f32[20,8,128]{2,1,0:T(8,128)S(1)} %pad_maximum_fusion), channel_id=1, source_target_pairs={{2,0},{3,1},{0,2},{1,3},{6,4},{7,5},{4,6},{5,7},{10,8},{11,9},{8,1... | collective-permute-start | bytes 245768 | tf_op jit(solution)/shard_map/ppermute | solution.py:563
  15.5 2.4 %inner_first.1 = (f32[4,2,32,512]{3,2,1,0:T(8,128)S(1)}, f32[4,32,512]{2,1,0:T(8,128)S(1)}, f32[4,32,512]{2,1,0:T(8,128)S(1)}) custom-call(s32[4]{0:T(128)S(1)} %pad_add_fusion.where, f32[8,32,512]{2,1,0:T(8,128)S(1)} %bitcast.10, f32[3,8,32,512]{3,2,1,0:T(8,128)S(1)} %copy-done, f32[8,32,512]{2,1,0:T(8,128)S(1)} %copy-done.1, f32[8,32,512]{2,1,0:T(8,128)S(1)} %bitcast.17, ...), custom_call_target="tpu_custom_call" | custom-call | flops 1 | bytes 1 | tf_op jit(solution)/shard_map/inner_first/pallas_call | solution.py:34
  17.9 0.5 collective-permute-start.8
  18.9 1.6 %wedge_first.1 = (f32[4,32,512]{2,1,0:T(8,128)S(1)}, f32[4,32,512]{2,1,0:T(8,128)S(1)}) custom-call(s32[4]{0:T(128)S(1)} %pad_add_fusion.where, f32[8,32,512]{2,1,0:T(8,128)S(1)} %bitcast.11, f32[3,8,32,512]{3,2,1,0:T(8,128)S(1)} %copy-done, f32[8,32,512]{2,1,0:T(8,128)S(1)} %copy-done.1, f32[4,2,32,512]{3,2,1,0:T(8,128)S(1)} %get-tuple-element.36.edge, ...), custom_call_target="tpu_custom_call" | custom-call | flops 1 | bytes 1 | tf_op jit(solution)/shard_map/wedge_first/pallas_call | solution.py:34
  20.5 3.2 %collective-permute-start.7 = (f32[4,32,512]{2,1,0:T(8,128)S(1)}, f32[4,32,512]{2,1,0:T(8,128)S(1)}, u32[]{:S(2)}, u32[]{:S(2)}) collective-permute-start(f32[4,32,512]{2,1,0:T(8,128)S(1)} %get-tuple-element.39), channel_id=1, source_target_pairs={{1,2},{2,1},{5,6},{6,5},{9,10},{10,9},{13,14},{14,13},{17,18},{18,... | collective-permute-start | bytes 786440 | tf_op jit(solution)/shard_map/ppermute | solution.py:563
  23.7 1.0 %prepare.1 = (f32[25,8,8,128]{3,2,1,0:T(8,128)S(1)}, f32[8,8,128]{2,1,0:T(8,128)S(1)}) custom-call(s32[4]{0:T(128)S(1)} %pad_add_fusion.where, f32[10,8,128]{2,1,0:T(8,128)S(1)} %restrict.1.own, f32[10,8,128]{2,1,0:T(8,128)S(1)} %collective-permute-done.2.one, f32[20,8,128]{2,1,0:T(8,128)S(1)} %collective-permute-done.3.pair), custom_call_target="tpu_custom_call" | custom-call | flops 1 | bytes 1 | tf_op jit(solution)/shard_map/prepare/pallas_call | solution.py:34
  24.7 2.6 %inner_last.1 = (f32[4,2,32,512]{3,2,1,0:T(8,128)S(1)}, f32[4,32,512]{2,1,0:T(8,128)S(1)}, f32[8,128]{1,0:T(8,128)S(1)}) custom-call(s32[4]{0:T(128)S(1)} %pad_add_fusion.where, f32[8,32,512]{2,1,0:T(8,128)S(1)} %bitcast.12, f32[3,8,32,512]{3,2,1,0:T(8,128)S(1)} %copy-done, f32[8,32,512]{2,1,0:T(8,128)S(1)} %copy-done.1, ...), custom_call_target="tpu_custom_call" | custom-call | flops 1 | bytes 1 | tf_op jit(solution)/shard_map/inner_last/pallas_call | solution.py:34
  27.3 0.8 %collective-permute-done.7.halo = f32[4,32,512]{2,1,0:T(8,128)S(1)} collective-permute-done((f32[4,32,512]{2,1,0:T(8,128)S(1)}, f32[4,32,512]{2,1,0:T(8,128)S(1)}, u32[]{:S(2)}, u32[]{:S(2)}) %collective-permute-start.7) | collective-permute-done | bytes 262176 | tf_op jit(solution)/shard_map/ppermute | solution.py:563
  28.2 1.8 %wedge_last.1 = (f32[4,32,512]{2,1,0:T(8,128)S(1)}, f32[16,2,8,128]{3,2,1,0:T(8,128)S(1)}, f32[2,8,128]{2,1,0:T(8,128)S(1)}) custom-call(s32[4]{0:T(128)S(1)} %pad_add_fusion.where, f32[8,32,512]{2,1,0:T(8,128)S(1)} %bitcast.13, f32[3,8,32,512]{3,2,1,0:T(8,128)S(1)} %copy-done, f32[8,32,512]{2,1,0:T(8,128)S(1)} %copy-done.1, ...), custom_call_target="tpu_custom_call" | custom-call | flops 1 | bytes 1 | tf_op jit(solution)/shard_map/wedge_last/pallas_call | solution.py:34
  30.0 11.7 %all_to_all.10.own = f32[16,2,8,128]{3,2,1,0:T(8,128)S(1)} all-to-all(f32[16,2,8,128]{3,2,1,0:T(8,128)S(1)} %get-tuple-element.52), channel_id=1, replica_groups=mesh['group'=8,'place'=8,'chip'=2,'core'=2] {'group','chip'}, dimensions={0} | all-to-all | bytes 262144 | tf_op jit(solution)/shard_map/all_to_all | solution.py:594
  41.7 1.8 %collective-permute-start.9 = (f32[16,2,8,128]{3,2,1,0:T(8,128)S(1)}, f32[16,2,8,128]{3,2,1,0:T(8,128)S(1)}, u32[]{:S(2)}, u32[]{:S(2)}) collective-permute-start(f32[16,2,8,128]{3,2,1,0:T(8,128)S(1)} %all_to_all.10.own), channel_id=1, source_target_pairs={{1,0},{0,1},{3,2},{2,3},{5,4},{4,5},{7,6},{6,7},{9,8},{8,9},{11,10... | collective-permute-start | bytes 393224 | tf_op jit(solution)/shard_map/ppermute | solution.py:563
  43.5 1.0 %collective-permute-done.9.other = f32[16,2,8,128]{3,2,1,0:T(8,128)S(1)} collective-permute-done((f32[16,2,8,128]{3,2,1,0:T(8,128)S(1)}, f32[16,2,8,128]{3,2,1,0:T(8,128)S(1)}, u32[]{:S(2)}, u32[]{:S(2)}) %collective-permute-start.9) | collective-permute-done | bytes 131104 | tf_op jit(solution)/shard_map/ppermute | solution.py:563
  44.5 6.3 %outer.1 = f32[8,4,8,128]{3,2,1,0:T(8,128)S(1)} custom-call(s32[4]{0:T(128)S(1)} %pad_add_fusion.where, f32[25,8,8,128]{3,2,1,0:T(8,128)S(1)} %get-tuple-element.47.coef, f32[16,2,8,128]{3,2,1,0:T(8,128)S(1)} %all_to_all.10.own, f32[16,2,8,128]{3,2,1,0:T(8,128)S(1)} %collective-permute-done.9.other), custom_call_target="tpu_custom_call" | custom-call | flops 1 | bytes 1 | tf_op jit(solution)/shard_map/outer/pallas_call | solution.py:34
  50.8 15.9 %all_to_all.11.own = f32[8,4,8,128]{3,2,1,0:T(8,128)S(1)} all-to-all(f32[8,4,8,128]{3,2,1,0:T(8,128)S(1)} %outer.1), channel_id=1, replica_groups=mesh['group'=8,'place'=8,'chip'=2,'core'=2] {'place'}, dimensions={0} | all-to-all | bytes 262144 | tf_op jit(solution)/shard_map/all_to_all | solution.py:596
  66.7 2.1 %collective-permute-start.10 = (f32[8,4,8,128]{3,2,1,0:T(8,128)S(1)}, f32[8,4,8,128]{3,2,1,0:T(8,128)S(1)}, u32[]{:S(2)}, u32[]{:S(2)}) collective-permute-start(f32[8,4,8,128]{3,2,1,0:T(8,128)S(1)} %all_to_all.11.own), channel_id=1, source_target_pairs={{1,0},{0,1},{3,2},{2,3},{5,4},{4,5},{7,6},{6,7},{9,8},{8,9},{11,10... | collective-permute-start | bytes 393224 | tf_op jit(solution)/shard_map/ppermute | solution.py:563
  68.8 1.0 %collective-permute-done.10.other = f32[8,4,8,128]{3,2,1,0:T(8,128)S(1)} collective-permute-done((f32[8,4,8,128]{3,2,1,0:T(8,128)S(1)}, f32[8,4,8,128]{3,2,1,0:T(8,128)S(1)}, u32[]{:S(2)}, u32[]{:S(2)}) %collective-permute-start.10) | collective-permute-done | bytes 131104 | tf_op jit(solution)/shard_map/ppermute | solution.py:563
  69.8 2.4 %finish.1 = (f32[8,32,512]{2,1,0:T(8,128)}, f32[8,8,128]{2,1,0:T(8,128)}) custom-call(s32[4]{0:T(128)S(1)} %pad_add_fusion.where, f32[25,8,8,128]{3,2,1,0:T(8,128)S(1)} %get-tuple-element.47.coef, f32[8,4,8,128]{3,2,1,0:T(8,128)S(1)} %all_to_all.11.own, f32[8,4,8,128]{3,2,1,0:T(8,128)S(1)} %collective-permute-done.10.other, ...), custom_call_target="tpu_custom_call" | custom-call | flops 1 | bytes 1 | tf_op jit(solution)/shard_map/finish/pallas_call | solution.py:34
  (20 shorter events, 1.2 us)
Async XLA Ops:
  0.7 10.7 %copy-start = (f32[3,8,32,512]{3,2,1,0:T(8,128)S(1)}, f32[3,8,32,512]{3,2,1,0:T(8,128)}, u32[]{:S(2)}) copy-start(f32[3,8,32,512]{3,2,1,0:T(8,128)} %vel.13) | copy-start | bytes 4718596
  0.7 10.7 %copy-start.1 = (f32[8,32,512]{2,1,0:T(8,128)S(1)}, f32[8,32,512]{2,1,0:T(8,128)}, u32[]{:S(2)}) copy-start(f32[8,32,512]{2,1,0:T(8,128)} %upt.13) | copy-start | bytes 1572868
  0.7 10.7 %copy-start.3 = (f32[1,8,32,512]{3,2,1,0:T(8,128)S(1)}, f32[1,8,32,512]{3,2,1,0:T(8,128)}, u32[]{:S(2)}) copy-start(f32[1,8,32,512]{3,2,1,0:T(8,128)} %param.4) | copy-start | bytes 1572868
  3.1 8.9 %copy-start.2 = (f32[1,8,32,512]{3,2,1,0:T(8,128)S(1)}, f32[1,8,32,512]{3,2,1,0:T(8,128)}, u32[]{:S(2)}) copy-start(f32[1,8,32,512]{3,2,1,0:T(8,128)} %param.5) | copy-start | bytes 1572868
  3.1 15.3 %collective-permute-start = (f32[7,32,512]{2,1,0:T(8,128)S(1)}, f32[7,32,512]{2,1,0:T(8,128)S(1)}, u32[]{:S(2)}, u32[]{:S(2)}) collective-permute-start(f32[7,32,512]{2,1,0:T(8,128)S(1)} %get-tuple-element.30), channel_id=1, source_target_pairs={{1,2},{2,1},{5,6},{6,5},{9,10},{10,9},{13,14},{14,13},{17,18},{18,... | collective-permute-start | bytes 1376264 | tf_op jit(solution)/shard_map/ppermute | solution.py:563
  7.9 11.0 %collective-permute-start.1 = (f32[7,32,512]{2,1,0:T(8,128)S(1)}, f32[7,32,512]{2,1,0:T(8,128)S(1)}, u32[]{:S(2)}, u32[]{:S(2)}) collective-permute-start(f32[7,32,512]{2,1,0:T(8,128)S(1)} %get-tuple-element.31), channel_id=1, source_target_pairs={{1,130},{2,129},{5,134},{6,133},{9,138},{10,137},{13,142},{14,141}... | collective-permute-start | bytes 1376264 | tf_op jit(solution)/shard_map/ppermute | solution.py:563
  11.9 1.5 %collective-permute-start.2 = (f32[10,8,128]{2,1,0:T(8,128)S(1)}, f32[10,8,128]{2,1,0:T(8,128)S(1)}, u32[]{:S(2)}, u32[]{:S(2)}) collective-permute-start(f32[10,8,128]{2,1,0:T(8,128)S(1)} %restrict.1.own), channel_id=1, source_target_pairs={{1,0},{0,1},{3,2},{2,3},{5,4},{4,5},{7,6},{6,7},{9,8},{8,9},{11,10... | collective-permute-start | bytes 122888 | tf_op jit(solution)/shard_map/ppermute | solution.py:563
  12.8 1.7 %collective-permute-start.6 = (f32[4,32,512]{2,1,0:T(8,128)S(1)}, f32[4,32,512]{2,1,0:T(8,128)S(1)}, u32[]{:S(2)}, u32[]{:S(2)}) collective-permute-start(f32[4,32,512]{2,1,0:T(8,128)S(1)} %get-tuple-element.34), channel_id=1, source_target_pairs={{1,0},{0,1},{3,2},{2,3},{5,4},{4,5},{7,6},{6,7},{9,8},{8,9},{11,10... | collective-permute-start | bytes 786440 | tf_op jit(solution)/shard_map/ppermute | solution.py:563
  13.4 2.1 %collective-permute-start.4 = (f32[5,32,512]{2,1,0:T(8,128)S(1)}, f32[5,32,512]{2,1,0:T(8,128)S(1)}, u32[]{:S(2)}, u32[]{:S(2)}) collective-permute-start(f32[5,32,512]{2,1,0:T(8,128)S(1)} %get-tuple-element.32), channel_id=1, source_target_pairs={{1,0},{0,1},{3,2},{2,3},{5,4},{4,5},{7,6},{6,7},{9,8},{8,9},{11,10... | collective-permute-start | bytes 983048 | tf_op jit(solution)/shard_map/ppermute | solution.py:563
  13.5 2.0 %collective-permute-start.5 = (f32[5,32,512]{2,1,0:T(8,128)S(1)}, f32[5,32,512]{2,1,0:T(8,128)S(1)}, u32[]{:S(2)}, u32[]{:S(2)}) collective-permute-start(f32[5,32,512]{2,1,0:T(8,128)S(1)} %get-tuple-element.33), channel_id=1, source_target_pairs={{1,0},{0,1},{3,2},{2,3},{5,4},{4,5},{7,6},{6,7},{9,8},{8,9},{11,10... | collective-permute-start | bytes 983048 | tf_op jit(solution)/shard_map/ppermute | solution.py:563
  14.5 3.9 %collective-permute-start.3 = (f32[20,8,128]{2,1,0:T(8,128)S(1)}, f32[20,8,128]{2,1,0:T(8,128)S(1)}, u32[]{:S(2)}, u32[]{:S(2)}) collective-permute-start(f32[20,8,128]{2,1,0:T(8,128)S(1)} %pad_maximum_fusion), channel_id=1, source_target_pairs={{2,0},{3,1},{0,2},{1,3},{6,4},{7,5},{4,6},{5,7},{10,8},{11,9},{8,1... | collective-permute-start | bytes 245768 | tf_op jit(solution)/shard_map/ppermute | solution.py:563
  17.9 6.8 %collective-permute-start.8 = (f32[4,32,512]{2,1,0:T(8,128)S(1)}, f32[4,32,512]{2,1,0:T(8,128)S(1)}, u32[]{:S(2)}, u32[]{:S(2)}) collective-permute-start(f32[4,32,512]{2,1,0:T(8,128)S(1)} %get-tuple-element.42), channel_id=1, source_target_pairs={{1,0},{0,1},{3,2},{2,3},{5,4},{4,5},{7,6},{6,7},{9,8},{8,9},{11,10... | collective-permute-start | bytes 786440 | tf_op jit(solution)/shard_map/ppermute | solution.py:563
  20.5 7.7 %collective-permute-start.7 = (f32[4,32,512]{2,1,0:T(8,128)S(1)}, f32[4,32,512]{2,1,0:T(8,128)S(1)}, u32[]{:S(2)}, u32[]{:S(2)}) collective-permute-start(f32[4,32,512]{2,1,0:T(8,128)S(1)} %get-tuple-element.39), channel_id=1, source_target_pairs={{1,2},{2,1},{5,6},{6,5},{9,10},{10,9},{13,14},{14,13},{17,18},{18,... | collective-permute-start | bytes 786440 | tf_op jit(solution)/shard_map/ppermute | solution.py:563
  41.7 2.8 %collective-permute-start.9 = (f32[16,2,8,128]{3,2,1,0:T(8,128)S(1)}, f32[16,2,8,128]{3,2,1,0:T(8,128)S(1)}, u32[]{:S(2)}, u32[]{:S(2)}) collective-permute-start(f32[16,2,8,128]{3,2,1,0:T(8,128)S(1)} %all_to_all.10.own), channel_id=1, source_target_pairs={{1,0},{0,1},{3,2},{2,3},{5,4},{4,5},{7,6},{6,7},{9,8},{8,9},{11,10... | collective-permute-start | bytes 393224 | tf_op jit(solution)/shard_map/ppermute | solution.py:563
  66.7 3.1 %collective-permute-start.10 = (f32[8,4,8,128]{3,2,1,0:T(8,128)S(1)}, f32[8,4,8,128]{3,2,1,0:T(8,128)S(1)}, u32[]{:S(2)}, u32[]{:S(2)}) collective-permute-start(f32[8,4,8,128]{3,2,1,0:T(8,128)S(1)} %all_to_all.11.own), channel_id=1, source_target_pairs={{1,0},{0,1},{3,2},{2,3},{5,4},{4,5},{7,6},{6,7},{9,8},{8,9},{11,10... | collective-permute-start | bytes 393224 | tf_op jit(solution)/shard_map/ppermute | solution.py:563
